TPU v7x, 32 devices: a whole 2x2x4 slice. The times are simulated.
32 devices in a mesh: grp: 4 (over y, x), sfc: 8 (over z, core).
Axes of the slice: x: 2, y: 2, z: 4, core: 2. Of those that a mesh axis runs over, the one named last changes fastest.
Arguments:
- flow_fields: float32 [4, 5, 2048, 128], P('grp', None, 'sfc'), may hold values from -6 to 6
- mean_velocity: float32 [4, 3, 2048, 128], P('grp', None, 'sfc'), may hold values from -3 to 3
- cell_eddy_viscosity: float32 [4, 2048, 128], P('grp', 'sfc'), may hold values from 0.01 to 0.08
- tile_links: int32 [4, 4, 2048], P('grp', None, 'sfc'), may hold values from -1 to 2047, as said below
- tile_target: int32 [4, 2048], P('grp', 'sfc'), may hold values from 0 to 2047, as said below
- projector: float32 [64, 128], replicated, may hold values from -0.5 to 0.5
- acoustic_state: float32 [4, 4, 64, 2048], P('grp', None, None, 'sfc'), may hold values from -6 to 6
- element_face_neighbours: int32 [4, 6, 2048], P('grp', None, 'sfc'), may hold values from -1 to 2047, as said below
- face_codes: int32 [4, 6, 2048], P('grp', None, 'sfc'), may hold values from 0 to 3
Outputs:
- flow_out: float32 [4, 5, 2048, 128], P('grp', None, 'sfc')
- mean_velocity_output: float32 [4, 3, 2048, 128], P('grp', None, 'sfc')
- acoustic_out: float32 [4, 4, 64, 2048], P('grp', None, None, 'sfc')
Inputs may be any that keep to these rules, and one draw needn't show every extreme that they name: `tile_links`: each entry is -1 or a tile of the same grp index whose position differs from the tile's own by at most 16. `tile_target`: element e lies on acoustic device e // 256. A tile held at sfc index s targets an element of acoustic device s or s + 1; one flow device sends at most 160 tiles to device s + 1, and in every draw some flow device sends exactly 160. Entries of grp index 3 are not read. `element_face_neighbours`: each entry is -1 or an element whose index differs from the element's own by at most 16.
All inputs are finite; a program needn't handle non-finite values.
Results may differ from a plain program's by a relative error of at most 0.0008.
Values may be sent and summed in bfloat16 or wider, within the bound.
No kernel may reach another device: no remote copies, remote signals or barrier semaphores. Data moves between devices by JAX's collectives and lax.ppermute only.
A program may use at most 128 MiB of HBM per device.

v0:
```python
import jax
import jax.numpy as jnp
import numpy as np
from jax import lax
from jax.sharding import PartitionSpec as P

HW = 16
HE = 16
CAP = 160


ADVECT = 0.1
RELAX = 0.1
PENALTY = 1.5
ACOUSTIC_STEP = 0.08


def for_sending(x):

    def short(part):
        return part.astype(jnp.bfloat16) if part.dtype == jnp.float32 else part

    return jax.tree.map(short, x)


def with_halo(x, sides, width):
    for axis, dim in sides:
        count, length = (lax.axis_size(axis), x.shape[dim])
        up = [(i, (i + 1) % count) for i in range(count - 1)]
        down = [(j, i) for i, j in up]
        last = lax.slice_in_dim(x, length - width, length, axis=dim)
        first = lax.slice_in_dim(x, 0, width, axis=dim)
        before = lax.ppermute(last, axis, up)
        after = lax.ppermute(first, axis, down)
        x = jnp.concatenate([before, x, after], axis=dim)
    return x


def shifted(value, axis, steps):
    count = lax.axis_size(axis)
    first, last = (max(0, -steps), min(count, count - steps))
    return lax.ppermute(value, axis, [(source, source + steps) for source in range(first, last)])


def derivative_operators():
    points = np.array([-1.0, -1.0 / np.sqrt(5.0), 1.0 / np.sqrt(5.0), 1.0])
    weights = np.array(
        [
            1.0 / np.prod([points[col] - points[other] for other in range(4) if other != col])
            for col in range(4)
        ]
    )
    derivative_matrix = np.zeros((4, 4))
    for line in range(4):
        for col in range(4):
            if line != col:
                derivative_matrix[line, col] = (
                    weights[col] / weights[line] / (points[line] - points[col])
                )
        derivative_matrix[line, line] = -derivative_matrix[line].sum()
    identity = np.eye(4)
    return np.stack(
        [
            np.kron(identity, np.kron(identity, derivative_matrix)),
            np.kron(identity, np.kron(derivative_matrix, identity)),
            np.kron(derivative_matrix, np.kron(identity, identity)),
        ]
    ).astype(np.float32)


def near_take(field, links, dimension):
    return jnp.take(field, links, axis=dimension)


def flow_advance(solver_state, anchor, links, viscosity):
    amount_rows = links.shape[1]
    center = lax.slice_in_dim(solver_state, anchor, anchor + amount_rows, axis=1)
    north = near_take(solver_state, links[0], 1)
    south = near_take(solver_state, links[1], 1)
    upper = near_take(solver_state, links[2], 1)
    lower = near_take(solver_state, links[3], 1)
    east = jnp.roll(center, -1, axis=2)
    west = jnp.roll(center, 1, axis=2)
    laplace = east + west + north + south + upper + lower - 6.0 * center
    advection = (
        center[1] * (east - west) * 0.5
        + center[2] * (north - south) * 0.5
        + center[3] * (upper - lower) * 0.5
    )
    return center + viscosity * laplace - ADVECT * advection


def lamb_vector(solver_state, anchor, links):
    velocity = solver_state[1:4]
    amount_rows = links.shape[1]
    center = lax.slice_in_dim(velocity, anchor, anchor + amount_rows, axis=1)
    east = jnp.roll(center, -1, axis=2)
    west = jnp.roll(center, 1, axis=2)
    along_x = (east - west) * 0.5
    along_y = (near_take(velocity, links[0], 1) - near_take(velocity, links[1], 1)) * 0.5
    along_z = (near_take(velocity, links[2], 1) - near_take(velocity, links[3], 1)) * 0.5
    vort_x = along_y[2] - along_z[1]
    vort_y = along_z[0] - along_x[2]
    vort_z = along_x[1] - along_y[0]
    return jnp.stack(
        [
            vort_y * center[2] - vort_z * center[1],
            vort_z * center[0] - vort_x * center[2],
            vort_x * center[1] - vort_y * center[0],
        ]
    )


def project(lamb, average, projector):
    packed = jnp.concatenate([lamb, average], 0)
    mapped = jnp.einsum("ctm,nm->tcn", packed, projector, precision=lax.Precision.HIGHEST)
    return mapped.reshape(mapped.shape[0], -1).astype(jnp.bfloat16)


def face_view(grid, face):
    axis_id = face // 2
    level = 3 * (face % 2)
    if axis_id == 0:
        return grid[:, :, :, level]
    if axis_id == 1:
        return grid[:, :, level, :]
    return grid[:, level]


def face_added(grid, face, update):
    axis_id = face // 2
    level = 3 * (face % 2)
    if axis_id == 0:
        return grid.at[:, :, :, level].add(update)
    if axis_id == 1:
        return grid.at[:, :, level, :].add(update)
    return grid.at[:, level].add(update)


def turned_face(remote, turn):
    if turn == 0:
        return remote
    if turn == 1:
        return jnp.swapaxes(jnp.flip(remote, 2), 1, 2)
    if turn == 2:
        return jnp.flip(remote, (1, 2))
    return jnp.swapaxes(jnp.flip(remote, 1), 1, 2)


def acoustic_advance(solver_state, wide, links, valid, codes, source):
    derivative_matrix = jnp.asarray(derivative_operators())
    gradient_fields = jnp.einsum(
        "yws,lsb->ylwb", derivative_matrix, solver_state, precision=lax.Precision.HIGHEST
    )
    lamb_src = source[0:3]
    mean_flow = source[3:6]
    convect = (
        mean_flow[0][None] * gradient_fields[0]
        + mean_flow[1][None] * gradient_fields[1]
        + mean_flow[2][None] * gradient_fields[2]
    )
    rhs_parts = [
        -(gradient_fields[0, 1] + gradient_fields[1, 2] + gradient_fields[2, 3]) - convect[0]
    ]
    for direction in range(3):
        rhs_parts.append(
            -gradient_fields[direction, 0] - convect[1 + direction] - lamb_src[direction]
        )
    elements = solver_state.shape[2]
    rhs_grid = jnp.stack(rhs_parts).reshape(4, 4, 4, 4, elements)
    state_grid = solver_state.reshape(4, 4, 4, 4, elements)
    wide_grid = wide.reshape(4, 4, 4, 4, wide.shape[2])
    for face in range(6):
        facing = face_view(wide_grid, face ^ 1)
        remote = near_take(facing, links[face], 3)
        turned = None
        for turn in range(4):
            term = jnp.where(
                codes[face][None, None, None, :] == turn,
                turned_face(remote, turn),
                jnp.float32(0.0),
            )
            turned = term if turned is None else turned + term
        jump = jnp.where(
            valid[face][None, None, None, :], turned - face_view(state_grid, face), jnp.float32(0.0)
        )
        rhs_grid = face_added(rhs_grid, face, PENALTY * jump)
    return solver_state + ACOUSTIC_STEP * rhs_grid.reshape(4, 64, elements)


def gather_sources(rows, ids, count):
    index = jnp.where(ids < 0, count, ids).astype(jnp.int32)
    sums = (
        jnp.zeros((count + 1, rows.shape[1]), jnp.float32).at[index].add(rows.astype(jnp.float32))
    )
    counts = (
        jnp.zeros((count + 1,), jnp.float32)
        .at[index]
        .add(jnp.where(ids < 0, jnp.float32(0.0), jnp.float32(1.0)))
    )
    source = sums[:count] / jnp.maximum(counts[:count], 1.0)[:, None]
    return jnp.transpose(source.reshape(count, 6, -1), (1, 2, 0))


def localize(global_links, own_global, base, extent):
    resolved = jnp.where(global_links < 0, own_global[None, :], global_links)
    return jnp.clip(resolved - base, 0, extent - 1)


def widen_trace(field):
    return with_halo(for_sending(field), (("sfc", 2),), HE).astype(field.dtype)


def body(
    flow_fields,
    mean_velocity,
    cell_eddy_viscosity,
    tile_links,
    tile_target,
    projector,
    acoustic_state,
    element_face_neighbours,
    face_codes,
):
    groups = lax.axis_size("grp")
    group_index = lax.axis_index("grp")
    column = lax.axis_index("sfc")
    is_flow = group_index < groups - 1
    solver_state = flow_fields[0]
    average = mean_velocity[0]
    viscosity = cell_eddy_viscosity[0]
    global_links = tile_links[0]
    tile_count = solver_state.shape[1]
    first_tile = column * tile_count
    own_global = first_tile + jnp.arange(tile_count, dtype=jnp.int32)
    payloads = []
    packed = jnp.concatenate([solver_state, viscosity[None]], 0)
    wide = with_halo(packed, (("sfc", 1),), 3 * HW)
    wide_links = with_halo(global_links, (("sfc", 1),), 2 * HW)
    field = wide[:5]
    wide_visc = wide[5]
    band = tile_count + 4 * HW
    narrow = tile_count + 2 * HW
    band_global = first_tile - 2 * HW + jnp.arange(band, dtype=jnp.int32)
    links_one = localize(wide_links, band_global, first_tile - 3 * HW, tile_count + 6 * HW)
    section_one = flow_advance(field, HW, links_one, wide_visc[HW : HW + band])
    own_links = localize(
        wide_links[:, 2 * HW : 2 * HW + tile_count], own_global, first_tile - 2 * HW, band
    )
    lamb = lamb_vector(section_one, 2 * HW, own_links)
    average = (1.0 - RELAX) * average + RELAX * section_one[1:4, 2 * HW : 2 * HW + tile_count]
    payloads.append(project(lamb, average, projector))
    narrow_global = first_tile - HW + jnp.arange(narrow, dtype=jnp.int32)
    links_two = localize(wide_links[:, HW : HW + narrow], narrow_global, first_tile - 2 * HW, band)
    section_two = flow_advance(section_one, HW, links_two, wide_visc[2 * HW : 2 * HW + narrow])
    final_links = localize(
        wide_links[:, 2 * HW : 2 * HW + tile_count], own_global, first_tile - HW, narrow
    )
    lamb = lamb_vector(section_two, HW, final_links)
    solver_state = section_two[:, HW : HW + tile_count]
    average = (1.0 - RELAX) * average + RELAX * solver_state[1:4]
    payloads.append(project(lamb, average, projector))
    elements = acoustic_state.shape[3]
    targets = tile_target[0]
    owner = targets // elements
    local = targets % elements
    is_next = is_flow & (owner != column)
    own_marks = jnp.where(is_flow & (owner == column), local + 1, 0)
    next_marks = jnp.where(is_next, local + 1, 0)
    width = payloads[0].shape[1]
    sound = acoustic_state[0]
    neighbours = element_face_neighbours[0]
    valid = neighbours >= 0
    trace_links = jnp.clip(neighbours - (column * elements - HE), 0, elements + 2 * HE - 1)
    for turn in range(2):
        got_rows = lax.all_gather(payloads[turn][None], "grp", axis=0, tiled=True)
        got_marks = lax.all_gather(own_marks[None], "grp", axis=0, tiled=True)
        got_next = lax.all_gather(next_marks[None], "grp", axis=0, tiled=True)
        flags = (got_next > 0).astype(jnp.int32)
        rank = jnp.cumsum(flags, axis=1) - flags
        row_base = (jnp.arange(groups, dtype=jnp.int32) * CAP)[:, None]
        slot = jnp.where(flags > 0, row_base + rank, groups * CAP).reshape(-1)
        passed = (
            jnp.zeros((groups * CAP, width), jnp.bfloat16)
            .at[slot]
            .set(got_rows.reshape(-1, width), mode="drop")
        )
        passed_marks = (
            jnp.zeros((groups * CAP,), jnp.int32).at[slot].set(got_next.reshape(-1), mode="drop")
        )
        moved, moved_marks = shifted((passed, passed_marks), "sfc", 1)
        rows = jnp.concatenate([got_rows.reshape(-1, width), moved], 0)
        marks = jnp.concatenate([got_marks.reshape(-1), moved_marks], 0)
        source = gather_sources(rows, marks - 1, elements)
        wide_sound = widen_trace(sound)
        sound = acoustic_advance(sound, wide_sound, trace_links, valid, face_codes[0], source)
    flow_out = jnp.where(is_flow, solver_state, flow_fields[0])[None]
    mean_velocity_output = jnp.where(is_flow, average, mean_velocity[0])[None]
    acoustic_out = jnp.where(group_index == groups - 1, sound, acoustic_state[0])[None]
    return (flow_out, mean_velocity_output, acoustic_out)


def solution(mesh):
    placed = (
        P("grp", None, "sfc", None),
        P("grp", None, "sfc", None),
        P("grp", "sfc", None),
        P("grp", None, "sfc"),
        P("grp", "sfc"),
        P(),
        P("grp", None, None, "sfc"),
        P("grp", None, "sfc"),
        P("grp", None, "sfc"),
    )
    return jax.shard_map(
        body,
        mesh=mesh,
        in_specs=placed,
        out_specs=(
            P("grp", None, "sfc", None),
            P("grp", None, "sfc", None),
            P("grp", None, None, "sfc"),
        ),
        check_vma=False,
    )
```

profile of v0, /device:TPU:1, one launch (start us, length us, event | category | flops | bytes accessed | tf_op | source)
XLA Modules:
  0.0 355.5 jit_solution(16286035844007991819)
XLA Ops:
  1.5 4.6 %collective-permute-start.2 = (s32[4,32]{1,0:T(4,128)S(1)}, s32[4,32]{1,0:T(4,128)S(1)}, u32[]{:S(2)}, u32[]{:S(2)}) collective-permute-start(s32[4,32]{1,0:T(4,128)S(1)} %get-tuple-element.336), channel_id=1, source_target_pairs={{0,1},{1,2},{2,3},{3,4},{4,5},{5,6},{6,7},{8,9},{9,10},{10,11},{11... | collective-permute-start | bytes 1544 | tf_op jit(solution)/shard_map/ppermute | solution.py:33
  6.1 1.9 collective-permute-start.3
  9.8 3.6 %collective-permute-start = (f32[6,48,128]{2,1,0:T(8,128)}, f32[6,48,128]{2,1,0:T(8,128)}, u32[]{:S(2)}, u32[]{:S(2)}) collective-permute-start(f32[6,48,128]{2,1,0:T(8,128)} %get-tuple-element.273), channel_id=1, source_target_pairs={{0,1},{1,2},{2,3},{3,4},{4,5},{5,6},{6,7},{8,9},{9,10},{10,11},{11... | collective-permute-start | bytes 442376 | tf_op jit(solution)/shard_map/ppermute | solution.py:33
  13.4 1.9 collective-permute-start.1
  16.1 6.0 %all-gather.1 = s32[4,1,256]{2,1,0:T(1,128)S(1)} all-gather(s32[1,1,256]{2,1,0:T(1,128)S(1)} %fusion.165), channel_id=1, replica_groups=mesh['grp'=4,'sfc'=8] {'grp'}, dimensions={0}, use_global_device_ids=true | all-gather | bytes 5120 | tf_op jit(solution)/shard_map/all_gather | solution.py:278
  23.9 4.3 %scatter_custom_fusion = s32[640]{0:T(1024)S(1)} fusion(s32[1024]{0:T(1024)S(1)} %bitcast.727, s32[1024]{0:T(1024)S(1)} %bitcast.696, s32[]{:T(128)} %constant.409.clone.1), kind=kCustom, calls=%fused_computation.498 | custom fusion | bytes 2564 | tf_op jit(solution)/shard_map/scatter | solution.py:289
  28.2 5.7 %collective-permute-start.4 = (s32[640]{0:T(1024)S(1)}, s32[640]{0:T(1024)S(1)}, u32[]{:S(2)}, u32[]{:S(2)}) collective-permute-start(s32[640]{0:T(1024)S(1)} %scatter_custom_fusion), channel_id=1, source_target_pairs={{0,1},{1,2},{2,3},{3,4},{4,5},{5,6},{6,7},{8,9},{9,10},{10,11},{11... | collective-permute-start | bytes 7688 | tf_op jit(solution)/shard_map/ppermute | solution.py:42
  49.2 6.0 %all-gather = s32[4,1,256]{2,1,0:T(1,128)S(1)} all-gather(s32[1,1,256]{2,1,0:T(1,128)S(1)} %get-tuple-element.232), channel_id=1, replica_groups=mesh['grp'=4,'sfc'=8] {'grp'}, dimensions={0}, use_global_device_ids=true | all-gather | bytes 5120 | tf_op jit(solution)/shard_map/all_gather | solution.py:277
  56.7 3.9 %collective-permute-start.6 = (bf16[4,64,16]{2,1,0:T(8,128)(2,1)S(1)}, bf16[4,64,16]{2,1,0:T(8,128)(2,1)S(1)}, u32[]{:S(2)}, u32[]{:S(2)}) collective-permute-start(bf16[4,64,16]{2,1,0:T(8,128)(2,1)S(1)} %get-tuple-element.308), channel_id=1, source_target_pairs={{0,1},{1,2},{2,3},{3,4},{4,5},{5,6},{6,7},{8,9},{9,10},{10,11},{11... | collective-permute-start | bytes 24584 | tf_op jit(solution)/shard_map/ppermute | solution.py:33
  60.6 1.9 collective-permute-start.7
  67.6 12.7 %scatter_custom_fusion.3 = f32[257]{0:T(512)S(1)} fusion(s32[1664]{0:T(1024)S(1)} %fusion.151, f32[1664]{0:T(1024)S(1)} %fusion.150, f32[]{:T(128)} %constant.421.clone.1), kind=kCustom, calls=%fused_computation.534 | custom fusion | flops 1664 | bytes 1032 | tf_op jit(solution)/shard_map/scatter-add | solution.py:199
  82.5 3.4 gather_fusion.12
  90.9 3.4 gather_fusion.13
  99.3 3.4 gather_fusion.14
  105.9 3.4 gather_fusion.15
  113.6 3.4 gather_fusion.16
  121.9 3.4 gather_fusion.17
  125.3 2.0 copy.2772
  139.3 2.4 gather_fusion
  141.8 2.4 gather_fusion.1
  144.2 2.4 gather_fusion.2
  146.6 2.4 gather_fusion.3
  149.1 4.4 %fusion.13 = f32[5,320,128]{2,1,0:T(8,128)S(1)} fusion(f32[320,5,128]{2,1,0:T(8,128)} %gather_fusion.3, f32[320,5,128]{2,1,0:T(8,128)} %gather_fusion.2, f32[320,5,128]{2,1,0:T(8,128)} %gather_fusion.1, f32[320,5,128]{2,1,0:T(8,128)} %gather_fusion, f32[6,352,128]{2,1,0:T(8,128)S(1)} %pad_maximum_fusion, f32[5,320,127]{2,1,0:T(8,128)} %get-tuple-element.257, ...), kind=kLoop, calls=%fused_computation.56 | loop fusion | flops 5120000 | bytes 7210240 | tf_op jit(solution)/shard_map/sub | solution.py:90
  158.1 2.4 gather_fusion.4
  160.5 2.4 gather_fusion.5
  162.9 2.4 gather_fusion.6
  165.3 2.4 gather_fusion.7
  167.7 4.2 %fusion.36 = f32[5,288,128]{2,1,0:T(8,128)S(1)} fusion(f32[288,5,128]{2,1,0:T(8,128)} %gather_fusion.7, f32[288,5,128]{2,1,0:T(8,128)} %gather_fusion.6, f32[288,5,128]{2,1,0:T(8,128)} %gather_fusion.5, f32[288,5,128]{2,1,0:T(8,128)} %gather_fusion.4, f32[5,320,128]{2,1,0:T(8,128)S(1)} %fusion.13, f32[5,288,127]{2,1,0:T(8,128)} %get-tuple-element.270, ...), kind=kLoop, calls=%fused_computation.91 | loop fusion | flops 4608000 | bytes 6489216 | tf_op jit(solution)/shard_map/sub | solution.py:90
  182.5 2.1 fusion.51
  186.6 9.4 %all_gather.17 = bf16[4,256,384]{2,1,0:T(8,128)(2,1)S(1)} all-gather(bf16[1,256,384]{2,1,0:T(8,128)(2,1)S(1)} %copy.2796), channel_id=1, replica_groups=mesh['grp'=4,'sfc'=8] {'grp'}, dimensions={0}, use_global_device_ids=true | all-gather | bytes 983040 | tf_op jit(solution)/shard_map/all_gather | solution.py:276
  196.0 5.9 %scatter_custom_fusion.4 = bf16[640,384]{1,0:T(8,128)(2,1)} fusion(s32[1024]{0:T(1024)} %bitcast.728, bf16[1024,384]{1,0:T(8,128)(2,1)S(1)} %bitcast.672, bf16[]{:T(256)} %constant.430.clone.1), kind=kCustom, calls=%fused_computation.159 | custom fusion | bytes 492032 | tf_op jit(solution)/shard_map/scatter | solution.py:286
  201.8 5.0 %collective-permute-start.8 = (bf16[640,384]{1,0:T(8,128)(2,1)}, bf16[640,384]{1,0:T(8,128)(2,1)}, u32[]{:S(2)}, u32[]{:S(2)}) collective-permute-start(bf16[640,384]{1,0:T(8,128)(2,1)} %scatter_custom_fusion.4), channel_id=1, source_target_pairs={{0,1},{1,2},{2,3},{3,4},{4,5},{5,6},{6,7},{8,9},{9,10},{10,11},{11... | collective-permute-start | bytes 1474568 | tf_op jit(solution)/shard_map/ppermute | solution.py:42
  209.1 2.0 gather_fusion.11
  217.4 11.5 %all_gather.16 = bf16[4,256,384]{2,1,0:T(8,128)(2,1)} all-gather(bf16[1,256,384]{2,1,0:T(8,128)(2,1)S(1)} %copy.2704), channel_id=1, replica_groups=mesh['grp'=4,'sfc'=8] {'grp'}, dimensions={0}, use_global_device_ids=true | all-gather | bytes 983040 | tf_op jit(solution)/shard_map/all_gather | solution.py:276
  228.9 5.9 %scatter_custom_fusion.1 = bf16[640,384]{1,0:T(8,128)(2,1)S(1)} fusion(s32[1024]{0:T(1024)} %bitcast.729, bf16[1024,384]{1,0:T(8,128)(2,1)} %bitcast.674, bf16[]{:T(256)} %constant.430.clone.1), kind=kCustom, calls=%fused_computation.161 | custom fusion | bytes 492032 | tf_op jit(solution)/shard_map/scatter | solution.py:286
  234.8 4.4 %collective-permute-start.5 = (bf16[640,384]{1,0:T(8,128)(2,1)S(1)}, bf16[640,384]{1,0:T(8,128)(2,1)S(1)}, u32[]{:S(2)}, u32[]{:S(2)}) collective-permute-start(bf16[640,384]{1,0:T(8,128)(2,1)S(1)} %scatter_custom_fusion.1), channel_id=1, source_target_pairs={{0,1},{1,2},{2,3},{3,4},{4,5},{5,6},{6,7},{8,9},{9,10},{10,11},{11... | collective-permute-start | bytes 1474568 | tf_op jit(solution)/shard_map/ppermute | solution.py:42
  240.8 14.9 %scatter_custom_fusion.5 = f32[257,384]{1,0:T(8,128)S(1)} fusion(s32[1664]{0:T(1024)} %copy-done.88, bf16[640,384]{1,0:T(8,128)(2,1)} %collective-permute-done.8, bf16[]{:T(256)} %constant.486, bf16[1024,384]{1,0:T(8,128)(2,1)S(1)} %bitcast.673, f32[]{:T(128)} %constant.421.clone.1), kind=kCustom, calls=%fused_computation.34 | custom fusion | flops 3194880 | bytes 1673728 | tf_op jit(solution)/shard_map/scatter-add | solution.py:194
  255.7 15.3 %scatter_custom_fusion.2 = f32[257,384]{1,0:T(8,128)S(1)} fusion(s32[1664]{0:T(1024)} %copy-done.88, bf16[640,384]{1,0:T(8,128)(2,1)S(1)} %collective-permute-done.5, bf16[]{:T(256)} %constant.486, bf16[1024,384]{1,0:T(8,128)(2,1)} %bitcast.675, f32[]{:T(128)} %constant.421.clone.1), kind=kCustom, calls=%fused_computation.36 | custom fusion | flops 3194880 | bytes 1673728 | tf_op jit(solution)/shard_map/scatter-add | solution.py:194
  279.0 1.9 collective-permute-start.9
  281.0 2.4 collective-permute-start.10
  288.7 4.0 %gather_fusion.27 = f32[256,4,4,4]{3,2,1,0:T(4,128)S(1)} fusion(f32[4,4,4,288]{2,1,3,0:T(4,128)} %copy.2869, s32[1024]{0:T(1024)} %copy-done.75), kind=kCustom, calls=%fused_computation.24.clone | custom fusion | bytes 132096 | tf_op jit(solution)/shard_map/jit(_take)/gather | solution.py:72
  297.6 4.0 %gather_fusion.26 = f32[256,4,4,4]{3,2,1,0:T(4,128)S(1)} fusion(f32[4,4,4,288]{2,1,3,0:T(4,128)} %copy.2859, s32[1024]{0:T(1024)} %copy-done.74), kind=kCustom, calls=%fused_computation.23.clone | custom fusion | bytes 132096 | tf_op jit(solution)/shard_map/jit(_take)/gather | solution.py:72
  307.1 4.0 %gather_fusion.25 = f32[256,4,4,4]{3,2,1,0:T(4,128)S(1)} fusion(f32[4,4,4,288]{2,1,3,0:T(4,128)} %copy.2848, s32[1024]{0:T(1024)} %copy-done.73), kind=kCustom, calls=%fused_computation.22.clone | custom fusion | bytes 132096 | tf_op jit(solution)/shard_map/jit(_take)/gather | solution.py:72
  315.4 2.7 copy.2836
  318.1 4.0 %gather_fusion.24 = f32[256,4,4,4]{3,2,1,0:T(4,128)S(1)} fusion(f32[4,4,4,288]{2,1,3,0:T(4,128)} %copy.2836, s32[1024]{0:T(1024)} %copy-done.72), kind=kCustom, calls=%fused_computation.21.clone | custom fusion | bytes 132096 | tf_op jit(solution)/shard_map/jit(_take)/gather | solution.py:72
  327.3 2.1 copy.2901
  329.4 4.0 %gather_fusion.23 = f32[256,4,4,4]{3,2,1,0:T(4,128)S(1)} fusion(f32[4,4,4,288]{2,1,3,0:T(4,128)} %bitcast.676, s32[1024]{0:T(1024)} %copy-done.71), kind=kCustom, calls=%fused_computation.20.clone | custom fusion | bytes 132096 | tf_op jit(solution)/shard_map/jit(_take)/gather | solution.py:72
  337.6 4.0 %gather_fusion.22 = f32[256,4,4,4]{3,2,1,0:T(4,128)S(1)} fusion(f32[4,4,4,288]{2,1,3,0:T(4,128)} %bitcast.677, s32[1024]{0:T(1024)} %copy-done.70), kind=kCustom, calls=%fused_computation.19.clone | custom fusion | bytes 132096 | tf_op jit(solution)/shard_map/jit(_take)/gather | solution.py:72
  (582 shorter events, 139.4 us)
Async XLA Ops:
  0.6 184.8 %copy-start = (f32[64,128]{1,0:T(8,128)S(1)}, f32[64,128]{1,0:T(8,128)}, u32[]{:S(2)}) copy-start(f32[64,128]{1,0:T(8,128)} %param.50) | copy-start | bytes 98308
  0.6 45.4 %copy-start.66 = (f32[3,64,64,1]{2,1,3,0:T(8,128)S(1)}, f32[3,64,64,1]{2,1,3,0:T(8,128)}, u32[]{:S(2)}) copy-start(f32[3,64,64,1]{2,1,3,0:T(8,128)} %constant.445) | copy-start | bytes 147460
  0.7 45.3 %copy-start.3 = (f32[1,4,64,256]{3,2,1,0:T(8,128)S(1)}, f32[1,4,64,256]{3,2,1,0:T(8,128)}, u32[]{:S(2)}) copy-start(f32[1,4,64,256]{3,2,1,0:T(8,128)} %param.51) | copy-start | bytes 786436
  0.7 38.5 %copy-start.69 = (s32[1,6,256]{2,0,1:T(1,128)S(1)}, s32[1,6,256]{2,0,1:T(1,128)}, u32[]{:S(2)}) copy-start(s32[1,6,256]{2,0,1:T(1,128)} %param.52) | copy-start | bytes 18436
  1.5 55.2 %collective-permute-start.2 = (s32[4,32]{1,0:T(4,128)S(1)}, s32[4,32]{1,0:T(4,128)S(1)}, u32[]{:S(2)}, u32[]{:S(2)}) collective-permute-start(s32[4,32]{1,0:T(4,128)S(1)} %get-tuple-element.336), channel_id=1, source_target_pairs={{0,1},{1,2},{2,3},{3,4},{4,5},{5,6},{6,7},{8,9},{9,10},{10,11},{11... | collective-permute-start | bytes 1544 | tf_op jit(solution)/shard_map/ppermute | solution.py:33
  6.1 54.5 %collective-permute-start.3 = (s32[4,32]{1,0:T(4,128)S(1)}, s32[4,32]{1,0:T(4,128)S(1)}, u32[]{:S(2)}, u32[]{:S(2)}) collective-permute-start(s32[4,32]{1,0:T(4,128)S(1)} %get-tuple-element.337), channel_id=1, source_target_pairs={{1,0},{2,1},{3,2},{4,3},{5,4},{6,5},{7,6},{9,8},{10,9},{11,10},{12... | collective-permute-start | bytes 1544 | tf_op jit(solution)/shard_map/ppermute | solution.py:34
  8.0 39.8 %copy-start.89 = (s32[1,6,256]{2,0,1:T(1,128)S(1)}, s32[1,6,256]{2,0,1:T(1,128)}, u32[]{:S(2)}) copy-start(s32[1,6,256]{2,0,1:T(1,128)} %param.53) | copy-start | bytes 18436
  9.8 124.1 %collective-permute-start = (f32[6,48,128]{2,1,0:T(8,128)}, f32[6,48,128]{2,1,0:T(8,128)}, u32[]{:S(2)}, u32[]{:S(2)}) collective-permute-start(f32[6,48,128]{2,1,0:T(8,128)} %get-tuple-element.273), channel_id=1, source_target_pairs={{0,1},{1,2},{2,3},{3,4},{4,5},{5,6},{6,7},{8,9},{9,10},{10,11},{11... | collective-permute-start | bytes 442376 | tf_op jit(solution)/shard_map/ppermute | solution.py:33
  13.4 120.4 %collective-permute-start.1 = (f32[6,48,128]{2,1,0:T(8,128)}, f32[6,48,128]{2,1,0:T(8,128)}, u32[]{:S(2)}, u32[]{:S(2)}) collective-permute-start(f32[6,48,128]{2,1,0:T(8,128)} %get-tuple-element.274), channel_id=1, source_target_pairs={{1,0},{2,1},{3,2},{4,3},{5,4},{6,5},{7,6},{9,8},{10,9},{11,10},{12... | collective-permute-start | bytes 442376 | tf_op jit(solution)/shard_map/ppermute | solution.py:34
  28.2 39.3 %collective-permute-start.4 = (s32[640]{0:T(1024)S(1)}, s32[640]{0:T(1024)S(1)}, u32[]{:S(2)}, u32[]{:S(2)}) collective-permute-start(s32[640]{0:T(1024)S(1)} %scatter_custom_fusion), channel_id=1, source_target_pairs={{0,1},{1,2},{2,3},{3,4},{4,5},{5,6},{6,7},{8,9},{9,10},{10,11},{11... | collective-permute-start | bytes 7688 | tf_op jit(solution)/shard_map/ppermute | solution.py:42
  34.6 28.0 %copy-start.68 = (s32[1,4,256]{2,1,0:T(4,128)S(1)}, s32[1,4,256]{2,1,0:T(4,128)}, u32[]{:S(2)}) copy-start(s32[1,4,256]{2,1,0:T(4,128)} %param.48) | copy-start | bytes 12292
  38.1 17.8 %copy-start.5 = (f32[1,4,64,256]{3,1,2,0:T(4,128)}, f32[1,4,64,256]{3,1,2,0:T(4,128)S(1)}, u32[]{:S(2)}) copy-start(f32[1,4,64,256]{3,1,2,0:T(4,128)S(1)} %copy.2782) | copy-start | bytes 786436
  39.2 48.6 %copy-start.123 = (pred[256]{0:T(512)(128)(4,1)}, pred[256]{0:T(512)(128)(4,1)S(1)}, u32[]{:S(2)}) copy-start(pred[256]{0:T(512)(128)(4,1)S(1)} %get-tuple-element.371) | copy-start | bytes 772
  39.2 91.1 %copy-start.86 = (pred[256]{0:T(512)(128)(4,1)}, pred[256]{0:T(512)(128)(4,1)S(1)}, u32[]{:S(2)}) copy-start(pred[256]{0:T(512)(128)(4,1)S(1)} %get-tuple-element.370) | copy-start | bytes 772
  39.3 65.2 %copy-start.84 = (pred[256]{0:T(512)(128)(4,1)}, pred[256]{0:T(512)(128)(4,1)S(1)}, u32[]{:S(2)}) copy-start(pred[256]{0:T(512)(128)(4,1)S(1)} %get-tuple-element.369) | copy-start | bytes 772
  39.3 71.8 %copy-start.82 = (pred[256]{0:T(512)(128)(4,1)}, pred[256]{0:T(512)(128)(4,1)S(1)}, u32[]{:S(2)}) copy-start(pred[256]{0:T(512)(128)(4,1)S(1)} %get-tuple-element.368) | copy-start | bytes 772
  41.2 77.6 %copy-start.80 = (pred[256]{0:T(512)(128)(4,1)}, pred[256]{0:T(512)(128)(4,1)S(1)}, u32[]{:S(2)}) copy-start(pred[256]{0:T(512)(128)(4,1)S(1)} %get-tuple-element.367) | copy-start | bytes 772
  47.7 34.8 %copy-start.70 = (s32[1024]{0:T(1024)}, s32[1024]{0:T(1024)S(1)}, u32[]{:S(2)}) copy-start(s32[1024]{0:T(1024)S(1)} %pad_clamp_fusion.9) | copy-start | bytes 12292
  48.5 39.3 %copy-start.120 = (pred[256]{0:T(512)(128)(4,1)}, pred[256]{0:T(512)(128)(4,1)S(1)}, u32[]{:S(2)}) copy-start(pred[256]{0:T(512)(128)(4,1)S(1)} %get-tuple-element.321) | copy-start | bytes 772
  48.5 84.0 %copy-start.97 = (pred[256]{0:T(512)(128)(4,1)}, pred[256]{0:T(512)(128)(4,1)S(1)}, u32[]{:S(2)}) copy-start(pred[256]{0:T(512)(128)(4,1)S(1)} %get-tuple-element.206) | copy-start | bytes 772
  49.1 41.8 %copy-start.71 = (s32[1024]{0:T(1024)}, s32[1024]{0:T(1024)S(1)}, u32[]{:S(2)}) copy-start(s32[1024]{0:T(1024)S(1)} %pad_clamp_fusion.8) | copy-start | bytes 12292
  49.1 50.2 %copy-start.72 = (s32[1024]{0:T(1024)}, s32[1024]{0:T(1024)S(1)}, u32[]{:S(2)}) copy-start(s32[1024]{0:T(1024)S(1)} %pad_clamp_fusion.7) | copy-start | bytes 12292
  49.1 56.7 %copy-start.73 = (s32[1024]{0:T(1024)}, s32[1024]{0:T(1024)S(1)}, u32[]{:S(2)}) copy-start(s32[1024]{0:T(1024)S(1)} %pad_clamp_fusion.6) | copy-start | bytes 12292
  49.2 64.5 %copy-start.74 = (s32[1024]{0:T(1024)}, s32[1024]{0:T(1024)S(1)}, u32[]{:S(2)}) copy-start(s32[1024]{0:T(1024)S(1)} %pad_clamp_fusion.5) | copy-start | bytes 12292
  49.2 72.6 %copy-start.75 = (s32[1024]{0:T(1024)}, s32[1024]{0:T(1024)S(1)}, u32[]{:S(2)}) copy-start(s32[1024]{0:T(1024)S(1)} %pad_clamp_fusion.4) | copy-start | bytes 12292
  56.7 24.2 %collective-permute-start.6 = (bf16[4,64,16]{2,1,0:T(8,128)(2,1)S(1)}, bf16[4,64,16]{2,1,0:T(8,128)(2,1)S(1)}, u32[]{:S(2)}, u32[]{:S(2)}) collective-permute-start(bf16[4,64,16]{2,1,0:T(8,128)(2,1)S(1)} %get-tuple-element.308), channel_id=1, source_target_pairs={{0,1},{1,2},{2,3},{3,4},{4,5},{5,6},{6,7},{8,9},{9,10},{10,11},{11... | collective-permute-start | bytes 24584 | tf_op jit(solution)/shard_map/ppermute | solution.py:33
  60.6 20.3 %collective-permute-start.7 = (bf16[4,64,16]{2,1,0:T(8,128)(2,1)S(1)}, bf16[4,64,16]{2,1,0:T(8,128)(2,1)S(1)}, u32[]{:S(2)}, u32[]{:S(2)}) collective-permute-start(bf16[4,64,16]{2,1,0:T(8,128)(2,1)S(1)} %get-tuple-element.309), channel_id=1, source_target_pairs={{1,0},{2,1},{3,2},{4,3},{5,4},{6,5},{7,6},{9,8},{10,9},{11,10},{12... | collective-permute-start | bytes 24584 | tf_op jit(solution)/shard_map/ppermute | solution.py:34
  67.6 20.2 %copy-start.88 = (s32[1664]{0:T(1024)}, s32[1664]{0:T(1024)S(1)}, u32[]{:S(2)}) copy-start(s32[1664]{0:T(1024)S(1)} %fusion.151) | copy-start | bytes 19972
  121.8 10.7 %copy-start.99 = (pred[256]{0:T(512)(128)(4,1)S(1)}, pred[256]{0:T(512)(128)(4,1)}, u32[]{:S(2)}) copy-start(pred[256]{0:T(512)(128)(4,1)} %get-tuple-element.204) | copy-start | bytes 772
  121.8 10.6 %copy-start.101 = (pred[256]{0:T(512)(128)(4,1)S(1)}, pred[256]{0:T(512)(128)(4,1)}, u32[]{:S(2)}) copy-start(pred[256]{0:T(512)(128)(4,1)} %get-tuple-element.205) | copy-start | bytes 772
  121.8 10.6 %copy-start.103 = (pred[256]{0:T(512)(128)(4,1)S(1)}, pred[256]{0:T(512)(128)(4,1)}, u32[]{:S(2)}) copy-start(pred[256]{0:T(512)(128)(4,1)} %get-tuple-element.324) | copy-start | bytes 772
  121.8 11.4 %copy-start.107 = (pred[256]{0:T(512)(128)(4,1)S(1)}, pred[256]{0:T(512)(128)(4,1)}, u32[]{:S(2)}) copy-start(pred[256]{0:T(512)(128)(4,1)} %get-tuple-element.196) | copy-start | bytes 772
  121.8 12.0 %copy-start.7 = (f32[1,5,256,128]{3,2,1,0:T(8,128)S(1)}, f32[1,5,256,128]{3,2,1,0:T(8,128)}, u32[]{:S(2)}) copy-start(f32[1,5,256,128]{3,2,1,0:T(8,128)} %param.45) | copy-start | bytes 1966084
  121.8 12.0 %copy-start.31 = (f32[1,256,128]{2,1,0:T(8,128)S(1)}, f32[1,256,128]{2,1,0:T(8,128)}, u32[]{:S(2)}) copy-start(f32[1,256,128]{2,1,0:T(8,128)} %param.47) | copy-start | bytes 393220
  153.5 28.9 %copy-start.1 = (f32[5,320,128]{2,1,0:T(8,128)}, f32[5,320,128]{2,1,0:T(8,128)S(1)}, u32[]{:S(2)}) copy-start(f32[5,320,128]{2,1,0:T(8,128)S(1)} %fusion.13) | copy-start | bytes 2457604
  185.3 21.6 %slice-start = ((f32[5,320,128]{2,1,0:T(8,128)}), f32[3,320,128]{2,1,0:T(8,128)S(1)}, s32[]{:S(2)}) async-start(f32[5,320,128]{2,1,0:T(8,128)} %copy-done.1), calls=%async_computation | async-start | bytes 983040 | tf_op jit(solution)/shard_map/slice | solution.py:94
  201.8 11.6 %copy-start.136 = (pred[256]{0:T(512)(128)(4,1)S(1)}, pred[256]{0:T(512)(128)(4,1)}, u32[]{:S(2)}) copy-start(pred[256]{0:T(512)(128)(4,1)} %get-tuple-element.372) | copy-start | bytes 772
  201.8 11.7 %copy-start.137 = (pred[256]{0:T(512)(128)(4,1)S(1)}, pred[256]{0:T(512)(128)(4,1)}, u32[]{:S(2)}) copy-start(pred[256]{0:T(512)(128)(4,1)} %get-tuple-element.373) | copy-start | bytes 772
  201.8 39.0 %collective-permute-start.8 = (bf16[640,384]{1,0:T(8,128)(2,1)}, bf16[640,384]{1,0:T(8,128)(2,1)}, u32[]{:S(2)}, u32[]{:S(2)}) collective-permute-start(bf16[640,384]{1,0:T(8,128)(2,1)} %scatter_custom_fusion.4), channel_id=1, source_target_pairs={{0,1},{1,2},{2,3},{3,4},{4,5},{5,6},{6,7},{8,9},{9,10},{10,11},{11... | collective-permute-start | bytes 1474568 | tf_op jit(solution)/shard_map/ppermute | solution.py:42
  215.5 23.8 %copy-start.45 = (f32[4,4,4,256]{3,1,2,0:T(4,128)S(1)}, f32[4,4,4,256]{3,1,2,0:T(4,128)}, u32[]{:S(2)}) copy-start(f32[4,4,4,256]{3,1,2,0:T(4,128)} %rev.127) | copy-start | bytes 196612
  215.5 23.8 %copy-start.119 = (pred[256]{0:T(512)(128)(4,1)S(1)}, pred[256]{0:T(512)(128)(4,1)}, u32[]{:S(2)}) copy-start(pred[256]{0:T(512)(128)(4,1)} %get-tuple-element.210) | copy-start | bytes 772
  215.5 24.4 %copy-start.8 = (f32[1,5,256,128]{3,2,1,0:T(8,128)S(1)}, f32[1,5,256,128]{3,2,1,0:T(8,128)}, u32[]{:S(2)}) copy-start(f32[1,5,256,128]{3,2,1,0:T(8,128)} %param.45) | copy-start | bytes 1966084
  234.8 20.9 %collective-permute-start.5 = (bf16[640,384]{1,0:T(8,128)(2,1)S(1)}, bf16[640,384]{1,0:T(8,128)(2,1)S(1)}, u32[]{:S(2)}, u32[]{:S(2)}) collective-permute-start(bf16[640,384]{1,0:T(8,128)(2,1)S(1)} %scatter_custom_fusion.1), channel_id=1, source_target_pairs={{0,1},{1,2},{2,3},{3,4},{4,5},{5,6},{6,7},{8,9},{9,10},{10,11},{11... | collective-permute-start | bytes 1474568 | tf_op jit(solution)/shard_map/ppermute | solution.py:42
  240.8 30.2 %copy-start.135 = (f32[256]{0:T(256)S(1)}, f32[256]{0:T(256)}, u32[]{:S(2)}) copy-start(f32[256]{0:T(256)} %slice_maximum_fusion) | copy-start | bytes 3076
  255.7 15.7 %copy-start.9 = (f32[3,4,64,256]{3,2,1,0:T(8,128)S(1)}, f32[3,4,64,256]{3,2,1,0:T(8,128)}, u32[]{:S(2)}) copy-start(f32[3,4,64,256]{3,2,1,0:T(8,128)} %convolution_bitcast_fusion.1) | copy-start | bytes 2359300
  279.0 5.8 %collective-permute-start.9 = (bf16[4,64,16]{2,1,0:T(8,128)(2,1)S(1)}, bf16[4,64,16]{2,1,0:T(8,128)(2,1)S(1)}, u32[]{:S(2)}, u32[]{:S(2)}) collective-permute-start(bf16[4,64,16]{2,1,0:T(8,128)(2,1)S(1)} %get-tuple-element.306), channel_id=1, source_target_pairs={{0,1},{1,2},{2,3},{3,4},{4,5},{5,6},{6,7},{8,9},{9,10},{10,11},{11... | collective-permute-start | bytes 24584 | tf_op jit(solution)/shard_map/ppermute | solution.py:33
  281.0 5.6 %collective-permute-start.10 = (bf16[4,64,16]{2,1,0:T(8,128)(2,1)S(1)}, bf16[4,64,16]{2,1,0:T(8,128)(2,1)S(1)}, u32[]{:S(2)}, u32[]{:S(2)}) collective-permute-start(bf16[4,64,16]{2,1,0:T(8,128)(2,1)S(1)} %get-tuple-element.307), channel_id=1, source_target_pairs={{1,0},{2,1},{3,2},{4,3},{5,4},{6,5},{7,6},{9,8},{10,9},{11,10},{12... | collective-permute-start | bytes 24584 | tf_op jit(solution)/shard_map/ppermute | solution.py:34
  337.6 10.9 %copy-start.28 = (f32[256,4,4,4]{0,2,3,1:T(4,128)S(1)}, f32[256,4,4,4]{0,2,3,1:T(4,128)}, u32[]{:S(2)}) copy-start(f32[256,4,4,4]{0,2,3,1:T(4,128)} %copy.2837) | copy-start | bytes 196612
  (112 other events, 585.1 us)
where the time goes:
time: 362 us; the launch traced here: 356 us
  local copies, waits for them, and re-layouts  179 us (49%)
  other arithmetic  96.2 us (27%)
  starting transfers between devices  37.4 us (10%)
  blocking collectives  33 us (9%)
  matrix products  4.44 us (1%)
  between operations  3.94 us (1%)
    gather x40, local copies, waits for them, and re-layouts, near_take(): return jnp.take(field, links, axis=dimension)  93.3 us
    scatter-add x2, other arithmetic, gather_sources(): jnp.zeros((count + 1, rows.shape[1]), jnp.float32).at[index]  30.2 us
    all_gather x2, blocking collectives, body(): got_rows = lax.all_gather(payloads[turn][None], 'grp', axis=0, tiled=True)  20.9 us
    ppermute x3, starting transfers between devices, shifted(): lax.ppermute(value, axis, [(source, source + steps) for source in range(f...  15.1 us
    ppermute x4, starting transfers between devices, with_halo(): before = lax.ppermute(last, axis, up)  14.1 us
    scatter-add x1, other arithmetic, gather_sources(): counts = jnp.zeros((count + 1,), jnp.float32).at[index].add(jnp.where(ids...  12.7 us
    scatter x2, local copies, waits for them, and re-layouts, body(): passed = jnp.zeros((groups * CAP, width), jnp.bfloat16).at[slot].set(got_...  11.8 us
    sub x2, other arithmetic, flow_advance(): return center + viscosity * laplace - ADVECT * advection  8.61 us
  transfers between devices with their start and end apart: 11, of which 1 were waited for; matrix products, arithmetic and copies ran while one was open for 36% of the time, Pallas kernels for 0%

commit v1 on v0

v1 whole, which is shorter than its diff:
```python
import jax
import jax.numpy as jnp
import numpy as np
from jax import lax
from jax.experimental import pallas as pl
from jax.experimental.pallas import tpu as pltpu
from jax.sharding import PartitionSpec as P

HW = 16
HE = 16

ADVECT = 0.1
RELAX = 0.1
PENALTY = 1.5
ACOUSTIC_STEP = 0.08

LANES = 128
EDGE = 3 * HW
FIELD_ORDER = (1, 2, 3, 0, 4)
BASE = 32.0
EXTRA = 16
VMEM_LIMIT = 48 * 1024 * 1024

F32 = jnp.float32
BF16 = jnp.bfloat16


def lobatto_matrix():
    points = np.array([-1.0, -1.0 / np.sqrt(5.0), 1.0 / np.sqrt(5.0), 1.0])
    weights = np.array(
        [
            1.0 / np.prod([points[col] - points[other] for other in range(4) if other != col])
            for col in range(4)
        ]
    )
    matrix = np.zeros((4, 4))
    for line in range(4):
        for col in range(4):
            if line != col:
                matrix[line, col] = weights[col] / weights[line] / (points[line] - points[col])
        matrix[line, line] = -matrix[line].sum()
    return matrix.astype(np.float32)


def face_nodes(face):
    axis, level = face // 2, 3 * (face % 2)
    nodes = []
    for second in range(4):
        for first in range(4):
            coords = [first, second]
            coords.insert(axis, level)
            nodes.append(coords[0] + 4 * coords[1] + 16 * coords[2])
    return nodes


def turned_position(turn, position):
    a, b = position % 4, position // 4
    a, b = ((a, b), (3 - b, a), (3 - a, 3 - b), (b, 3 - a))[turn]
    return a + 4 * b


def split_parts(x):
    high = x.astype(BF16)
    return high, (x - high.astype(F32)).astype(BF16)


def dot(a, b):
    return jnp.dot(a, b, preferred_element_type=F32)


def dot_t(a, b):
    return lax.dot_general(a, b, (((1,), (1,)), ((), ())), preferred_element_type=F32)


def pack_kernel(meta, flow, visc, links, sound, first_out, last_out):
    is_flow, even = meta[0] == 1, meta[1] == 1
    tiles = flow.shape[1]
    elements = sound.shape[2]
    nodes = sound.shape[1]
    off_a = pl.multiple_of(jnp.where(even, 0, tiles - EDGE), 8)
    off_b = pl.multiple_of(jnp.where(even, tiles - EDGE, 0), 8)

    @pl.when(is_flow)
    def _():
        for out, off in ((first_out, off_a), (last_out, off_b)):
            for place, f in enumerate(FIELD_ORDER):
                out[place * EDGE : (place + 1) * EDGE, :] = flow[f, pl.ds(off, EDGE), :]
            out[5 * EDGE : 6 * EDGE, :] = visc[pl.ds(off, EDGE), :]
        low = links[:, :LANES].astype(F32)
        high = links[:, tiles - LANES :].astype(F32)
        first_out[6 * EDGE : 6 * EDGE + 4, :] = jnp.where(even, low, high)
        last_out[6 * EDGE : 6 * EDGE + 4, :] = jnp.where(even, high, low)
        pad = jnp.zeros((4, LANES), F32)
        first_out[6 * EDGE + 4 : 6 * EDGE + 8, :] = pad
        last_out[6 * EDGE + 4 : 6 * EDGE + 8, :] = pad

    @pl.when(jnp.logical_not(is_flow))
    def _():
        for v in range(4):
            low = sound[v, :, :LANES]
            high = sound[v, :, elements - LANES :]
            first_out[v * nodes : (v + 1) * nodes, :] = jnp.where(even, low, high)
            last_out[v * nodes : (v + 1) * nodes, :] = jnp.where(even, high, low)
        rest = jnp.zeros((first_out.shape[0] - 4 * nodes, LANES), F32)
        first_out[4 * nodes :, :] = rest
        last_out[4 * nodes :, :] = rest


def flow_kernel(
    meta, flow, mean, visc, links, target, projector, part_a, part_b,
    flow_out, mean_out, own_one, own_two, next_one, next_two,
    state, high0, low0, high1, low1, vwide, lcol, square, mats, packed, pay,
):
    is_flow, even = meta[0] == 1, meta[1] == 1
    tiles = flow.shape[1]
    wide = tiles + 2 * EDGE
    elements = own_one.shape[1]
    nodes = projector.shape[0]
    band = tiles + 4 * HW
    blocks = 4
    rows = band // blocks
    span = rows + 2 * HW

    @pl.when(jnp.logical_not(is_flow))
    def _():
        flow_out[...] = flow[...]
        mean_out[...] = mean[...]
        own_one[...] = jnp.zeros_like(own_one)
        own_two[...] = jnp.zeros_like(own_two)
        next_one[...] = jnp.zeros_like(next_one)
        next_two[...] = jnp.zeros_like(next_two)

    @pl.when(is_flow)
    def _():
        first_tile = meta[2]
        first_element = meta[3]

        def pick(at, size):
            a, b = part_a[at : at + size, :], part_b[at : at + size, :]
            return jnp.where(even, a, b), jnp.where(even, b, a)

        def put(high, low, at, size, place, value):
            columns = slice(place * LANES, (place + 1) * LANES)
            h, l = split_parts(value)
            high[at : at + size, columns] = h
            low[at : at + size, columns] = l

        for place, f in enumerate(FIELD_ORDER):
            columns = slice(place * LANES, (place + 1) * LANES)
            before, after = pick(place * EDGE, EDGE)
            center = flow[f]
            state[:EDGE, columns] = before
            state[EDGE : EDGE + tiles, columns] = center
            state[EDGE + tiles :, columns] = after
            put(high0, low0, 0, EDGE, place, before)
            put(high0, low0, EDGE, tiles, place, center)
            put(high0, low0, EDGE + tiles, EDGE, place, after)
        before, after = pick(5 * EDGE, EDGE)
        vwide[:EDGE, :] = before
        vwide[EDGE : EDGE + tiles, :] = visc[...]
        vwide[EDGE + tiles :, :] = after
        for ref in (high1, low1):
            ref[:HW, :] = jnp.zeros((HW, ref.shape[1]), BF16)
            ref[wide - HW :, :] = jnp.zeros((HW, ref.shape[1]), BF16)

        before, after = pick(6 * EDGE, 8)
        square[...] = jnp.zeros_like(square)
        square[:8, :] = before
        lcol[:EDGE, :] = square[...].T[LANES - EDGE :, :]
        square[:8, :] = after
        lcol[EDGE + tiles :, :] = square[...].T[:EDGE, :]
        for part in range(tiles // LANES):
            square[:4, :] = links[:, part * LANES : (part + 1) * LANES].astype(F32)
            lcol[EDGE + part * LANES : EDGE + (part + 1) * LANES, :] = square[...].T

        lane = lax.broadcasted_iota(jnp.int32, (rows, 2 * span), 1)
        lane = jnp.where(lane >= span, lane - span, lane)
        for b in range(blocks):
            at = HW + b * rows
            own = (
                first_tile - EDGE + at + lax.broadcasted_iota(jnp.int32, (rows, LANES), 0)
            ).astype(F32)
            given = lcol[at : at + rows, :]
            place = jnp.where(given < 0, own, given).astype(jnp.int32) - (
                first_tile - EDGE + b * rows
            )
            hot = [jnp.where(place[:, k : k + 1] == lane, F32(1.0), F32(0.0)) for k in range(4)]
            mats[b, :rows, :] = (hot[0] + hot[1] + hot[2] + hot[3]).astype(BF16)
            mats[b, rows : 2 * rows, :] = (hot[0] - hot[1]).astype(BF16)
            mats[b, 2 * rows :, :] = (hot[2] - hot[3]).astype(BF16)

        def gathered(high, low, b, columns, at_row):
            at = b * rows
            both = jnp.concatenate([high[at : at + span, columns], low[at : at + span, columns]], 0)
            return dot(mats[b, at_row:, :], both)

        def east_west(x):
            return pltpu.roll(x, LANES - 1, 1), pltpu.roll(x, 1, 1)

        def lamb_block(b, center, shift, dy, dz, average):
            d1 = [(east - west) * 0.5 for east, west in shift]
            d2 = [y * 0.5 for y in dy]
            d3 = [z * 0.5 for z in dz]
            vx = d2[2] - d3[1]
            vy = d3[0] - d1[2]
            vz = d1[1] - d2[0]
            lamb = (
                vy * center[2] - vz * center[1],
                vz * center[0] - vx * center[2],
                vx * center[1] - vy * center[0],
            )
            at = HW + b * rows - EDGE
            low = max(0, -at)
            top = min(rows, tiles - at)
            for i in range(3):
                packed[i, at + low : at + top, :] = lamb[i][low:top]
                mixed = (1.0 - RELAX) * average[i, at + low : at + top, :] + RELAX * center[i][low:top]
                mean_out[i, at + low : at + top, :] = mixed
                packed[3 + i, at + low : at + top, :] = mixed

        def advance(b, high, low, high_next, low_next, average):
            at = HW + b * rows
            center = [state[at : at + rows, k * LANES : (k + 1) * LANES] for k in range(3)]
            scaled = [(0.5 * ADVECT) * c for c in center]
            v = vwide[at : at + rows, :]
            shift, dys, dzs = [], [], []
            for pair in (slice(0, 2), slice(2, 4), slice(4, 5)):
                got = gathered(high, low, b, slice(pair.start * LANES, pair.stop * LANES), 0)
                for place in range(pair.start, pair.stop):
                    inner = slice((place - pair.start) * LANES, (place - pair.start + 1) * LANES)
                    total, dy, dz = (
                        got[:rows, inner],
                        got[rows : 2 * rows, inner],
                        got[2 * rows :, inner],
                    )
                    c = (
                        center[place]
                        if place < 3
                        else state[at : at + rows, place * LANES : (place + 1) * LANES]
                    )
                    east, west = east_west(c)
                    if place < 3:
                        shift.append((east, west))
                        dys.append(dy)
                        dzs.append(dz)
                    new = (
                        c
                        + v * (east + west + total - 6.0 * c)
                        - (scaled[0] * (east - west) + scaled[1] * dy + scaled[2] * dz)
                    )
                    state[at : at + rows, place * LANES : (place + 1) * LANES] = new
                    if place < 3 or average is None:
                        put(high_next, low_next, at, rows, place, new)
            if average is not None:
                lamb_block(b, center, shift, dys, dzs, average)

        proj_high, proj_low = split_parts(projector[...])
        proj_both = jnp.concatenate([proj_high, proj_low], 0)
        local = target[...] - first_element
        hits = jnp.where(
            lax.broadcasted_iota(jnp.int32, (2 * elements, tiles), 0) == local, F32(1.0), F32(0.0)
        ).astype(BF16)

        def send(own_ref, next_ref):
            for c in range(6):
                x_high, x_low = split_parts(packed[c])
                main = dot_t(proj_both, x_high)
                mapped = main[:nodes] + main[nodes:] + dot_t(proj_high, x_low)
                pay[c * nodes : (c + 1) * nodes, :] = mapped.astype(BF16)
            count = own_ref.shape[0]
            sums = dot_t(pay[:count, :], hits)
            if count > 6 * nodes:
                body = sums[: 6 * nodes]
                tail = sums[6 * nodes :]
                line = lax.broadcasted_iota(jnp.int32, tail.shape, 0)
                big = jnp.floor(tail * (1.0 / BASE))
                tail = jnp.where(line == 0, tail - BASE * big, jnp.where(line == 1, big, 0.0))
                own_ref[6 * nodes :, :] = tail[:, :elements]
                next_ref[6 * nodes :, :] = tail[:, elements:].astype(BF16)
            else:
                body = sums
            own_ref[: 6 * nodes, :] = body[:, :elements]
            next_ref[: 6 * nodes, :] = body[:, elements:].astype(BF16)

        pay[6 * nodes :, :] = jnp.ones((EXTRA, tiles), BF16)
        for b in range(blocks):
            advance(b, high0, low0, high1, low1, None)
        for b in range(blocks):
            advance(b, high1, low1, high0, low0, mean)
        send(own_one, next_one)
        for place, f in enumerate(FIELD_ORDER):
            flow_out[f] = state[EDGE : EDGE + tiles, place * LANES : (place + 1) * LANES]
        for b in range(blocks):
            at = HW + b * rows
            center = [state[at : at + rows, k * LANES : (k + 1) * LANES] for k in range(3)]
            first = gathered(high0, low0, b, slice(0, 2 * LANES), rows)
            second = gathered(high0, low0, b, slice(2 * LANES, 3 * LANES), rows)
            all_d = jnp.concatenate([first, second], 1)
            dys = [all_d[:rows, k * LANES : (k + 1) * LANES] for k in range(3)]
            dzs = [all_d[rows:, k * LANES : (k + 1) * LANES] for k in range(3)]
            lamb_block(b, center, [east_west(c) for c in center], dys, dzs, mean_out)
        send(own_two, next_two)


def acoustic_kernel(
    first_step, meta, sound, part_a, part_b, neighbours, codes, source_a, source_b, *refs
):
    if first_step:
        (out, scale_out, edge_a, edge_b, wide, facing, remote, node, rhs, lamb, mean, flat) = refs
    else:
        (scale, out, wide, facing, remote, node, rhs, lamb, mean, flat) = refs
    is_flow, even = meta[0] == 1, meta[1] == 1
    nodes = sound.shape[1]
    elements = sound.shape[2]
    halves = elements // LANES
    matrix = lobatto_matrix()
    block = 4 * nodes

    @pl.when(is_flow)
    def _():
        out[...] = sound[...]
        if first_step:
            scale_out[...] = jnp.zeros_like(scale_out)
            edge_a[...] = jnp.zeros_like(edge_a)
            edge_b[...] = jnp.zeros_like(edge_b)

    @pl.when(jnp.logical_not(is_flow))
    def _():
        first_element = meta[3]
        for v in range(4):
            for h in range(halves):
                wide[h * block + v * nodes : h * block + (v + 1) * nodes, :] = sound[
                    v, :, h * LANES : (h + 1) * LANES
                ]
        a, b = part_a[:block, :].astype(F32), part_b[:block, :].astype(F32)
        wide[halves * block : (halves + 1) * block, :] = jnp.where(even, a, b)
        wide[(halves + 1) * block : (halves + 2) * block, :] = jnp.where(even, b, a)
        for n in range(nodes):
            node[n] = wide[pl.ds(n, 8, stride=nodes), :]

        for face in range(6):
            other = face ^ 1
            axis, level = other // 2, 3 * (other % 2)
            for part in range(halves + 2):
                base = part * block
                if axis == 0:
                    facing[face, part] = wide[pl.ds(base + level, 64, stride=4), :]
                elif axis == 1:
                    for i in range(4):
                        facing[face, part, pl.ds(i, 16, stride=4), :] = wide[
                            pl.ds(base + i + 4 * level, 16, stride=16), :
                        ]
                else:
                    for v in range(4):
                        facing[face, part, v * 16 : (v + 1) * 16, :] = wide[
                            base + v * nodes + 16 * level : base + v * nodes + 16 * level + 16, :
                        ]

        key = lax.broadcasted_iota(jnp.int32, ((halves + 2) * LANES, elements), 0)
        for face in range(6):
            link = neighbours[face : face + 1, :]
            near = link - first_element
            place = jnp.where(
                near < 0, elements + LANES + near, jnp.where(near < elements, near, near + LANES)
            )
            place = jnp.where(link < 0, -1, place)
            hot = jnp.where(key == place, F32(1.0), F32(0.0)).astype(BF16)
            x = jnp.concatenate([facing[face, part] for part in range(halves + 2)], 1)
            high, low = split_parts(x)
            got = dot(jnp.concatenate([high, low], 0), hot)
            got = got[:64] + got[64:]
            for h in range(halves):
                remote[face, h * 64 : (h + 1) * 64, :] = got[:, h * LANES : (h + 1) * LANES]

        total = source_a[...].astype(F32) + source_b[...].astype(F32)
        if first_step:
            count = total[6 * nodes : 6 * nodes + 1] + BASE * total[6 * nodes + 1 : 6 * nodes + 2]
            inverse = 1.0 / jnp.maximum(count, 1.0)
            scale_out[...] = jnp.broadcast_to(inverse, scale_out.shape)
        else:
            inverse = scale[0:1, :]
        total = total[: 6 * nodes] * inverse
        for h in range(halves):
            columns = slice(h * LANES, (h + 1) * LANES)
            lamb[h * block : h * block + nodes, :] = jnp.zeros((nodes, LANES), F32)
            for d in range(3):
                at = h * block + (1 + d) * nodes
                lamb[at : at + nodes, :] = total[d * nodes : (d + 1) * nodes, columns]
                value = total[(3 + d) * nodes : (4 + d) * nodes, columns]
                for v in range(4):
                    at = h * block + v * nodes
                    mean[d, at : at + nodes, :] = value

        line = lax.broadcasted_iota(jnp.int32, (8, LANES), 0)
        component = line % 4
        is_v = [component == v for v in range(4)]
        for n in range(nodes):
            i, j, k = n % 4, n // 4 % 4, n // 16
            lines = (
                [m + 4 * j + 16 * k for m in range(4)],
                [i + 4 * m + 16 * k for m in range(4)],
                [i + 4 * j + 16 * m for m in range(4)],
            )
            grads = []
            for d, at in enumerate((i, j, k)):
                total_d = None
                for m in range(4):
                    if abs(matrix[at, m]) > 1e-12:
                        term = F32(matrix[at, m]) * node[lines[d][m]]
                        total_d = term if total_d is None else total_d + term
                grads.append(total_d)
            div = sum(pltpu.roll(grads[d], 8 - (1 + d), 0) for d in range(3))
            coupled = jnp.where(is_v[0], div, 0.0)
            for d in range(3):
                coupled = jnp.where(is_v[1 + d], pltpu.roll(grads[d], 1 + d, 0), coupled)
            convect = sum(mean[d, pl.ds(n, 8, stride=nodes), :] * grads[d] for d in range(3))
            rhs[n] = -coupled - convect - lamb[pl.ds(n, 8, stride=nodes), :]

        upper = line >= 4
        for face in range(6):
            link = neighbours[face : face + 1, :]
            code = codes[face : face + 1, :]

            def both(row):
                return jnp.where(
                    upper,
                    jnp.broadcast_to(row[:, LANES:], (8, LANES)),
                    jnp.broadcast_to(row[:, :LANES], (8, LANES)),
                )

            valid = both(link) >= 0
            code = both(code)
            is_turn = [code == t for t in range(4)]
            planes = [remote[face, pl.ds(p, 8, stride=16), :] for p in range(16)]
            for p, n in enumerate(face_nodes(face)):
                turned = planes[turned_position(3, p)]
                for t in range(3):
                    turned = jnp.where(is_turn[t], planes[turned_position(t, p)], turned)
                jump = jnp.where(valid, turned - node[n], 0.0)
                rhs[n] = rhs[n] + PENALTY * jump

        for n in range(nodes):
            flat[pl.ds(n, 8, stride=nodes), :] = node[n] + ACOUSTIC_STEP * rhs[n]
        for v in range(4):
            for h in range(halves):
                out[v, :, h * LANES : (h + 1) * LANES] = flat[
                    h * block + v * nodes : h * block + (v + 1) * nodes, :
                ]
        if first_step:
            off_a = pl.multiple_of(jnp.where(even, 0, block), 8)
            off_b = pl.multiple_of(jnp.where(even, block, 0), 8)
            edge_a[...] = flat[pl.ds(off_a, block), :]
            edge_b[...] = flat[pl.ds(off_b, block), :]


def call(kernel, outs, scratch, operands, flops=1e8):
    vmem = pl.BlockSpec(memory_space=pltpu.VMEM)
    moved = sum(int(np.prod(x.shape)) * x.dtype.itemsize for x in (*operands, *outs))
    return pl.pallas_call(
        kernel,
        out_shape=tuple(outs),
        in_specs=[pl.BlockSpec(memory_space=pltpu.SMEM)] + [vmem] * (len(operands) - 1),
        out_specs=tuple([vmem] * len(outs)),
        scratch_shapes=scratch,
        compiler_params=pltpu.CompilerParams(vmem_limit_bytes=VMEM_LIMIT),
        cost_estimate=pl.CostEstimate(flops=int(flops), bytes_accessed=moved, transcendentals=0),
    )(*operands)


def acoustic_step(first_step, meta, sound, parts, neighbours, codes, sources, scale=None):
    _, nodes, elements = sound.shape
    halves = elements // LANES
    block = 4 * nodes
    shape = jax.ShapeDtypeStruct
    outs = [shape(sound.shape, F32)]
    if first_step:
        outs += [shape((8, elements), F32), shape((block, LANES), F32), shape((block, LANES), F32)]
    scratch = [
        pltpu.VMEM(((halves + 2) * block, LANES), F32),
        pltpu.VMEM((6, halves + 2, 64, LANES), F32),
        pltpu.VMEM((6, halves * 64, LANES), F32),
        pltpu.VMEM((nodes, 8, LANES), F32),
        pltpu.VMEM((nodes, 8, LANES), F32),
        pltpu.VMEM((halves * block, LANES), F32),
        pltpu.VMEM((3, halves * block, LANES), F32),
        pltpu.VMEM((halves * block, LANES), F32),
    ]
    operands = [meta, sound, *parts, neighbours, codes, *sources]
    if not first_step:
        operands.append(scale)

    def kernel(*refs):
        acoustic_kernel(first_step, *refs)

    return call(kernel, outs, scratch, operands)


def body(
    flow_fields,
    mean_velocity,
    cell_eddy_viscosity,
    tile_links,
    tile_target,
    projector,
    acoustic_state,
    element_face_neighbours,
    face_codes,
):
    groups = lax.axis_size("grp")
    count = lax.axis_size("sfc")
    group_index = lax.axis_index("grp")
    column = lax.axis_index("sfc")
    flow = flow_fields[0]
    mean = mean_velocity[0]
    visc = cell_eddy_viscosity[0]
    links = tile_links[0]
    sound = acoustic_state[0]
    neighbours = element_face_neighbours[0]
    codes = face_codes[0]
    tiles = flow.shape[1]
    _, nodes, elements = sound.shape
    shape = jax.ShapeDtypeStruct
    meta = jnp.stack(
        [
            (group_index < groups - 1).astype(jnp.int32),
            (column % 2 == 0).astype(jnp.int32),
            (column * tiles).astype(jnp.int32),
            (column * elements).astype(jnp.int32),
        ]
    )

    pairs_a = [p for i in range(1, count - 1, 2) for p in ((i, i + 1), (i + 1, i))]
    pairs_b = [p for i in range(0, count - 1, 2) for p in ((i, i + 1), (i + 1, i))]

    edge_rows = 6 * EDGE + 8
    pack_a, pack_b = call(
        pack_kernel,
        [shape((edge_rows, LANES), F32)] * 2,
        [],
        [meta, flow, visc, links, sound],
    )
    part_a = lax.ppermute(pack_a, "sfc", pairs_a)
    part_b = lax.ppermute(pack_b, "sfc", pairs_b)

    wide = tiles + 2 * EDGE
    band = tiles + 4 * HW
    rows = band // 4
    columns = 5 * LANES
    count_one, count_two = 6 * nodes + EXTRA, 6 * nodes
    flow_out, mean_out, own_one, own_two, next_one, next_two = call(
        flow_kernel,
        [
            shape(flow.shape, F32),
            shape(mean.shape, F32),
            shape((count_one, elements), F32),
            shape((count_two, elements), F32),
            shape((count_one, elements), BF16),
            shape((count_two, elements), BF16),
        ],
        [
            pltpu.VMEM((wide, columns), F32),
            pltpu.VMEM((wide, columns), BF16),
            pltpu.VMEM((wide, columns), BF16),
            pltpu.VMEM((wide, columns), BF16),
            pltpu.VMEM((wide, columns), BF16),
            pltpu.VMEM((wide, LANES), F32),
            pltpu.VMEM((wide, LANES), F32),
            pltpu.VMEM((LANES, LANES), F32),
            pltpu.VMEM((4, 3 * rows, 2 * (rows + 2 * HW)), BF16),
            pltpu.VMEM((6, tiles, LANES), F32),
            pltpu.VMEM((count_one, tiles), BF16),
        ],
        [meta, flow, mean, visc, links, tile_target, projector, part_a, part_b],
        flops=2e9,
    )

    up = [(i, i + 1) for i in range(count - 1)]
    flow_groups = range(groups - 1)

    def climb(x):
        chosen = [(g * count + i, g * count + j) for g in flow_groups for i, j in up]
        return lax.ppermute(x, ("grp", "sfc"), chosen)

    def combined(*xs):
        total = xs[0]
        for x in xs[1:]:
            total = total + x.astype(F32)
        return total.astype(BF16)

    got_one, got_two = climb(next_one), climb(next_two)
    x_one = lax.ppermute(combined(own_one, got_one), "grp", [(0, 1), (2, 3)])
    y_two = lax.ppermute(combined(own_two, got_two), "grp", [(0, 2), (1, 3)])
    y_one = lax.ppermute(combined(own_one, got_one, x_one), "grp", [(1, 3)])
    x_two = lax.ppermute(combined(own_two, got_two, y_two), "grp", [(2, 3)])

    sound, scale, edge_a, edge_b = acoustic_step(
        True, meta, sound, (part_a, part_b), neighbours, codes, (x_one, y_one)
    )
    base = (groups - 1) * count
    part_a = lax.ppermute(edge_a, ("grp", "sfc"), [(base + i, base + j) for i, j in pairs_a])
    part_b = lax.ppermute(edge_b, ("grp", "sfc"), [(base + i, base + j) for i, j in pairs_b])
    (sound,) = acoustic_step(
        False, meta, sound, (part_a, part_b), neighbours, codes, (y_two, x_two), scale
    )
    return flow_out[None], mean_out[None], sound[None]


def solution(mesh):
    placed = (
        P("grp", None, "sfc", None),
        P("grp", None, "sfc", None),
        P("grp", "sfc", None),
        P("grp", None, "sfc"),
        P("grp", "sfc"),
        P(),
        P("grp", None, None, "sfc"),
        P("grp", None, "sfc"),
        P("grp", None, "sfc"),
    )
    return jax.shard_map(
        body,
        mesh=mesh,
        in_specs=placed,
        out_specs=(
            P("grp", None, "sfc", None),
            P("grp", None, "sfc", None),
            P("grp", None, None, "sfc"),
        ),
        check_vma=False,
    )
```

time: 362 us -> 53.7 us (0.15)
  the two profiles are of different devices: /device:TPU:1 before, /device:TPU:23 now
where the time goes in v1:
time: 53.7 us; the launch traced here: 53.3 us
  waiting for transfers between devices  21.1 us (39%)
  starting transfers between devices  19.6 us (36%)
  Pallas kernels  7.82 us (15%)
  local copies, waits for them, and re-layouts  3.67 us (7%)
  between operations  0.85 us (2%)
    ppermute x1, waiting for transfers between devices, body(): y_two = lax.ppermute(combined(own_two, got_two), 'grp', [(0, 2), (1, 3)])  10.5 us
    pallas_call x4, Pallas kernels, call(): pl.pallas_call(kernel, out_shape=tuple(outs), in_specs=[pl.BlockSpec(memo...  7.82 us
    ppermute x1, starting transfers between devices, body(): lax.ppermute(edge_a, ('grp', 'sfc'), [(base + i, base + j) for i, j in pa...  7.22 us
    ppermute x1, waiting for transfers between devices, body(): y_one = lax.ppermute(combined(own_one, got_one, x_one), 'grp', [(1, 3)])  5.46 us
    ppermute x1, starting transfers between devices, body(): part_a = lax.ppermute(pack_a, 'sfc', pairs_a)  3.77 us
    unnamed x21, local copies, waits for them, and re-layouts  3.67 us
    ppermute x1, waiting for transfers between devices, body(): part_a = lax.ppermute(pack_a, 'sfc', pairs_a)  2.92 us
    ppermute x1, starting transfers between devices, body(): lax.ppermute(edge_b, ('grp', 'sfc'), [(base + i, base + j) for i, j in pa...  1.92 us
  transfers between devices with their start and end apart: 10, of which 6 were waited for; matrix products, arithmetic and copies ran while one was open for 0% of the time, Pallas kernels for 5%

profile of v1, /device:TPU:23, one launch (start us, length us, event | category | flops | bytes accessed | tf_op | source)
XLA Modules:
  0.0 53.3 jit_solution(10065650327921279110)
XLA Ops:
  0.6 0.1 pad_add_fusion.meta.refs_0_
  0.7 0.0 copy-start.4
  0.7 0.7 %copy-done.4 = s32[1,4,256]{2,1,0:T(4,128)S(1)} copy-done((s32[1,4,256]{2,1,0:T(4,128)S(1)}, s32[1,4,256]{2,1,0:T(4,128)}, u32[]{:S(2)}) %copy-start.4) | copy-done | bytes 4120
  1.4 0.0 copy-start
  1.4 0.9 %copy-done = f32[1,4,64,256]{3,2,1,0:T(8,128)S(1)} copy-done((f32[1,4,64,256]{3,2,1,0:T(8,128)S(1)}, f32[1,4,64,256]{3,2,1,0:T(8,128)}, u32[]{:S(2)}) %copy-start) | copy-done | bytes 262168
  2.4 0.0 copy-start.2
  2.4 1.1 %copy-done.2 = f32[1,5,256,128]{3,2,1,0:T(8,128)S(1)} copy-done((f32[1,5,256,128]{3,2,1,0:T(8,128)S(1)}, f32[1,5,256,128]{3,2,1,0:T(8,128)}, u32[]{:S(2)}) %copy-start.2) | copy-done | bytes 655384
  3.5 0.0 copy-start.3
  3.5 0.9 %copy-done.3 = f32[1,256,128]{2,1,0:T(8,128)S(1)} copy-done((f32[1,256,128]{2,1,0:T(8,128)S(1)}, f32[1,256,128]{2,1,0:T(8,128)}, u32[]{:S(2)}) %copy-start.3) | copy-done | bytes 131096
  4.4 0.0 copy-start.5
  4.4 0.6 %shard_map.112 = (f32[296,128]{1,0:T(8,128)S(1)}, f32[296,128]{1,0:T(8,128)S(1)}) custom-call(s32[4]{0:T(128)S(1)} %pad_add_fusion.meta.refs_0_, f32[5,256,128]{2,1,0:T(8,128)S(1)} %bitcast.17, f32[256,128]{1,0:T(8,128)S(1)} %bitcast.19, s32[4,256]{1,0:T(4,128)S(1)} %bitcast.21, f32[4,64,256]{2,1,0:T(8,128)S(1)} %bitcast.15), custom_call_target="tpu_custom_call" | custom-call | flops 100000000 | bytes 1355792 | tf_op jit(solution)/shard_map/pallas_call | solution.py:459
  4.9 3.8 %collective-permute-start = (f32[296,128]{1,0:T(8,128)S(1)}, f32[296,128]{1,0:T(8,128)S(1)}, u32[]{:S(2)}, u32[]{:S(2)}) collective-permute-start(f32[296,128]{1,0:T(8,128)S(1)} %get-tuple-element.15), channel_id=1, source_target_pairs={{1,2},{2,1},{3,4},{4,3},{5,6},{6,5},{9,10},{10,9},{11,12},{12,11},... | collective-permute-start | bytes 454664 | tf_op jit(solution)/shard_map/ppermute | solution.py:542
  8.7 0.0 copy-start.7
  8.7 0.1 collective-permute-start.1
  8.8 2.9 %collective-permute-done.part_a.refs_2_ = f32[296,128]{1,0:T(8,128)S(1)} collective-permute-done((f32[296,128]{1,0:T(8,128)S(1)}, f32[296,128]{1,0:T(8,128)S(1)}, u32[]{:S(2)}, u32[]{:S(2)}) %collective-permute-start) | collective-permute-done | bytes 151584 | tf_op jit(solution)/shard_map/ppermute | solution.py:542
  11.7 0.0 collective-permute-done.1.part_b.refs_3_
  11.7 0.0 copy-done.5
  11.7 0.0 copy-done.6
  11.7 0.0 copy-done.7
  11.7 1.7 %shard_map.113 = (f32[5,256,128]{2,1,0:T(8,128)}, f32[3,256,128]{2,1,0:T(8,128)}, f32[400,256]{1,0:T(8,128)S(1)}, f32[384,256]{1,0:T(8,128)S(1)}, bf16[400,256]{...) custom-call(s32[4]{0:T(128)S(1)} %pad_add_fusion.meta.refs_0_, f32[5,256,128]{2,1,0:T(8,128)S(1)} %bitcast.18, ...), custom_call_target="tpu_custom_call" | custom-call | flops 2000000000 | bytes 3773456 | tf_op jit(solution)/shard_map/pallas_call | solution.py:459
  13.4 0.7 %collective-permute-start.7 = (bf16[384,256]{1,0:T(8,128)(2,1)S(1)}, bf16[384,256]{1,0:T(8,128)(2,1)S(1)}, u32[]{:S(2)}, u32[]{:S(2)}) collective-permute-start(bf16[384,256]{1,0:T(8,128)(2,1)S(1)} %get-tuple-element.25), channel_id=1, source_target_pairs={{0,1},{1,2},{2,3},{3,4},{4,5},{5,6},{6,7},{8,9},{9,10},{10,11},{11... | collective-permute-start | bytes 589832 | tf_op jit(solution)/shard_map/ppermute | solution.py:582
  14.1 0.7 %collective-permute-start.2 = (bf16[400,256]{1,0:T(8,128)(2,1)S(1)}, bf16[400,256]{1,0:T(8,128)(2,1)S(1)}, u32[]{:S(2)}, u32[]{:S(2)}) collective-permute-start(bf16[400,256]{1,0:T(8,128)(2,1)S(1)} %get-tuple-element.20), channel_id=1, source_target_pairs={{0,1},{1,2},{2,3},{3,4},{4,5},{5,6},{6,7},{8,9},{9,10},{10,11},{11... | collective-permute-start | bytes 614408 | tf_op jit(solution)/shard_map/ppermute | solution.py:582
  14.8 0.0 collective-permute-done.7
  14.8 0.1 fusion.1
  14.8 1.3 %collective-permute-start.8 = (bf16[384,256]{1,0:T(8,128)(2,1)S(1)}, bf16[384,256]{1,0:T(8,128)(2,1)S(1)}, u32[]{:S(2)}, u32[]{:S(2)}) collective-permute-start(bf16[384,256]{1,0:T(8,128)(2,1)S(1)} %fusion.1), channel_id=1, source_target_pairs={{0,16},{8,24},{1,17},{9,25},{2,18},{10,26},{3,19},{11,27},{4,20},{... | collective-permute-start | bytes 589832 | tf_op jit(solution)/shard_map/ppermute | solution.py:592
  16.1 0.0 collective-permute-done.2
  16.1 0.1 fusion
  16.2 1.3 %collective-permute-start.3 = (bf16[400,256]{1,0:T(8,128)(2,1)S(1)}, bf16[400,256]{1,0:T(8,128)(2,1)S(1)}, u32[]{:S(2)}, u32[]{:S(2)}) collective-permute-start(bf16[400,256]{1,0:T(8,128)(2,1)S(1)} %fusion), channel_id=1, source_target_pairs={{0,8},{16,24},{1,9},{17,25},{2,10},{18,26},{3,11},{19,27},{4,12},{... | collective-permute-start | bytes 614408 | tf_op jit(solution)/shard_map/ppermute | solution.py:591
  17.5 10.5 %collective-permute-done.8.refs_6_ = bf16[384,256]{1,0:T(8,128)(2,1)S(1)} collective-permute-done((bf16[384,256]{1,0:T(8,128)(2,1)S(1)}, bf16[384,256]{1,0:T(8,128)(2,1)S(1)}, u32[]{:S(2)}, u32[]{:S(2)}) %collective-permute-start.8) | collective-permute-done | bytes 196640 | tf_op jit(solution)/shard_map/ppermute | solution.py:592
  28.0 0.1 add_convert_fusion.1
  28.1 0.0 copy-start.8
  28.1 0.0 copy-start.9
  28.1 0.0 copy-start.1
  28.1 1.4 %collective-permute-start.9 = (bf16[384,256]{1,0:T(8,128)(2,1)S(1)}, bf16[384,256]{1,0:T(8,128)(2,1)S(1)}, u32[]{:S(2)}, u32[]{:S(2)}) collective-permute-start(bf16[384,256]{1,0:T(8,128)(2,1)S(1)} %add_convert_fusion.1), channel_id=1, source_target_pairs={{16,24},{17,25},{18,26},{19,27},{20,28},{21,29},{22,30},{23,31}} | collective-permute-start | bytes 589832 | tf_op jit(solution)/shard_map/ppermute | solution.py:594
  29.6 0.8 %collective-permute-done.3.refs_6_ = bf16[400,256]{1,0:T(8,128)(2,1)S(1)} collective-permute-done((bf16[400,256]{1,0:T(8,128)(2,1)S(1)}, bf16[400,256]{1,0:T(8,128)(2,1)S(1)}, u32[]{:S(2)}, u32[]{:S(2)}) %collective-permute-start.3) | collective-permute-done | bytes 204832 | tf_op jit(solution)/shard_map/ppermute | solution.py:591
  30.4 0.1 add_convert_fusion
  30.5 1.3 %collective-permute-start.4 = (bf16[400,256]{1,0:T(8,128)(2,1)S(1)}, bf16[400,256]{1,0:T(8,128)(2,1)S(1)}, u32[]{:S(2)}, u32[]{:S(2)}) collective-permute-start(bf16[400,256]{1,0:T(8,128)(2,1)S(1)} %add_convert_fusion), channel_id=1, source_target_pairs={{8,24},{9,25},{10,26},{11,27},{12,28},{13,29},{14,30},{15,31}} | collective-permute-start | bytes 614408 | tf_op jit(solution)/shard_map/ppermute | solution.py:593
  31.8 0.0 copy-done.8
  31.8 0.0 copy-done.9
  31.8 5.5 %collective-permute-done.4.refs_7_ = bf16[400,256]{1,0:T(8,128)(2,1)S(1)} collective-permute-done((bf16[400,256]{1,0:T(8,128)(2,1)S(1)}, bf16[400,256]{1,0:T(8,128)(2,1)S(1)}, u32[]{:S(2)}, u32[]{:S(2)}) %collective-permute-start.4) | collective-permute-done | bytes 204832 | tf_op jit(solution)/shard_map/ppermute | solution.py:593
  37.3 0.0 copy-done.1
  37.3 2.4 %shard_map.114 = (f32[4,64,256]{2,1,0:T(8,128)S(1)}, f32[8,256]{1,0:T(8,128)S(1)}, f32[256,128]{1,0:T(8,128)S(1)}, f32[256,128]{1,0:T(8,128)S(1)}) custom-call(s32[4]{0:T(128)S(1)} %pad_add_fusion.meta.refs_0_, f32[4,64,256]{2,1,0:T(8,128)S(1)} %bitcast.16, f32[296,128]{1,0:T(8,128)S(1)} %collective-permute-done.part_a.refs_2_, ...), custom_call_target="tpu_custom_call" | custom-call | flops 100000000 | bytes 1519632 | tf_op jit(solution)/shard_map/pallas_call | solution.py:459
  39.7 7.2 %collective-permute-start.5 = (f32[256,128]{1,0:T(8,128)S(1)}, f32[256,128]{1,0:T(8,128)S(1)}, u32[]{:S(2)}, u32[]{:S(2)}) collective-permute-start(f32[256,128]{1,0:T(8,128)S(1)} %get-tuple-element.22), channel_id=1, source_target_pairs={{25,26},{26,25},{27,28},{28,27},{29,30},{30,29}} | collective-permute-start | bytes 393224 | tf_op jit(solution)/shard_map/ppermute | solution.py:600
  47.0 1.9 %collective-permute-start.6 = (f32[256,128]{1,0:T(8,128)S(1)}, f32[256,128]{1,0:T(8,128)S(1)}, u32[]{:S(2)}, u32[]{:S(2)}) collective-permute-start(f32[256,128]{1,0:T(8,128)S(1)} %get-tuple-element.23), channel_id=1, source_target_pairs={{24,25},{25,24},{26,27},{27,26},{28,29},{29,28},{30,31},{31,30}} | collective-permute-start | bytes 393224 | tf_op jit(solution)/shard_map/ppermute | solution.py:601
  48.9 0.0 collective-permute-done.9.refs_7_
  48.9 0.7 %collective-permute-done.5.refs_2_ = f32[256,128]{1,0:T(8,128)S(1)} collective-permute-done((f32[256,128]{1,0:T(8,128)S(1)}, f32[256,128]{1,0:T(8,128)S(1)}, u32[]{:S(2)}, u32[]{:S(2)}) %collective-permute-start.5) | collective-permute-done | bytes 131104 | tf_op jit(solution)/shard_map/ppermute | solution.py:600
  49.6 0.6 %collective-permute-done.6.refs_3_ = f32[256,128]{1,0:T(8,128)S(1)} collective-permute-done((f32[256,128]{1,0:T(8,128)S(1)}, f32[256,128]{1,0:T(8,128)S(1)}, u32[]{:S(2)}, u32[]{:S(2)}) %collective-permute-start.6) | collective-permute-done | bytes 131104 | tf_op jit(solution)/shard_map/ppermute | solution.py:601
  50.2 3.1 %shard_map.115 = f32[4,64,256]{2,1,0:T(8,128)} custom-call(s32[4]{0:T(128)S(1)} %pad_add_fusion.meta.refs_0_, f32[4,64,256]{2,1,0:T(8,128)S(1)} %get-tuple-element.21.refs_1_, f32[256,128]{1,0:T(8,128)S(1)} %collective-permute-done.5.refs_2_, f32[256,128]{1,0:T(8,128)S(1)} %collective-permute-done.6.refs_3_, s32[6,256]{1,0:T(8,128)S(1)} %get-tuple-element.28.refs_4_, ...), custom_call_target="tpu_custom_call" | custom-call | flops 100000000 | bytes 1200144 | tf_op jit(solution)/shard_map/pallas_call | solution.py:459
  (2 shorter events, 0.0 us)
Async XLA Ops:
  0.7 0.7 %copy-start.4 = (s32[1,4,256]{2,1,0:T(4,128)S(1)}, s32[1,4,256]{2,1,0:T(4,128)}, u32[]{:S(2)}) copy-start(s32[1,4,256]{2,1,0:T(4,128)} %param.12) | copy-start | bytes 12292
  1.4 0.9 %copy-start = (f32[1,4,64,256]{3,2,1,0:T(8,128)S(1)}, f32[1,4,64,256]{3,2,1,0:T(8,128)}, u32[]{:S(2)}) copy-start(f32[1,4,64,256]{3,2,1,0:T(8,128)} %param.15) | copy-start | bytes 786436
  2.4 1.1 %copy-start.2 = (f32[1,5,256,128]{3,2,1,0:T(8,128)S(1)}, f32[1,5,256,128]{3,2,1,0:T(8,128)}, u32[]{:S(2)}) copy-start(f32[1,5,256,128]{3,2,1,0:T(8,128)} %param.9) | copy-start | bytes 1966084
  3.5 0.9 %copy-start.3 = (f32[1,256,128]{2,1,0:T(8,128)S(1)}, f32[1,256,128]{2,1,0:T(8,128)}, u32[]{:S(2)}) copy-start(f32[1,256,128]{2,1,0:T(8,128)} %param.11) | copy-start | bytes 393220
  4.4 7.4 %copy-start.5 = (f32[1,3,256,128]{3,2,1,0:T(8,128)S(1)}, f32[1,3,256,128]{3,2,1,0:T(8,128)}, u32[]{:S(2)}) copy-start(f32[1,3,256,128]{3,2,1,0:T(8,128)} %param.10) | copy-start | bytes 1179652
  4.4 7.4 %copy-start.6 = (f32[64,128]{1,0:T(8,128)S(1)}, f32[64,128]{1,0:T(8,128)}, u32[]{:S(2)}) copy-start(f32[64,128]{1,0:T(8,128)} %projector.1) | copy-start | bytes 98308
  4.9 6.8 %collective-permute-start = (f32[296,128]{1,0:T(8,128)S(1)}, f32[296,128]{1,0:T(8,128)S(1)}, u32[]{:S(2)}, u32[]{:S(2)}) collective-permute-start(f32[296,128]{1,0:T(8,128)S(1)} %get-tuple-element.15), channel_id=1, source_target_pairs={{1,2},{2,1},{3,4},{4,3},{5,6},{6,5},{9,10},{10,9},{11,12},{12,11},... | collective-permute-start | bytes 454664 | tf_op jit(solution)/shard_map/ppermute | solution.py:542
  8.7 3.0 %copy-start.7 = (s32[1,256]{1,0:T(1,128)S(1)}, s32[1,256]{1,0:T(1,128)}, u32[]{:S(2)}) copy-start(s32[1,256]{1,0:T(1,128)} %target.1) | copy-start | bytes 3076
  8.7 3.0 %collective-permute-start.1 = (f32[296,128]{1,0:T(8,128)S(1)}, f32[296,128]{1,0:T(8,128)S(1)}, u32[]{:S(2)}, u32[]{:S(2)}) collective-permute-start(f32[296,128]{1,0:T(8,128)S(1)} %get-tuple-element.16), channel_id=1, source_target_pairs={{0,1},{1,0},{2,3},{3,2},{4,5},{5,4},{6,7},{7,6},{8,9},{9,8},{10,11... | collective-permute-start | bytes 454664 | tf_op jit(solution)/shard_map/ppermute | solution.py:543
  13.4 1.4 %collective-permute-start.7 = (bf16[384,256]{1,0:T(8,128)(2,1)S(1)}, bf16[384,256]{1,0:T(8,128)(2,1)S(1)}, u32[]{:S(2)}, u32[]{:S(2)}) collective-permute-start(bf16[384,256]{1,0:T(8,128)(2,1)S(1)} %get-tuple-element.25), channel_id=1, source_target_pairs={{0,1},{1,2},{2,3},{3,4},{4,5},{5,6},{6,7},{8,9},{9,10},{10,11},{11... | collective-permute-start | bytes 589832 | tf_op jit(solution)/shard_map/ppermute | solution.py:582
  14.1 2.1 %collective-permute-start.2 = (bf16[400,256]{1,0:T(8,128)(2,1)S(1)}, bf16[400,256]{1,0:T(8,128)(2,1)S(1)}, u32[]{:S(2)}, u32[]{:S(2)}) collective-permute-start(bf16[400,256]{1,0:T(8,128)(2,1)S(1)} %get-tuple-element.20), channel_id=1, source_target_pairs={{0,1},{1,2},{2,3},{3,4},{4,5},{5,6},{6,7},{8,9},{9,10},{10,11},{11... | collective-permute-start | bytes 614408 | tf_op jit(solution)/shard_map/ppermute | solution.py:582
  14.8 13.2 %collective-permute-start.8 = (bf16[384,256]{1,0:T(8,128)(2,1)S(1)}, bf16[384,256]{1,0:T(8,128)(2,1)S(1)}, u32[]{:S(2)}, u32[]{:S(2)}) collective-permute-start(bf16[384,256]{1,0:T(8,128)(2,1)S(1)} %fusion.1), channel_id=1, source_target_pairs={{0,16},{8,24},{1,17},{9,25},{2,18},{10,26},{3,19},{11,27},{4,20},{... | collective-permute-start | bytes 589832 | tf_op jit(solution)/shard_map/ppermute | solution.py:592
  16.2 14.2 %collective-permute-start.3 = (bf16[400,256]{1,0:T(8,128)(2,1)S(1)}, bf16[400,256]{1,0:T(8,128)(2,1)S(1)}, u32[]{:S(2)}, u32[]{:S(2)}) collective-permute-start(bf16[400,256]{1,0:T(8,128)(2,1)S(1)} %fusion), channel_id=1, source_target_pairs={{0,8},{16,24},{1,9},{17,25},{2,10},{18,26},{3,11},{19,27},{4,12},{... | collective-permute-start | bytes 614408 | tf_op jit(solution)/shard_map/ppermute | solution.py:591
  28.1 3.7 %copy-start.8 = (s32[1,6,256]{2,0,1:T(1,128)S(1)}, s32[1,6,256]{2,0,1:T(1,128)}, u32[]{:S(2)}) copy-start(s32[1,6,256]{2,0,1:T(1,128)} %param.17) | copy-start | bytes 18436
  28.1 3.7 %copy-start.9 = (s32[1,6,256]{2,0,1:T(1,128)S(1)}, s32[1,6,256]{2,0,1:T(1,128)}, u32[]{:S(2)}) copy-start(s32[1,6,256]{2,0,1:T(1,128)} %param.16) | copy-start | bytes 18436
  28.1 9.2 %copy-start.1 = (f32[1,4,64,256]{3,2,1,0:T(8,128)S(1)}, f32[1,4,64,256]{3,2,1,0:T(8,128)}, u32[]{:S(2)}) copy-start(f32[1,4,64,256]{3,2,1,0:T(8,128)} %param.15) | copy-start | bytes 786436
  28.1 20.8 %collective-permute-start.9 = (bf16[384,256]{1,0:T(8,128)(2,1)S(1)}, bf16[384,256]{1,0:T(8,128)(2,1)S(1)}, u32[]{:S(2)}, u32[]{:S(2)}) collective-permute-start(bf16[384,256]{1,0:T(8,128)(2,1)S(1)} %add_convert_fusion.1), channel_id=1, source_target_pairs={{16,24},{17,25},{18,26},{19,27},{20,28},{21,29},{22,30},{23,31}} | collective-permute-start | bytes 589832 | tf_op jit(solution)/shard_map/ppermute | solution.py:594
  30.5 6.8 %collective-permute-start.4 = (bf16[400,256]{1,0:T(8,128)(2,1)S(1)}, bf16[400,256]{1,0:T(8,128)(2,1)S(1)}, u32[]{:S(2)}, u32[]{:S(2)}) collective-permute-start(bf16[400,256]{1,0:T(8,128)(2,1)S(1)} %add_convert_fusion), channel_id=1, source_target_pairs={{8,24},{9,25},{10,26},{11,27},{12,28},{13,29},{14,30},{15,31}} | collective-permute-start | bytes 614408 | tf_op jit(solution)/shard_map/ppermute | solution.py:593
  39.7 9.9 %collective-permute-start.5 = (f32[256,128]{1,0:T(8,128)S(1)}, f32[256,128]{1,0:T(8,128)S(1)}, u32[]{:S(2)}, u32[]{:S(2)}) collective-permute-start(f32[256,128]{1,0:T(8,128)S(1)} %get-tuple-element.22), channel_id=1, source_target_pairs={{25,26},{26,25},{27,28},{28,27},{29,30},{30,29}} | collective-permute-start | bytes 393224 | tf_op jit(solution)/shard_map/ppermute | solution.py:600
  47.0 3.2 %collective-permute-start.6 = (f32[256,128]{1,0:T(8,128)S(1)}, f32[256,128]{1,0:T(8,128)S(1)}, u32[]{:S(2)}, u32[]{:S(2)}) collective-permute-start(f32[256,128]{1,0:T(8,128)S(1)} %get-tuple-element.23), channel_id=1, source_target_pairs={{24,25},{25,24},{26,27},{27,26},{28,29},{29,28},{30,31},{31,30}} | collective-permute-start | bytes 393224 | tf_op jit(solution)/shard_map/ppermute | solution.py:601

commit v2 on v0

v2 whole, which is shorter than its diff:
```python
import jax
import jax.numpy as jnp
import numpy as np
from jax import lax
from jax.experimental import pallas as pl
from jax.experimental.pallas import tpu as pltpu
from jax.sharding import PartitionSpec as P

HW = 16
HE = 16

ADVECT = 0.1
RELAX = 0.1
PENALTY = 1.5
ACOUSTIC_STEP = 0.08

LANES = 128
EDGE = 3 * HW
FIELD_ORDER = (1, 2, 3, 0, 4)
BASE = 32.0
EXTRA = 16
VMEM_LIMIT = 48 * 1024 * 1024
PACK_LIMIT = 63 * 1024 * 1024

F32 = jnp.float32
BF16 = jnp.bfloat16


def lobatto_matrix():
    points = np.array([-1.0, -1.0 / np.sqrt(5.0), 1.0 / np.sqrt(5.0), 1.0])
    weights = np.array(
        [
            1.0 / np.prod([points[col] - points[other] for other in range(4) if other != col])
            for col in range(4)
        ]
    )
    matrix = np.zeros((4, 4))
    for line in range(4):
        for col in range(4):
            if line != col:
                matrix[line, col] = weights[col] / weights[line] / (points[line] - points[col])
        matrix[line, line] = -matrix[line].sum()
    return matrix.astype(np.float32)


def face_nodes(face):
    axis, level = face // 2, 3 * (face % 2)
    nodes = []
    for second in range(4):
        for first in range(4):
            coords = [first, second]
            coords.insert(axis, level)
            nodes.append(coords[0] + 4 * coords[1] + 16 * coords[2])
    return nodes


def turned_position(turn, position):
    a, b = position % 4, position // 4
    a, b = ((a, b), (3 - b, a), (3 - a, 3 - b), (b, 3 - a))[turn]
    return a + 4 * b


def split_parts(x):
    high = x.astype(BF16)
    return high, (x - high.astype(F32)).astype(BF16)


def dot(a, b):
    return jnp.dot(a, b, preferred_element_type=F32)


def dot_t(a, b):
    return lax.dot_general(a, b, (((1,), (1,)), ((), ())), preferred_element_type=F32)


def pack_kernel(meta, flow, visc, links, sound, out_a, out_b, links_in, sems, link_sem):
    is_flow, even = meta[0] == 1, meta[1] == 1
    tiles = flow.shape[1]
    _, nodes, elements = sound.shape
    outs = (out_a, out_b)

    @pl.when(is_flow)
    def _():
        fetch = pltpu.make_async_copy(links, links_in, link_sem)
        fetch.start()
        copies = []
        for side, out in enumerate(outs):
            off = pl.multiple_of(jnp.where(even == (side == 0), 0, tiles - EDGE), 8)
            for place, f in enumerate(FIELD_ORDER):
                copies.append(
                    pltpu.make_async_copy(
                        flow.at[f, pl.ds(off, EDGE), :],
                        out.at[pl.ds(place * EDGE, EDGE), :],
                        sems.at[side, place],
                    )
                )
            copies.append(
                pltpu.make_async_copy(
                    visc.at[pl.ds(off, EDGE), :], out.at[pl.ds(5 * EDGE, EDGE), :], sems.at[side, 5]
                )
            )
        for copy in copies:
            copy.start()
        fetch.wait()
        low = links_in[:, :LANES].astype(F32)
        high = links_in[:, tiles - LANES :].astype(F32)
        pad = jnp.zeros((4, LANES), F32)
        out_a[6 * EDGE : 6 * EDGE + 4, :] = jnp.where(even, low, high)
        out_b[6 * EDGE : 6 * EDGE + 4, :] = jnp.where(even, high, low)
        out_a[6 * EDGE + 4 :, :] = pad
        out_b[6 * EDGE + 4 :, :] = pad
        for copy in copies:
            copy.wait()

    @pl.when(jnp.logical_not(is_flow))
    def _():
        copies = []
        for side, out in enumerate(outs):
            off = pl.multiple_of(jnp.where(even == (side == 0), 0, elements - LANES), LANES)
            for v in range(4):
                copies.append(
                    pltpu.make_async_copy(
                        sound.at[v, :, pl.ds(off, LANES)],
                        out.at[pl.ds(v * nodes, nodes), :],
                        sems.at[side, v],
                    )
                )
        for copy in copies:
            copy.start()
        rest = jnp.zeros((out_a.shape[0] - 4 * nodes, LANES), F32)
        out_a[4 * nodes :, :] = rest
        out_b[4 * nodes :, :] = rest
        for copy in copies:
            copy.wait()


class FlowPlan:
    def __init__(self, tiles):
        self.tiles = tiles
        self.wide = tiles + 2 * EDGE
        self.blocks = 4
        self.rows = (tiles + 4 * HW) // self.blocks
        self.span = self.rows + 2 * HW

    def at(self, b):
        return HW + b * self.rows

    def inner(self):
        return range(1, self.blocks - 1)


def columns_of(place):
    return slice(place * LANES, (place + 1) * LANES)


def rows_between(parts, low, high, columns):
    taken = []
    for start, ref in parts:
        a, b = max(low, start), min(high, start + ref.shape[0])
        if a < b:
            taken.append(ref[a - start : b - start, columns])
    return taken[0] if len(taken) == 1 else jnp.concatenate(taken, 0)


def put(high, low, at, place, value):
    h, l = split_parts(value)
    high[at : at + value.shape[0], columns_of(place)] = h
    low[at : at + value.shape[0], columns_of(place)] = l


def east_west(x):
    return pltpu.roll(x, LANES - 1, 1), pltpu.roll(x, 1, 1)


def link_matrix(plan, b, first_tile, given, mat):
    rows, span = plan.rows, plan.span
    lane = lax.broadcasted_iota(jnp.int32, (rows, 2 * span), 1)
    lane = jnp.where(lane >= span, lane - span, lane)
    own = first_tile - EDGE + plan.at(b) + lax.broadcasted_iota(jnp.int32, (rows, LANES), 0)
    place = jnp.where(given < 0, own, given.astype(jnp.int32)) - (first_tile - EDGE + b * rows)
    hot = [jnp.where(place[:, k : k + 1] == lane, F32(1.0), F32(0.0)) for k in range(4)]
    mat[:rows, :] = (hot[0] + hot[1] + hot[2] + hot[3]).astype(BF16)
    mat[rows : 2 * rows, :] = (hot[0] - hot[1]).astype(BF16)
    mat[2 * rows :, :] = (hot[2] - hot[3]).astype(BF16)


def gathered(plan, mat, high, low, b, columns, at_row):
    at = b * plan.rows
    both = [rows_between(x, at, at + plan.span, columns) for x in (high, low)]
    return dot(mat[at_row:, :], jnp.concatenate(both, 0))


def advance(plan, b, mat, high, low, state, v, new_state, new_high, new_low, new_at, wanted):
    rows = plan.rows
    center = [state(k) for k in range(3)]
    scaled = [(0.5 * ADVECT) * c for c in center]
    for first, last in ((0, 2), (2, 4), (4, 5)):
        got = gathered(plan, mat, high, low, b, slice(first * LANES, last * LANES), 0)
        for place in range(first, last):
            inner = columns_of(place - first)
            total, dy, dz = got[:rows, inner], got[rows : 2 * rows, inner], got[2 * rows :, inner]
            c = center[place] if place < 3 else state(place)
            east, west = east_west(c)
            new = (
                c
                + v * (east + west + total - 6.0 * c)
                - (scaled[0] * (east - west) + scaled[1] * dy + scaled[2] * dz)
            )
            new_state[new_at : new_at + rows, columns_of(place)] = new
            if place < wanted:
                put(new_high, new_low, new_at, place, new)


def lamb_block(plan, b, mat, high, low, state, average, average_out, packed):
    rows = plan.rows
    center = [state(k) for k in range(3)]
    got = [
        gathered(plan, mat, high, low, b, slice(0, 2 * LANES), rows),
        gathered(plan, mat, high, low, b, slice(2 * LANES, 3 * LANES), rows),
    ]
    d1, d2, d3 = [], [], []
    for k in range(3):
        east, west = east_west(center[k])
        d1.append((east - west) * 0.5)
        inner = columns_of(k % 2)
        d2.append(got[k // 2][:rows, inner] * 0.5)
        d3.append(got[k // 2][rows:, inner] * 0.5)
    vx = d2[2] - d3[1]
    vy = d3[0] - d1[2]
    vz = d1[1] - d2[0]
    lamb = (
        vy * center[2] - vz * center[1],
        vz * center[0] - vx * center[2],
        vx * center[1] - vy * center[0],
    )
    to = plan.at(b) - EDGE
    low_row, top_row = max(0, -to), min(rows, plan.tiles - to)
    own = slice(to + low_row, to + top_row)
    for i in range(3):
        packed[i, own, :] = lamb[i][low_row:top_row]
        mixed = (1.0 - RELAX) * average[i, own, :] + RELAX * center[i][low_row:top_row]
        average_out[i, own, :] = mixed
        packed[3 + i, own, :] = mixed


def element_sums(projector, packed, hits, pay, own_ref, next_ref):
    nodes = projector.shape[0]
    count, elements = own_ref.shape
    proj_high, proj_low = split_parts(projector[...])
    proj_both = jnp.concatenate([proj_high, proj_low], 0)
    for c in range(6):
        x_high, x_low = split_parts(packed[c])
        main = dot_t(proj_both, x_high)
        mapped = main[:nodes] + main[nodes:] + dot_t(proj_high, x_low)
        pay[c * nodes : (c + 1) * nodes, :] = mapped.astype(BF16)
    if count > 6 * nodes:
        pay[6 * nodes :, :] = jnp.ones((count - 6 * nodes, pay.shape[1]), BF16)
    sums = dot_t(pay[...], hits[...])
    if count > 6 * nodes:
        tail = sums[6 * nodes :]
        line = lax.broadcasted_iota(jnp.int32, tail.shape, 0)
        big = jnp.floor(tail * (1.0 / BASE))
        tail = jnp.where(line == 0, tail - BASE * big, jnp.where(line == 1, big, 0.0))
        sums = jnp.concatenate([sums[: 6 * nodes], tail], 0)
    own_ref[...] = sums[:, :elements]
    next_ref[...] = sums[:, elements:].astype(BF16)


def inner_kernel(
    meta, flow, visc, links, target,
    inner_state, inner_high, inner_low, lcol, inner_mats, hits, high0, low0, square,
):
    plan = FlowPlan(flow.shape[1])
    tiles, rows = plan.tiles, plan.rows

    @pl.when(meta[0] == 1)
    def _():
        first_tile, first_element = meta[2], meta[3]
        for place, f in enumerate(FIELD_ORDER):
            put(high0, low0, 0, place, flow[f])
        square[...] = jnp.zeros_like(square)
        for part in range(tiles // LANES):
            square[:4, :] = links[:, part * LANES : (part + 1) * LANES].astype(F32)
            lcol[part * LANES : (part + 1) * LANES, :] = square[...].T
        local = target[...] - first_element
        hits[...] = jnp.where(
            lax.broadcasted_iota(jnp.int32, hits.shape, 0) == local, F32(1.0), F32(0.0)
        ).astype(BF16)
        for at, b in enumerate(plan.inner()):
            own = slice(plan.at(b) - EDGE, plan.at(b) - EDGE + rows)
            link_matrix(plan, b, first_tile, lcol[own, :], inner_mats.at[at])
            advance(
                plan, b, inner_mats.at[at], [(EDGE, high0)], [(EDGE, low0)],
                lambda place, own=own: flow[FIELD_ORDER[place], own, :],
                visc[own, :], inner_state, inner_high, inner_low, at * rows, 5,
            )


def band_parts(plan, edge, inner):
    rows, last = plan.rows, plan.blocks - 1
    return [
        (plan.at(0), edge.at[:rows]),
        (plan.at(1), inner),
        (plan.at(last), edge.at[rows:]),
    ]


def band_state(plan, b, edge, inner):
    at = plan.at(b)
    parts = band_parts(plan, edge, inner)
    return lambda place: rows_between(parts, at, at + plan.rows, columns_of(place))


def closed(plan, parts, zero):
    return [(0, zero), *parts, (plan.wide - HW, zero)]


def mats_of(plan, b, edge_mats, inner_mats):
    if b in plan.inner():
        return inner_mats.at[b - 1]
    return edge_mats.at[0 if b == 0 else 1]


def first_kernel(
    meta, flow, visc, mean, projector, part_a, part_b, sound, neighbours, codes,
    inner_state, inner_high, inner_low, lcol, inner_mats, hits,
    own_one, next_one, mean_one, base, grads,
    edge_state, edge_high, edge_low, edge_mats, edge_visc,
    square, state0, high0, low0, zero, packed, pay, rows_of, facing, remote, rhs,
):
    is_flow, even = meta[0] == 1, meta[1] == 1
    plan = FlowPlan(packed.shape[1])
    tiles, rows, span = plan.tiles, plan.rows, plan.span
    own_rows = span - EDGE

    @pl.when(is_flow)
    def _():
        first_tile = meta[2]

        def pick(at, size):
            a, b = part_a[at : at + size, :], part_b[at : at + size, :]
            return jnp.where(even, a, b), jnp.where(even, b, a)

        zero[...] = jnp.zeros_like(zero)
        for place, f in enumerate(FIELD_ORDER):
            before, after = pick(place * EDGE, EDGE)
            ends = (
                jnp.concatenate([before, flow[f, :own_rows, :]], 0),
                jnp.concatenate([flow[f, tiles - own_rows :, :], after], 0),
            )
            for side in range(2):
                state0[side, :, columns_of(place)] = ends[side]
                put(high0.at[side], low0.at[side], 0, place, ends[side])
        before, after = pick(5 * EDGE, EDGE)
        edge_visc[:rows, :] = jnp.concatenate([before[HW:], visc[: rows - EDGE + HW, :]], 0)
        edge_visc[rows:, :] = jnp.concatenate(
            [visc[tiles - (rows - EDGE + HW) :, :], after[: EDGE - HW]], 0
        )
        before, after = pick(6 * EDGE, 8)
        given = []
        for side, block in enumerate((before, after)):
            square[...] = jnp.zeros_like(square)
            square[:8, :] = block
            turned = square[...].T
            given.append(
                jnp.concatenate([turned[LANES - EDGE + HW :], lcol[: rows - EDGE + HW, :]], 0)
                if side == 0
                else jnp.concatenate(
                    [lcol[tiles - (rows - EDGE + HW) :, :], turned[: EDGE - HW]], 0
                )
            )
        for side, b in enumerate((0, plan.blocks - 1)):
            link_matrix(plan, b, first_tile, given[side], edge_mats.at[side])
            advance(
                plan, b, edge_mats.at[side],
                [(b * rows, high0.at[side])], [(b * rows, low0.at[side])],
                lambda place, side=side: state0[side, HW : HW + rows, columns_of(place)],
                edge_visc[side * rows : (side + 1) * rows, :],
                edge_state, edge_high, edge_low, side * rows, 5,
            )
        high1 = closed(plan, band_parts(plan, edge_high, inner_high), zero)
        low1 = closed(plan, band_parts(plan, edge_low, inner_low), zero)
        for b in range(plan.blocks):
            lamb_block(
                plan, b, mats_of(plan, b, edge_mats, inner_mats), high1, low1,
                band_state(plan, b, edge_state, inner_state), mean, mean_one, packed,
            )
        element_sums(projector, packed, hits, pay, own_one, next_one)

    @pl.when(jnp.logical_not(is_flow))
    def _():
        own_one[...] = jnp.zeros_like(own_one)
        next_one[...] = jnp.zeros_like(next_one)
        nodes, elements = sound.shape[1:]
        halves = elements // LANES
        block = 4 * nodes
        for v in range(4):
            for h in range(halves):
                rows_of[h * block + v * nodes : h * block + (v + 1) * nodes, :] = sound[
                    v, :, h * LANES : (h + 1) * LANES
                ]
        a, b = part_a[:block, :], part_b[:block, :]
        rows_of[halves * block : (halves + 1) * block, :] = jnp.where(even, a, b)
        rows_of[(halves + 1) * block : (halves + 2) * block, :] = jnp.where(even, b, a)
        for face in range(6):
            for part in range(halves + 2):
                facing_rows(rows_of, part * block, nodes, face ^ 1, facing.at[face, part])
            hot = hot_links(neighbours, face, meta[3], elements, True, True)
            remote_rows([facing[face, part] for part in range(halves + 2)], hot, remote, face)
        derivatives(rows_of, nodes, grads, rhs)
        add_faces(rows_of, nodes, remote, neighbours, codes, rhs, True)
        for n in range(nodes):
            base[n] = rows_of[pl.ds(n, 8, stride=nodes), :] + ACOUSTIC_STEP * rhs[n]


def second_kernel(
    meta, flow, visc, inner_state, inner_high, inner_low, inner_mats,
    edge_state, edge_high, edge_low, edge_mats, edge_visc,
    flow_out, state, high, low, passive, zero,
):
    plan = FlowPlan(flow.shape[1])
    rows = plan.rows
    is_flow = meta[0] == 1

    @pl.when(jnp.logical_not(is_flow))
    def _():
        flow_out[...] = flow[...]

    @pl.when(is_flow)
    def _():
        zero[...] = jnp.zeros_like(zero)
        high1 = closed(plan, band_parts(plan, edge_high, inner_high), zero)
        low1 = closed(plan, band_parts(plan, edge_low, inner_low), zero)
        for b in range(plan.blocks):
            if b in plan.inner():
                v = visc[plan.at(b) - EDGE : plan.at(b) - EDGE + rows, :]
            else:
                v = edge_visc[:rows, :] if b == 0 else edge_visc[rows:, :]
            advance(
                plan, b, mats_of(plan, b, edge_mats, inner_mats), high1, low1,
                band_state(plan, b, edge_state, inner_state), v,
                passive, high, low, b * rows, 3,
            )
        own = slice(EDGE - HW, EDGE - HW + plan.tiles)
        state[...] = passive[:, : state.shape[1]]
        for place, f in enumerate(FIELD_ORDER):
            flow_out[f] = passive[own, columns_of(place)]


def sums_kernel(
    meta, mean, mean_one, projector, inner_mats, edge_mats, hits, state, high, low,
    mean_out, own_two, next_two, zero, packed, pay,
):
    plan = FlowPlan(packed.shape[1])
    rows = plan.rows
    is_flow = meta[0] == 1

    @pl.when(jnp.logical_not(is_flow))
    def _():
        mean_out[...] = mean[...]
        own_two[...] = jnp.zeros_like(own_two)
        next_two[...] = jnp.zeros_like(next_two)

    @pl.when(is_flow)
    def _():
        zero[...] = jnp.zeros_like(zero)
        for b in range(plan.blocks):
            lamb_block(
                plan, b, mats_of(plan, b, edge_mats, inner_mats),
                closed(plan, [(HW, high)], zero), closed(plan, [(HW, low)], zero),
                lambda place, b=b: state[b * rows : (b + 1) * rows, columns_of(place)],
                mean_one, mean_out, packed,
            )
        element_sums(projector, packed, hits, pay, own_two, next_two)


def facing_rows(rows_of, base, nodes, face, to):
    axis, level = face // 2, 3 * (face % 2)
    if axis == 0:
        to[...] = rows_of[pl.ds(base + level, 64, stride=4), :]
    elif axis == 1:
        for i in range(4):
            to[pl.ds(i, 16, stride=4), :] = rows_of[pl.ds(base + i + 4 * level, 16, stride=16), :]
    else:
        for v in range(4):
            at = base + v * nodes + 16 * level
            to[v * 16 : (v + 1) * 16, :] = rows_of[at : at + 16, :]


def hot_links(neighbours, face, first_element, elements, own, beside):
    link = neighbours[face : face + 1, :]
    near = link - first_element
    size = (elements if own else 0) + (2 * LANES if beside else 0)
    start = elements if own else 0
    place = jnp.where(near < 0, start + LANES + near, near - elements + start + LANES)
    inside = (near >= 0) & (near < elements)
    place = jnp.where(inside, near if own else -1, place if beside else -1)
    place = jnp.where(link < 0, -1, place)
    key = lax.broadcasted_iota(jnp.int32, (size, elements), 0)
    return jnp.where(key == place, F32(1.0), F32(0.0)).astype(BF16)


def remote_rows(parts, hot, remote, face):
    x = jnp.concatenate(parts, 1)
    if x.dtype == BF16:
        got = dot(x, hot)
    else:
        high, low = split_parts(x)
        got = dot(jnp.concatenate([high, low], 0), hot)
        got = got[:64] + got[64:]
    for h in range(got.shape[1] // LANES):
        remote[face, h * 64 : (h + 1) * 64, :] = got[:, h * LANES : (h + 1) * LANES]


def derivatives(rows_of, nodes, grads_out, rhs):
    matrix = lobatto_matrix()
    line = lax.broadcasted_iota(jnp.int32, (8, LANES), 0)
    is_v = [line % 4 == v for v in range(4)]
    node = [rows_of[pl.ds(n, 8, stride=nodes), :] for n in range(nodes)]
    for n in range(nodes):
        i, j, k = n % 4, n // 4 % 4, n // 16
        lines = (
            [m + 4 * j + 16 * k for m in range(4)],
            [i + 4 * m + 16 * k for m in range(4)],
            [i + 4 * j + 16 * m for m in range(4)],
        )
        grads = []
        for d, at in enumerate((i, j, k)):
            total = None
            for m in range(4):
                if abs(matrix[at, m]) > 1e-12:
                    term = F32(matrix[at, m]) * node[lines[d][m]]
                    total = term if total is None else total + term
            grads.append(total)
            grads_out[d, n] = total
        div = sum(pltpu.roll(grads[d], 8 - (1 + d), 0) for d in range(3))
        coupled = jnp.where(is_v[0], div, 0.0)
        for d in range(3):
            coupled = jnp.where(is_v[1 + d], pltpu.roll(grads[d], 1 + d, 0), coupled)
        rhs[n] = -coupled


def add_faces(rows_of, nodes, remote, neighbours, codes, rhs, own):
    upper = lax.broadcasted_iota(jnp.int32, (8, LANES), 0) >= 4
    for face in range(6):

        def both(row):
            return jnp.where(
                upper,
                jnp.broadcast_to(row[:, LANES:], (8, LANES)),
                jnp.broadcast_to(row[:, :LANES], (8, LANES)),
            )

        code = both(codes[face : face + 1, :])
        valid = both(neighbours[face : face + 1, :]) >= 0
        is_turn = [code == t for t in range(4)]
        planes = [remote[face, pl.ds(p, 8, stride=16), :] for p in range(16)]
        for p, n in enumerate(face_nodes(face)):
            jump = planes[turned_position(3, p)]
            for t in range(3):
                jump = jnp.where(is_turn[t], planes[turned_position(t, p)], jump)
            if own:
                jump = jnp.where(valid, jump - rows_of[pl.ds(n, 8, stride=nodes), :], 0.0)
            rhs[n] = rhs[n] + PENALTY * jump


def source_rows(total, nodes, lamb, mean):
    block = 4 * nodes
    for h in range(total.shape[1] // LANES):
        columns = slice(h * LANES, (h + 1) * LANES)
        lamb[h * block : h * block + nodes, :] = jnp.zeros((nodes, LANES), F32)
        for d in range(3):
            at = h * block + (1 + d) * nodes
            lamb[at : at + nodes, :] = total[d * nodes : (d + 1) * nodes, columns]
            value = total[(3 + d) * nodes : (4 + d) * nodes, columns]
            for v in range(4):
                at = h * block + v * nodes
                mean[d, at : at + nodes, :] = value


def source_terms(nodes, grads, lamb, mean, n):
    total = lamb[pl.ds(n, 8, stride=nodes), :]
    for d in range(3):
        total = total + mean[d, pl.ds(n, 8, stride=nodes), :] * grads[d, n]
    return total


def sound_one_kernel(
    meta, base, grads, source_a, source_b, rows_of, scale_out, edge_a, edge_b, lamb, mean
):
    is_flow, even = meta[0] == 1, meta[1] == 1
    nodes = base.shape[0]
    block = 4 * nodes

    @pl.when(jnp.logical_not(is_flow))
    def _():
        total = source_a[...].astype(F32) + source_b[...].astype(F32)
        count = total[6 * nodes : 6 * nodes + 1] + BASE * total[6 * nodes + 1 : 6 * nodes + 2]
        inverse = 1.0 / jnp.maximum(count, 1.0)
        scale_out[...] = jnp.broadcast_to(inverse, scale_out.shape)
        source_rows(total[: 6 * nodes] * inverse, nodes, lamb, mean)
        for n in range(nodes):
            rows_of[pl.ds(n, 8, stride=nodes), :] = base[n] - ACOUSTIC_STEP * source_terms(
                nodes, grads, lamb, mean, n
            )
        off_a = pl.multiple_of(jnp.where(even, 0, block), 16)
        off_b = pl.multiple_of(jnp.where(even, block, 0), 16)
        edge_a[...] = rows_of[pl.ds(off_a, block), :].astype(BF16)
        edge_b[...] = rows_of[pl.ds(off_b, block), :].astype(BF16)


def sound_inner_kernel(
    meta, rows_of, neighbours, codes, base, grads, hot_beside, facing, remote, rhs
):
    nodes = base.shape[0]
    elements = neighbours.shape[1]
    halves = elements // LANES
    block = 4 * nodes

    @pl.when(meta[0] == 0)
    def _():
        for face in range(6):
            for part in range(halves):
                facing_rows(rows_of, part * block, nodes, face ^ 1, facing.at[face, part])
            hot = hot_links(neighbours, face, meta[3], elements, True, False)
            remote_rows([facing[face, part] for part in range(halves)], hot, remote, face)
            hot_beside[face] = hot_links(neighbours, face, meta[3], elements, False, True)
        derivatives(rows_of, nodes, grads, rhs)
        add_faces(rows_of, nodes, remote, neighbours, codes, rhs, True)
        for n in range(nodes):
            base[n] = rows_of[pl.ds(n, 8, stride=nodes), :] + ACOUSTIC_STEP * rhs[n]


def sound_two_kernel(
    meta, sound, base, grads, hot_beside, neighbours, codes, scale, source_a, source_b,
    part_a, part_b,
    out, rows_of, facing, remote, rhs, lamb, mean,
):
    is_flow, even = meta[0] == 1, meta[1] == 1
    nodes = base.shape[0]
    elements = sound.shape[2]
    halves = elements // LANES
    block = 4 * nodes

    @pl.when(is_flow)
    def _():
        out[...] = sound[...]

    @pl.when(jnp.logical_not(is_flow))
    def _():
        total = source_a[...].astype(F32) + source_b[...].astype(F32)
        source_rows(total * scale[0:1, :], nodes, lamb, mean)
        a, b = part_a[...].astype(F32), part_b[...].astype(F32)
        rows_of[:block, :] = jnp.where(even, a, b)
        rows_of[block:, :] = jnp.where(even, b, a)
        for face in range(6):
            for part in range(2):
                facing_rows(rows_of, part * block, nodes, face ^ 1, facing.at[face, part])
            remote_rows(
                [facing[face, part].astype(BF16) for part in range(2)], hot_beside[face], remote, face
            )
        for n in range(nodes):
            rhs[n] = -source_terms(nodes, grads, lamb, mean, n)
        add_faces(rows_of, nodes, remote, neighbours, codes, rhs, False)
        for n in range(nodes):
            rows_of[pl.ds(n, 8, stride=nodes), :] = base[n] + ACOUSTIC_STEP * rhs[n]
        for v in range(4):
            for h in range(halves):
                out[v, :, h * LANES : (h + 1) * LANES] = rows_of[
                    h * block + v * nodes : h * block + (v + 1) * nodes, :
                ]


def call(kernel, outs, scratch, operands, flops=1e8, in_hbm=(), limit=VMEM_LIMIT):
    spaces = [pltpu.SMEM] + [
        pltpu.HBM if at in in_hbm else pltpu.VMEM for at in range(1, len(operands))
    ]
    moved = sum(int(np.prod(x.shape)) * x.dtype.itemsize for x in (*operands, *outs))
    return pl.pallas_call(
        kernel,
        out_shape=tuple(outs),
        in_specs=[pl.BlockSpec(memory_space=space) for space in spaces],
        out_specs=tuple([pl.BlockSpec(memory_space=pltpu.VMEM)] * len(outs)),
        scratch_shapes=scratch,
        compiler_params=pltpu.CompilerParams(vmem_limit_bytes=limit),
        cost_estimate=pl.CostEstimate(flops=int(flops), bytes_accessed=moved, transcendentals=0),
    )(*operands)


def body(
    flow_fields,
    mean_velocity,
    cell_eddy_viscosity,
    tile_links,
    tile_target,
    projector,
    acoustic_state,
    element_face_neighbours,
    face_codes,
):
    groups = lax.axis_size("grp")
    count = lax.axis_size("sfc")
    group_index = lax.axis_index("grp")
    column = lax.axis_index("sfc")
    flow = flow_fields[0]
    mean = mean_velocity[0]
    visc = cell_eddy_viscosity[0]
    links = tile_links[0]
    sound = acoustic_state[0]
    neighbours = element_face_neighbours[0]
    codes = face_codes[0]
    tiles = flow.shape[1]
    _, nodes, elements = sound.shape
    halves = elements // LANES
    block = 4 * nodes
    plan = FlowPlan(tiles)
    shape = jax.ShapeDtypeStruct
    vmem = pltpu.VMEM
    meta = jnp.stack(
        [
            (group_index < groups - 1).astype(jnp.int32),
            (column % 2 == 0).astype(jnp.int32),
            (column * tiles).astype(jnp.int32),
            (column * elements).astype(jnp.int32),
        ]
    )

    pairs_a = [p for i in range(1, count - 1, 2) for p in ((i, i + 1), (i + 1, i))]
    pairs_b = [p for i in range(0, count - 1, 2) for p in ((i, i + 1), (i + 1, i))]

    edge_rows = 6 * EDGE + 8
    pack_a, pack_b = call(
        pack_kernel,
        [shape((edge_rows, LANES), F32)] * 2,
        [
            vmem(links.shape, jnp.int32),
            pltpu.SemaphoreType.DMA((2, 6)),
            pltpu.SemaphoreType.DMA,
        ],
        [meta, flow, visc, links, sound],
        in_hbm=(1, 2, 3, 4),
        limit=PACK_LIMIT,
    )
    part_a = lax.ppermute(pack_a, "sfc", pairs_a)
    part_b = lax.ppermute(pack_b, "sfc", pairs_b)

    fields = 5 * LANES
    rows, span = plan.rows, plan.span
    inner_rows = (plan.blocks - 2) * rows
    square = vmem((LANES, LANES), F32)
    packed = vmem((6, tiles, LANES), F32)
    inner_state, inner_high, inner_low, lcol, inner_mats, hits = call(
        inner_kernel,
        [
            shape((inner_rows, fields), F32),
            shape((inner_rows, fields), BF16),
            shape((inner_rows, fields), BF16),
            shape((tiles, LANES), F32),
            shape((plan.blocks - 2, 3 * rows, 2 * span), BF16),
            shape((2 * elements, tiles), BF16),
        ],
        [vmem((tiles, fields), BF16), vmem((tiles, fields), BF16), square],
        [meta, flow, visc, links, tile_target],
        flops=1e9,
    )
    lines = 6 * nodes + EXTRA
    by_node = shape((nodes, 8, LANES), F32)
    by_node_3 = shape((3, nodes, 8, LANES), F32)
    node_rows = vmem((nodes, 8, LANES), F32)
    (
        own_one, next_one, mean_one, base, grads,
        edge_state, edge_high, edge_low, edge_mats, edge_visc,
    ) = call(
        first_kernel,
        [
            shape((lines, elements), F32),
            shape((lines, elements), BF16),
            shape(mean.shape, F32),
            by_node,
            by_node_3,
            shape((2 * rows, fields), F32),
            shape((2 * rows, fields), BF16),
            shape((2 * rows, fields), BF16),
            shape((2, 3 * rows, 2 * span), BF16),
            shape((2 * rows, LANES), F32),
        ],
        [
            square,
            vmem((2, span, fields), F32),
            vmem((2, span, fields), BF16),
            vmem((2, span, fields), BF16),
            vmem((HW, fields), BF16),
            packed,
            vmem((lines, tiles), BF16),
            vmem(((halves + 2) * block, LANES), F32),
            vmem((6, halves + 2, 64, LANES), F32),
            vmem((6, halves * 64, LANES), F32),
            node_rows,
        ],
        [
            meta, flow, visc, mean, projector, part_a, part_b, sound, neighbours, codes,
            inner_state, inner_high, inner_low, lcol, inner_mats, hits,
        ],
        flops=1e9,
    )

    up = [(i, i + 1) for i in range(count - 1)]

    def climb(x):
        chosen = [(g * count + i, g * count + j) for g in range(groups - 1) for i, j in up]
        return lax.ppermute(x, ("grp", "sfc"), chosen)

    def combined(*xs):
        total = xs[0]
        for x in xs[1:]:
            total = total + x.astype(F32)
        return total.astype(BF16)

    got_one = climb(next_one)
    velocity = 3 * LANES
    band = plan.blocks * rows
    flow_out, state2, high2, low2 = call(
        second_kernel,
        [
            shape(flow.shape, F32),
            shape((band, velocity), F32),
            shape((band, velocity), BF16),
            shape((band, velocity), BF16),
        ],
        [vmem((band, fields), F32), vmem((HW, fields), BF16)],
        [
            meta, flow, visc, inner_state, inner_high, inner_low, inner_mats,
            edge_state, edge_high, edge_low, edge_mats, edge_visc,
        ],
        flops=1e9,
    )
    sum_one, high2 = lax.optimization_barrier((combined(own_one, got_one), high2))
    x_one = lax.ppermute(sum_one, "grp", [(0, 1), (2, 3)])
    mean_out, own_two, next_two = call(
        sums_kernel,
        [
            shape(mean.shape, F32),
            shape((6 * nodes, elements), F32),
            shape((6 * nodes, elements), BF16),
        ],
        [vmem((HW, velocity), BF16), packed, vmem((6 * nodes, tiles), BF16)],
        [meta, mean, mean_one, projector, inner_mats, edge_mats, hits, state2, high2, low2],
        flops=1e9,
    )
    got_two = climb(next_two)
    sum_one = combined(own_one, got_one, x_one)
    sum_one, own_two = lax.optimization_barrier((sum_one, own_two))
    sum_two = lax.optimization_barrier(combined(own_two, got_two))
    padded = jnp.pad(sum_two, ((0, EXTRA), (0, 0)))
    cross = lax.ppermute(jnp.where(group_index == 0, padded, sum_one), "grp", [(0, 2), (1, 3)])
    y_two = lax.ppermute(sum_two, "grp", [(1, 3)])

    sound_rows, scale, edge_a, edge_b = call(
        sound_one_kernel,
        [
            shape((halves * block, LANES), F32),
            shape((8, elements), F32),
            shape((block, LANES), BF16),
            shape((block, LANES), BF16),
        ],
        [vmem((halves * block, LANES), F32), vmem((3, halves * block, LANES), F32)],
        [meta, base, grads, x_one, cross],
    )
    last = (groups - 1) * count
    part_a = lax.ppermute(edge_a, ("grp", "sfc"), [(last + i, last + j) for i, j in pairs_a])
    part_b = lax.ppermute(edge_b, ("grp", "sfc"), [(last + i, last + j) for i, j in pairs_b])
    base, grads, hot_beside = call(
        sound_inner_kernel,
        [by_node, by_node_3, shape((6, 2 * LANES, elements), BF16)],
        [
            vmem((6, halves, 64, LANES), F32),
            vmem((6, halves * 64, LANES), F32),
            node_rows,
        ],
        [meta, sound_rows, neighbours, codes],
    )
    x_two = lax.ppermute(combined(own_two, got_two, cross[: 6 * nodes]), "grp", [(2, 3)])
    (sound_out,) = call(
        sound_two_kernel,
        [shape(sound.shape, F32)],
        [
            vmem((halves * block, LANES), F32),
            vmem((6, 2, 64, LANES), F32),
            vmem((6, halves * 64, LANES), F32),
            node_rows,
            vmem((halves * block, LANES), F32),
            vmem((3, halves * block, LANES), F32),
        ],
        [
            meta, sound, base, grads, hot_beside, neighbours, codes, scale,
            x_two, y_two, part_a, part_b,
        ],
    )
    return flow_out[None], mean_out[None], sound_out[None]


def solution(mesh):
    placed = (
        P("grp", None, "sfc", None),
        P("grp", None, "sfc", None),
        P("grp", "sfc", None),
        P("grp", None, "sfc"),
        P("grp", "sfc"),
        P(),
        P("grp", None, None, "sfc"),
        P("grp", None, "sfc"),
        P("grp", None, "sfc"),
    )
    return jax.shard_map(
        body,
        mesh=mesh,
        in_specs=placed,
        out_specs=(
            P("grp", None, "sfc", None),
            P("grp", None, "sfc", None),
            P("grp", None, None, "sfc"),
        ),
        check_vma=False,
    )
```

time: 362 us -> 55.2 us (0.15)
  the two profiles are of different devices: /device:TPU:1 before, /device:TPU:15 now
where the time goes in v2:
time: 55.2 us; the launch traced here: 54.7 us
  starting transfers between devices  18.9 us (34%)
  waiting for transfers between devices  15.4 us (28%)
  Pallas kernels  14.4 us (26%)
  local copies, waits for them, and re-layouts  4.13 us (7%)
  between operations  0.97 us (2%)
  other arithmetic  0.9 us (2%)
    pallas_call x8, Pallas kernels, call(): pl.pallas_call(kernel, out_shape=tuple(outs), in_specs=[pl.BlockSpec(memo...  14.4 us
    ppermute x1, waiting for transfers between devices, body(): lax.ppermute(jnp.where(group_index == 0, padded, sum_one), 'grp', [(0, 2)...  8.6 us
    ppermute x1, starting transfers between devices, body(): lax.ppermute(edge_a, ('grp', 'sfc'), [(last + i, last + j) for i, j in pa...  6.58 us
    ppermute x1, waiting for transfers between devices, body(): x_one = lax.ppermute(sum_one, 'grp', [(0, 1), (2, 3)])  4.87 us
    unnamed x43, local copies, waits for them, and re-layouts  4.13 us
    ppermute x1, starting transfers between devices, body(): part_a = lax.ppermute(pack_a, 'sfc', pairs_a)  3.76 us
    ppermute x1, waiting for transfers between devices, body(): part_a = lax.ppermute(pack_a, 'sfc', pairs_a)  1.95 us
    ppermute x1, starting transfers between devices, body(): lax.ppermute(edge_b, ('grp', 'sfc'), [(last + i, last + j) for i, j in pa...  1.92 us
  transfers between devices with their start and end apart: 10, of which 3 were waited for; matrix products, arithmetic and copies ran while one was open for 0% of the time, Pallas kernels for 12%

profile of v2, /device:TPU:15, one launch (start us, length us, event | category | flops | bytes accessed | tf_op | source)
XLA Modules:
  0.0 54.7 jit_solution(13242716840817712319)
XLA Ops:
  0.6 0.0 copy-start.2
  0.7 0.6 %pad_add_fusion.meta = s32[4]{0:T(128)} fusion(s32[1]{0:T(128)} %bitcast.2, s32[1]{0:T(128)} %bitcast.1, s32[1]{0:T(128)} %bitcast), kind=kLoop, calls=%fused_computation.9 | loop fusion | flops 12 | bytes 28 | tf_op jit(solution)/shard_map/stack | solution.py:719
  1.2 2.5 %shard_map.113 = (f32[296,128]{1,0:T(8,128)}, f32[296,128]{1,0:T(8,128)}) custom-call(s32[4]{0:T(128)} %pad_add_fusion.meta, f32[5,256,128]{2,1,0:T(8,128)} %bitcast.18, f32[256,128]{1,0:T(8,128)} %bitcast.22, s32[4,256]{1,0:T(4,128)} %bitcast.26, f32[4,64,256]{2,1,0:T(8,128)} %bitcast.15), custom_call_target="tpu_custom_call" | custom-call | flops 100000000 | bytes 1355792 | tf_op jit(solution)/shard_map/pallas_call | solution.py:679
  3.8 3.8 %collective-permute-start = (f32[296,128]{1,0:T(8,128)}, f32[296,128]{1,0:T(8,128)S(1)}, u32[]{:S(2)}, u32[]{:S(2)}) collective-permute-start(f32[296,128]{1,0:T(8,128)} %get-tuple-element.43), channel_id=1, source_target_pairs={{1,2},{2,1},{3,4},{4,3},{5,6},{6,5},{9,10},{10,9},{11,12},{12,11},... | collective-permute-start | bytes 454664 | tf_op jit(solution)/shard_map/ppermute | solution.py:744
  7.5 0.0 copy-start.5
  7.6 0.0 copy-start.8
  7.6 0.1 collective-permute-start.1
  7.6 0.0 copy-done.19
  7.7 0.4 copy-done.4
  8.1 0.1 copy-done.5
  8.2 0.0 copy-done.8
  8.2 0.5 %shard_map.112 = (f32[160,640]{1,0:T(8,128)S(1)}, bf16[160,640]{1,0:T(8,128)(2,1)S(1)}, bf16[160,640]{1,0:T(8,128)(2,1)S(1)}, f32[256,128]{1,0:T(8,128)S(1)}, bf...) custom-call(s32[4]{0:T(128)S(1)} %copy-done.4, f32[5,256,128]{2,1,0:T(8,128)S(1)} %bitcast.19, ...), custom_call_target="tpu_custom_call" | custom-call | flops 1000000000 | bytes 2219024 | tf_op jit(solution)/shard_map/pallas_call | solution.py:679
  8.8 2.0 %collective-permute-done.part_a = f32[296,128]{1,0:T(8,128)S(1)} collective-permute-done((f32[296,128]{1,0:T(8,128)}, f32[296,128]{1,0:T(8,128)S(1)}, u32[]{:S(2)}, u32[]{:S(2)}) %collective-permute-start) | collective-permute-done | bytes 151584 | tf_op jit(solution)/shard_map/ppermute | solution.py:744
  10.8 0.0 collective-permute-done.1.part_b
  10.8 2.8 %shard_map.114 = (f32[400,256]{1,0:T(8,128)S(1)}, bf16[400,256]{1,0:T(8,128)(2,1)S(1)}, f32[3,256,128]{2,1,0:T(8,128)S(1)}, f32[64,8,128]{2,1,0:T(8,128)S(1)}, f...) custom-call(s32[4]{0:T(128)S(1)} %copy-done.4, ...), custom_call_target="tpu_custom_call" | custom-call | flops 1000000000 | bytes 6389776 | tf_op jit(solution)/shard_map/pallas_call | solution.py:679
  13.6 0.7 %collective-permute-start.2 = (bf16[400,256]{1,0:T(8,128)(2,1)S(1)}, bf16[400,256]{1,0:T(8,128)(2,1)S(1)}, u32[]{:S(2)}, u32[]{:S(2)}) collective-permute-start(bf16[400,256]{1,0:T(8,128)(2,1)S(1)} %get-tuple-element.56), channel_id=1, source_target_pairs={{0,1},{1,2},{2,3},{3,4},{4,5},{5,6},{6,7},{8,9},{9,10},{10,11},{11... | collective-permute-start | bytes 614408 | tf_op jit(solution)/shard_map/ppermute | solution.py:811
  14.2 1.4 %shard_map.115 = (f32[5,256,128]{2,1,0:T(8,128)}, f32[320,384]{1,0:T(8,128)S(1)}, bf16[320,384]{1,0:T(8,128)(2,1)S(1)}, bf16[320,384]{1,0:T(8,128)(2,1)S(1)}) custom-call(s32[4]{0:T(128)S(1)} %copy-done.4, f32[5,256,128]{2,1,0:T(8,128)S(1)} %bitcast.21, f32[256,128]{1,0:T(8,128)S(1)} %bitcast.25, f32[160,640]{1,0:T(8,128)S(1)} %get-tuple-element.39.inner_state, ...), custom_call_target="tpu_custom_call" | custom-call | flops 1000000000 | bytes 4575248 | tf_op jit(solution)/shard_map/pallas_call | solution.py:679
  15.7 0.7 %copy-done.15 = bf16[320,384]{1,0:T(8,128)(2,1)} copy-done((bf16[320,384]{1,0:T(8,128)(2,1)}, bf16[320,384]{1,0:T(8,128)(2,1)S(1)}, u32[]{:S(2)}) %copy-start.15) | copy-done | bytes 245784
  16.4 0.0 collective-permute-done.2
  16.4 0.0 copy-start.10
  16.4 0.1 fusion
  16.5 0.7 %copy-done.11 = f32[320,384]{1,0:T(8,128)} copy-done((f32[320,384]{1,0:T(8,128)}, f32[320,384]{1,0:T(8,128)S(1)}, u32[]{:S(2)}) %copy-start.11) | copy-done | bytes 491544
  17.2 0.1 copy-done.13
  17.2 0.1 copy-done.17
  17.3 1.3 %collective-permute-start.3 = (bf16[400,256]{1,0:T(8,128)(2,1)S(1)}, bf16[400,256]{1,0:T(8,128)(2,1)S(1)}, u32[]{:S(2)}, u32[]{:S(2)}) collective-permute-start(bf16[400,256]{1,0:T(8,128)(2,1)S(1)} %fusion), channel_id=1, source_target_pairs={{0,8},{16,24},{1,9},{17,25},{2,10},{18,26},{3,11},{19,27},{4,12},{... | collective-permute-start | bytes 614408 | tf_op jit(solution)/shard_map/ppermute | solution.py:838
  18.6 1.0 %copy-done.12 = f32[320,384]{1,0:T(8,128)S(1)} copy-done((f32[320,384]{1,0:T(8,128)S(1)}, f32[320,384]{1,0:T(8,128)}, u32[]{:S(2)}) %copy-start.12) | copy-done | bytes 491544
  19.7 0.9 %copy-done.14 = bf16[320,384]{1,0:T(8,128)(2,1)S(1)} copy-done((bf16[320,384]{1,0:T(8,128)(2,1)S(1)}, bf16[320,384]{1,0:T(8,128)(2,1)}, u32[]{:S(2)}) %copy-start.14) | copy-done | bytes 245784
  20.6 1.4 %shard_map.116 = (f32[3,256,128]{2,1,0:T(8,128)}, f32[384,256]{1,0:T(8,128)S(1)}, bf16[384,256]{1,0:T(8,128)(2,1)S(1)}) custom-call(s32[4]{0:T(128)S(1)} %copy-done.4, f32[3,256,128]{2,1,0:T(8,128)S(1)} %bitcast.29, f32[3,256,128]{2,1,0:T(8,128)S(1)} %get-tuple-element.53.mean_one, f32[64,128]{1,0:T(8,128)S(1)} %copy-done.7, ...), custom_call_target="tpu_custom_call" | custom-call | flops 1000000000 | bytes 3477520 | tf_op jit(solution)/shard_map/pallas_call | solution.py:679
  22.0 0.7 %collective-permute-start.4 = (bf16[384,256]{1,0:T(8,128)(2,1)S(1)}, bf16[384,256]{1,0:T(8,128)(2,1)S(1)}, u32[]{:S(2)}, u32[]{:S(2)}) collective-permute-start(bf16[384,256]{1,0:T(8,128)(2,1)S(1)} %get-tuple-element.66), channel_id=1, source_target_pairs={{0,1},{1,2},{2,3},{3,4},{4,5},{5,6},{6,7},{8,9},{9,10},{10,11},{11... | collective-permute-start | bytes 589832 | tf_op jit(solution)/shard_map/ppermute | solution.py:811
  22.6 4.9 %collective-permute-done.3.source_a = bf16[400,256]{1,0:T(8,128)(2,1)S(1)} collective-permute-done((bf16[400,256]{1,0:T(8,128)(2,1)S(1)}, bf16[400,256]{1,0:T(8,128)(2,1)S(1)}, u32[]{:S(2)}, u32[]{:S(2)}) %collective-permute-start.3) | collective-permute-done | bytes 204832 | tf_op jit(solution)/shard_map/ppermute | solution.py:838
  27.5 0.1 add_convert_fusion
  27.6 0.0 collective-permute-done.4
  27.6 0.1 fusion.1
  27.7 0.1 pad_select_fusion
  27.7 1.4 %collective-permute-start.5 = (bf16[400,256]{1,0:T(8,128)(2,1)S(1)}, bf16[400,256]{1,0:T(8,128)(2,1)S(1)}, u32[]{:S(2)}, u32[]{:S(2)}) collective-permute-start(bf16[400,256]{1,0:T(8,128)(2,1)S(1)} %pad_select_fusion), channel_id=1, source_target_pairs={{0,16},{8,24},{1,17},{9,25},{2,18},{10,26},{3,19},{11,27},{4,20},{... | collective-permute-start | bytes 614408 | tf_op jit(solution)/shard_map/ppermute | solution.py:855
  29.2 1.3 %collective-permute-start.7 = (bf16[384,256]{1,0:T(8,128)(2,1)S(1)}, bf16[384,256]{1,0:T(8,128)(2,1)S(1)}, u32[]{:S(2)}, u32[]{:S(2)}) collective-permute-start(bf16[384,256]{1,0:T(8,128)(2,1)S(1)} %fusion.1), channel_id=1, source_target_pairs={{8,24},{9,25},{10,26},{11,27},{12,28},{13,29},{14,30},{15,31}} | collective-permute-start | bytes 589832 | tf_op jit(solution)/shard_map/ppermute | solution.py:856
  30.5 8.6 %collective-permute-done.5.source_b = bf16[400,256]{1,0:T(8,128)(2,1)S(1)} collective-permute-done((bf16[400,256]{1,0:T(8,128)(2,1)S(1)}, bf16[400,256]{1,0:T(8,128)(2,1)S(1)}, u32[]{:S(2)}, u32[]{:S(2)}) %collective-permute-start.5) | collective-permute-done | bytes 204832 | tf_op jit(solution)/shard_map/ppermute | solution.py:855
  39.1 0.1 add_convert_fusion.1
  39.1 1.3 %collective-permute-start.6 = (bf16[384,256]{1,0:T(8,128)(2,1)S(1)}, bf16[384,256]{1,0:T(8,128)(2,1)S(1)}, u32[]{:S(2)}, u32[]{:S(2)}) collective-permute-start(bf16[384,256]{1,0:T(8,128)(2,1)S(1)} %add_convert_fusion.1), channel_id=1, source_target_pairs={{16,24},{17,25},{18,26},{19,27},{20,28},{21,29},{22,30},{23,31}} | collective-permute-start | bytes 589832 | tf_op jit(solution)/shard_map/ppermute | solution.py:882
  40.4 1.5 %shard_map.117 = (f32[512,128]{1,0:T(8,128)S(1)}, f32[8,256]{1,0:T(8,128)S(1)}, bf16[256,128]{1,0:T(8,128)(2,1)S(1)}, bf16[256,128]{1,0:T(8,128)(2,1)S(1)}) custom-call(s32[4]{0:T(128)S(1)} %copy-done.4, f32[64,8,128]{2,1,0:T(8,128)S(1)} %get-tuple-element.61.base, f32[3,64,8,128]{3,2,1,0:T(8,128)S(1)} %copy-done.1, ...), custom_call_target="tpu_custom_call" | custom-call | flops 100000000 | bytes 1859600 | tf_op jit(solution)/shard_map/pallas_call | solution.py:679
  41.9 6.6 %collective-permute-start.8 = (bf16[256,128]{1,0:T(8,128)(2,1)S(1)}, bf16[256,128]{1,0:T(8,128)(2,1)S(1)}, u32[]{:S(2)}, u32[]{:S(2)}) collective-permute-start(bf16[256,128]{1,0:T(8,128)(2,1)S(1)} %get-tuple-element.73), channel_id=1, source_target_pairs={{25,26},{26,25},{27,28},{28,27},{29,30},{30,29}} | collective-permute-start | bytes 196616 | tf_op jit(solution)/shard_map/ppermute | solution.py:870
  48.5 1.9 %collective-permute-start.9 = (bf16[256,128]{1,0:T(8,128)(2,1)S(1)}, bf16[256,128]{1,0:T(8,128)(2,1)S(1)}, u32[]{:S(2)}, u32[]{:S(2)}) collective-permute-start(bf16[256,128]{1,0:T(8,128)(2,1)S(1)} %get-tuple-element.74), channel_id=1, source_target_pairs={{24,25},{25,24},{26,27},{27,26},{28,29},{29,28},{30,31},{31,30}} | collective-permute-start | bytes 196616 | tf_op jit(solution)/shard_map/ppermute | solution.py:871
  50.4 1.7 %shard_map.118 = (f32[64,8,128]{2,1,0:T(8,128)S(1)}, f32[3,64,8,128]{3,2,1,0:T(8,128)S(1)}, bf16[6,256,256]{2,1,0:T(8,128)(2,1)S(1)}) custom-call(s32[4]{0:T(128)S(1)} %copy-done.4, f32[512,128]{1,0:T(8,128)S(1)} %get-tuple-element.68.rows_of, s32[6,256]{1,0:T(8,128)S(1)} %get-tuple-element.76.neighbours, s32[6,256]{1,0:T(8,128)S(1)} %get-tuple-element.75.codes), custom_call_target="tpu_custom_call" | custom-call | flops 100000000 | bytes 2109456 | tf_op jit(solution)/shard_map/pallas_call | solution.py:679
  52.1 0.0 collective-permute-done.7.source_b
  52.2 0.0 collective-permute-done.8.part_a
  52.2 0.0 collective-permute-done.9.part_b
  52.2 0.0 collective-permute-done.6.source_a
  52.2 2.5 %shard_map.119 = f32[4,64,256]{2,1,0:T(8,128)} custom-call(s32[4]{0:T(128)S(1)} %copy-done.4, f32[4,64,256]{2,1,0:T(8,128)S(1)} %bitcast.17, f32[64,8,128]{2,1,0:T(8,128)S(1)} %get-tuple-element.69.base, f32[3,64,8,128]{3,2,1,0:T(8,128)S(1)} %get-tuple-element.70.grads, bf16[6,256,256]{2,1,0:T(8,128)(2,1)S(1)} %get-tuple-element.71.hot_beside, ...), custom_call_target="tpu_custom_call" | custom-call | flops 100000000 | bytes 2904080 | tf_op jit(solution)/shard_map/pallas_call | solution.py:679
  (29 shorter events, 0.1 us)
Async XLA Ops:
  0.6 7.0 %copy-start.2 = (f32[1,5,256,128]{3,2,1,0:T(8,128)S(1)}, f32[1,5,256,128]{3,2,1,0:T(8,128)}, u32[]{:S(2)}) copy-start(f32[1,5,256,128]{3,2,1,0:T(8,128)} %param.9) | copy-start | bytes 1966084
  1.2 6.4 %copy-start.19 = (s32[1,6,256]{2,0,1:T(1,128)S(1)}, s32[1,6,256]{2,0,1:T(1,128)}, u32[]{:S(2)}) copy-start(s32[1,6,256]{2,0,1:T(1,128)} %param.17) | copy-start | bytes 18436
  1.2 6.4 %copy-start.20 = (s32[1,6,256]{2,0,1:T(1,128)S(1)}, s32[1,6,256]{2,0,1:T(1,128)}, u32[]{:S(2)}) copy-start(s32[1,6,256]{2,0,1:T(1,128)} %param.16) | copy-start | bytes 18436
  1.2 6.4 %copy-start.3 = (f32[1,256,128]{2,1,0:T(8,128)S(1)}, f32[1,256,128]{2,1,0:T(8,128)}, u32[]{:S(2)}) copy-start(f32[1,256,128]{2,1,0:T(8,128)} %param.11) | copy-start | bytes 393220
  3.8 7.0 %collective-permute-start = (f32[296,128]{1,0:T(8,128)}, f32[296,128]{1,0:T(8,128)S(1)}, u32[]{:S(2)}, u32[]{:S(2)}) collective-permute-start(f32[296,128]{1,0:T(8,128)} %get-tuple-element.43), channel_id=1, source_target_pairs={{1,2},{2,1},{3,4},{4,3},{5,6},{6,5},{9,10},{10,9},{11,12},{12,11},... | collective-permute-start | bytes 454664 | tf_op jit(solution)/shard_map/ppermute | solution.py:744
  7.5 0.6 %copy-start.4 = (s32[4]{0:T(128)S(1)}, s32[4]{0:T(128)}, u32[]{:S(2)}) copy-start(s32[4]{0:T(128)} %pad_add_fusion.meta) | copy-start | bytes 52
  7.5 0.7 %copy-start.5 = (s32[1,4,256]{2,1,0:T(4,128)S(1)}, s32[1,4,256]{2,1,0:T(4,128)}, u32[]{:S(2)}) copy-start(s32[1,4,256]{2,1,0:T(4,128)} %param.12) | copy-start | bytes 12292
  7.6 0.7 %copy-start.8 = (s32[1,256]{1,0:T(1,128)S(1)}, s32[1,256]{1,0:T(1,128)}, u32[]{:S(2)}) copy-start(s32[1,256]{1,0:T(1,128)} %target.1) | copy-start | bytes 3076
  7.6 3.2 %collective-permute-start.1 = (f32[296,128]{1,0:T(8,128)}, f32[296,128]{1,0:T(8,128)S(1)}, u32[]{:S(2)}, u32[]{:S(2)}) collective-permute-start(f32[296,128]{1,0:T(8,128)} %get-tuple-element.44), channel_id=1, source_target_pairs={{0,1},{1,0},{2,3},{3,2},{4,5},{5,4},{6,7},{7,6},{8,9},{9,8},{10,11... | collective-permute-start | bytes 454664 | tf_op jit(solution)/shard_map/ppermute | solution.py:745
  8.2 2.5 %copy-start = (f32[1,4,64,256]{3,2,1,0:T(8,128)S(1)}, f32[1,4,64,256]{3,2,1,0:T(8,128)}, u32[]{:S(2)}) copy-start(f32[1,4,64,256]{3,2,1,0:T(8,128)} %param.15) | copy-start | bytes 786436
  8.2 2.5 %copy-start.6 = (f32[1,3,256,128]{3,2,1,0:T(8,128)S(1)}, f32[1,3,256,128]{3,2,1,0:T(8,128)}, u32[]{:S(2)}) copy-start(f32[1,3,256,128]{3,2,1,0:T(8,128)} %param.10) | copy-start | bytes 1179652
  8.2 2.5 %copy-start.7 = (f32[64,128]{1,0:T(8,128)S(1)}, f32[64,128]{1,0:T(8,128)}, u32[]{:S(2)}) copy-start(f32[64,128]{1,0:T(8,128)} %projector.3) | copy-start | bytes 98308
  13.6 2.1 %copy-start.9 = (bf16[2,240,224]{2,1,0:T(8,128)(2,1)}, bf16[2,240,224]{2,1,0:T(8,128)(2,1)S(1)}, u32[]{:S(2)}) copy-start(bf16[2,240,224]{2,1,0:T(8,128)(2,1)S(1)} %get-tuple-element.50.edge_mats) | copy-start | bytes 645124
  13.6 2.8 %collective-permute-start.2 = (bf16[400,256]{1,0:T(8,128)(2,1)S(1)}, bf16[400,256]{1,0:T(8,128)(2,1)S(1)}, u32[]{:S(2)}, u32[]{:S(2)}) collective-permute-start(bf16[400,256]{1,0:T(8,128)(2,1)S(1)} %get-tuple-element.56), channel_id=1, source_target_pairs={{0,1},{1,2},{2,3},{3,4},{4,5},{5,6},{6,7},{8,9},{9,10},{10,11},{11... | collective-permute-start | bytes 614408 | tf_op jit(solution)/shard_map/ppermute | solution.py:811
  15.7 0.7 %copy-start.15 = (bf16[320,384]{1,0:T(8,128)(2,1)}, bf16[320,384]{1,0:T(8,128)(2,1)S(1)}, u32[]{:S(2)}) copy-start(bf16[320,384]{1,0:T(8,128)(2,1)S(1)} %get-tuple-element.59.low) | copy-start | bytes 737284
  16.4 0.8 %copy-start.11 = (f32[320,384]{1,0:T(8,128)}, f32[320,384]{1,0:T(8,128)S(1)}, u32[]{:S(2)}) copy-start(f32[320,384]{1,0:T(8,128)S(1)} %get-tuple-element.54.state) | copy-start | bytes 1474564
  16.4 0.9 %copy-start.13 = (bf16[320,384]{1,0:T(8,128)(2,1)}, bf16[320,384]{1,0:T(8,128)(2,1)S(1)}, u32[]{:S(2)}) copy-start(bf16[320,384]{1,0:T(8,128)(2,1)S(1)} %get-tuple-element.58.high) | copy-start | bytes 737284
  16.4 0.9 %copy-start.17 = (bf16[400,256]{1,0:T(8,128)(2,1)}, bf16[400,256]{1,0:T(8,128)(2,1)S(1)}, u32[]{:S(2)}) copy-start(bf16[400,256]{1,0:T(8,128)(2,1)S(1)} %collective-permute-done.2) | copy-start | bytes 614404
  16.4 2.2 %copy-start.10 = (bf16[2,240,224]{2,1,0:T(8,128)(2,1)S(1)}, bf16[2,240,224]{2,1,0:T(8,128)(2,1)}, u32[]{:S(2)}) copy-start(bf16[2,240,224]{2,1,0:T(8,128)(2,1)} %copy-done.9) | copy-start | bytes 645124
  16.4 2.2 %copy-start.16 = (bf16[320,384]{1,0:T(8,128)(2,1)S(1)}, bf16[320,384]{1,0:T(8,128)(2,1)}, u32[]{:S(2)}) copy-start(bf16[320,384]{1,0:T(8,128)(2,1)} %copy-done.15) | copy-start | bytes 737284
  17.3 10.2 %collective-permute-start.3 = (bf16[400,256]{1,0:T(8,128)(2,1)S(1)}, bf16[400,256]{1,0:T(8,128)(2,1)S(1)}, u32[]{:S(2)}, u32[]{:S(2)}) collective-permute-start(bf16[400,256]{1,0:T(8,128)(2,1)S(1)} %fusion), channel_id=1, source_target_pairs={{0,8},{16,24},{1,9},{17,25},{2,10},{18,26},{3,11},{19,27},{4,12},{... | collective-permute-start | bytes 614408 | tf_op jit(solution)/shard_map/ppermute | solution.py:838
  18.6 1.0 %copy-start.12 = (f32[320,384]{1,0:T(8,128)S(1)}, f32[320,384]{1,0:T(8,128)}, u32[]{:S(2)}) copy-start(f32[320,384]{1,0:T(8,128)} %copy-done.11) | copy-start | bytes 1474564
  19.7 0.9 %copy-start.14 = (bf16[320,384]{1,0:T(8,128)(2,1)S(1)}, bf16[320,384]{1,0:T(8,128)(2,1)}, u32[]{:S(2)}) copy-start(bf16[320,384]{1,0:T(8,128)(2,1)} %copy-done.13) | copy-start | bytes 737284
  20.6 6.9 %copy-start.18 = (bf16[400,256]{1,0:T(8,128)(2,1)S(1)}, bf16[400,256]{1,0:T(8,128)(2,1)}, u32[]{:S(2)}) copy-start(bf16[400,256]{1,0:T(8,128)(2,1)} %copy-done.17) | copy-start | bytes 614404
  22.0 5.6 %collective-permute-start.4 = (bf16[384,256]{1,0:T(8,128)(2,1)S(1)}, bf16[384,256]{1,0:T(8,128)(2,1)S(1)}, u32[]{:S(2)}, u32[]{:S(2)}) collective-permute-start(bf16[384,256]{1,0:T(8,128)(2,1)S(1)} %get-tuple-element.66), channel_id=1, source_target_pairs={{0,1},{1,2},{2,3},{3,4},{4,5},{5,6},{6,7},{8,9},{9,10},{10,11},{11... | collective-permute-start | bytes 589832 | tf_op jit(solution)/shard_map/ppermute | solution.py:811
  27.7 12.8 %copy-start.1 = (f32[3,64,8,128]{3,2,1,0:T(8,128)S(1)}, f32[3,64,8,128]{3,2,1,0:T(8,128)}, u32[]{:S(2)}) copy-start(f32[3,64,8,128]{3,2,1,0:T(8,128)} %get-tuple-element.62.grads) | copy-start | bytes 2359300
  27.7 11.3 %collective-permute-start.5 = (bf16[400,256]{1,0:T(8,128)(2,1)S(1)}, bf16[400,256]{1,0:T(8,128)(2,1)S(1)}, u32[]{:S(2)}, u32[]{:S(2)}) collective-permute-start(bf16[400,256]{1,0:T(8,128)(2,1)S(1)} %pad_select_fusion), channel_id=1, source_target_pairs={{0,16},{8,24},{1,17},{9,25},{2,18},{10,26},{3,19},{11,27},{4,20},{... | collective-permute-start | bytes 614408 | tf_op jit(solution)/shard_map/ppermute | solution.py:855
  29.2 23.0 %collective-permute-start.7 = (bf16[384,256]{1,0:T(8,128)(2,1)S(1)}, bf16[384,256]{1,0:T(8,128)(2,1)S(1)}, u32[]{:S(2)}, u32[]{:S(2)}) collective-permute-start(bf16[384,256]{1,0:T(8,128)(2,1)S(1)} %fusion.1), channel_id=1, source_target_pairs={{8,24},{9,25},{10,26},{11,27},{12,28},{13,29},{14,30},{15,31}} | collective-permute-start | bytes 589832 | tf_op jit(solution)/shard_map/ppermute | solution.py:856
  39.1 13.1 %collective-permute-start.6 = (bf16[384,256]{1,0:T(8,128)(2,1)S(1)}, bf16[384,256]{1,0:T(8,128)(2,1)S(1)}, u32[]{:S(2)}, u32[]{:S(2)}) collective-permute-start(bf16[384,256]{1,0:T(8,128)(2,1)S(1)} %add_convert_fusion.1), channel_id=1, source_target_pairs={{16,24},{17,25},{18,26},{19,27},{20,28},{21,29},{22,30},{23,31}} | collective-permute-start | bytes 589832 | tf_op jit(solution)/shard_map/ppermute | solution.py:882
  41.9 10.2 %collective-permute-start.8 = (bf16[256,128]{1,0:T(8,128)(2,1)S(1)}, bf16[256,128]{1,0:T(8,128)(2,1)S(1)}, u32[]{:S(2)}, u32[]{:S(2)}) collective-permute-start(bf16[256,128]{1,0:T(8,128)(2,1)S(1)} %get-tuple-element.73), channel_id=1, source_target_pairs={{25,26},{26,25},{27,28},{28,27},{29,30},{30,29}} | collective-permute-start | bytes 196616 | tf_op jit(solution)/shard_map/ppermute | solution.py:870
  48.5 3.7 %collective-permute-start.9 = (bf16[256,128]{1,0:T(8,128)(2,1)S(1)}, bf16[256,128]{1,0:T(8,128)(2,1)S(1)}, u32[]{:S(2)}, u32[]{:S(2)}) collective-permute-start(bf16[256,128]{1,0:T(8,128)(2,1)S(1)} %get-tuple-element.74), channel_id=1, source_target_pairs={{24,25},{25,24},{26,27},{27,26},{28,29},{29,28},{30,31},{31,30}} | collective-permute-start | bytes 196616 | tf_op jit(solution)/shard_map/ppermute | solution.py:871

commit v3 on v2

--- a/solution.py
+++ b/solution.py
@@ -19,8 +19,8 @@
 FIELD_ORDER = (1, 2, 3, 0, 4)
 BASE = 32.0
 EXTRA = 16
-VMEM_LIMIT = 48 * 1024 * 1024
-PACK_LIMIT = 63 * 1024 * 1024
+VMEM_LIMIT = 20 * 1024 * 1024
+PACK_LIMIT = 64 * 1024 * 1024 - 256 * 1024
 
 F32 = jnp.float32
 BF16 = jnp.bfloat16
@@ -73,7 +73,7 @@
     return lax.dot_general(a, b, (((1,), (1,)), ((), ())), preferred_element_type=F32)
 
 
-def pack_kernel(meta, flow, visc, links, sound, out_a, out_b, links_in, sems, link_sem):
+def pack_kernel(meta, flow, visc, links, sound, out_a, out_b, links_in, staged, sems, link_sem):
     is_flow, even = meta[0] == 1, meta[1] == 1
     tiles = flow.shape[1]
     _, nodes, elements = sound.shape
@@ -84,54 +84,59 @@
         fetch = pltpu.make_async_copy(links, links_in, link_sem)
         fetch.start()
         copies = []
-        for side, out in enumerate(outs):
+        for side in range(2):
             off = pl.multiple_of(jnp.where(even == (side == 0), 0, tiles - EDGE), 8)
             for place, f in enumerate(FIELD_ORDER):
                 copies.append(
                     pltpu.make_async_copy(
                         flow.at[f, pl.ds(off, EDGE), :],
-                        out.at[pl.ds(place * EDGE, EDGE), :],
+                        staged.at[side, pl.ds(place * EDGE, EDGE), :],
                         sems.at[side, place],
                     )
                 )
             copies.append(
                 pltpu.make_async_copy(
-                    visc.at[pl.ds(off, EDGE), :], out.at[pl.ds(5 * EDGE, EDGE), :], sems.at[side, 5]
+                    visc.at[pl.ds(off, EDGE), :],
+                    staged.at[side, pl.ds(5 * EDGE, EDGE), :],
+                    sems.at[side, 5],
                 )
             )
         for copy in copies:
             copy.start()
         fetch.wait()
-        low = links_in[:, :LANES].astype(F32)
-        high = links_in[:, tiles - LANES :].astype(F32)
-        pad = jnp.zeros((4, LANES), F32)
-        out_a[6 * EDGE : 6 * EDGE + 4, :] = jnp.where(even, low, high)
-        out_b[6 * EDGE : 6 * EDGE + 4, :] = jnp.where(even, high, low)
-        out_a[6 * EDGE + 4 :, :] = pad
-        out_b[6 * EDGE + 4 :, :] = pad
+        given = links_in[...]
+        own = meta[2] + lax.broadcasted_iota(jnp.int32, given.shape, 1)
+        offset = jnp.where(given < 0, 0, given - own).astype(F32)
+        low, high = offset[:, :LANES], offset[:, tiles - LANES :]
+        pad = jnp.zeros((EXTRA - 4, LANES), F32)
+        for side, (a, b) in enumerate(((low, high), (high, low))):
+            block = jnp.concatenate([jnp.where(even, a, b), pad], 0)
+            outs[side][6 * EDGE :, :] = block.astype(BF16)
         for copy in copies:
             copy.wait()
+        for side in range(2):
+            outs[side][: 6 * EDGE, :] = staged[side].astype(BF16)
 
     @pl.when(jnp.logical_not(is_flow))
     def _():
         copies = []
-        for side, out in enumerate(outs):
+        for side in range(2):
             off = pl.multiple_of(jnp.where(even == (side == 0), 0, elements - LANES), LANES)
             for v in range(4):
                 copies.append(
                     pltpu.make_async_copy(
                         sound.at[v, :, pl.ds(off, LANES)],
-                        out.at[pl.ds(v * nodes, nodes), :],
+                        staged.at[side, pl.ds(v * nodes, nodes), :],
                         sems.at[side, v],
                     )
                 )
         for copy in copies:
             copy.start()
-        rest = jnp.zeros((out_a.shape[0] - 4 * nodes, LANES), F32)
-        out_a[4 * nodes :, :] = rest
-        out_b[4 * nodes :, :] = rest
         for copy in copies:
             copy.wait()
+        for side, out in enumerate(outs):
+            out[: 4 * nodes, :] = staged[side, : 4 * nodes, :].astype(BF16)
+            out[4 * nodes :, :] = jnp.zeros((out.shape[0] - 4 * nodes, LANES), BF16)
 
 
 class FlowPlan:
@@ -172,12 +177,11 @@
     return pltpu.roll(x, LANES - 1, 1), pltpu.roll(x, 1, 1)
 
 
-def link_matrix(plan, b, first_tile, given, mat):
+def link_matrix(plan, offset, mat):
     rows, span = plan.rows, plan.span
     lane = lax.broadcasted_iota(jnp.int32, (rows, 2 * span), 1)
     lane = jnp.where(lane >= span, lane - span, lane)
-    own = first_tile - EDGE + plan.at(b) + lax.broadcasted_iota(jnp.int32, (rows, LANES), 0)
-    place = jnp.where(given < 0, own, given.astype(jnp.int32)) - (first_tile - EDGE + b * rows)
+    place = HW + lax.broadcasted_iota(jnp.int32, (rows, LANES), 0) + offset.astype(jnp.int32)
     hot = [jnp.where(place[:, k : k + 1] == lane, F32(1.0), F32(0.0)) for k in range(4)]
     mat[:rows, :] = (hot[0] + hot[1] + hot[2] + hot[3]).astype(BF16)
     mat[rows : 2 * rows, :] = (hot[0] - hot[1]).astype(BF16)
@@ -279,8 +283,10 @@
         for place, f in enumerate(FIELD_ORDER):
             put(high0, low0, 0, place, flow[f])
         square[...] = jnp.zeros_like(square)
+        own_tile = first_tile + lax.broadcasted_iota(jnp.int32, links.shape, 1)
+        offset = jnp.where(links[...] < 0, 0, links[...] - own_tile).astype(F32)
         for part in range(tiles // LANES):
-            square[:4, :] = links[:, part * LANES : (part + 1) * LANES].astype(F32)
+            square[:4, :] = offset[:, part * LANES : (part + 1) * LANES]
             lcol[part * LANES : (part + 1) * LANES, :] = square[...].T
         local = target[...] - first_element
         hits[...] = jnp.where(
@@ -288,7 +294,7 @@
         ).astype(BF16)
         for at, b in enumerate(plan.inner()):
             own = slice(plan.at(b) - EDGE, plan.at(b) - EDGE + rows)
-            link_matrix(plan, b, first_tile, lcol[own, :], inner_mats.at[at])
+            link_matrix(plan, lcol[own, :], inner_mats.at[at])
             advance(
                 plan, b, inner_mats.at[at], [(EDGE, high0)], [(EDGE, low0)],
                 lambda place, own=own: flow[FIELD_ORDER[place], own, :],
@@ -335,10 +341,8 @@
 
     @pl.when(is_flow)
     def _():
-        first_tile = meta[2]
-
         def pick(at, size):
-            a, b = part_a[at : at + size, :], part_b[at : at + size, :]
+            a, b = part_a[at : at + size, :].astype(F32), part_b[at : at + size, :].astype(F32)
             return jnp.where(even, a, b), jnp.where(even, b, a)
 
         zero[...] = jnp.zeros_like(zero)
@@ -356,11 +360,11 @@
         edge_visc[rows:, :] = jnp.concatenate(
             [visc[tiles - (rows - EDGE + HW) :, :], after[: EDGE - HW]], 0
         )
-        before, after = pick(6 * EDGE, 8)
+        before, after = pick(6 * EDGE, EXTRA)
         given = []
         for side, block in enumerate((before, after)):
             square[...] = jnp.zeros_like(square)
-            square[:8, :] = block
+            square[:EXTRA, :] = block
             turned = square[...].T
             given.append(
                 jnp.concatenate([turned[LANES - EDGE + HW :], lcol[: rows - EDGE + HW, :]], 0)
@@ -370,7 +374,7 @@
                 )
             )
         for side, b in enumerate((0, plan.blocks - 1)):
-            link_matrix(plan, b, first_tile, given[side], edge_mats.at[side])
+            link_matrix(plan, given[side], edge_mats.at[side])
             advance(
                 plan, b, edge_mats.at[side],
                 [(b * rows, high0.at[side])], [(b * rows, low0.at[side])],
@@ -399,7 +403,7 @@
                 rows_of[h * block + v * nodes : h * block + (v + 1) * nodes, :] = sound[
                     v, :, h * LANES : (h + 1) * LANES
                 ]
-        a, b = part_a[:block, :], part_b[:block, :]
+        a, b = part_a[:block, :].astype(F32), part_b[:block, :].astype(F32)
         rows_of[halves * block : (halves + 1) * block, :] = jnp.where(even, a, b)
         rows_of[(halves + 1) * block : (halves + 2) * block, :] = jnp.where(even, b, a)
         for face in range(6):
@@ -414,17 +418,22 @@
 
 
 def second_kernel(
-    meta, flow, visc, inner_state, inner_high, inner_low, inner_mats,
+    meta, flow, visc, mean, mean_one, projector,
+    inner_state, inner_high, inner_low, inner_mats, hits,
     edge_state, edge_high, edge_low, edge_mats, edge_visc,
-    flow_out, state, high, low, passive, zero,
+    flow_out, mean_out, own_two, next_two,
+    state, high, low, zero, packed, pay,
 ):
-    plan = FlowPlan(flow.shape[1])
+    plan = FlowPlan(packed.shape[1])
     rows = plan.rows
     is_flow = meta[0] == 1
 
     @pl.when(jnp.logical_not(is_flow))
     def _():
         flow_out[...] = flow[...]
+        mean_out[...] = mean[...]
+        own_two[...] = jnp.zeros_like(own_two)
+        next_two[...] = jnp.zeros_like(next_two)
 
     @pl.when(is_flow)
     def _():
@@ -439,31 +448,11 @@
             advance(
                 plan, b, mats_of(plan, b, edge_mats, inner_mats), high1, low1,
                 band_state(plan, b, edge_state, inner_state), v,
-                passive, high, low, b * rows, 3,
+                state, high, low, b * rows, 3,
             )
         own = slice(EDGE - HW, EDGE - HW + plan.tiles)
-        state[...] = passive[:, : state.shape[1]]
         for place, f in enumerate(FIELD_ORDER):
-            flow_out[f] = passive[own, columns_of(place)]
-
-
-def sums_kernel(
-    meta, mean, mean_one, projector, inner_mats, edge_mats, hits, state, high, low,
-    mean_out, own_two, next_two, zero, packed, pay,
-):
-    plan = FlowPlan(packed.shape[1])
-    rows = plan.rows
-    is_flow = meta[0] == 1
-
-    @pl.when(jnp.logical_not(is_flow))
-    def _():
-        mean_out[...] = mean[...]
-        own_two[...] = jnp.zeros_like(own_two)
-        next_two[...] = jnp.zeros_like(next_two)
-
-    @pl.when(is_flow)
-    def _():
-        zero[...] = jnp.zeros_like(zero)
+            flow_out[f] = state[own, columns_of(place)]
         for b in range(plan.blocks):
             lamb_block(
                 plan, b, mats_of(plan, b, edge_mats, inner_mats),
@@ -671,7 +660,7 @@
                 ]
 
 
-def call(kernel, outs, scratch, operands, flops=1e8, in_hbm=(), limit=VMEM_LIMIT):
+def call(kernel, outs, scratch, operands, in_hbm=(), limit=VMEM_LIMIT):
     spaces = [pltpu.SMEM] + [
         pltpu.HBM if at in in_hbm else pltpu.VMEM for at in range(1, len(operands))
     ]
@@ -683,7 +672,7 @@
         out_specs=tuple([pl.BlockSpec(memory_space=pltpu.VMEM)] * len(outs)),
         scratch_shapes=scratch,
         compiler_params=pltpu.CompilerParams(vmem_limit_bytes=limit),
-        cost_estimate=pl.CostEstimate(flops=int(flops), bytes_accessed=moved, transcendentals=0),
+        cost_estimate=pl.CostEstimate(flops=10**8, bytes_accessed=moved, transcendentals=0),
     )(*operands)
 
 
@@ -728,12 +717,13 @@
     pairs_a = [p for i in range(1, count - 1, 2) for p in ((i, i + 1), (i + 1, i))]
     pairs_b = [p for i in range(0, count - 1, 2) for p in ((i, i + 1), (i + 1, i))]
 
-    edge_rows = 6 * EDGE + 8
+    edge_rows = 6 * EDGE + EXTRA
     pack_a, pack_b = call(
         pack_kernel,
-        [shape((edge_rows, LANES), F32)] * 2,
+        [shape((edge_rows, LANES), BF16)] * 2,
         [
             vmem(links.shape, jnp.int32),
+            vmem((2, 6 * EDGE, LANES), F32),
             pltpu.SemaphoreType.DMA((2, 6)),
             pltpu.SemaphoreType.DMA,
         ],
@@ -761,7 +751,6 @@
         ],
         [vmem((tiles, fields), BF16), vmem((tiles, fields), BF16), square],
         [meta, flow, visc, links, tile_target],
-        flops=1e9,
     )
     lines = 6 * nodes + EXTRA
     by_node = shape((nodes, 8, LANES), F32)
@@ -801,7 +790,6 @@
             meta, flow, visc, mean, projector, part_a, part_b, sound, neighbours, codes,
             inner_state, inner_high, inner_low, lcol, inner_mats, hits,
         ],
-        flops=1e9,
     )
 
     up = [(i, i + 1) for i in range(count - 1)]
@@ -817,42 +805,43 @@
         return total.astype(BF16)
 
     got_one = climb(next_one)
+    band = plan.blocks * rows
     velocity = 3 * LANES
-    band = plan.blocks * rows
-    flow_out, state2, high2, low2 = call(
+    flow_out, mean_out, own_two, next_two = call(
         second_kernel,
         [
             shape(flow.shape, F32),
-            shape((band, velocity), F32),
-            shape((band, velocity), BF16),
-            shape((band, velocity), BF16),
-        ],
-        [vmem((band, fields), F32), vmem((HW, fields), BF16)],
-        [
-            meta, flow, visc, inner_state, inner_high, inner_low, inner_mats,
-            edge_state, edge_high, edge_low, edge_mats, edge_visc,
-        ],
-        flops=1e9,
-    )
-    sum_one, high2 = lax.optimization_barrier((combined(own_one, got_one), high2))
-    x_one = lax.ppermute(sum_one, "grp", [(0, 1), (2, 3)])
-    mean_out, own_two, next_two = call(
-        sums_kernel,
-        [
             shape(mean.shape, F32),
             shape((6 * nodes, elements), F32),
             shape((6 * nodes, elements), BF16),
         ],
-        [vmem((HW, velocity), BF16), packed, vmem((6 * nodes, tiles), BF16)],
-        [meta, mean, mean_one, projector, inner_mats, edge_mats, hits, state2, high2, low2],
-        flops=1e9,
-    )
+        [
+            vmem((band, fields), F32),
+            vmem((band, velocity), BF16),
+            vmem((band, velocity), BF16),
+            vmem((HW, fields), BF16),
+            packed,
+            vmem((6 * nodes, tiles), BF16),
+        ],
+        [
+            meta, flow, visc, mean, mean_one, projector,
+            inner_state, inner_high, inner_low, inner_mats, hits,
+            edge_state, edge_high, edge_low, edge_mats, edge_visc,
+        ],
+    )
+    sum_one, next_two, own_two = lax.optimization_barrier(
+        (combined(own_one, got_one), next_two, own_two)
+    )
+    x_one = lax.ppermute(sum_one, "grp", [(0, 1), (2, 3)])
     got_two = climb(next_two)
-    sum_one = combined(own_one, got_one, x_one)
-    sum_one, own_two = lax.optimization_barrier((sum_one, own_two))
+    sum_one, own_two = lax.optimization_barrier((combined(own_one, got_one, x_one), own_two))
     sum_two = lax.optimization_barrier(combined(own_two, got_two))
     padded = jnp.pad(sum_two, ((0, EXTRA), (0, 0)))
     cross = lax.ppermute(jnp.where(group_index == 0, padded, sum_one), "grp", [(0, 2), (1, 3)])
+    last_two, sum_two = lax.optimization_barrier(
+        (combined(own_two, got_two, cross[: 6 * nodes]), sum_two)
+    )
+    x_two = lax.ppermute(last_two, "grp", [(2, 3)])
     y_two = lax.ppermute(sum_two, "grp", [(1, 3)])
 
     sound_rows, scale, edge_a, edge_b = call(
@@ -879,7 +868,6 @@
         ],
         [meta, sound_rows, neighbours, codes],
     )
-    x_two = lax.ppermute(combined(own_two, got_two, cross[: 6 * nodes]), "grp", [(2, 3)])
     (sound_out,) = call(
         sound_two_kernel,
         [shape(sound.shape, F32)],

time: 55.2 us -> 50.6 us (0.917)
  the two profiles are of different devices: /device:TPU:15 before, /device:TPU:7 now
where the time goes in v3:
time: 50.6 us; the launch traced here: 50.2 us
  waiting for transfers between devices  16.6 us (33%)
  starting transfers between devices  15.7 us (31%)
  Pallas kernels  12.3 us (24%)
  local copies, waits for them, and re-layouts  2.84 us (6%)
  other arithmetic  1.91 us (4%)
  between operations  0.9 us (2%)
    pallas_call x7, Pallas kernels, call(): pl.pallas_call(kernel, out_shape=tuple(outs), in_specs=[pl.BlockSpec(memo...  12.3 us
    ppermute x1, waiting for transfers between devices, body(): x_one = lax.ppermute(sum_one, 'grp', [(0, 1), (2, 3)])  9 us
    ppermute x1, waiting for transfers between devices, body(): lax.ppermute(jnp.where(group_index == 0, padded, sum_one), 'grp', [(0, 2)...  7.56 us
    ppermute x1, starting transfers between devices, body(): part_a = lax.ppermute(pack_a, 'sfc', pairs_a)  3.76 us
    ppermute x1, starting transfers between devices, body(): lax.ppermute(edge_a, ('grp', 'sfc'), [(last + i, last + j) for i, j in pa...  3.41 us
    unnamed x25, local copies, waits for them, and re-layouts  2.84 us
    ppermute x1, starting transfers between devices, body(): lax.ppermute(edge_b, ('grp', 'sfc'), [(last + i, last + j) for i, j in pa...  1.92 us
    ppermute x2, starting transfers between devices, climb(): return lax.ppermute(x, ('grp', 'sfc'), chosen)  1.35 us
  transfers between devices with their start and end apart: 10, of which 2 were waited for; matrix products, arithmetic and copies ran while one was open for 2% of the time, Pallas kernels for 11%

profile of v3, /device:TPU:7, one launch (start us, length us, event | category | flops | bytes accessed | tf_op | source)
XLA Modules:
  0.0 50.2 jit_solution(9102489995777303417)
XLA Ops:
  0.6 0.7 %pad_add_fusion.meta = s32[4]{0:T(128)} fusion(s32[1]{0:T(128)} %bitcast.2, s32[1]{0:T(128)} %bitcast.1, s32[1]{0:T(128)} %bitcast), kind=kLoop, calls=%fused_computation.9 | loop fusion | flops 12 | bytes 28 | tf_op jit(solution)/shard_map/stack | solution.py:708
  1.3 2.5 %shard_map.112 = (bf16[304,128]{1,0:T(8,128)(2,1)}, bf16[304,128]{1,0:T(8,128)(2,1)}) custom-call(s32[4]{0:T(128)} %pad_add_fusion.meta, f32[5,256,128]{2,1,0:T(8,128)} %bitcast.15, f32[256,128]{1,0:T(8,128)} %bitcast.22, s32[4,256]{1,0:T(4,128)} %bitcast.28, f32[4,64,256]{2,1,0:T(8,128)} %bitcast.19), custom_call_target="tpu_custom_call" | custom-call | flops 100000000 | bytes 1208336 | tf_op jit(solution)/shard_map/pallas_call | solution.py:668
  3.8 3.8 %collective-permute-start = (bf16[304,128]{1,0:T(8,128)(2,1)}, bf16[304,128]{1,0:T(8,128)(2,1)S(1)}, u32[]{:S(2)}, u32[]{:S(2)}) collective-permute-start(bf16[304,128]{1,0:T(8,128)(2,1)} %get-tuple-element.39), channel_id=1, source_target_pairs={{1,2},{2,1},{3,4},{4,3},{5,6},{6,5},{9,10},{10,9},{11,12},{12,11},... | collective-permute-start | bytes 233480 | tf_op jit(solution)/shard_map/ppermute | solution.py:734
  7.6 0.0 copy-start.5
  7.6 0.0 copy-start.6
  7.6 0.0 copy-start.7
  7.6 0.1 collective-permute-start.1
  7.7 0.0 copy-done.10
  7.7 0.0 copy-done.11
  7.7 0.0 copy-done.2
  7.7 0.5 %copy-done.5 = s32[4]{0:T(128)S(1)} copy-done((s32[4]{0:T(128)S(1)}, s32[4]{0:T(128)}, u32[]{:S(2)}) %copy-start.5) | copy-done | bytes 40
  8.3 0.0 copy-done.6
  8.3 0.0 copy-done.7
  8.3 1.1 %copy-done = f32[1,5,256,128]{3,2,1,0:T(8,128)S(1)} copy-done((f32[1,5,256,128]{3,2,1,0:T(8,128)S(1)}, f32[1,5,256,128]{3,2,1,0:T(8,128)}, u32[]{:S(2)}) %copy-start) | copy-done | bytes 655384
  9.4 0.5 %shard_map.113 = (f32[160,640]{1,0:T(8,128)S(1)}, bf16[160,640]{1,0:T(8,128)(2,1)S(1)}, bf16[160,640]{1,0:T(8,128)(2,1)S(1)}, f32[256,128]{1,0:T(8,128)S(1)}, bf...) custom-call(s32[4]{0:T(128)S(1)} %copy-done.5, f32[5,256,128]{2,1,0:T(8,128)S(1)} %bitcast.16, ...), custom_call_target="tpu_custom_call" | custom-call | flops 100000000 | bytes 2219024 | tf_op jit(solution)/shard_map/pallas_call | solution.py:668
  9.9 0.0 collective-permute-done.part_a
  9.9 0.0 collective-permute-done.1.part_b
  9.9 0.4 copy-done.1
  10.3 0.1 copy-done.3
  10.4 0.0 copy-done.4
  10.4 1.9 %shard_map.114 = (f32[400,256]{1,0:T(8,128)S(1)}, bf16[400,256]{1,0:T(8,128)(2,1)S(1)}, f32[3,256,128]{2,1,0:T(8,128)S(1)}, f32[64,8,128]{2,1,0:T(8,128)S(1)}, f...) custom-call(s32[4]{0:T(128)S(1)} %copy-done.5, ...), custom_call_target="tpu_custom_call" | custom-call | flops 100000000 | bytes 6242320 | tf_op jit(solution)/shard_map/pallas_call | solution.py:668
  12.3 0.7 %collective-permute-start.2 = (bf16[400,256]{1,0:T(8,128)(2,1)S(1)}, bf16[400,256]{1,0:T(8,128)(2,1)S(1)}, u32[]{:S(2)}, u32[]{:S(2)}) collective-permute-start(bf16[400,256]{1,0:T(8,128)(2,1)S(1)} %get-tuple-element.58), channel_id=1, source_target_pairs={{0,1},{1,2},{2,3},{3,4},{4,5},{5,6},{6,7},{8,9},{9,10},{10,11},{11... | collective-permute-start | bytes 614408 | tf_op jit(solution)/shard_map/ppermute | solution.py:799
  13.0 1.6 %shard_map.115 = (f32[5,256,128]{2,1,0:T(8,128)}, f32[3,256,128]{2,1,0:T(8,128)}, f32[384,256]{1,0:T(8,128)S(1)}, bf16[384,256]{1,0:T(8,128)(2,1)S(1)}) custom-call(s32[4]{0:T(128)S(1)} %copy-done.5, f32[5,256,128]{2,1,0:T(8,128)S(1)} %bitcast.18, f32[256,128]{1,0:T(8,128)S(1)} %bitcast.25, f32[3,256,128]{2,1,0:T(8,128)S(1)} %bitcast.27, ...), custom_call_target="tpu_custom_call" | custom-call | flops 100000000 | bytes 5656592 | tf_op jit(solution)/shard_map/pallas_call | solution.py:668
  14.6 0.0 collective-permute-done.2
  14.7 0.1 fusion
  14.7 0.6 %copy-done.8 = bf16[384,256]{1,0:T(8,128)(2,1)} copy-done((bf16[384,256]{1,0:T(8,128)(2,1)}, bf16[384,256]{1,0:T(8,128)(2,1)S(1)}, u32[]{:S(2)}) %copy-start.8) | copy-done | bytes 196632
  15.3 0.0 copy-done.9
  15.4 1.3 %collective-permute-start.3 = (bf16[400,256]{1,0:T(8,128)(2,1)S(1)}, bf16[400,256]{1,0:T(8,128)(2,1)S(1)}, u32[]{:S(2)}, u32[]{:S(2)}) collective-permute-start(bf16[400,256]{1,0:T(8,128)(2,1)S(1)} %fusion), channel_id=1, source_target_pairs={{0,8},{16,24},{1,9},{17,25},{2,10},{18,26},{3,11},{19,27},{4,12},{... | collective-permute-start | bytes 614408 | tf_op jit(solution)/shard_map/ppermute | solution.py:835
  16.7 0.7 %collective-permute-start.4 = (bf16[384,256]{1,0:T(8,128)(2,1)}, bf16[384,256]{1,0:T(8,128)(2,1)S(1)}, u32[]{:S(2)}, u32[]{:S(2)}) collective-permute-start(bf16[384,256]{1,0:T(8,128)(2,1)} %copy-done.8), channel_id=1, source_target_pairs={{0,1},{1,2},{2,3},{3,4},{4,5},{5,6},{6,7},{8,9},{9,10},{10,11},{11... | collective-permute-start | bytes 589832 | tf_op jit(solution)/shard_map/ppermute | solution.py:799
  17.4 9.0 %collective-permute-done.3.source_a = bf16[400,256]{1,0:T(8,128)(2,1)S(1)} collective-permute-done((bf16[400,256]{1,0:T(8,128)(2,1)S(1)}, bf16[400,256]{1,0:T(8,128)(2,1)S(1)}, u32[]{:S(2)}, u32[]{:S(2)}) %collective-permute-start.3) | collective-permute-done | bytes 204832 | tf_op jit(solution)/shard_map/ppermute | solution.py:835
  26.4 1.0 %add_convert_fusion = bf16[400,256]{1,0:T(8,128)(2,1)S(1)} fusion(bf16[400,256]{1,0:T(8,128)(2,1)S(1)} %collective-permute-done.3.source_a, f32[400,256]{1,0:T(8,128)S(1)} %get-tuple-element.57, bf16[400,256]{1,0:T(8,128)(2,1)} %copy-done.9), kind=kLoop, calls=%fused_computation | loop fusion | flops 512000 | bytes 1024000 | tf_op jit(solution)/shard_map/convert_element_type | solution.py:805
  27.4 0.0 collective-permute-done.4
  27.4 0.1 fusion.1
  27.4 0.1 pad_select_fusion
  27.5 1.3 %collective-permute-start.5 = (bf16[400,256]{1,0:T(8,128)(2,1)S(1)}, bf16[400,256]{1,0:T(8,128)(2,1)S(1)}, u32[]{:S(2)}, u32[]{:S(2)}) collective-permute-start(bf16[400,256]{1,0:T(8,128)(2,1)S(1)} %pad_select_fusion), channel_id=1, source_target_pairs={{0,16},{8,24},{1,17},{9,25},{2,18},{10,26},{3,19},{11,27},{4,20},{... | collective-permute-start | bytes 614408 | tf_op jit(solution)/shard_map/ppermute | solution.py:840
  28.8 7.6 %collective-permute-done.5.source_b = bf16[400,256]{1,0:T(8,128)(2,1)S(1)} collective-permute-done((bf16[400,256]{1,0:T(8,128)(2,1)S(1)}, bf16[400,256]{1,0:T(8,128)(2,1)S(1)}, u32[]{:S(2)}, u32[]{:S(2)}) %collective-permute-start.5) | collective-permute-done | bytes 204832 | tf_op jit(solution)/shard_map/ppermute | solution.py:840
  36.3 0.1 add_convert_fusion.1
  36.4 1.3 %collective-permute-start.6 = (bf16[384,256]{1,0:T(8,128)(2,1)S(1)}, bf16[384,256]{1,0:T(8,128)(2,1)S(1)}, u32[]{:S(2)}, u32[]{:S(2)}) collective-permute-start(bf16[384,256]{1,0:T(8,128)(2,1)S(1)} %add_convert_fusion.1), channel_id=1, source_target_pairs={{16,24},{17,25},{18,26},{19,27},{20,28},{21,29},{22,30},{23,31}} | collective-permute-start | bytes 589832 | tf_op jit(solution)/shard_map/ppermute | solution.py:844
  37.7 1.3 %collective-permute-start.7 = (bf16[384,256]{1,0:T(8,128)(2,1)S(1)}, bf16[384,256]{1,0:T(8,128)(2,1)S(1)}, u32[]{:S(2)}, u32[]{:S(2)}) collective-permute-start(bf16[384,256]{1,0:T(8,128)(2,1)S(1)} %fusion.1), channel_id=1, source_target_pairs={{8,24},{9,25},{10,26},{11,27},{12,28},{13,29},{14,30},{15,31}} | collective-permute-start | bytes 589832 | tf_op jit(solution)/shard_map/ppermute | solution.py:845
  39.0 1.5 %shard_map.116 = (f32[512,128]{1,0:T(8,128)S(1)}, f32[8,256]{1,0:T(8,128)S(1)}, bf16[256,128]{1,0:T(8,128)(2,1)S(1)}, bf16[256,128]{1,0:T(8,128)(2,1)S(1)}) custom-call(s32[4]{0:T(128)S(1)} %copy-done.5, f32[64,8,128]{2,1,0:T(8,128)S(1)} %get-tuple-element.55.base, f32[3,64,8,128]{3,2,1,0:T(8,128)S(1)} %get-tuple-element.56.grads, ...), custom_call_target="tpu_custom_call" | custom-call | flops 100000000 | bytes 1859600 | tf_op jit(solution)/shard_map/pallas_call | solution.py:668
  40.5 3.4 %collective-permute-start.8 = (bf16[256,128]{1,0:T(8,128)(2,1)S(1)}, bf16[256,128]{1,0:T(8,128)(2,1)S(1)}, u32[]{:S(2)}, u32[]{:S(2)}) collective-permute-start(bf16[256,128]{1,0:T(8,128)(2,1)S(1)} %get-tuple-element.73), channel_id=1, source_target_pairs={{25,26},{26,25},{27,28},{28,27},{29,30},{30,29}} | collective-permute-start | bytes 196616 | tf_op jit(solution)/shard_map/ppermute | solution.py:859
  43.9 1.9 %collective-permute-start.9 = (bf16[256,128]{1,0:T(8,128)(2,1)S(1)}, bf16[256,128]{1,0:T(8,128)(2,1)S(1)}, u32[]{:S(2)}, u32[]{:S(2)}) collective-permute-start(bf16[256,128]{1,0:T(8,128)(2,1)S(1)} %get-tuple-element.74), channel_id=1, source_target_pairs={{24,25},{25,24},{26,27},{27,26},{28,29},{29,28},{30,31},{31,30}} | collective-permute-start | bytes 196616 | tf_op jit(solution)/shard_map/ppermute | solution.py:860
  45.8 1.7 %shard_map.117 = (f32[64,8,128]{2,1,0:T(8,128)S(1)}, f32[3,64,8,128]{3,2,1,0:T(8,128)S(1)}, bf16[6,256,256]{2,1,0:T(8,128)(2,1)S(1)}) custom-call(s32[4]{0:T(128)S(1)} %copy-done.5, f32[512,128]{1,0:T(8,128)S(1)} %get-tuple-element.66.rows_of, s32[6,256]{1,0:T(8,128)S(1)} %get-tuple-element.76.neighbours, s32[6,256]{1,0:T(8,128)S(1)} %get-tuple-element.75.codes), custom_call_target="tpu_custom_call" | custom-call | flops 100000000 | bytes 2109456 | tf_op jit(solution)/shard_map/pallas_call | solution.py:668
  47.6 0.0 collective-permute-done.8.part_a
  47.6 0.0 collective-permute-done.9.part_b
  47.6 0.0 collective-permute-done.6.source_a
  47.6 0.0 collective-permute-done.7.source_b
  47.6 2.5 %shard_map.118 = f32[4,64,256]{2,1,0:T(8,128)} custom-call(s32[4]{0:T(128)S(1)} %copy-done.5, f32[4,64,256]{2,1,0:T(8,128)S(1)} %bitcast.21, f32[64,8,128]{2,1,0:T(8,128)S(1)} %get-tuple-element.67.base, f32[3,64,8,128]{3,2,1,0:T(8,128)S(1)} %get-tuple-element.68.grads, bf16[6,256,256]{2,1,0:T(8,128)(2,1)S(1)} %get-tuple-element.69.hot_beside, ...), custom_call_target="tpu_custom_call" | custom-call | flops 100000000 | bytes 2904080 | tf_op jit(solution)/shard_map/pallas_call | solution.py:668
  (10 shorter events, 0.0 us)
Async XLA Ops:
  1.3 6.4 %copy-start.10 = (s32[1,6,256]{2,0,1:T(1,128)S(1)}, s32[1,6,256]{2,0,1:T(1,128)}, u32[]{:S(2)}) copy-start(s32[1,6,256]{2,0,1:T(1,128)} %param.17) | copy-start | bytes 18436
  1.3 6.4 %copy-start.11 = (s32[1,6,256]{2,0,1:T(1,128)S(1)}, s32[1,6,256]{2,0,1:T(1,128)}, u32[]{:S(2)}) copy-start(s32[1,6,256]{2,0,1:T(1,128)} %param.16) | copy-start | bytes 18436
  1.3 6.4 %copy-start.2 = (f32[1,256,128]{2,1,0:T(8,128)S(1)}, f32[1,256,128]{2,1,0:T(8,128)}, u32[]{:S(2)}) copy-start(f32[1,256,128]{2,1,0:T(8,128)} %param.11) | copy-start | bytes 393220
  3.8 6.1 %collective-permute-start = (bf16[304,128]{1,0:T(8,128)(2,1)}, bf16[304,128]{1,0:T(8,128)(2,1)S(1)}, u32[]{:S(2)}, u32[]{:S(2)}) collective-permute-start(bf16[304,128]{1,0:T(8,128)(2,1)} %get-tuple-element.39), channel_id=1, source_target_pairs={{1,2},{2,1},{3,4},{4,3},{5,6},{6,5},{9,10},{10,9},{11,12},{12,11},... | collective-permute-start | bytes 233480 | tf_op jit(solution)/shard_map/ppermute | solution.py:734
  7.6 0.7 %copy-start.5 = (s32[4]{0:T(128)S(1)}, s32[4]{0:T(128)}, u32[]{:S(2)}) copy-start(s32[4]{0:T(128)} %pad_add_fusion.meta) | copy-start | bytes 52
  7.6 0.7 %copy-start.6 = (s32[1,4,256]{2,1,0:T(4,128)S(1)}, s32[1,4,256]{2,1,0:T(4,128)}, u32[]{:S(2)}) copy-start(s32[1,4,256]{2,1,0:T(4,128)} %param.12) | copy-start | bytes 12292
  7.6 0.7 %copy-start.7 = (s32[1,256]{1,0:T(1,128)S(1)}, s32[1,256]{1,0:T(1,128)}, u32[]{:S(2)}) copy-start(s32[1,256]{1,0:T(1,128)} %target.1) | copy-start | bytes 3076
  7.6 2.3 %collective-permute-start.1 = (bf16[304,128]{1,0:T(8,128)(2,1)}, bf16[304,128]{1,0:T(8,128)(2,1)S(1)}, u32[]{:S(2)}, u32[]{:S(2)}) collective-permute-start(bf16[304,128]{1,0:T(8,128)(2,1)} %get-tuple-element.40), channel_id=1, source_target_pairs={{0,1},{1,0},{2,3},{3,2},{4,5},{5,4},{6,7},{7,6},{8,9},{9,8},{10,11... | collective-permute-start | bytes 233480 | tf_op jit(solution)/shard_map/ppermute | solution.py:735
  8.3 1.1 %copy-start = (f32[1,5,256,128]{3,2,1,0:T(8,128)S(1)}, f32[1,5,256,128]{3,2,1,0:T(8,128)}, u32[]{:S(2)}) copy-start(f32[1,5,256,128]{3,2,1,0:T(8,128)} %param.9) | copy-start | bytes 1966084
  9.4 0.9 %copy-start.1 = (f32[1,4,64,256]{3,2,1,0:T(8,128)S(1)}, f32[1,4,64,256]{3,2,1,0:T(8,128)}, u32[]{:S(2)}) copy-start(f32[1,4,64,256]{3,2,1,0:T(8,128)} %param.15) | copy-start | bytes 786436
  9.4 1.1 %copy-start.3 = (f32[1,3,256,128]{3,2,1,0:T(8,128)S(1)}, f32[1,3,256,128]{3,2,1,0:T(8,128)}, u32[]{:S(2)}) copy-start(f32[1,3,256,128]{3,2,1,0:T(8,128)} %param.10) | copy-start | bytes 1179652
  9.4 1.1 %copy-start.4 = (f32[64,128]{1,0:T(8,128)S(1)}, f32[64,128]{1,0:T(8,128)}, u32[]{:S(2)}) copy-start(f32[64,128]{1,0:T(8,128)} %projector.3) | copy-start | bytes 98308
  12.3 2.3 %collective-permute-start.2 = (bf16[400,256]{1,0:T(8,128)(2,1)S(1)}, bf16[400,256]{1,0:T(8,128)(2,1)S(1)}, u32[]{:S(2)}, u32[]{:S(2)}) collective-permute-start(bf16[400,256]{1,0:T(8,128)(2,1)S(1)} %get-tuple-element.58), channel_id=1, source_target_pairs={{0,1},{1,2},{2,3},{3,4},{4,5},{5,6},{6,7},{8,9},{9,10},{10,11},{11... | collective-permute-start | bytes 614408 | tf_op jit(solution)/shard_map/ppermute | solution.py:799
  14.6 0.7 %copy-start.8 = (bf16[384,256]{1,0:T(8,128)(2,1)}, bf16[384,256]{1,0:T(8,128)(2,1)S(1)}, u32[]{:S(2)}) copy-start(bf16[384,256]{1,0:T(8,128)(2,1)S(1)} %get-tuple-element.64) | copy-start | bytes 589828
  14.6 0.7 %copy-start.9 = (bf16[400,256]{1,0:T(8,128)(2,1)}, bf16[400,256]{1,0:T(8,128)(2,1)S(1)}, u32[]{:S(2)}) copy-start(bf16[400,256]{1,0:T(8,128)(2,1)S(1)} %collective-permute-done.2) | copy-start | bytes 614404
  15.4 11.0 %collective-permute-start.3 = (bf16[400,256]{1,0:T(8,128)(2,1)S(1)}, bf16[400,256]{1,0:T(8,128)(2,1)S(1)}, u32[]{:S(2)}, u32[]{:S(2)}) collective-permute-start(bf16[400,256]{1,0:T(8,128)(2,1)S(1)} %fusion), channel_id=1, source_target_pairs={{0,8},{16,24},{1,9},{17,25},{2,10},{18,26},{3,11},{19,27},{4,12},{... | collective-permute-start | bytes 614408 | tf_op jit(solution)/shard_map/ppermute | solution.py:835
  16.7 10.7 %collective-permute-start.4 = (bf16[384,256]{1,0:T(8,128)(2,1)}, bf16[384,256]{1,0:T(8,128)(2,1)S(1)}, u32[]{:S(2)}, u32[]{:S(2)}) collective-permute-start(bf16[384,256]{1,0:T(8,128)(2,1)} %copy-done.8), channel_id=1, source_target_pairs={{0,1},{1,2},{2,3},{3,4},{4,5},{5,6},{6,7},{8,9},{9,10},{10,11},{11... | collective-permute-start | bytes 589832 | tf_op jit(solution)/shard_map/ppermute | solution.py:799
  27.5 8.9 %collective-permute-start.5 = (bf16[400,256]{1,0:T(8,128)(2,1)S(1)}, bf16[400,256]{1,0:T(8,128)(2,1)S(1)}, u32[]{:S(2)}, u32[]{:S(2)}) collective-permute-start(bf16[400,256]{1,0:T(8,128)(2,1)S(1)} %pad_select_fusion), channel_id=1, source_target_pairs={{0,16},{8,24},{1,17},{9,25},{2,18},{10,26},{3,19},{11,27},{4,20},{... | collective-permute-start | bytes 614408 | tf_op jit(solution)/shard_map/ppermute | solution.py:840
  36.4 11.2 %collective-permute-start.6 = (bf16[384,256]{1,0:T(8,128)(2,1)S(1)}, bf16[384,256]{1,0:T(8,128)(2,1)S(1)}, u32[]{:S(2)}, u32[]{:S(2)}) collective-permute-start(bf16[384,256]{1,0:T(8,128)(2,1)S(1)} %add_convert_fusion.1), channel_id=1, source_target_pairs={{16,24},{17,25},{18,26},{19,27},{20,28},{21,29},{22,30},{23,31}} | collective-permute-start | bytes 589832 | tf_op jit(solution)/shard_map/ppermute | solution.py:844
  37.7 9.9 %collective-permute-start.7 = (bf16[384,256]{1,0:T(8,128)(2,1)S(1)}, bf16[384,256]{1,0:T(8,128)(2,1)S(1)}, u32[]{:S(2)}, u32[]{:S(2)}) collective-permute-start(bf16[384,256]{1,0:T(8,128)(2,1)S(1)} %fusion.1), channel_id=1, source_target_pairs={{8,24},{9,25},{10,26},{11,27},{12,28},{13,29},{14,30},{15,31}} | collective-permute-start | bytes 589832 | tf_op jit(solution)/shard_map/ppermute | solution.py:845
  40.5 7.1 %collective-permute-start.8 = (bf16[256,128]{1,0:T(8,128)(2,1)S(1)}, bf16[256,128]{1,0:T(8,128)(2,1)S(1)}, u32[]{:S(2)}, u32[]{:S(2)}) collective-permute-start(bf16[256,128]{1,0:T(8,128)(2,1)S(1)} %get-tuple-element.73), channel_id=1, source_target_pairs={{25,26},{26,25},{27,28},{28,27},{29,30},{30,29}} | collective-permute-start | bytes 196616 | tf_op jit(solution)/shard_map/ppermute | solution.py:859
  43.9 3.7 %collective-permute-start.9 = (bf16[256,128]{1,0:T(8,128)(2,1)S(1)}, bf16[256,128]{1,0:T(8,128)(2,1)S(1)}, u32[]{:S(2)}, u32[]{:S(2)}) collective-permute-start(bf16[256,128]{1,0:T(8,128)(2,1)S(1)} %get-tuple-element.74), channel_id=1, source_target_pairs={{24,25},{25,24},{26,27},{27,26},{28,29},{29,28},{30,31},{31,30}} | collective-permute-start | bytes 196616 | tf_op jit(solution)/shard_map/ppermute | solution.py:860

commit v4 on v3

--- a/solution.py
+++ b/solution.py
@@ -829,20 +829,11 @@
             edge_state, edge_high, edge_low, edge_mats, edge_visc,
         ],
     )
-    sum_one, next_two, own_two = lax.optimization_barrier(
-        (combined(own_one, got_one), next_two, own_two)
-    )
-    x_one = lax.ppermute(sum_one, "grp", [(0, 1), (2, 3)])
     got_two = climb(next_two)
-    sum_one, own_two = lax.optimization_barrier((combined(own_one, got_one, x_one), own_two))
-    sum_two = lax.optimization_barrier(combined(own_two, got_two))
-    padded = jnp.pad(sum_two, ((0, EXTRA), (0, 0)))
-    cross = lax.ppermute(jnp.where(group_index == 0, padded, sum_one), "grp", [(0, 2), (1, 3)])
-    last_two, sum_two = lax.optimization_barrier(
-        (combined(own_two, got_two, cross[: 6 * nodes]), sum_two)
-    )
-    x_two = lax.ppermute(last_two, "grp", [(2, 3)])
-    y_two = lax.ppermute(sum_two, "grp", [(1, 3)])
+    x_one = lax.ppermute(combined(own_one, got_one), "grp", [(0, 1), (2, 3)])
+    y_two = lax.ppermute(combined(own_two, got_two), "grp", [(0, 2), (1, 3)])
+    y_one = lax.ppermute(combined(own_one, got_one, x_one), "grp", [(1, 3)])
+    x_two = lax.ppermute(combined(own_two, got_two, y_two), "grp", [(2, 3)])
 
     sound_rows, scale, edge_a, edge_b = call(
         sound_one_kernel,
@@ -853,7 +844,7 @@
             shape((block, LANES), BF16),
         ],
         [vmem((halves * block, LANES), F32), vmem((3, halves * block, LANES), F32)],
-        [meta, base, grads, x_one, cross],
+        [meta, base, grads, x_one, y_one],
     )
     last = (groups - 1) * count
     part_a = lax.ppermute(edge_a, ("grp", "sfc"), [(last + i, last + j) for i, j in pairs_a])

time: 50.6 us -> 49.4 us (0.976)
  other arithmetic: 1.91 us -> 0.85 us
  starting transfers between devices: 15.7 us -> 16.7 us
  local copies, waits for them, and re-layouts: 2.84 us -> 2.16 us
  waiting for transfers between devices: 16.6 us -> 16 us
    ppermute x1, starting transfers between devices: 3.41 us -> 4.48 us  [body(): lax.ppermute(edge_a, ('grp', 'sfc'), [(last + i, last + j) for i, j in pa...]
    convert_element_type x4, other arithmetic: 1.18 us -> 0.25 us  [combined(): return total.astype(BF16)]
    unnamed x25 -> x21, local copies, waits for them, and re-layouts: 2.84 us -> 2.16 us
    ppermute x4, waiting for transfers between devices: 16.6 us -> 16 us  [the longest x1 10.7 us: body(): x_one = lax.ppermute(combined(own_one, got_one), 'grp', [(0, 1), (2, 3)])]
  transfers between devices with their start and end apart: 10 -> 10, of which waited for: 2 -> 2; matrix products, arithmetic and copies ran while one was open for 2% -> 1% of each run, Pallas kernels for 11% -> 11%
where the time goes in v4:
time: 49.4 us; the launch traced here: 48.9 us
  starting transfers between devices  16.7 us (34%)
  waiting for transfers between devices  16 us (32%)
  Pallas kernels  12.3 us (25%)
  local copies, waits for them, and re-layouts  2.16 us (4%)
  between operations  0.9 us (2%)
  other arithmetic  0.85 us (2%)
    pallas_call x7, Pallas kernels, call(): pl.pallas_call(kernel, out_shape=tuple(outs), in_specs=[pl.BlockSpec(memo...  12.3 us
    ppermute x1, waiting for transfers between devices, body(): x_one = lax.ppermute(combined(own_one, got_one), 'grp', [(0, 1), (2, 3)])  10.7 us
    ppermute x1, waiting for transfers between devices, body(): y_one = lax.ppermute(combined(own_one, got_one, x_one), 'grp', [(1, 3)])  5.3 us
    ppermute x1, starting transfers between devices, body(): lax.ppermute(edge_a, ('grp', 'sfc'), [(last + i, last + j) for i, j in pa...  4.48 us
    ppermute x1, starting transfers between devices, body(): part_a = lax.ppermute(pack_a, 'sfc', pairs_a)  3.76 us
    unnamed x21, local copies, waits for them, and re-layouts  2.16 us
    ppermute x1, starting transfers between devices, body(): lax.ppermute(edge_b, ('grp', 'sfc'), [(last + i, last + j) for i, j in pa...  1.92 us
    ppermute x2, starting transfers between devices, climb(): return lax.ppermute(x, ('grp', 'sfc'), chosen)  1.33 us
  transfers between devices with their start and end apart: 10, of which 2 were waited for; matrix products, arithmetic and copies ran while one was open for 1% of the time, Pallas kernels for 11%

profile of v4, /device:TPU:7, one launch (start us, length us, event | category | flops | bytes accessed | tf_op | source)
XLA Modules:
  0.0 48.9 jit_solution(16864121136391194139)
XLA Ops:
  0.6 0.6 %pad_add_fusion.meta = s32[4]{0:T(128)} fusion(s32[1]{0:T(128)} %bitcast.2, s32[1]{0:T(128)} %bitcast.1, s32[1]{0:T(128)} %bitcast), kind=kLoop, calls=%fused_computation.8 | loop fusion | flops 12 | bytes 28 | tf_op jit(solution)/shard_map/stack | solution.py:708
  1.2 0.0 copy-start.8
  1.2 0.0 copy-start.9
  1.2 0.0 copy-start.2
  1.2 2.5 %shard_map.112 = (bf16[304,128]{1,0:T(8,128)(2,1)}, bf16[304,128]{1,0:T(8,128)(2,1)}) custom-call(s32[4]{0:T(128)} %pad_add_fusion.meta, f32[5,256,128]{2,1,0:T(8,128)} %bitcast.15, f32[256,128]{1,0:T(8,128)} %bitcast.22, s32[4,256]{1,0:T(4,128)} %bitcast.28, f32[4,64,256]{2,1,0:T(8,128)} %bitcast.19), custom_call_target="tpu_custom_call" | custom-call | flops 100000000 | bytes 1208336 | tf_op jit(solution)/shard_map/pallas_call | solution.py:668
  3.7 3.8 %collective-permute-start = (bf16[304,128]{1,0:T(8,128)(2,1)}, bf16[304,128]{1,0:T(8,128)(2,1)S(1)}, u32[]{:S(2)}, u32[]{:S(2)}) collective-permute-start(bf16[304,128]{1,0:T(8,128)(2,1)} %get-tuple-element.32), channel_id=1, source_target_pairs={{1,2},{2,1},{3,4},{4,3},{5,6},{6,5},{9,10},{10,9},{11,12},{12,11},... | collective-permute-start | bytes 233480 | tf_op jit(solution)/shard_map/ppermute | solution.py:734
  7.5 0.0 copy-start.5
  7.5 0.0 copy-start.6
  7.5 0.0 copy-start.7
  7.5 0.1 collective-permute-start.1
  7.6 0.0 copy-done.8
  7.6 0.0 copy-done.9
  7.6 0.0 copy-done.2
  7.6 0.5 copy-done.5
  8.1 0.1 copy-done.6
  8.2 0.0 copy-done.7
  8.2 1.1 %copy-done = f32[1,5,256,128]{3,2,1,0:T(8,128)S(1)} copy-done((f32[1,5,256,128]{3,2,1,0:T(8,128)S(1)}, f32[1,5,256,128]{3,2,1,0:T(8,128)}, u32[]{:S(2)}) %copy-start) | copy-done | bytes 655384
  9.3 0.5 %shard_map.113 = (f32[160,640]{1,0:T(8,128)S(1)}, bf16[160,640]{1,0:T(8,128)(2,1)S(1)}, bf16[160,640]{1,0:T(8,128)(2,1)S(1)}, f32[256,128]{1,0:T(8,128)S(1)}, bf...) custom-call(s32[4]{0:T(128)S(1)} %copy-done.5, f32[5,256,128]{2,1,0:T(8,128)S(1)} %bitcast.16, ...), custom_call_target="tpu_custom_call" | custom-call | flops 100000000 | bytes 2219024 | tf_op jit(solution)/shard_map/pallas_call | solution.py:668
  9.9 0.0 collective-permute-done.part_a
  9.9 0.0 collective-permute-done.1.part_b
  9.9 0.4 copy-done.1
  10.2 0.1 copy-done.3
  10.4 0.0 copy-done.4
  10.4 1.9 %shard_map.114 = (f32[400,256]{1,0:T(8,128)S(1)}, bf16[400,256]{1,0:T(8,128)(2,1)S(1)}, f32[3,256,128]{2,1,0:T(8,128)S(1)}, f32[64,8,128]{2,1,0:T(8,128)S(1)}, f...) custom-call(s32[4]{0:T(128)S(1)} %copy-done.5, ...), custom_call_target="tpu_custom_call" | custom-call | flops 100000000 | bytes 6242320 | tf_op jit(solution)/shard_map/pallas_call | solution.py:668
  12.2 0.7 %collective-permute-start.2 = (bf16[400,256]{1,0:T(8,128)(2,1)S(1)}, bf16[400,256]{1,0:T(8,128)(2,1)S(1)}, u32[]{:S(2)}, u32[]{:S(2)}) collective-permute-start(bf16[400,256]{1,0:T(8,128)(2,1)S(1)} %get-tuple-element.51), channel_id=1, source_target_pairs={{0,1},{1,2},{2,3},{3,4},{4,5},{5,6},{6,7},{8,9},{9,10},{10,11},{11... | collective-permute-start | bytes 614408 | tf_op jit(solution)/shard_map/ppermute | solution.py:799
  12.9 1.6 %shard_map.115 = (f32[5,256,128]{2,1,0:T(8,128)}, f32[3,256,128]{2,1,0:T(8,128)}, f32[384,256]{1,0:T(8,128)S(1)}, bf16[384,256]{1,0:T(8,128)(2,1)S(1)}) custom-call(s32[4]{0:T(128)S(1)} %copy-done.5, f32[5,256,128]{2,1,0:T(8,128)S(1)} %bitcast.18, f32[256,128]{1,0:T(8,128)S(1)} %bitcast.25, f32[3,256,128]{2,1,0:T(8,128)S(1)} %bitcast.27, ...), custom_call_target="tpu_custom_call" | custom-call | flops 100000000 | bytes 5656592 | tf_op jit(solution)/shard_map/pallas_call | solution.py:668
  14.6 0.7 %collective-permute-start.5 = (bf16[384,256]{1,0:T(8,128)(2,1)S(1)}, bf16[384,256]{1,0:T(8,128)(2,1)S(1)}, u32[]{:S(2)}, u32[]{:S(2)}) collective-permute-start(bf16[384,256]{1,0:T(8,128)(2,1)S(1)} %get-tuple-element.58), channel_id=1, source_target_pairs={{0,1},{1,2},{2,3},{3,4},{4,5},{5,6},{6,7},{8,9},{9,10},{10,11},{11... | collective-permute-start | bytes 589832 | tf_op jit(solution)/shard_map/ppermute | solution.py:799
  15.2 0.0 collective-permute-done.2
  15.2 0.1 fusion
  15.3 1.3 %collective-permute-start.3 = (bf16[400,256]{1,0:T(8,128)(2,1)S(1)}, bf16[400,256]{1,0:T(8,128)(2,1)S(1)}, u32[]{:S(2)}, u32[]{:S(2)}) collective-permute-start(bf16[400,256]{1,0:T(8,128)(2,1)S(1)} %fusion), channel_id=1, source_target_pairs={{0,8},{16,24},{1,9},{17,25},{2,10},{18,26},{3,11},{19,27},{4,12},{... | collective-permute-start | bytes 614408 | tf_op jit(solution)/shard_map/ppermute | solution.py:833
  16.6 0.0 collective-permute-done.5
  16.6 0.1 fusion.1
  16.7 1.3 %collective-permute-start.6 = (bf16[384,256]{1,0:T(8,128)(2,1)S(1)}, bf16[384,256]{1,0:T(8,128)(2,1)S(1)}, u32[]{:S(2)}, u32[]{:S(2)}) collective-permute-start(bf16[384,256]{1,0:T(8,128)(2,1)S(1)} %fusion.1), channel_id=1, source_target_pairs={{0,16},{8,24},{1,17},{9,25},{2,18},{10,26},{3,19},{11,27},{4,20},{... | collective-permute-start | bytes 589832 | tf_op jit(solution)/shard_map/ppermute | solution.py:834
  18.0 10.7 %collective-permute-done.3.source_a = bf16[400,256]{1,0:T(8,128)(2,1)S(1)} collective-permute-done((bf16[400,256]{1,0:T(8,128)(2,1)S(1)}, bf16[400,256]{1,0:T(8,128)(2,1)S(1)}, u32[]{:S(2)}, u32[]{:S(2)}) %collective-permute-start.3) | collective-permute-done | bytes 204832 | tf_op jit(solution)/shard_map/ppermute | solution.py:833
  28.7 0.1 add_convert_fusion
  28.7 1.3 %collective-permute-start.4 = (bf16[400,256]{1,0:T(8,128)(2,1)S(1)}, bf16[400,256]{1,0:T(8,128)(2,1)S(1)}, u32[]{:S(2)}, u32[]{:S(2)}) collective-permute-start(bf16[400,256]{1,0:T(8,128)(2,1)S(1)} %add_convert_fusion), channel_id=1, source_target_pairs={{8,24},{9,25},{10,26},{11,27},{12,28},{13,29},{14,30},{15,31}} | collective-permute-start | bytes 614408 | tf_op jit(solution)/shard_map/ppermute | solution.py:835
  30.0 0.0 collective-permute-done.6.source_b
  30.0 0.1 add_convert_fusion.1
  30.1 1.3 %collective-permute-start.7 = (bf16[384,256]{1,0:T(8,128)(2,1)S(1)}, bf16[384,256]{1,0:T(8,128)(2,1)S(1)}, u32[]{:S(2)}, u32[]{:S(2)}) collective-permute-start(bf16[384,256]{1,0:T(8,128)(2,1)S(1)} %add_convert_fusion.1), channel_id=1, source_target_pairs={{16,24},{17,25},{18,26},{19,27},{20,28},{21,29},{22,30},{23,31}} | collective-permute-start | bytes 589832 | tf_op jit(solution)/shard_map/ppermute | solution.py:836
  31.4 5.3 %collective-permute-done.4.source_b = bf16[400,256]{1,0:T(8,128)(2,1)S(1)} collective-permute-done((bf16[400,256]{1,0:T(8,128)(2,1)S(1)}, bf16[400,256]{1,0:T(8,128)(2,1)S(1)}, u32[]{:S(2)}, u32[]{:S(2)}) %collective-permute-start.4) | collective-permute-done | bytes 204832 | tf_op jit(solution)/shard_map/ppermute | solution.py:835
  36.7 1.5 %shard_map.116 = (f32[512,128]{1,0:T(8,128)S(1)}, f32[8,256]{1,0:T(8,128)S(1)}, bf16[256,128]{1,0:T(8,128)(2,1)S(1)}, bf16[256,128]{1,0:T(8,128)(2,1)S(1)}) custom-call(s32[4]{0:T(128)S(1)} %copy-done.5, f32[64,8,128]{2,1,0:T(8,128)S(1)} %get-tuple-element.48.base, f32[3,64,8,128]{3,2,1,0:T(8,128)S(1)} %get-tuple-element.49.grads, ...), custom_call_target="tpu_custom_call" | custom-call | flops 100000000 | bytes 1859600 | tf_op jit(solution)/shard_map/pallas_call | solution.py:668
  38.2 4.5 %collective-permute-start.8 = (bf16[256,128]{1,0:T(8,128)(2,1)S(1)}, bf16[256,128]{1,0:T(8,128)(2,1)S(1)}, u32[]{:S(2)}, u32[]{:S(2)}) collective-permute-start(bf16[256,128]{1,0:T(8,128)(2,1)S(1)} %get-tuple-element.59), channel_id=1, source_target_pairs={{25,26},{26,25},{27,28},{28,27},{29,30},{30,29}} | collective-permute-start | bytes 196616 | tf_op jit(solution)/shard_map/ppermute | solution.py:850
  42.7 1.9 %collective-permute-start.9 = (bf16[256,128]{1,0:T(8,128)(2,1)S(1)}, bf16[256,128]{1,0:T(8,128)(2,1)S(1)}, u32[]{:S(2)}, u32[]{:S(2)}) collective-permute-start(bf16[256,128]{1,0:T(8,128)(2,1)S(1)} %get-tuple-element.60), channel_id=1, source_target_pairs={{24,25},{25,24},{26,27},{27,26},{28,29},{29,28},{30,31},{31,30}} | collective-permute-start | bytes 196616 | tf_op jit(solution)/shard_map/ppermute | solution.py:851
  44.6 1.7 %shard_map.117 = (f32[64,8,128]{2,1,0:T(8,128)S(1)}, f32[3,64,8,128]{3,2,1,0:T(8,128)S(1)}, bf16[6,256,256]{2,1,0:T(8,128)(2,1)S(1)}) custom-call(s32[4]{0:T(128)S(1)} %copy-done.5, f32[512,128]{1,0:T(8,128)S(1)} %get-tuple-element.52.rows_of, s32[6,256]{1,0:T(8,128)S(1)} %get-tuple-element.62.neighbours, s32[6,256]{1,0:T(8,128)S(1)} %get-tuple-element.61.codes), custom_call_target="tpu_custom_call" | custom-call | flops 100000000 | bytes 2109456 | tf_op jit(solution)/shard_map/pallas_call | solution.py:668
  46.3 0.0 collective-permute-done.7.source_a
  46.4 0.0 collective-permute-done.8.part_a
  46.4 0.0 collective-permute-done.9.part_b
  46.4 2.6 %shard_map.118 = f32[4,64,256]{2,1,0:T(8,128)} custom-call(s32[4]{0:T(128)S(1)} %copy-done.5, f32[4,64,256]{2,1,0:T(8,128)S(1)} %bitcast.21, f32[64,8,128]{2,1,0:T(8,128)S(1)} %get-tuple-element.53.base, f32[3,64,8,128]{3,2,1,0:T(8,128)S(1)} %get-tuple-element.54.grads, bf16[6,256,256]{2,1,0:T(8,128)(2,1)S(1)} %get-tuple-element.55.hot_beside, ...), custom_call_target="tpu_custom_call" | custom-call | flops 100000000 | bytes 2904080 | tf_op jit(solution)/shard_map/pallas_call | solution.py:668
  (5 shorter events, 0.0 us)
Async XLA Ops:
  1.2 6.4 %copy-start.8 = (s32[1,6,256]{2,0,1:T(1,128)S(1)}, s32[1,6,256]{2,0,1:T(1,128)}, u32[]{:S(2)}) copy-start(s32[1,6,256]{2,0,1:T(1,128)} %param.17) | copy-start | bytes 18436
  1.2 6.4 %copy-start.9 = (s32[1,6,256]{2,0,1:T(1,128)S(1)}, s32[1,6,256]{2,0,1:T(1,128)}, u32[]{:S(2)}) copy-start(s32[1,6,256]{2,0,1:T(1,128)} %param.16) | copy-start | bytes 18436
  1.2 6.4 %copy-start.2 = (f32[1,256,128]{2,1,0:T(8,128)S(1)}, f32[1,256,128]{2,1,0:T(8,128)}, u32[]{:S(2)}) copy-start(f32[1,256,128]{2,1,0:T(8,128)} %param.11) | copy-start | bytes 393220
  3.7 6.1 %collective-permute-start = (bf16[304,128]{1,0:T(8,128)(2,1)}, bf16[304,128]{1,0:T(8,128)(2,1)S(1)}, u32[]{:S(2)}, u32[]{:S(2)}) collective-permute-start(bf16[304,128]{1,0:T(8,128)(2,1)} %get-tuple-element.32), channel_id=1, source_target_pairs={{1,2},{2,1},{3,4},{4,3},{5,6},{6,5},{9,10},{10,9},{11,12},{12,11},... | collective-permute-start | bytes 233480 | tf_op jit(solution)/shard_map/ppermute | solution.py:734
  7.5 0.6 %copy-start.5 = (s32[4]{0:T(128)S(1)}, s32[4]{0:T(128)}, u32[]{:S(2)}) copy-start(s32[4]{0:T(128)} %pad_add_fusion.meta) | copy-start | bytes 52
  7.5 0.7 %copy-start.6 = (s32[1,4,256]{2,1,0:T(4,128)S(1)}, s32[1,4,256]{2,1,0:T(4,128)}, u32[]{:S(2)}) copy-start(s32[1,4,256]{2,1,0:T(4,128)} %param.12) | copy-start | bytes 12292
  7.5 0.7 %copy-start.7 = (s32[1,256]{1,0:T(1,128)S(1)}, s32[1,256]{1,0:T(1,128)}, u32[]{:S(2)}) copy-start(s32[1,256]{1,0:T(1,128)} %target.1) | copy-start | bytes 3076
  7.5 2.3 %collective-permute-start.1 = (bf16[304,128]{1,0:T(8,128)(2,1)}, bf16[304,128]{1,0:T(8,128)(2,1)S(1)}, u32[]{:S(2)}, u32[]{:S(2)}) collective-permute-start(bf16[304,128]{1,0:T(8,128)(2,1)} %get-tuple-element.33), channel_id=1, source_target_pairs={{0,1},{1,0},{2,3},{3,2},{4,5},{5,4},{6,7},{7,6},{8,9},{9,8},{10,11... | collective-permute-start | bytes 233480 | tf_op jit(solution)/shard_map/ppermute | solution.py:735
  8.2 1.1 %copy-start = (f32[1,5,256,128]{3,2,1,0:T(8,128)S(1)}, f32[1,5,256,128]{3,2,1,0:T(8,128)}, u32[]{:S(2)}) copy-start(f32[1,5,256,128]{3,2,1,0:T(8,128)} %param.9) | copy-start | bytes 1966084
  9.3 0.9 %copy-start.1 = (f32[1,4,64,256]{3,2,1,0:T(8,128)S(1)}, f32[1,4,64,256]{3,2,1,0:T(8,128)}, u32[]{:S(2)}) copy-start(f32[1,4,64,256]{3,2,1,0:T(8,128)} %param.15) | copy-start | bytes 786436
  9.3 1.1 %copy-start.3 = (f32[1,3,256,128]{3,2,1,0:T(8,128)S(1)}, f32[1,3,256,128]{3,2,1,0:T(8,128)}, u32[]{:S(2)}) copy-start(f32[1,3,256,128]{3,2,1,0:T(8,128)} %param.10) | copy-start | bytes 1179652
  9.3 1.1 %copy-start.4 = (f32[64,128]{1,0:T(8,128)S(1)}, f32[64,128]{1,0:T(8,128)}, u32[]{:S(2)}) copy-start(f32[64,128]{1,0:T(8,128)} %projector.3) | copy-start | bytes 98308
  12.2 3.0 %collective-permute-start.2 = (bf16[400,256]{1,0:T(8,128)(2,1)S(1)}, bf16[400,256]{1,0:T(8,128)(2,1)S(1)}, u32[]{:S(2)}, u32[]{:S(2)}) collective-permute-start(bf16[400,256]{1,0:T(8,128)(2,1)S(1)} %get-tuple-element.51), channel_id=1, source_target_pairs={{0,1},{1,2},{2,3},{3,4},{4,5},{5,6},{6,7},{8,9},{9,10},{10,11},{11... | collective-permute-start | bytes 614408 | tf_op jit(solution)/shard_map/ppermute | solution.py:799
  14.6 2.0 %collective-permute-start.5 = (bf16[384,256]{1,0:T(8,128)(2,1)S(1)}, bf16[384,256]{1,0:T(8,128)(2,1)S(1)}, u32[]{:S(2)}, u32[]{:S(2)}) collective-permute-start(bf16[384,256]{1,0:T(8,128)(2,1)S(1)} %get-tuple-element.58), channel_id=1, source_target_pairs={{0,1},{1,2},{2,3},{3,4},{4,5},{5,6},{6,7},{8,9},{9,10},{10,11},{11... | collective-permute-start | bytes 589832 | tf_op jit(solution)/shard_map/ppermute | solution.py:799
  15.3 13.4 %collective-permute-start.3 = (bf16[400,256]{1,0:T(8,128)(2,1)S(1)}, bf16[400,256]{1,0:T(8,128)(2,1)S(1)}, u32[]{:S(2)}, u32[]{:S(2)}) collective-permute-start(bf16[400,256]{1,0:T(8,128)(2,1)S(1)} %fusion), channel_id=1, source_target_pairs={{0,8},{16,24},{1,9},{17,25},{2,10},{18,26},{3,11},{19,27},{4,12},{... | collective-permute-start | bytes 614408 | tf_op jit(solution)/shard_map/ppermute | solution.py:833
  16.7 13.4 %collective-permute-start.6 = (bf16[384,256]{1,0:T(8,128)(2,1)S(1)}, bf16[384,256]{1,0:T(8,128)(2,1)S(1)}, u32[]{:S(2)}, u32[]{:S(2)}) collective-permute-start(bf16[384,256]{1,0:T(8,128)(2,1)S(1)} %fusion.1), channel_id=1, source_target_pairs={{0,16},{8,24},{1,17},{9,25},{2,18},{10,26},{3,19},{11,27},{4,20},{... | collective-permute-start | bytes 589832 | tf_op jit(solution)/shard_map/ppermute | solution.py:834
  28.7 8.0 %collective-permute-start.4 = (bf16[400,256]{1,0:T(8,128)(2,1)S(1)}, bf16[400,256]{1,0:T(8,128)(2,1)S(1)}, u32[]{:S(2)}, u32[]{:S(2)}) collective-permute-start(bf16[400,256]{1,0:T(8,128)(2,1)S(1)} %add_convert_fusion), channel_id=1, source_target_pairs={{8,24},{9,25},{10,26},{11,27},{12,28},{13,29},{14,30},{15,31}} | collective-permute-start | bytes 614408 | tf_op jit(solution)/shard_map/ppermute | solution.py:835
  30.1 16.2 %collective-permute-start.7 = (bf16[384,256]{1,0:T(8,128)(2,1)S(1)}, bf16[384,256]{1,0:T(8,128)(2,1)S(1)}, u32[]{:S(2)}, u32[]{:S(2)}) collective-permute-start(bf16[384,256]{1,0:T(8,128)(2,1)S(1)} %add_convert_fusion.1), channel_id=1, source_target_pairs={{16,24},{17,25},{18,26},{19,27},{20,28},{21,29},{22,30},{23,31}} | collective-permute-start | bytes 589832 | tf_op jit(solution)/shard_map/ppermute | solution.py:836
  38.2 8.2 %collective-permute-start.8 = (bf16[256,128]{1,0:T(8,128)(2,1)S(1)}, bf16[256,128]{1,0:T(8,128)(2,1)S(1)}, u32[]{:S(2)}, u32[]{:S(2)}) collective-permute-start(bf16[256,128]{1,0:T(8,128)(2,1)S(1)} %get-tuple-element.59), channel_id=1, source_target_pairs={{25,26},{26,25},{27,28},{28,27},{29,30},{30,29}} | collective-permute-start | bytes 196616 | tf_op jit(solution)/shard_map/ppermute | solution.py:850
  42.7 3.7 %collective-permute-start.9 = (bf16[256,128]{1,0:T(8,128)(2,1)S(1)}, bf16[256,128]{1,0:T(8,128)(2,1)S(1)}, u32[]{:S(2)}, u32[]{:S(2)}) collective-permute-start(bf16[256,128]{1,0:T(8,128)(2,1)S(1)} %get-tuple-element.60), channel_id=1, source_target_pairs={{24,25},{25,24},{26,27},{27,26},{28,29},{29,28},{30,31},{31,30}} | collective-permute-start | bytes 196616 | tf_op jit(solution)/shard_map/ppermute | solution.py:851

commit v5 on v4

--- a/solution.py
+++ b/solution.py
@@ -17,10 +17,11 @@
 LANES = 128
 EDGE = 3 * HW
 FIELD_ORDER = (1, 2, 3, 0, 4)
+ALL_FIELDS = ((0, 2), (2, 4), (4, 5))
 BASE = 32.0
 EXTRA = 16
 VMEM_LIMIT = 20 * 1024 * 1024
-PACK_LIMIT = 64 * 1024 * 1024 - 256 * 1024
+PACK_LIMIT = 62 * 1024 * 1024
 
 F32 = jnp.float32
 BF16 = jnp.bfloat16
@@ -73,8 +74,16 @@
     return lax.dot_general(a, b, (((1,), (1,)), ((), ())), preferred_element_type=F32)
 
 
-def pack_kernel(meta, flow, visc, links, sound, out_a, out_b, links_in, staged, sems, link_sem):
-    is_flow, even = meta[0] == 1, meta[1] == 1
+def on_flow_row():
+    return lax.axis_index("grp") < lax.axis_size("grp") - 1
+
+
+def on_even_column():
+    return lax.rem(lax.axis_index("sfc"), 2) == 0
+
+
+def pack_kernel(flow, visc, links, sound, out_a, out_b, links_in, staged, sems, link_sem):
+    is_flow, even = on_flow_row(), on_even_column()
     tiles = flow.shape[1]
     _, nodes, elements = sound.shape
     outs = (out_a, out_b)
@@ -105,7 +114,7 @@
             copy.start()
         fetch.wait()
         given = links_in[...]
-        own = meta[2] + lax.broadcasted_iota(jnp.int32, given.shape, 1)
+        own = lax.axis_index("sfc") * tiles + lax.broadcasted_iota(jnp.int32, given.shape, 1)
         offset = jnp.where(given < 0, 0, given - own).astype(F32)
         low, high = offset[:, :LANES], offset[:, tiles - LANES :]
         pad = jnp.zeros((EXTRA - 4, LANES), F32)
@@ -194,11 +203,11 @@
     return dot(mat[at_row:, :], jnp.concatenate(both, 0))
 
 
-def advance(plan, b, mat, high, low, state, v, new_state, new_high, new_low, new_at, wanted):
+def advance(plan, b, mat, high, low, state, v, places, new_state, new_high, new_low, new_at, split):
     rows = plan.rows
     center = [state(k) for k in range(3)]
     scaled = [(0.5 * ADVECT) * c for c in center]
-    for first, last in ((0, 2), (2, 4), (4, 5)):
+    for first, last in places:
         got = gathered(plan, mat, high, low, b, slice(first * LANES, last * LANES), 0)
         for place in range(first, last):
             inner = columns_of(place - first)
@@ -211,7 +220,7 @@
                 - (scaled[0] * (east - west) + scaled[1] * dy + scaled[2] * dz)
             )
             new_state[new_at : new_at + rows, columns_of(place)] = new
-            if place < wanted:
+            if split:
                 put(new_high, new_low, new_at, place, new)
 
 
@@ -271,15 +280,16 @@
 
 
 def inner_kernel(
-    meta, flow, visc, links, target,
+    flow, visc, links, target,
     inner_state, inner_high, inner_low, lcol, inner_mats, hits, high0, low0, square,
 ):
     plan = FlowPlan(flow.shape[1])
     tiles, rows = plan.tiles, plan.rows
 
-    @pl.when(meta[0] == 1)
-    def _():
-        first_tile, first_element = meta[2], meta[3]
+    @pl.when(on_flow_row())
+    def _():
+        column = lax.axis_index("sfc")
+        first_tile, first_element = column * tiles, column * (hits.shape[0] // 2)
         for place, f in enumerate(FIELD_ORDER):
             put(high0, low0, 0, place, flow[f])
         square[...] = jnp.zeros_like(square)
@@ -298,7 +308,7 @@
             advance(
                 plan, b, inner_mats.at[at], [(EDGE, high0)], [(EDGE, low0)],
                 lambda place, own=own: flow[FIELD_ORDER[place], own, :],
-                visc[own, :], inner_state, inner_high, inner_low, at * rows, 5,
+                visc[own, :], ALL_FIELDS, inner_state, inner_high, inner_low, at * rows, True,
             )
 
 
@@ -328,13 +338,13 @@
 
 
 def first_kernel(
-    meta, flow, visc, mean, projector, part_a, part_b, sound, neighbours, codes,
+    flow, visc, mean, projector, part_a, part_b, sound, neighbours, codes,
     inner_state, inner_high, inner_low, lcol, inner_mats, hits,
     own_one, next_one, mean_one, base, grads,
     edge_state, edge_high, edge_low, edge_mats, edge_visc,
     square, state0, high0, low0, zero, packed, pay, rows_of, facing, remote, rhs,
 ):
-    is_flow, even = meta[0] == 1, meta[1] == 1
+    is_flow, even = on_flow_row(), on_even_column()
     plan = FlowPlan(packed.shape[1])
     tiles, rows, span = plan.tiles, plan.rows, plan.span
     own_rows = span - EDGE
@@ -379,8 +389,8 @@
                 plan, b, edge_mats.at[side],
                 [(b * rows, high0.at[side])], [(b * rows, low0.at[side])],
                 lambda place, side=side: state0[side, HW : HW + rows, columns_of(place)],
-                edge_visc[side * rows : (side + 1) * rows, :],
-                edge_state, edge_high, edge_low, side * rows, 5,
+                edge_visc[side * rows : (side + 1) * rows, :], ALL_FIELDS,
+                edge_state, edge_high, edge_low, side * rows, True,
             )
         high1 = closed(plan, band_parts(plan, edge_high, inner_high), zero)
         low1 = closed(plan, band_parts(plan, edge_low, inner_low), zero)
@@ -409,7 +419,7 @@
         for face in range(6):
             for part in range(halves + 2):
                 facing_rows(rows_of, part * block, nodes, face ^ 1, facing.at[face, part])
-            hot = hot_links(neighbours, face, meta[3], elements, True, True)
+            hot = hot_links(neighbours, face, elements, True, True)
             remote_rows([facing[face, part] for part in range(halves + 2)], hot, remote, face)
         derivatives(rows_of, nodes, grads, rhs)
         add_faces(rows_of, nodes, remote, neighbours, codes, rhs, True)
@@ -417,50 +427,88 @@
             base[n] = rows_of[pl.ds(n, 8, stride=nodes), :] + ACOUSTIC_STEP * rhs[n]
 
 
+def second_block(plan, b, carried, visc, places, new_state, new_parts):
+    (inner_state, inner_high, inner_low, inner_mats, edge_state, edge_high, edge_low, edge_mats,
+     edge_visc, zero) = carried
+    rows = plan.rows
+    if b in plan.inner():
+        v = visc[plan.at(b) - EDGE : plan.at(b) - EDGE + rows, :]
+    else:
+        v = edge_visc[:rows, :] if b == 0 else edge_visc[rows:, :]
+    advance(
+        plan, b, mats_of(plan, b, edge_mats, inner_mats),
+        closed(plan, band_parts(plan, edge_high, inner_high), zero),
+        closed(plan, band_parts(plan, edge_low, inner_low), zero),
+        band_state(plan, b, edge_state, inner_state), v, places,
+        new_state, *new_parts, b * rows, new_parts[0] is not None,
+    )
+
+
 def second_kernel(
-    meta, flow, visc, mean, mean_one, projector,
+    visc, mean, mean_one, projector,
     inner_state, inner_high, inner_low, inner_mats, hits,
     edge_state, edge_high, edge_low, edge_mats, edge_visc,
-    flow_out, mean_out, own_two, next_two,
-    state, high, low, zero, packed, pay,
+    state, mean_two, own_two, next_two,
+    high, low, zero, packed, pay,
 ):
     plan = FlowPlan(packed.shape[1])
     rows = plan.rows
-    is_flow = meta[0] == 1
+    is_flow = on_flow_row()
 
     @pl.when(jnp.logical_not(is_flow))
     def _():
-        flow_out[...] = flow[...]
-        mean_out[...] = mean[...]
         own_two[...] = jnp.zeros_like(own_two)
         next_two[...] = jnp.zeros_like(next_two)
 
     @pl.when(is_flow)
     def _():
         zero[...] = jnp.zeros_like(zero)
-        high1 = closed(plan, band_parts(plan, edge_high, inner_high), zero)
-        low1 = closed(plan, band_parts(plan, edge_low, inner_low), zero)
+        carried = (
+            inner_state, inner_high, inner_low, inner_mats,
+            edge_state, edge_high, edge_low, edge_mats, edge_visc, zero,
+        )
         for b in range(plan.blocks):
-            if b in plan.inner():
-                v = visc[plan.at(b) - EDGE : plan.at(b) - EDGE + rows, :]
-            else:
-                v = edge_visc[:rows, :] if b == 0 else edge_visc[rows:, :]
-            advance(
-                plan, b, mats_of(plan, b, edge_mats, inner_mats), high1, low1,
-                band_state(plan, b, edge_state, inner_state), v,
-                state, high, low, b * rows, 3,
-            )
-        own = slice(EDGE - HW, EDGE - HW + plan.tiles)
-        for place, f in enumerate(FIELD_ORDER):
-            flow_out[f] = state[own, columns_of(place)]
+            second_block(plan, b, carried, visc, ((0, 2), (2, 3)), state, (high, low))
         for b in range(plan.blocks):
             lamb_block(
                 plan, b, mats_of(plan, b, edge_mats, inner_mats),
                 closed(plan, [(HW, high)], zero), closed(plan, [(HW, low)], zero),
                 lambda place, b=b: state[b * rows : (b + 1) * rows, columns_of(place)],
-                mean_one, mean_out, packed,
+                mean_one, mean_two, packed,
             )
         element_sums(projector, packed, hits, pay, own_two, next_two)
+
+
+def output_kernel(
+    flow, visc, mean, state, mean_two,
+    inner_state, inner_high, inner_low, inner_mats,
+    edge_state, edge_high, edge_low, edge_mats, edge_visc, after,
+    flow_out, mean_out, token, passive, zero,
+):
+    plan = FlowPlan(flow.shape[1])
+    is_flow = on_flow_row()
+    token[...] = jnp.zeros_like(token)
+
+    @pl.when(jnp.logical_not(is_flow))
+    def _():
+        flow_out[...] = flow[...]
+        mean_out[...] = mean[...]
+
+    @pl.when(is_flow)
+    def _():
+        zero[...] = jnp.zeros_like(zero)
+        mean_out[...] = mean_two[...]
+        carried = (
+            inner_state, inner_high, inner_low, inner_mats,
+            edge_state, edge_high, edge_low, edge_mats, edge_visc, zero,
+        )
+        own = slice(EDGE - HW, EDGE - HW + plan.tiles)
+        for place in range(3):
+            flow_out[FIELD_ORDER[place]] = state[own, columns_of(place)]
+        for b in range(plan.blocks):
+            second_block(plan, b, carried, visc, ((3, 5),), passive, (None, None))
+        for place in (3, 4):
+            flow_out[FIELD_ORDER[place]] = passive[own, columns_of(place)]
 
 
 def facing_rows(rows_of, base, nodes, face, to):
@@ -476,9 +524,9 @@
             to[v * 16 : (v + 1) * 16, :] = rows_of[at : at + 16, :]
 
 
-def hot_links(neighbours, face, first_element, elements, own, beside):
+def hot_links(neighbours, face, elements, own, beside):
     link = neighbours[face : face + 1, :]
-    near = link - first_element
+    near = link - lax.axis_index("sfc") * elements
     size = (elements if own else 0) + (2 * LANES if beside else 0)
     start = elements if own else 0
     place = jnp.where(near < 0, start + LANES + near, near - elements + start + LANES)
@@ -575,9 +623,9 @@
 
 
 def sound_one_kernel(
-    meta, base, grads, source_a, source_b, rows_of, scale_out, edge_a, edge_b, lamb, mean
+    base, grads, source_a, source_b, rows_of, scale_out, edge_a, edge_b, lamb, mean
 ):
-    is_flow, even = meta[0] == 1, meta[1] == 1
+    is_flow, even = on_flow_row(), on_even_column()
     nodes = base.shape[0]
     block = 4 * nodes
 
@@ -599,33 +647,37 @@
 
 
 def sound_inner_kernel(
-    meta, rows_of, neighbours, codes, base, grads, hot_beside, facing, remote, rhs
+    rows_of, neighbours, codes, scale, source_a, source_b,
+    base, hot_beside, facing, remote, rhs, grads, lamb, mean,
 ):
     nodes = base.shape[0]
     elements = neighbours.shape[1]
     halves = elements // LANES
     block = 4 * nodes
 
-    @pl.when(meta[0] == 0)
+    @pl.when(jnp.logical_not(on_flow_row()))
     def _():
         for face in range(6):
             for part in range(halves):
                 facing_rows(rows_of, part * block, nodes, face ^ 1, facing.at[face, part])
-            hot = hot_links(neighbours, face, meta[3], elements, True, False)
+            hot = hot_links(neighbours, face, elements, True, False)
             remote_rows([facing[face, part] for part in range(halves)], hot, remote, face)
-            hot_beside[face] = hot_links(neighbours, face, meta[3], elements, False, True)
+            hot_beside[face] = hot_links(neighbours, face, elements, False, True)
         derivatives(rows_of, nodes, grads, rhs)
         add_faces(rows_of, nodes, remote, neighbours, codes, rhs, True)
+        total = source_a[...].astype(F32) + source_b[...].astype(F32)
+        source_rows(total * scale[0:1, :], nodes, lamb, mean)
         for n in range(nodes):
-            base[n] = rows_of[pl.ds(n, 8, stride=nodes), :] + ACOUSTIC_STEP * rhs[n]
+            base[n] = rows_of[pl.ds(n, 8, stride=nodes), :] + ACOUSTIC_STEP * (
+                rhs[n] - source_terms(nodes, grads, lamb, mean, n)
+            )
 
 
 def sound_two_kernel(
-    meta, sound, base, grads, hot_beside, neighbours, codes, scale, source_a, source_b,
-    part_a, part_b,
-    out, rows_of, facing, remote, rhs, lamb, mean,
+    sound, base, hot_beside, neighbours, codes, part_a, part_b,
+    out, rows_of, facing, remote, rhs,
 ):
-    is_flow, even = meta[0] == 1, meta[1] == 1
+    is_flow, even = on_flow_row(), on_even_column()
     nodes = base.shape[0]
     elements = sound.shape[2]
     halves = elements // LANES
@@ -637,8 +689,6 @@
 
     @pl.when(jnp.logical_not(is_flow))
     def _():
-        total = source_a[...].astype(F32) + source_b[...].astype(F32)
-        source_rows(total * scale[0:1, :], nodes, lamb, mean)
         a, b = part_a[...].astype(F32), part_b[...].astype(F32)
         rows_of[:block, :] = jnp.where(even, a, b)
         rows_of[block:, :] = jnp.where(even, b, a)
@@ -648,8 +698,7 @@
             remote_rows(
                 [facing[face, part].astype(BF16) for part in range(2)], hot_beside[face], remote, face
             )
-        for n in range(nodes):
-            rhs[n] = -source_terms(nodes, grads, lamb, mean, n)
+        rhs[...] = jnp.zeros_like(rhs)
         add_faces(rows_of, nodes, remote, neighbours, codes, rhs, False)
         for n in range(nodes):
             rows_of[pl.ds(n, 8, stride=nodes), :] = base[n] + ACOUSTIC_STEP * rhs[n]
@@ -661,9 +710,7 @@
 
 
 def call(kernel, outs, scratch, operands, in_hbm=(), limit=VMEM_LIMIT):
-    spaces = [pltpu.SMEM] + [
-        pltpu.HBM if at in in_hbm else pltpu.VMEM for at in range(1, len(operands))
-    ]
+    spaces = [pltpu.HBM if at in in_hbm else pltpu.VMEM for at in range(len(operands))]
     moved = sum(int(np.prod(x.shape)) * x.dtype.itemsize for x in (*operands, *outs))
     return pl.pallas_call(
         kernel,
@@ -689,8 +736,6 @@
 ):
     groups = lax.axis_size("grp")
     count = lax.axis_size("sfc")
-    group_index = lax.axis_index("grp")
-    column = lax.axis_index("sfc")
     flow = flow_fields[0]
     mean = mean_velocity[0]
     visc = cell_eddy_viscosity[0]
@@ -705,15 +750,6 @@
     plan = FlowPlan(tiles)
     shape = jax.ShapeDtypeStruct
     vmem = pltpu.VMEM
-    meta = jnp.stack(
-        [
-            (group_index < groups - 1).astype(jnp.int32),
-            (column % 2 == 0).astype(jnp.int32),
-            (column * tiles).astype(jnp.int32),
-            (column * elements).astype(jnp.int32),
-        ]
-    )
-
     pairs_a = [p for i in range(1, count - 1, 2) for p in ((i, i + 1), (i + 1, i))]
     pairs_b = [p for i in range(0, count - 1, 2) for p in ((i, i + 1), (i + 1, i))]
 
@@ -727,8 +763,8 @@
             pltpu.SemaphoreType.DMA((2, 6)),
             pltpu.SemaphoreType.DMA,
         ],
-        [meta, flow, visc, links, sound],
-        in_hbm=(1, 2, 3, 4),
+        [flow, visc, links, sound],
+        in_hbm=(0, 1, 2, 3),
         limit=PACK_LIMIT,
     )
     part_a = lax.ppermute(pack_a, "sfc", pairs_a)
@@ -750,7 +786,7 @@
             shape((2 * elements, tiles), BF16),
         ],
         [vmem((tiles, fields), BF16), vmem((tiles, fields), BF16), square],
-        [meta, flow, visc, links, tile_target],
+        [flow, visc, links, tile_target],
     )
     lines = 6 * nodes + EXTRA
     by_node = shape((nodes, 8, LANES), F32)
@@ -787,7 +823,7 @@
             node_rows,
         ],
         [
-            meta, flow, visc, mean, projector, part_a, part_b, sound, neighbours, codes,
+            flow, visc, mean, projector, part_a, part_b, sound, neighbours, codes,
             inner_state, inner_high, inner_low, lcol, inner_mats, hits,
         ],
     )
@@ -807,31 +843,35 @@
     got_one = climb(next_one)
     band = plan.blocks * rows
     velocity = 3 * LANES
-    flow_out, mean_out, own_two, next_two = call(
+    step_one = [inner_state, inner_high, inner_low, inner_mats]
+    edges = [edge_state, edge_high, edge_low, edge_mats, edge_visc]
+    state_two, mean_two, own_two, next_two = call(
         second_kernel,
         [
-            shape(flow.shape, F32),
+            shape((band, velocity), F32),
             shape(mean.shape, F32),
             shape((6 * nodes, elements), F32),
             shape((6 * nodes, elements), BF16),
         ],
         [
-            vmem((band, fields), F32),
             vmem((band, velocity), BF16),
             vmem((band, velocity), BF16),
             vmem((HW, fields), BF16),
             packed,
             vmem((6 * nodes, tiles), BF16),
         ],
-        [
-            meta, flow, visc, mean, mean_one, projector,
-            inner_state, inner_high, inner_low, inner_mats, hits,
-            edge_state, edge_high, edge_low, edge_mats, edge_visc,
-        ],
+        [visc, mean, mean_one, projector, *step_one, hits, *edges],
     )
     got_two = climb(next_two)
-    x_one = lax.ppermute(combined(own_one, got_one), "grp", [(0, 1), (2, 3)])
-    y_two = lax.ppermute(combined(own_two, got_two), "grp", [(0, 2), (1, 3)])
+    sum_one = combined(own_one, got_one)
+    x_one = lax.ppermute(sum_one, "grp", [(0, 1), (2, 3)])
+    flow_out, mean_out, token = call(
+        output_kernel,
+        [shape(flow.shape, F32), shape(mean.shape, F32), shape((8, LANES), F32)],
+        [vmem((band, fields), F32), vmem((HW, fields), BF16)],
+        [flow, visc, mean, state_two, mean_two, *step_one, *edges, sum_one],
+    )
+    y_two = lax.ppermute(combined(own_two, got_two, token[0, 0]), "grp", [(0, 2), (1, 3)])
     y_one = lax.ppermute(combined(own_one, got_one, x_one), "grp", [(1, 3)])
     x_two = lax.ppermute(combined(own_two, got_two, y_two), "grp", [(2, 3)])
 
@@ -844,20 +884,23 @@
             shape((block, LANES), BF16),
         ],
         [vmem((halves * block, LANES), F32), vmem((3, halves * block, LANES), F32)],
-        [meta, base, grads, x_one, y_one],
+        [base, grads, x_one, y_one],
     )
     last = (groups - 1) * count
     part_a = lax.ppermute(edge_a, ("grp", "sfc"), [(last + i, last + j) for i, j in pairs_a])
     part_b = lax.ppermute(edge_b, ("grp", "sfc"), [(last + i, last + j) for i, j in pairs_b])
-    base, grads, hot_beside = call(
+    base, hot_beside = call(
         sound_inner_kernel,
-        [by_node, by_node_3, shape((6, 2 * LANES, elements), BF16)],
+        [by_node, shape((6, 2 * LANES, elements), BF16)],
         [
             vmem((6, halves, 64, LANES), F32),
             vmem((6, halves * 64, LANES), F32),
             node_rows,
+            vmem((3, nodes, 8, LANES), F32),
+            vmem((halves * block, LANES), F32),
+            vmem((3, halves * block, LANES), F32),
         ],
-        [meta, sound_rows, neighbours, codes],
+        [sound_rows, neighbours, codes, scale, x_two, y_two],
     )
     (sound_out,) = call(
         sound_two_kernel,
@@ -867,13 +910,8 @@
             vmem((6, 2, 64, LANES), F32),
             vmem((6, halves * 64, LANES), F32),
             node_rows,
-            vmem((halves * block, LANES), F32),
-            vmem((3, halves * block, LANES), F32),
         ],
-        [
-            meta, sound, base, grads, hot_beside, neighbours, codes, scale,
-            x_two, y_two, part_a, part_b,
-        ],
+        [sound, base, hot_beside, neighbours, codes, part_a, part_b],
     )
     return flow_out[None], mean_out[None], sound_out[None]
 

time: 49.4 us -> 42.7 us (0.86)
  the two profiles are of different devices: /device:TPU:7 before, /device:TPU:15 now
where the time goes in v5:
time: 42.7 us; the launch traced here: 42.1 us
  starting transfers between devices  17.1 us (40%)
  waiting for transfers between devices  13.7 us (32%)
  Pallas kernels  8.39 us (20%)
  local copies, waits for them, and re-layouts  1.09 us (3%)
  between operations  0.91 us (2%)
  other arithmetic  0.89 us (2%)
    pallas_call x8, Pallas kernels, call(): pl.pallas_call(kernel, out_shape=tuple(outs), in_specs=[pl.BlockSpec(memo...  8.39 us
    ppermute x1, waiting for transfers between devices, body(): x_one = lax.ppermute(sum_one, 'grp', [(0, 1), (2, 3)])  7.3 us
    ppermute x1, starting transfers between devices, body(): lax.ppermute(edge_a, ('grp', 'sfc'), [(last + i, last + j) for i, j in pa...  4.85 us
    ppermute x1, starting transfers between devices, body(): part_a = lax.ppermute(pack_a, 'sfc', pairs_a)  3.76 us
    ppermute x1, waiting for transfers between devices, body(): y_one = lax.ppermute(combined(own_one, got_one, x_one), 'grp', [(1, 3)])  2.47 us
    ppermute x1, waiting for transfers between devices, body(): lax.ppermute(combined(own_two, got_two, token[0, 0]), 'grp', [(0, 2), (1,...  2.24 us
    ppermute x1, starting transfers between devices, body(): lax.ppermute(edge_b, ('grp', 'sfc'), [(last + i, last + j) for i, j in pa...  1.92 us
    ppermute x1, waiting for transfers between devices, body(): part_a = lax.ppermute(pack_a, 'sfc', pairs_a)  1.71 us
  transfers between devices with their start and end apart: 10, of which 4 were waited for; matrix products, arithmetic and copies ran while one was open for 3% of the time, Pallas kernels for 10%

profile of v5, /device:TPU:15, one launch (start us, length us, event | category | flops | bytes accessed | tf_op | source)
XLA Modules:
  0.0 42.1 jit_solution(5795814036475403533)
XLA Ops:
  0.6 0.0 copy-start
  0.6 0.0 copy-start.7
  0.7 0.0 copy-start.8
  0.7 0.0 copy-start.2
  0.7 1.7 %shard_map.112 = (bf16[304,128]{1,0:T(8,128)(2,1)}, bf16[304,128]{1,0:T(8,128)(2,1)}) custom-call(f32[5,256,128]{2,1,0:T(8,128)} %bitcast.13, f32[256,128]{1,0:T(8,128)} %bitcast.20, s32[4,256]{1,0:T(4,128)} %bitcast.28, f32[4,64,256]{2,1,0:T(8,128)} %bitcast.25), custom_call_target="tpu_custom_call" | custom-call | flops 100000000 | bytes 1208320 | tf_op jit(solution)/shard_map/pallas_call | solution.py:715
  2.4 3.8 %collective-permute-start = (bf16[304,128]{1,0:T(8,128)(2,1)}, bf16[304,128]{1,0:T(8,128)(2,1)S(1)}, u32[]{:S(2)}, u32[]{:S(2)}) collective-permute-start(bf16[304,128]{1,0:T(8,128)(2,1)} %get-tuple-element.34), channel_id=1, source_target_pairs={{1,2},{2,1},{3,4},{4,3},{5,6},{6,5},{9,10},{10,9},{11,12},{12,11},... | collective-permute-start | bytes 233480 | tf_op jit(solution)/shard_map/ppermute | solution.py:770
  6.2 0.0 copy-start.5
  6.2 0.0 copy-start.6
  6.2 0.1 collective-permute-start.1
  6.3 0.0 copy-done.7
  6.3 0.0 copy-done.8
  6.3 0.0 copy-done
  6.3 0.0 copy-done.2
  6.3 0.5 %copy-done.5 = s32[1,4,256]{2,1,0:T(4,128)S(1)} copy-done((s32[1,4,256]{2,1,0:T(4,128)S(1)}, s32[1,4,256]{2,1,0:T(4,128)}, u32[]{:S(2)}) %copy-start.5) | copy-done | bytes 4120
  6.9 0.0 copy-done.6
  6.9 0.0 copy-start.1
  6.9 0.0 copy-start.3
  6.9 1.7 %collective-permute-done.part_a = bf16[304,128]{1,0:T(8,128)(2,1)S(1)} collective-permute-done((bf16[304,128]{1,0:T(8,128)(2,1)}, bf16[304,128]{1,0:T(8,128)(2,1)S(1)}, u32[]{:S(2)}, u32[]{:S(2)}) %collective-permute-start) | collective-permute-done | bytes 77856 | tf_op jit(solution)/shard_map/ppermute | solution.py:770
  8.6 0.0 collective-permute-done.1.part_b
  8.6 0.0 copy-done.1
  8.6 0.0 copy-done.3
  8.6 0.0 copy-done.4
  8.6 1.4 %shard_map.114 = (f32[400,256]{1,0:T(8,128)S(1)}, bf16[400,256]{1,0:T(8,128)(2,1)S(1)}, f32[3,256,128]{2,1,0:T(8,128)S(1)}, f32[64,8,128]{2,1,0:T(8,128)S(1)}, f...) custom-call(f32[5,256,128]{2,1,0:T(8,128)S(1)} %bitcast.15, ...), custom_call_target="tpu_custom_call" | custom-call | flops 100000000 | bytes 6242304 | tf_op jit(solution)/shard_map/pallas_call | solution.py:715
  10.0 0.7 %collective-permute-start.2 = (bf16[400,256]{1,0:T(8,128)(2,1)S(1)}, bf16[400,256]{1,0:T(8,128)(2,1)S(1)}, u32[]{:S(2)}, u32[]{:S(2)}) collective-permute-start(bf16[400,256]{1,0:T(8,128)(2,1)S(1)} %get-tuple-element.51), channel_id=1, source_target_pairs={{0,1},{1,2},{2,3},{3,4},{4,5},{5,6},{6,7},{8,9},{9,10},{10,11},{11... | collective-permute-start | bytes 614408 | tf_op jit(solution)/shard_map/ppermute | solution.py:835
  10.7 0.1 shard_map.115
  10.8 0.7 %collective-permute-start.5 = (bf16[384,256]{1,0:T(8,128)(2,1)S(1)}, bf16[384,256]{1,0:T(8,128)(2,1)S(1)}, u32[]{:S(2)}, u32[]{:S(2)}) collective-permute-start(bf16[384,256]{1,0:T(8,128)(2,1)S(1)} %get-tuple-element.59), channel_id=1, source_target_pairs={{0,1},{1,2},{2,3},{3,4},{4,5},{5,6},{6,7},{8,9},{9,10},{10,11},{11... | collective-permute-start | bytes 589832 | tf_op jit(solution)/shard_map/ppermute | solution.py:835
  11.5 0.0 collective-permute-done.2
  11.5 1.3 %collective-permute-start.3 = (bf16[400,256]{1,0:T(8,128)(2,1)S(1)}, bf16[400,256]{1,0:T(8,128)(2,1)S(1)}, u32[]{:S(2)}, u32[]{:S(2)}) collective-permute-start(bf16[400,256]{1,0:T(8,128)(2,1)S(1)} %fusion.after), channel_id=1, source_target_pairs={{0,8},{16,24},{1,9},{17,25},{2,10},{18,26},{3,11},{19,27},{4,12},{... | collective-permute-start | bytes 614408 | tf_op jit(solution)/shard_map/ppermute | solution.py:867
  12.8 1.1 %shard_map.116 = (f32[5,256,128]{2,1,0:T(8,128)}, f32[3,256,128]{2,1,0:T(8,128)}, f32[8,128]{1,0:T(8,128)S(1)}) custom-call(f32[5,256,128]{2,1,0:T(8,128)S(1)} %bitcast.16, f32[256,128]{1,0:T(8,128)S(1)} %bitcast.24, f32[3,256,128]{2,1,0:T(8,128)S(1)} %bitcast.19, f32[320,384]{1,0:T(8,128)S(1)} %get-tuple-element.48.state, ...), custom_call_target="tpu_custom_call" | custom-call | flops 100000000 | bytes 5472256 | tf_op jit(solution)/shard_map/pallas_call | solution.py:715
  13.9 0.5 %slice.3 = f32[1,1]{1,0:T(1,128)} slice(f32[8,128]{1,0:T(8,128)S(1)} %get-tuple-element.60), slice={[0:1], [0:1]} | slice | bytes 8 | tf_op jit(solution)/shard_map/slice | solution.py:874
  14.4 0.0 collective-permute-done.5
  14.4 0.7 %add_convert_fusion.2 = bf16[384,256]{1,0:T(8,128)(2,1)S(1)} fusion(f32[384,256]{1,0:T(8,128)S(1)} %get-tuple-element.58, bf16[384,256]{1,0:T(8,128)(2,1)S(1)} %collective-permute-done.5, f32[]{:T(128)} %bitcast.7), kind=kLoop, calls=%fused_computation.3 | loop fusion | flops 393216 | bytes 786436 | tf_op jit(solution)/shard_map/convert_element_type | solution.py:841
  15.1 1.3 %collective-permute-start.6 = (bf16[384,256]{1,0:T(8,128)(2,1)S(1)}, bf16[384,256]{1,0:T(8,128)(2,1)S(1)}, u32[]{:S(2)}, u32[]{:S(2)}) collective-permute-start(bf16[384,256]{1,0:T(8,128)(2,1)S(1)} %add_convert_fusion.2), channel_id=1, source_target_pairs={{0,16},{8,24},{1,17},{9,25},{2,18},{10,26},{3,19},{11,27},{4,20},{... | collective-permute-start | bytes 589832 | tf_op jit(solution)/shard_map/ppermute | solution.py:874
  16.4 7.3 %collective-permute-done.3.source_a = bf16[400,256]{1,0:T(8,128)(2,1)S(1)} collective-permute-done((bf16[400,256]{1,0:T(8,128)(2,1)S(1)}, bf16[400,256]{1,0:T(8,128)(2,1)S(1)}, u32[]{:S(2)}, u32[]{:S(2)}) %collective-permute-start.3) | collective-permute-done | bytes 204832 | tf_op jit(solution)/shard_map/ppermute | solution.py:867
  23.7 0.1 add_convert_fusion
  23.8 1.3 %collective-permute-start.4 = (bf16[400,256]{1,0:T(8,128)(2,1)S(1)}, bf16[400,256]{1,0:T(8,128)(2,1)S(1)}, u32[]{:S(2)}, u32[]{:S(2)}) collective-permute-start(bf16[400,256]{1,0:T(8,128)(2,1)S(1)} %add_convert_fusion), channel_id=1, source_target_pairs={{8,24},{9,25},{10,26},{11,27},{12,28},{13,29},{14,30},{15,31}} | collective-permute-start | bytes 614408 | tf_op jit(solution)/shard_map/ppermute | solution.py:875
  25.1 2.2 %collective-permute-done.6.source_b = bf16[384,256]{1,0:T(8,128)(2,1)S(1)} collective-permute-done((bf16[384,256]{1,0:T(8,128)(2,1)S(1)}, bf16[384,256]{1,0:T(8,128)(2,1)S(1)}, u32[]{:S(2)}, u32[]{:S(2)}) %collective-permute-start.6) | collective-permute-done | bytes 196640 | tf_op jit(solution)/shard_map/ppermute | solution.py:874
  27.3 0.1 add_convert_fusion.1
  27.4 1.3 %collective-permute-start.7 = (bf16[384,256]{1,0:T(8,128)(2,1)S(1)}, bf16[384,256]{1,0:T(8,128)(2,1)S(1)}, u32[]{:S(2)}, u32[]{:S(2)}) collective-permute-start(bf16[384,256]{1,0:T(8,128)(2,1)S(1)} %add_convert_fusion.1), channel_id=1, source_target_pairs={{16,24},{17,25},{18,26},{19,27},{20,28},{21,29},{22,30},{23,31}} | collective-permute-start | bytes 589832 | tf_op jit(solution)/shard_map/ppermute | solution.py:876
  28.7 2.5 %collective-permute-done.4.source_b = bf16[400,256]{1,0:T(8,128)(2,1)S(1)} collective-permute-done((bf16[400,256]{1,0:T(8,128)(2,1)S(1)}, bf16[400,256]{1,0:T(8,128)(2,1)S(1)}, u32[]{:S(2)}, u32[]{:S(2)}) %collective-permute-start.4) | collective-permute-done | bytes 204832 | tf_op jit(solution)/shard_map/ppermute | solution.py:875
  31.2 0.9 %shard_map.117 = (f32[512,128]{1,0:T(8,128)S(1)}, f32[8,256]{1,0:T(8,128)S(1)}, bf16[256,128]{1,0:T(8,128)(2,1)S(1)}, bf16[256,128]{1,0:T(8,128)(2,1)S(1)}) custom-call(f32[64,8,128]{2,1,0:T(8,128)S(1)} %get-tuple-element.54.base, f32[3,64,8,128]{3,2,1,0:T(8,128)S(1)} %get-tuple-element.55.grads, bf16[400,256]{1,0:T(8,128)(2,1)S(1)} %collective-permute-done.3.source_a, ...), custom_call_target="tpu_custom_call" | custom-call | flops 100000000 | bytes 1859584 | tf_op jit(solution)/shard_map/pallas_call | solution.py:715
  32.1 4.8 %collective-permute-start.8 = (bf16[256,128]{1,0:T(8,128)(2,1)S(1)}, bf16[256,128]{1,0:T(8,128)(2,1)S(1)}, u32[]{:S(2)}, u32[]{:S(2)}) collective-permute-start(bf16[256,128]{1,0:T(8,128)(2,1)S(1)} %get-tuple-element.63), channel_id=1, source_target_pairs={{25,26},{26,25},{27,28},{28,27},{29,30},{30,29}} | collective-permute-start | bytes 196616 | tf_op jit(solution)/shard_map/ppermute | solution.py:890
  36.9 1.9 %collective-permute-start.9 = (bf16[256,128]{1,0:T(8,128)(2,1)S(1)}, bf16[256,128]{1,0:T(8,128)(2,1)S(1)}, u32[]{:S(2)}, u32[]{:S(2)}) collective-permute-start(bf16[256,128]{1,0:T(8,128)(2,1)S(1)} %get-tuple-element.64), channel_id=1, source_target_pairs={{24,25},{25,24},{26,27},{27,26},{28,29},{29,28},{30,31},{31,30}} | collective-permute-start | bytes 196616 | tf_op jit(solution)/shard_map/ppermute | solution.py:891
  38.8 0.0 collective-permute-done.7.source_a
  38.9 2.0 %shard_map.118 = (f32[64,8,128]{2,1,0:T(8,128)S(1)}, bf16[6,256,256]{2,1,0:T(8,128)(2,1)S(1)}) custom-call(f32[512,128]{1,0:T(8,128)S(1)} %get-tuple-element.56.rows_of, s32[6,256]{1,0:T(8,128)S(1)} %get-tuple-element.66.neighbours, s32[6,256]{1,0:T(8,128)S(1)} %get-tuple-element.65.codes, f32[8,256]{1,0:T(8,128)S(1)} %get-tuple-element.57.scale, ...), custom_call_target="tpu_custom_call" | custom-call | flops 100000000 | bytes 1724416 | tf_op jit(solution)/shard_map/pallas_call | solution.py:715
  40.9 0.0 collective-permute-done.8.part_a
  40.9 0.0 collective-permute-done.9.part_b
  40.9 1.3 %shard_map.119 = f32[4,64,256]{2,1,0:T(8,128)} custom-call(f32[4,64,256]{2,1,0:T(8,128)S(1)} %bitcast.27, f32[64,8,128]{2,1,0:T(8,128)S(1)} %get-tuple-element.61.base, bf16[6,256,256]{2,1,0:T(8,128)(2,1)S(1)} %get-tuple-element.62.hot_beside, s32[6,256]{1,0:T(8,128)S(1)} %get-tuple-element.66.neighbours, s32[6,256]{1,0:T(8,128)S(1)} %get-tuple-element.65.codes, ...), custom_call_target="tpu_custom_call" | custom-call | flops 100000000 | bytes 1716224 | tf_op jit(solution)/shard_map/pallas_call | solution.py:715
  (4 shorter events, 0.1 us)
Async XLA Ops:
  0.6 5.7 %copy-start = (f32[1,5,256,128]{3,2,1,0:T(8,128)S(1)}, f32[1,5,256,128]{3,2,1,0:T(8,128)}, u32[]{:S(2)}) copy-start(f32[1,5,256,128]{3,2,1,0:T(8,128)} %param.9) | copy-start | bytes 1966084
  0.6 5.7 %copy-start.7 = (s32[1,6,256]{2,0,1:T(1,128)S(1)}, s32[1,6,256]{2,0,1:T(1,128)}, u32[]{:S(2)}) copy-start(s32[1,6,256]{2,0,1:T(1,128)} %param.17) | copy-start | bytes 18436
  0.7 5.7 %copy-start.8 = (s32[1,6,256]{2,0,1:T(1,128)S(1)}, s32[1,6,256]{2,0,1:T(1,128)}, u32[]{:S(2)}) copy-start(s32[1,6,256]{2,0,1:T(1,128)} %param.16) | copy-start | bytes 18436
  0.7 5.7 %copy-start.2 = (f32[1,256,128]{2,1,0:T(8,128)S(1)}, f32[1,256,128]{2,1,0:T(8,128)}, u32[]{:S(2)}) copy-start(f32[1,256,128]{2,1,0:T(8,128)} %param.11) | copy-start | bytes 393220
  2.4 6.2 %collective-permute-start = (bf16[304,128]{1,0:T(8,128)(2,1)}, bf16[304,128]{1,0:T(8,128)(2,1)S(1)}, u32[]{:S(2)}, u32[]{:S(2)}) collective-permute-start(bf16[304,128]{1,0:T(8,128)(2,1)} %get-tuple-element.34), channel_id=1, source_target_pairs={{1,2},{2,1},{3,4},{4,3},{5,6},{6,5},{9,10},{10,9},{11,12},{12,11},... | collective-permute-start | bytes 233480 | tf_op jit(solution)/shard_map/ppermute | solution.py:770
  6.2 0.7 %copy-start.5 = (s32[1,4,256]{2,1,0:T(4,128)S(1)}, s32[1,4,256]{2,1,0:T(4,128)}, u32[]{:S(2)}) copy-start(s32[1,4,256]{2,1,0:T(4,128)} %param.12) | copy-start | bytes 12292
  6.2 0.7 %copy-start.6 = (s32[1,256]{1,0:T(1,128)S(1)}, s32[1,256]{1,0:T(1,128)}, u32[]{:S(2)}) copy-start(s32[1,256]{1,0:T(1,128)} %target.1) | copy-start | bytes 3076
  6.2 2.4 %collective-permute-start.1 = (bf16[304,128]{1,0:T(8,128)(2,1)}, bf16[304,128]{1,0:T(8,128)(2,1)S(1)}, u32[]{:S(2)}, u32[]{:S(2)}) collective-permute-start(bf16[304,128]{1,0:T(8,128)(2,1)} %get-tuple-element.35), channel_id=1, source_target_pairs={{0,1},{1,0},{2,3},{3,2},{4,5},{5,4},{6,7},{7,6},{8,9},{9,8},{10,11... | collective-permute-start | bytes 233480 | tf_op jit(solution)/shard_map/ppermute | solution.py:771
  6.9 1.7 %copy-start.1 = (f32[1,3,256,128]{3,2,1,0:T(8,128)S(1)}, f32[1,3,256,128]{3,2,1,0:T(8,128)}, u32[]{:S(2)}) copy-start(f32[1,3,256,128]{3,2,1,0:T(8,128)} %param.10) | copy-start | bytes 1179652
  6.9 1.7 %copy-start.3 = (f32[1,4,64,256]{3,2,1,0:T(8,128)S(1)}, f32[1,4,64,256]{3,2,1,0:T(8,128)}, u32[]{:S(2)}) copy-start(f32[1,4,64,256]{3,2,1,0:T(8,128)} %param.15) | copy-start | bytes 786436
  6.9 1.7 %copy-start.4 = (f32[64,128]{1,0:T(8,128)S(1)}, f32[64,128]{1,0:T(8,128)}, u32[]{:S(2)}) copy-start(f32[64,128]{1,0:T(8,128)} %projector.3) | copy-start | bytes 98308
  10.0 1.4 %collective-permute-start.2 = (bf16[400,256]{1,0:T(8,128)(2,1)S(1)}, bf16[400,256]{1,0:T(8,128)(2,1)S(1)}, u32[]{:S(2)}, u32[]{:S(2)}) collective-permute-start(bf16[400,256]{1,0:T(8,128)(2,1)S(1)} %get-tuple-element.51), channel_id=1, source_target_pairs={{0,1},{1,2},{2,3},{3,4},{4,5},{5,6},{6,7},{8,9},{9,10},{10,11},{11... | collective-permute-start | bytes 614408 | tf_op jit(solution)/shard_map/ppermute | solution.py:835
  10.8 3.6 %collective-permute-start.5 = (bf16[384,256]{1,0:T(8,128)(2,1)S(1)}, bf16[384,256]{1,0:T(8,128)(2,1)S(1)}, u32[]{:S(2)}, u32[]{:S(2)}) collective-permute-start(bf16[384,256]{1,0:T(8,128)(2,1)S(1)} %get-tuple-element.59), channel_id=1, source_target_pairs={{0,1},{1,2},{2,3},{3,4},{4,5},{5,6},{6,7},{8,9},{9,10},{10,11},{11... | collective-permute-start | bytes 589832 | tf_op jit(solution)/shard_map/ppermute | solution.py:835
  11.5 12.2 %collective-permute-start.3 = (bf16[400,256]{1,0:T(8,128)(2,1)S(1)}, bf16[400,256]{1,0:T(8,128)(2,1)S(1)}, u32[]{:S(2)}, u32[]{:S(2)}) collective-permute-start(bf16[400,256]{1,0:T(8,128)(2,1)S(1)} %fusion.after), channel_id=1, source_target_pairs={{0,8},{16,24},{1,9},{17,25},{2,10},{18,26},{3,11},{19,27},{4,12},{... | collective-permute-start | bytes 614408 | tf_op jit(solution)/shard_map/ppermute | solution.py:867
  15.1 12.2 %collective-permute-start.6 = (bf16[384,256]{1,0:T(8,128)(2,1)S(1)}, bf16[384,256]{1,0:T(8,128)(2,1)S(1)}, u32[]{:S(2)}, u32[]{:S(2)}) collective-permute-start(bf16[384,256]{1,0:T(8,128)(2,1)S(1)} %add_convert_fusion.2), channel_id=1, source_target_pairs={{0,16},{8,24},{1,17},{9,25},{2,18},{10,26},{3,19},{11,27},{4,20},{... | collective-permute-start | bytes 589832 | tf_op jit(solution)/shard_map/ppermute | solution.py:874
  23.8 7.4 %collective-permute-start.4 = (bf16[400,256]{1,0:T(8,128)(2,1)S(1)}, bf16[400,256]{1,0:T(8,128)(2,1)S(1)}, u32[]{:S(2)}, u32[]{:S(2)}) collective-permute-start(bf16[400,256]{1,0:T(8,128)(2,1)S(1)} %add_convert_fusion), channel_id=1, source_target_pairs={{8,24},{9,25},{10,26},{11,27},{12,28},{13,29},{14,30},{15,31}} | collective-permute-start | bytes 614408 | tf_op jit(solution)/shard_map/ppermute | solution.py:875
  27.4 11.5 %collective-permute-start.7 = (bf16[384,256]{1,0:T(8,128)(2,1)S(1)}, bf16[384,256]{1,0:T(8,128)(2,1)S(1)}, u32[]{:S(2)}, u32[]{:S(2)}) collective-permute-start(bf16[384,256]{1,0:T(8,128)(2,1)S(1)} %add_convert_fusion.1), channel_id=1, source_target_pairs={{16,24},{17,25},{18,26},{19,27},{20,28},{21,29},{22,30},{23,31}} | collective-permute-start | bytes 589832 | tf_op jit(solution)/shard_map/ppermute | solution.py:876
  32.1 8.8 %collective-permute-start.8 = (bf16[256,128]{1,0:T(8,128)(2,1)S(1)}, bf16[256,128]{1,0:T(8,128)(2,1)S(1)}, u32[]{:S(2)}, u32[]{:S(2)}) collective-permute-start(bf16[256,128]{1,0:T(8,128)(2,1)S(1)} %get-tuple-element.63), channel_id=1, source_target_pairs={{25,26},{26,25},{27,28},{28,27},{29,30},{30,29}} | collective-permute-start | bytes 196616 | tf_op jit(solution)/shard_map/ppermute | solution.py:890
  36.9 3.9 %collective-permute-start.9 = (bf16[256,128]{1,0:T(8,128)(2,1)S(1)}, bf16[256,128]{1,0:T(8,128)(2,1)S(1)}, u32[]{:S(2)}, u32[]{:S(2)}) collective-permute-start(bf16[256,128]{1,0:T(8,128)(2,1)S(1)} %get-tuple-element.64), channel_id=1, source_target_pairs={{24,25},{25,24},{26,27},{27,26},{28,29},{29,28},{30,31},{31,30}} | collective-permute-start | bytes 196616 | tf_op jit(solution)/shard_map/ppermute | solution.py:891

commit v6 on v5

--- a/solution.py
+++ b/solution.py
@@ -16,12 +16,13 @@
 
 LANES = 128
 EDGE = 3 * HW
+NO_LINK = 64
 FIELD_ORDER = (1, 2, 3, 0, 4)
 ALL_FIELDS = ((0, 2), (2, 4), (4, 5))
 BASE = 32.0
 EXTRA = 16
 VMEM_LIMIT = 20 * 1024 * 1024
-PACK_LIMIT = 62 * 1024 * 1024
+PACK_LIMIT = 60 * 1024 * 1024
 
 F32 = jnp.float32
 BF16 = jnp.bfloat16
@@ -82,7 +83,10 @@
     return lax.rem(lax.axis_index("sfc"), 2) == 0
 
 
-def pack_kernel(flow, visc, links, sound, out_a, out_b, links_in, staged, sems, link_sem):
+def pack_kernel(
+    flow, visc, links, sound, neighbours, codes,
+    out_a, out_b, links_in, faces_in, staged, sems, link_sems,
+):
     is_flow, even = on_flow_row(), on_even_column()
     tiles = flow.shape[1]
     _, nodes, elements = sound.shape
@@ -90,7 +94,7 @@
 
     @pl.when(is_flow)
     def _():
-        fetch = pltpu.make_async_copy(links, links_in, link_sem)
+        fetch = pltpu.make_async_copy(links, links_in, link_sems.at[0])
         fetch.start()
         copies = []
         for side in range(2):
@@ -139,13 +143,27 @@
                         sems.at[side, v],
                     )
                 )
+        for at, ref in enumerate((neighbours, codes)):
+            copies.append(pltpu.make_async_copy(ref, faces_in.at[at], link_sems.at[at]))
         for copy in copies:
             copy.start()
         for copy in copies:
             copy.wait()
+        first = lax.axis_index("sfc") * elements
+        own = first + lax.broadcasted_iota(jnp.int32, (1, elements), 1)
+        for face in range(6):
+            link = faces_in[0, face]
+            offset = jnp.where(link < 0, NO_LINK, link - own).astype(F32)
+            for at, row in enumerate((offset, faces_in[1, face].astype(F32))):
+                line = 4 * nodes + 6 * at + face
+                low, high = row[:, :LANES], row[:, elements - LANES :]
+                staged[0, line : line + 1, :] = jnp.where(even, low, high)
+                staged[1, line : line + 1, :] = jnp.where(even, high, low)
+        used = 4 * nodes + 12
         for side, out in enumerate(outs):
-            out[: 4 * nodes, :] = staged[side, : 4 * nodes, :].astype(BF16)
-            out[4 * nodes :, :] = jnp.zeros((out.shape[0] - 4 * nodes, LANES), BF16)
+            staged[side, used:, :] = jnp.zeros((staged.shape[1] - used, LANES), F32)
+            out[: 6 * EDGE, :] = staged[side].astype(BF16)
+            out[6 * EDGE :, :] = jnp.zeros((out.shape[0] - 6 * EDGE, LANES), BF16)
 
 
 class FlowPlan:
@@ -340,7 +358,7 @@
 def first_kernel(
     flow, visc, mean, projector, part_a, part_b, sound, neighbours, codes,
     inner_state, inner_high, inner_low, lcol, inner_mats, hits,
-    own_one, next_one, mean_one, base, grads,
+    own_one, next_one, mean_one, base, grads, hot_two,
     edge_state, edge_high, edge_low, edge_mats, edge_visc,
     square, state0, high0, low0, zero, packed, pay, rows_of, facing, remote, rhs,
 ):
@@ -414,17 +432,52 @@
                     v, :, h * LANES : (h + 1) * LANES
                 ]
         a, b = part_a[:block, :].astype(F32), part_b[:block, :].astype(F32)
-        rows_of[halves * block : (halves + 1) * block, :] = jnp.where(even, a, b)
-        rows_of[(halves + 1) * block : (halves + 2) * block, :] = jnp.where(even, b, a)
+        before, after = jnp.where(even, a, b), jnp.where(even, b, a)
+        lane = lax.broadcasted_iota(jnp.int32, (1, LANES), 1)
+        beside = lane < LANES // 2
+        rows_of[halves * block : (halves + 1) * block, :] = jnp.where(beside, after, before)
+        rows_of[(halves + 1) * block : (halves + 2) * block, :] = jnp.zeros_like(before)
+        rows_of[(halves + 2) * block : (halves + 3) * block, :] = before
+        rows_of[(halves + 3) * block :, :] = after
+        a = part_a[block : block + EXTRA, :].astype(F32)
+        b = part_b[block : block + EXTRA, :].astype(F32)
+        given = jnp.where(beside, jnp.where(even, b, a), jnp.where(even, a, b)).astype(jnp.int32)
+        own_parts = [0, 1, halves + 2, halves + 3]
+        first = lax.axis_index("sfc") * elements
+        masks = []
         for face in range(6):
-            for part in range(halves + 2):
-                facing_rows(rows_of, part * block, nodes, face ^ 1, facing.at[face, part])
-            hot = hot_links(neighbours, face, elements, True, True)
-            remote_rows([facing[face, part] for part in range(halves + 2)], hot, remote, face)
-        derivatives(rows_of, nodes, grads, rhs)
-        add_faces(rows_of, nodes, remote, neighbours, codes, rhs, True)
-        for n in range(nodes):
-            base[n] = rows_of[pl.ds(n, 8, stride=nodes), :] + ACOUSTIC_STEP * rhs[n]
+            for at, part in enumerate(own_parts):
+                facing_rows(rows_of, part * block, nodes, face ^ 1, facing.at[face, at])
+            link, code = neighbours[face], codes[face]
+            offset, extra_code = given[face : face + 1, :], given[6 + face : 7 + face, :]
+            extra = jnp.where(beside, elements + lane, lane - LANES) + offset
+            near = jnp.concatenate([link - first, extra], 1)
+            valid = jnp.concatenate([link, jnp.where(offset >= NO_LINK, -1, 0)], 1) >= 0
+            place = jnp.where(
+                near < 0, elements + LANES + near, jnp.where(near < elements, near, near + LANES)
+            )
+            hot = hot_columns(jnp.where(valid, place, -1), elements + 2 * LANES)
+            remote_rows([facing[face, at] for at in range(4)], hot, remote, face)
+            near = link - first
+            place = jnp.where(near < 0, elements + LANES + near, near)
+            hot_two[face] = hot_columns(jnp.where(link < 0, -1, place), elements + LANES)
+            masks.append(
+                (
+                    face_masks(link[:, :LANES], link[:, LANES:], code[:, :LANES], code[:, LANES:]),
+                    face_masks(
+                        jnp.where(offset >= NO_LINK, -1, 0), jnp.full((1, LANES), -1, jnp.int32),
+                        extra_code, extra_code,
+                    ),
+                )
+            )
+        for group in range(2):
+            start = group * halves * block
+            derivatives(rows_of, start, nodes, grads.at[group], rhs)
+            add_faces(
+                rows_of, start, nodes, remote, group * halves * 64, [m[group] for m in masks], rhs
+            )
+            for n in range(nodes):
+                base[group, n] = node_of(rows_of, start, nodes, n) + ACOUSTIC_STEP * rhs[n]
 
 
 def second_block(plan, b, carried, visc, places, new_state, new_parts):
@@ -482,12 +535,12 @@
 def output_kernel(
     flow, visc, mean, state, mean_two,
     inner_state, inner_high, inner_low, inner_mats,
-    edge_state, edge_high, edge_low, edge_mats, edge_visc, after,
-    flow_out, mean_out, token, passive, zero,
+    edge_state, edge_high, edge_low, edge_mats, edge_visc, after, after_up, after_down, own_one,
+    flow_out, mean_out, own_one_out, passive, zero,
 ):
     plan = FlowPlan(flow.shape[1])
     is_flow = on_flow_row()
-    token[...] = jnp.zeros_like(token)
+    own_one_out[...] = own_one[...]
 
     @pl.when(jnp.logical_not(is_flow))
     def _():
@@ -524,36 +577,28 @@
             to[v * 16 : (v + 1) * 16, :] = rows_of[at : at + 16, :]
 
 
-def hot_links(neighbours, face, elements, own, beside):
-    link = neighbours[face : face + 1, :]
-    near = link - lax.axis_index("sfc") * elements
-    size = (elements if own else 0) + (2 * LANES if beside else 0)
-    start = elements if own else 0
-    place = jnp.where(near < 0, start + LANES + near, near - elements + start + LANES)
-    inside = (near >= 0) & (near < elements)
-    place = jnp.where(inside, near if own else -1, place if beside else -1)
-    place = jnp.where(link < 0, -1, place)
-    key = lax.broadcasted_iota(jnp.int32, (size, elements), 0)
+def hot_columns(place, size):
+    key = lax.broadcasted_iota(jnp.int32, (size, place.shape[1]), 0)
     return jnp.where(key == place, F32(1.0), F32(0.0)).astype(BF16)
 
 
+def node_of(rows_of, start, nodes, n):
+    return rows_of[pl.ds(start + n, 8, stride=nodes), :]
+
+
 def remote_rows(parts, hot, remote, face):
-    x = jnp.concatenate(parts, 1)
-    if x.dtype == BF16:
-        got = dot(x, hot)
-    else:
-        high, low = split_parts(x)
-        got = dot(jnp.concatenate([high, low], 0), hot)
-        got = got[:64] + got[64:]
+    high, low = split_parts(jnp.concatenate(parts, 1))
+    got = dot(jnp.concatenate([high, low], 0), hot)
+    got = got[:64] + got[64:]
     for h in range(got.shape[1] // LANES):
         remote[face, h * 64 : (h + 1) * 64, :] = got[:, h * LANES : (h + 1) * LANES]
 
 
-def derivatives(rows_of, nodes, grads_out, rhs):
+def derivatives(rows_of, start, nodes, grads_out, rhs):
     matrix = lobatto_matrix()
     line = lax.broadcasted_iota(jnp.int32, (8, LANES), 0)
     is_v = [line % 4 == v for v in range(4)]
-    node = [rows_of[pl.ds(n, 8, stride=nodes), :] for n in range(nodes)]
+    node = [node_of(rows_of, start, nodes, n) for n in range(nodes)]
     for n in range(nodes):
         i, j, k = n % 4, n // 4 % 4, n // 16
         lines = (
@@ -577,131 +622,157 @@
         rhs[n] = -coupled
 
 
-def add_faces(rows_of, nodes, remote, neighbours, codes, rhs, own):
+def face_masks(link_low, link_high, code_low, code_high):
     upper = lax.broadcasted_iota(jnp.int32, (8, LANES), 0) >= 4
+
+    def both(low, high):
+        return jnp.where(
+            upper, jnp.broadcast_to(high, (8, LANES)), jnp.broadcast_to(low, (8, LANES))
+        )
+
+    code = both(code_low, code_high)
+    return both(link_low, link_high) >= 0, [code == t for t in range(3)]
+
+
+def add_faces(rows_of, start, nodes, remote, remote_start, masks, rhs):
     for face in range(6):
-
-        def both(row):
-            return jnp.where(
-                upper,
-                jnp.broadcast_to(row[:, LANES:], (8, LANES)),
-                jnp.broadcast_to(row[:, :LANES], (8, LANES)),
-            )
-
-        code = both(codes[face : face + 1, :])
-        valid = both(neighbours[face : face + 1, :]) >= 0
-        is_turn = [code == t for t in range(4)]
-        planes = [remote[face, pl.ds(p, 8, stride=16), :] for p in range(16)]
+        valid, is_turn = masks[face]
+        planes = [remote[face, pl.ds(remote_start + p, 8, stride=16), :] for p in range(16)]
         for p, n in enumerate(face_nodes(face)):
-            jump = planes[turned_position(3, p)]
+            turned = planes[turned_position(3, p)]
             for t in range(3):
-                jump = jnp.where(is_turn[t], planes[turned_position(t, p)], jump)
-            if own:
-                jump = jnp.where(valid, jump - rows_of[pl.ds(n, 8, stride=nodes), :], 0.0)
+                turned = jnp.where(is_turn[t], planes[turned_position(t, p)], turned)
+            jump = jnp.where(valid, turned - node_of(rows_of, start, nodes, n), 0.0)
             rhs[n] = rhs[n] + PENALTY * jump
 
 
-def source_rows(total, nodes, lamb, mean):
+def source_rows(total, start, nodes, lamb, mean):
     block = 4 * nodes
     for h in range(total.shape[1] // LANES):
         columns = slice(h * LANES, (h + 1) * LANES)
-        lamb[h * block : h * block + nodes, :] = jnp.zeros((nodes, LANES), F32)
+        low = start + h * block
+        lamb[low : low + nodes, :] = jnp.zeros((nodes, LANES), F32)
         for d in range(3):
-            at = h * block + (1 + d) * nodes
+            at = low + (1 + d) * nodes
             lamb[at : at + nodes, :] = total[d * nodes : (d + 1) * nodes, columns]
             value = total[(3 + d) * nodes : (4 + d) * nodes, columns]
             for v in range(4):
-                at = h * block + v * nodes
-                mean[d, at : at + nodes, :] = value
-
-
-def source_terms(nodes, grads, lamb, mean, n):
-    total = lamb[pl.ds(n, 8, stride=nodes), :]
+                mean[d, low + v * nodes : low + (v + 1) * nodes, :] = value
+
+
+def source_terms(start, nodes, grads, lamb, mean, n):
+    total = node_of(lamb, start, nodes, n)
     for d in range(3):
-        total = total + mean[d, pl.ds(n, 8, stride=nodes), :] * grads[d, n]
+        total = total + mean[d, pl.ds(start + n, 8, stride=nodes), :] * grads[d, n]
     return total
 
 
+def border_kernel(sums, up, down):
+    nodes_rows = (sums.shape[0] - EXTRA) // (LANES // HE)
+    group = lax.broadcasted_iota(jnp.int32, (1, LANES), 1) // HE
+
+    @pl.when(on_flow_row())
+    def _():
+        for out, tile, shift in ((up, sums.shape[1] - LANES, HE), (down, 0, 0)):
+            columns = slice(tile, tile + LANES)
+            total = jnp.zeros((nodes_rows, LANES), F32)
+            for i in range(LANES // HE):
+                x = sums[i * nodes_rows : (i + 1) * nodes_rows, columns].astype(F32)
+                turn = (HE * i + shift) % LANES
+                x = pltpu.roll(x, turn, 1) if turn else x
+                total = jnp.where(group == i, x, total)
+            out[:nodes_rows, :] = total.astype(BF16)
+            x = sums[sums.shape[0] - EXTRA :, columns].astype(F32)
+            x = pltpu.roll(x, shift, 1) if shift else x
+            out[nodes_rows:, :] = jnp.where(group == 0, x, 0.0).astype(BF16)
+
+
+def border_sums(up, down):
+    lines = up.shape[0] - EXTRA
+    lane = lax.broadcasted_iota(jnp.int32, (1, LANES), 1)
+    parts = []
+    for i in range(LANES // HE + 1):
+        rows = slice(0, lines) if i < LANES // HE else slice(lines, lines + EXTRA)
+        at = HE * (i % (LANES // HE))
+        x = pltpu.roll(up[rows], (2 * LANES - HE - at) % LANES, 1)
+        y = pltpu.roll(down[rows], (LANES - at) % LANES, 1) if at else down[rows]
+        parts.append(jnp.where(lane >= LANES - HE, x, jnp.where(lane < HE, y, 0.0)))
+    return jnp.concatenate(parts, 0)
+
+
+def scaled_sums(total, nodes):
+    count = total[6 * nodes : 6 * nodes + 1] + BASE * total[6 * nodes + 1 : 6 * nodes + 2]
+    inverse = 1.0 / jnp.maximum(count, 1.0)
+    return total[: 6 * nodes] * inverse, inverse
+
+
 def sound_one_kernel(
-    base, grads, source_a, source_b, rows_of, scale_out, edge_a, edge_b, lamb, mean
+    base, grads, hot_two, neighbours, codes, source_a, source_b, up_a, up_b, down_a, down_b,
+    base_two, grads_two, scale_out, rows_of, facing, remote, rhs, lamb, mean,
 ):
-    is_flow, even = on_flow_row(), on_even_column()
+    nodes = base.shape[1]
+    elements = source_a.shape[1]
+    halves = elements // LANES
+    block = 4 * nodes
+
+    @pl.when(jnp.logical_not(on_flow_row()))
+    def _():
+        own, inverse = scaled_sums(source_a[...].astype(F32) + source_b[...].astype(F32), nodes)
+        scale_out[...] = jnp.broadcast_to(inverse, scale_out.shape)
+        source_rows(own, 0, nodes, lamb, mean)
+        extra = border_sums(
+            up_a[...].astype(F32) + up_b[...].astype(F32),
+            down_a[...].astype(F32) + down_b[...].astype(F32),
+        )
+        extra, _ = scaled_sums(extra, nodes)
+        none = (halves + 1) * block
+        lamb[none:, :] = jnp.zeros((block, LANES), F32)
+        for d in range(3):
+            mean[d, none:, :] = jnp.zeros((block, LANES), F32)
+        source_rows(extra, halves * block, nodes, lamb, mean)
+        for group in range(2):
+            start = group * halves * block
+            for n in range(nodes):
+                rows_of[pl.ds(start + n, 8, stride=nodes), :] = base[
+                    group, n
+                ] - ACOUSTIC_STEP * source_terms(start, nodes, grads.at[group], lamb, mean, n)
+        masks = []
+        for face in range(6):
+            for part in range(halves + 1):
+                facing_rows(rows_of, part * block, nodes, face ^ 1, facing.at[face, part])
+            remote_rows(
+                [facing[face, part] for part in range(halves + 1)], hot_two[face], remote, face
+            )
+            link, code = neighbours[face], codes[face]
+            masks.append(
+                face_masks(link[:, :LANES], link[:, LANES:], code[:, :LANES], code[:, LANES:])
+            )
+        derivatives(rows_of, 0, nodes, grads_two, rhs)
+        add_faces(rows_of, 0, nodes, remote, 0, masks, rhs)
+        for n in range(nodes):
+            base_two[n] = node_of(rows_of, 0, nodes, n) + ACOUSTIC_STEP * rhs[n]
+
+
+def sound_two_kernel(
+    sound, base, grads, scale, source_a, source_b, out, rows_of, lamb, mean
+):
     nodes = base.shape[0]
+    halves = sound.shape[2] // LANES
     block = 4 * nodes
+    is_flow = on_flow_row()
+
+    @pl.when(is_flow)
+    def _():
+        out[...] = sound[...]
 
     @pl.when(jnp.logical_not(is_flow))
     def _():
         total = source_a[...].astype(F32) + source_b[...].astype(F32)
-        count = total[6 * nodes : 6 * nodes + 1] + BASE * total[6 * nodes + 1 : 6 * nodes + 2]
-        inverse = 1.0 / jnp.maximum(count, 1.0)
-        scale_out[...] = jnp.broadcast_to(inverse, scale_out.shape)
-        source_rows(total[: 6 * nodes] * inverse, nodes, lamb, mean)
+        source_rows(total * scale[0:1, :], 0, nodes, lamb, mean)
         for n in range(nodes):
             rows_of[pl.ds(n, 8, stride=nodes), :] = base[n] - ACOUSTIC_STEP * source_terms(
-                nodes, grads, lamb, mean, n
-            )
-        off_a = pl.multiple_of(jnp.where(even, 0, block), 16)
-        off_b = pl.multiple_of(jnp.where(even, block, 0), 16)
-        edge_a[...] = rows_of[pl.ds(off_a, block), :].astype(BF16)
-        edge_b[...] = rows_of[pl.ds(off_b, block), :].astype(BF16)
-
-
-def sound_inner_kernel(
-    rows_of, neighbours, codes, scale, source_a, source_b,
-    base, hot_beside, facing, remote, rhs, grads, lamb, mean,
-):
-    nodes = base.shape[0]
-    elements = neighbours.shape[1]
-    halves = elements // LANES
-    block = 4 * nodes
-
-    @pl.when(jnp.logical_not(on_flow_row()))
-    def _():
-        for face in range(6):
-            for part in range(halves):
-                facing_rows(rows_of, part * block, nodes, face ^ 1, facing.at[face, part])
-            hot = hot_links(neighbours, face, elements, True, False)
-            remote_rows([facing[face, part] for part in range(halves)], hot, remote, face)
-            hot_beside[face] = hot_links(neighbours, face, elements, False, True)
-        derivatives(rows_of, nodes, grads, rhs)
-        add_faces(rows_of, nodes, remote, neighbours, codes, rhs, True)
-        total = source_a[...].astype(F32) + source_b[...].astype(F32)
-        source_rows(total * scale[0:1, :], nodes, lamb, mean)
-        for n in range(nodes):
-            base[n] = rows_of[pl.ds(n, 8, stride=nodes), :] + ACOUSTIC_STEP * (
-                rhs[n] - source_terms(nodes, grads, lamb, mean, n)
-            )
-
-
-def sound_two_kernel(
-    sound, base, hot_beside, neighbours, codes, part_a, part_b,
-    out, rows_of, facing, remote, rhs,
-):
-    is_flow, even = on_flow_row(), on_even_column()
-    nodes = base.shape[0]
-    elements = sound.shape[2]
-    halves = elements // LANES
-    block = 4 * nodes
-
-    @pl.when(is_flow)
-    def _():
-        out[...] = sound[...]
-
-    @pl.when(jnp.logical_not(is_flow))
-    def _():
-        a, b = part_a[...].astype(F32), part_b[...].astype(F32)
-        rows_of[:block, :] = jnp.where(even, a, b)
-        rows_of[block:, :] = jnp.where(even, b, a)
-        for face in range(6):
-            for part in range(2):
-                facing_rows(rows_of, part * block, nodes, face ^ 1, facing.at[face, part])
-            remote_rows(
-                [facing[face, part].astype(BF16) for part in range(2)], hot_beside[face], remote, face
-            )
-        rhs[...] = jnp.zeros_like(rhs)
-        add_faces(rows_of, nodes, remote, neighbours, codes, rhs, False)
-        for n in range(nodes):
-            rows_of[pl.ds(n, 8, stride=nodes), :] = base[n] + ACOUSTIC_STEP * rhs[n]
+                0, nodes, grads, lamb, mean, n
+            )
         for v in range(4):
             for h in range(halves):
                 out[v, :, h * LANES : (h + 1) * LANES] = rows_of[
@@ -709,7 +780,7 @@
                 ]
 
 
-def call(kernel, outs, scratch, operands, in_hbm=(), limit=VMEM_LIMIT):
+def call(kernel, outs, scratch, operands, flops=10**8, in_hbm=(), limit=VMEM_LIMIT):
     spaces = [pltpu.HBM if at in in_hbm else pltpu.VMEM for at in range(len(operands))]
     moved = sum(int(np.prod(x.shape)) * x.dtype.itemsize for x in (*operands, *outs))
     return pl.pallas_call(
@@ -719,7 +790,7 @@
         out_specs=tuple([pl.BlockSpec(memory_space=pltpu.VMEM)] * len(outs)),
         scratch_shapes=scratch,
         compiler_params=pltpu.CompilerParams(vmem_limit_bytes=limit),
-        cost_estimate=pl.CostEstimate(flops=10**8, bytes_accessed=moved, transcendentals=0),
+        cost_estimate=pl.CostEstimate(flops=flops, bytes_accessed=moved, transcendentals=0),
     )(*operands)
 
 
@@ -741,8 +812,9 @@
     visc = cell_eddy_viscosity[0]
     links = tile_links[0]
     sound = acoustic_state[0]
-    neighbours = element_face_neighbours[0]
-    codes = face_codes[0]
+    faces, span = element_face_neighbours.shape[1:]
+    neighbours = element_face_neighbours.reshape(faces, 1, span)
+    codes = face_codes.reshape(faces, 1, span)
     tiles = flow.shape[1]
     _, nodes, elements = sound.shape
     halves = elements // LANES
@@ -759,13 +831,15 @@
         [shape((edge_rows, LANES), BF16)] * 2,
         [
             vmem(links.shape, jnp.int32),
+            vmem((2, *neighbours.shape), jnp.int32),
             vmem((2, 6 * EDGE, LANES), F32),
             pltpu.SemaphoreType.DMA((2, 6)),
-            pltpu.SemaphoreType.DMA,
+            pltpu.SemaphoreType.DMA((2,)),
         ],
-        [flow, visc, links, sound],
-        in_hbm=(0, 1, 2, 3),
+        [flow, visc, links, sound, neighbours, codes],
+        in_hbm=(0, 1, 2, 3, 4, 5),
         limit=PACK_LIMIT,
+        flops=10**10,
     )
     part_a = lax.ppermute(pack_a, "sfc", pairs_a)
     part_b = lax.ppermute(pack_b, "sfc", pairs_b)
@@ -789,11 +863,10 @@
         [flow, visc, links, tile_target],
     )
     lines = 6 * nodes + EXTRA
-    by_node = shape((nodes, 8, LANES), F32)
-    by_node_3 = shape((3, nodes, 8, LANES), F32)
+    by_node = (nodes, 8, LANES)
     node_rows = vmem((nodes, 8, LANES), F32)
     (
-        own_one, next_one, mean_one, base, grads,
+        own_one, next_one, mean_one, base, grads, hot_two,
         edge_state, edge_high, edge_low, edge_mats, edge_visc,
     ) = call(
         first_kernel,
@@ -801,8 +874,9 @@
             shape((lines, elements), F32),
             shape((lines, elements), BF16),
             shape(mean.shape, F32),
-            by_node,
-            by_node_3,
+            shape((2, *by_node), F32),
+            shape((2, 3, *by_node), F32),
+            shape((6, elements + LANES, elements), BF16),
             shape((2 * rows, fields), F32),
             shape((2 * rows, fields), BF16),
             shape((2 * rows, fields), BF16),
@@ -817,9 +891,9 @@
             vmem((HW, fields), BF16),
             packed,
             vmem((lines, tiles), BF16),
-            vmem(((halves + 2) * block, LANES), F32),
-            vmem((6, halves + 2, 64, LANES), F32),
-            vmem((6, halves * 64, LANES), F32),
+            vmem(((halves + 4) * block, LANES), F32),
+            vmem((6, 4, 64, LANES), F32),
+            vmem((6, (halves + 2) * 64, LANES), F32),
             node_rows,
         ],
         [
@@ -862,56 +936,63 @@
         ],
         [visc, mean, mean_one, projector, *step_one, hits, *edges],
     )
+    def borders(sums, row):
+        lines = 6 * nodes // (LANES // HE) + EXTRA
+        up, down = call(border_kernel, [shape((lines, LANES), BF16)] * 2, [], [sums])
+        last = (groups - 1) * count
+        return [
+            lax.ppermute(
+                x, ("grp", "sfc"),
+                [(row * count + i, last + i + step) for i in range(count) if 0 <= i + step < count],
+            )
+            for x, step in ((up, 1), (down, -1))
+        ]
+
     got_two = climb(next_two)
     sum_one = combined(own_one, got_one)
     x_one = lax.ppermute(sum_one, "grp", [(0, 1), (2, 3)])
-    flow_out, mean_out, token = call(
+    up_a, down_a = borders(sum_one, 2)
+    sum_two = combined(own_two, got_two)
+    y_two = lax.ppermute(sum_two, "grp", [(0, 2), (1, 3)])
+    flow_out, mean_out, own_one = call(
         output_kernel,
-        [shape(flow.shape, F32), shape(mean.shape, F32), shape((8, LANES), F32)],
+        [shape(flow.shape, F32), shape(mean.shape, F32), shape(own_one.shape, F32)],
         [vmem((band, fields), F32), vmem((HW, fields), BF16)],
-        [flow, visc, mean, state_two, mean_two, *step_one, *edges, sum_one],
-    )
-    y_two = lax.ppermute(combined(own_two, got_two, token[0, 0]), "grp", [(0, 2), (1, 3)])
-    y_one = lax.ppermute(combined(own_one, got_one, x_one), "grp", [(1, 3)])
+        [flow, visc, mean, state_two, mean_two, *step_one, *edges, sum_two, up_a, down_a, own_one],
+    )
+    sum_one = combined(own_one, got_one, x_one)
+    y_one = lax.ppermute(sum_one, "grp", [(1, 3)])
+    up_b, down_b = borders(sum_one, 1)
     x_two = lax.ppermute(combined(own_two, got_two, y_two), "grp", [(2, 3)])
 
-    sound_rows, scale, edge_a, edge_b = call(
+    held = vmem(((halves + 2) * block, LANES), F32)
+    held_3 = vmem((3, (halves + 2) * block, LANES), F32)
+    base, grads, scale = call(
         sound_one_kernel,
+        [shape(by_node, F32), shape((3, *by_node), F32), shape((8, elements), F32)],
         [
-            shape((halves * block, LANES), F32),
-            shape((8, elements), F32),
-            shape((block, LANES), BF16),
-            shape((block, LANES), BF16),
-        ],
-        [vmem((halves * block, LANES), F32), vmem((3, halves * block, LANES), F32)],
-        [base, grads, x_one, y_one],
-    )
-    last = (groups - 1) * count
-    part_a = lax.ppermute(edge_a, ("grp", "sfc"), [(last + i, last + j) for i, j in pairs_a])
-    part_b = lax.ppermute(edge_b, ("grp", "sfc"), [(last + i, last + j) for i, j in pairs_b])
-    base, hot_beside = call(
-        sound_inner_kernel,
-        [by_node, shape((6, 2 * LANES, elements), BF16)],
-        [
-            vmem((6, halves, 64, LANES), F32),
+            held,
+            vmem((6, halves + 1, 64, LANES), F32),
             vmem((6, halves * 64, LANES), F32),
             node_rows,
-            vmem((3, nodes, 8, LANES), F32),
-            vmem((halves * block, LANES), F32),
-            vmem((3, halves * block, LANES), F32),
+            held,
+            held_3,
         ],
-        [sound_rows, neighbours, codes, scale, x_two, y_two],
+        [
+            base, grads, hot_two, neighbours, codes, x_one, y_one,
+            up_a, up_b, down_a, down_b,
+        ],
+        flops=10**10,
     )
     (sound_out,) = call(
         sound_two_kernel,
         [shape(sound.shape, F32)],
         [
             vmem((halves * block, LANES), F32),
-            vmem((6, 2, 64, LANES), F32),
-            vmem((6, halves * 64, LANES), F32),
-            node_rows,
+            vmem((halves * block, LANES), F32),
+            vmem((3, halves * block, LANES), F32),
         ],
-        [sound, base, hot_beside, neighbours, codes, part_a, part_b],
+        [sound, base, grads, scale, x_two, y_two],
     )
     return flow_out[None], mean_out[None], sound_out[None]
 

time: 42.7 us -> 41 us (0.960)
  starting transfers between devices: 17.1 us -> 15.5 us
  Pallas kernels: 8.39 us -> 9.8 us
  local copies, waits for them, and re-layouts: 1.09 us -> 0.04 us
  other arithmetic: 0.89 us -> 0.23 us
    ppermute x1, waiting for transfers between devices: 7.3 us -> 0.01 us  [body(): x_one = lax.ppermute(sum_one, 'grp', [(0, 1), (2, 3)])]
    ppermute x4 -> x6, waiting for transfers between devices: 4.72 us -> 11.5 us  [the longest x4 11.5 us: borders(): lax.ppermute(x, ('grp', 'sfc'), [(row * count + i, last + i + step) for i...]
    ppermute x4 -> x6, starting transfers between devices: 9.35 us -> 7.75 us  [the longest x4 5.17 us: borders(): lax.ppermute(x, ('grp', 'sfc'), [(row * count + i, last + i + step) for i...]
    pallas_call x8 -> x9, Pallas kernels: 8.39 us -> 9.8 us  [call(): pl.pallas_call(kernel, out_shape=tuple(outs), in_specs=[pl.BlockSpec(memo...]
    convert_element_type x4, other arithmetic: 0.89 us -> 0.23 us  [combined(): return total.astype(BF16)]
    ppermute x1, waiting for transfers between devices: 1.71 us -> 2.29 us  [body(): part_a = lax.ppermute(pack_a, 'sfc', pairs_a)]
    unnamed x19 -> x18, local copies, waits for them, and re-layouts: 0.58 us -> 0.04 us
    slice x1 -> x0, local copies, waits for them, and re-layouts: 0.51 us -> none  [body(): token[0, 0]]
  transfers between devices with their start and end apart: 10 -> 12, of which waited for: 4 -> 4; matrix products, arithmetic and copies ran while one was open for 3% -> 1% of each run, Pallas kernels for 10% -> 10%
where the time goes in v6:
time: 41 us; the launch traced here: 40.7 us
  starting transfers between devices  15.5 us (38%)
  waiting for transfers between devices  14.1 us (34%)
  Pallas kernels  9.8 us (24%)
  between operations  0.96 us (2%)
    ppermute x4, waiting for transfers between devices, borders(): lax.ppermute(x, ('grp', 'sfc'), [(row * count + i, last + i + step) for i...  11.5 us
    pallas_call x9, Pallas kernels, call(): pl.pallas_call(kernel, out_shape=tuple(outs), in_specs=[pl.BlockSpec(memo...  9.8 us
    ppermute x4, starting transfers between devices, borders(): lax.ppermute(x, ('grp', 'sfc'), [(row * count + i, last + i + step) for i...  5.17 us
    ppermute x1, starting transfers between devices, body(): part_a = lax.ppermute(pack_a, 'sfc', pairs_a)  3.76 us
    ppermute x1, waiting for transfers between devices, body(): part_a = lax.ppermute(pack_a, 'sfc', pairs_a)  2.29 us
    ppermute x2, starting transfers between devices, climb(): return lax.ppermute(x, ('grp', 'sfc'), chosen)  1.35 us
    ppermute x1, starting transfers between devices, body(): x_one = lax.ppermute(sum_one, 'grp', [(0, 1), (2, 3)])  1.29 us
    ppermute x1, starting transfers between devices, body(): y_two = lax.ppermute(sum_two, 'grp', [(0, 2), (1, 3)])  1.29 us
  transfers between devices with their start and end apart: 12, of which 4 were waited for; matrix products, arithmetic and copies ran while one was open for 1% of the time, Pallas kernels for 10%

profile of v6, /device:TPU:15, one launch (start us, length us, event | category | flops | bytes accessed | tf_op | source)
XLA Modules:
  0.0 40.7 jit_solution(12402786674506596979)
XLA Ops:
  0.6 0.0 copy-start
  0.6 0.0 copy-start.2
  0.7 0.0 copy-start.7
  0.7 0.0 copy-start.8
  0.7 0.0 copy-start.1
  0.7 0.0 copy-start.3
  0.7 0.0 copy-start.4
  0.7 0.0 copy-start.5
  0.7 0.0 copy-start.6
  0.7 1.8 %shard_map.112 = (bf16[304,128]{1,0:T(8,128)(2,1)}, bf16[304,128]{1,0:T(8,128)(2,1)}) custom-call(f32[5,256,128]{2,1,0:T(8,128)} %bitcast.10, f32[256,128]{1,0:T(8,128)} %bitcast.17, s32[4,256]{1,0:T(4,128)} %bitcast.31, f32[4,64,256]{2,1,0:T(8,128)} %bitcast.22, s32[6,1,256]{2,1,0:T(1,128)} %bitcast.25, s32[6,1,256]{2,1,0:T(1,128)} %bitcast.28), custom_call_target="tpu_custom_call" | custom-call | flops 10000000000 | bytes 1220608 | tf_op jit(solution)/shard_map/pallas_call | solution.py:786
  2.5 3.8 %collective-permute-start = (bf16[304,128]{1,0:T(8,128)(2,1)}, bf16[304,128]{1,0:T(8,128)(2,1)S(1)}, u32[]{:S(2)}, u32[]{:S(2)}) collective-permute-start(bf16[304,128]{1,0:T(8,128)(2,1)} %get-tuple-element.36), channel_id=1, source_target_pairs={{1,2},{2,1},{3,4},{4,3},{5,6},{6,5},{9,10},{10,9},{11,12},{12,11},... | collective-permute-start | bytes 233480 | tf_op jit(solution)/shard_map/ppermute | solution.py:844
  6.3 0.1 collective-permute-start.1
  6.4 0.0 copy-done
  6.4 0.0 copy-done.2
  6.4 0.0 copy-done.7
  6.4 0.0 copy-done.8
  6.4 2.3 %collective-permute-done.part_a = bf16[304,128]{1,0:T(8,128)(2,1)S(1)} collective-permute-done((bf16[304,128]{1,0:T(8,128)(2,1)}, bf16[304,128]{1,0:T(8,128)(2,1)S(1)}, u32[]{:S(2)}, u32[]{:S(2)}) %collective-permute-start) | collective-permute-done | bytes 77856 | tf_op jit(solution)/shard_map/ppermute | solution.py:844
  8.7 0.0 collective-permute-done.1.part_b
  8.7 0.0 copy-done.1
  8.7 0.0 copy-done.3
  8.8 2.5 %shard_map.114 = (f32[400,256]{1,0:T(8,128)S(1)}, bf16[400,256]{1,0:T(8,128)(2,1)S(1)}, f32[3,256,128]{2,1,0:T(8,128)S(1)}, f32[2,64,8,128]{3,2,1,0:T(8,128)S(1)...) custom-call(f32[5,256,128]{2,1,0:T(8,128)S(1)} %bitcast.12, ...), custom_call_target="tpu_custom_call" | custom-call | flops 100000000 | bytes 8470528 | tf_op jit(solution)/shard_map/pallas_call | solution.py:786
  11.3 0.7 %collective-permute-start.3 = (bf16[400,256]{1,0:T(8,128)(2,1)S(1)}, bf16[400,256]{1,0:T(8,128)(2,1)S(1)}, u32[]{:S(2)}, u32[]{:S(2)}) collective-permute-start(bf16[400,256]{1,0:T(8,128)(2,1)S(1)} %get-tuple-element.55), channel_id=1, source_target_pairs={{0,1},{1,2},{2,3},{3,4},{4,5},{5,6},{6,7},{8,9},{9,10},{10,11},{11... | collective-permute-start | bytes 614408 | tf_op jit(solution)/shard_map/ppermute | solution.py:909
  12.0 0.1 shard_map.115
  12.0 0.7 %collective-permute-start.2 = (bf16[384,256]{1,0:T(8,128)(2,1)S(1)}, bf16[384,256]{1,0:T(8,128)(2,1)S(1)}, u32[]{:S(2)}, u32[]{:S(2)}) collective-permute-start(bf16[384,256]{1,0:T(8,128)(2,1)S(1)} %get-tuple-element.53), channel_id=1, source_target_pairs={{0,1},{1,2},{2,3},{3,4},{4,5},{5,6},{6,7},{8,9},{9,10},{10,11},{11... | collective-permute-start | bytes 589832 | tf_op jit(solution)/shard_map/ppermute | solution.py:909
  12.7 0.0 collective-permute-done.3
  12.7 0.1 fusion.sums
  12.8 1.3 %collective-permute-start.6 = (bf16[400,256]{1,0:T(8,128)(2,1)S(1)}, bf16[400,256]{1,0:T(8,128)(2,1)S(1)}, u32[]{:S(2)}, u32[]{:S(2)}) collective-permute-start(bf16[400,256]{1,0:T(8,128)(2,1)S(1)} %fusion.sums), channel_id=1, source_target_pairs={{0,8},{16,24},{1,9},{17,25},{2,10},{18,26},{3,11},{19,27},{4,12},{... | collective-permute-start | bytes 614408 | tf_op jit(solution)/shard_map/ppermute | solution.py:953
  14.1 1.3 %collective-permute-start.4 = (bf16[64,128]{1,0:T(8,128)(2,1)S(1)}, bf16[64,128]{1,0:T(8,128)(2,1)S(1)}, u32[]{:S(2)}, u32[]{:S(2)}) collective-permute-start(bf16[64,128]{1,0:T(8,128)(2,1)S(1)} %get-tuple-element.56), channel_id=1, source_target_pairs={{16,25},{17,26},{18,27},{19,28},{20,29},{21,30},{22,31}} | collective-permute-start | bytes 49160 | tf_op jit(solution)/shard_map/ppermute | solution.py:944
  15.4 1.3 %collective-permute-start.5 = (bf16[64,128]{1,0:T(8,128)(2,1)S(1)}, bf16[64,128]{1,0:T(8,128)(2,1)S(1)}, u32[]{:S(2)}, u32[]{:S(2)}) collective-permute-start(bf16[64,128]{1,0:T(8,128)(2,1)S(1)} %get-tuple-element.57), channel_id=1, source_target_pairs={{17,24},{18,25},{19,26},{20,27},{21,28},{22,29},{23,30}} | collective-permute-start | bytes 49160 | tf_op jit(solution)/shard_map/ppermute | solution.py:944
  16.7 0.0 collective-permute-done.2
  16.8 1.3 %collective-permute-start.10 = (bf16[384,256]{1,0:T(8,128)(2,1)S(1)}, bf16[384,256]{1,0:T(8,128)(2,1)S(1)}, u32[]{:S(2)}, u32[]{:S(2)}) collective-permute-start(bf16[384,256]{1,0:T(8,128)(2,1)S(1)} %fusion.3.after), channel_id=1, source_target_pairs={{0,16},{8,24},{1,17},{9,25},{2,18},{10,26},{3,19},{11,27},{4,20},{... | collective-permute-start | bytes 589832 | tf_op jit(solution)/shard_map/ppermute | solution.py:956
  18.1 7.1 %collective-permute-done.4.after_up.up_a = bf16[64,128]{1,0:T(8,128)(2,1)S(1)} collective-permute-done((bf16[64,128]{1,0:T(8,128)(2,1)S(1)}, bf16[64,128]{1,0:T(8,128)(2,1)S(1)}, u32[]{:S(2)}, u32[]{:S(2)}) %collective-permute-start.4) | collective-permute-done | bytes 16416 | tf_op jit(solution)/shard_map/ppermute | solution.py:944
  25.2 0.0 collective-permute-done.5.after_down.down_a
  25.2 1.1 %shard_map.117 = (f32[5,256,128]{2,1,0:T(8,128)}, f32[3,256,128]{2,1,0:T(8,128)}, f32[400,256]{1,0:T(8,128)S(1)}) custom-call(f32[5,256,128]{2,1,0:T(8,128)S(1)} %bitcast.13, f32[256,128]{1,0:T(8,128)S(1)} %bitcast.21, f32[3,256,128]{2,1,0:T(8,128)S(1)} %bitcast.16, f32[320,384]{1,0:T(8,128)S(1)} %get-tuple-element.50.state, ...), custom_call_target="tpu_custom_call" | custom-call | flops 100000000 | bytes 6311936 | tf_op jit(solution)/shard_map/pallas_call | solution.py:786
  26.2 0.0 collective-permute-done.6.source_a
  26.2 0.1 fusion.2.sums
  26.3 1.3 %collective-permute-start.7 = (bf16[400,256]{1,0:T(8,128)(2,1)S(1)}, bf16[400,256]{1,0:T(8,128)(2,1)S(1)}, u32[]{:S(2)}, u32[]{:S(2)}) collective-permute-start(bf16[400,256]{1,0:T(8,128)(2,1)S(1)} %fusion.2.sums), channel_id=1, source_target_pairs={{8,24},{9,25},{10,26},{11,27},{12,28},{13,29},{14,30},{15,31}} | collective-permute-start | bytes 614408 | tf_op jit(solution)/shard_map/ppermute | solution.py:964
  27.6 1.3 %collective-permute-start.8 = (bf16[64,128]{1,0:T(8,128)(2,1)S(1)}, bf16[64,128]{1,0:T(8,128)(2,1)S(1)}, u32[]{:S(2)}, u32[]{:S(2)}) collective-permute-start(bf16[64,128]{1,0:T(8,128)(2,1)S(1)} %get-tuple-element.64), channel_id=1, source_target_pairs={{8,25},{9,26},{10,27},{11,28},{12,29},{13,30},{14,31}} | collective-permute-start | bytes 49160 | tf_op jit(solution)/shard_map/ppermute | solution.py:944
  28.9 1.3 %collective-permute-start.9 = (bf16[64,128]{1,0:T(8,128)(2,1)S(1)}, bf16[64,128]{1,0:T(8,128)(2,1)S(1)}, u32[]{:S(2)}, u32[]{:S(2)}) collective-permute-start(bf16[64,128]{1,0:T(8,128)(2,1)S(1)} %get-tuple-element.65), channel_id=1, source_target_pairs={{9,24},{10,25},{11,26},{12,27},{13,28},{14,29},{15,30}} | collective-permute-start | bytes 49160 | tf_op jit(solution)/shard_map/ppermute | solution.py:944
  30.2 0.0 collective-permute-done.10.source_b
  30.2 0.1 add_convert_fusion
  30.3 1.3 %collective-permute-start.11 = (bf16[384,256]{1,0:T(8,128)(2,1)S(1)}, bf16[384,256]{1,0:T(8,128)(2,1)S(1)}, u32[]{:S(2)}, u32[]{:S(2)}) collective-permute-start(bf16[384,256]{1,0:T(8,128)(2,1)S(1)} %add_convert_fusion), channel_id=1, source_target_pairs={{16,24},{17,25},{18,26},{19,27},{20,28},{21,29},{22,30},{23,31}} | collective-permute-start | bytes 589832 | tf_op jit(solution)/shard_map/ppermute | solution.py:966
  31.6 4.4 %collective-permute-done.8.up_b = bf16[64,128]{1,0:T(8,128)(2,1)S(1)} collective-permute-done((bf16[64,128]{1,0:T(8,128)(2,1)S(1)}, bf16[64,128]{1,0:T(8,128)(2,1)S(1)}, u32[]{:S(2)}, u32[]{:S(2)}) %collective-permute-start.8) | collective-permute-done | bytes 16416 | tf_op jit(solution)/shard_map/ppermute | solution.py:944
  36.0 0.0 collective-permute-done.9.down_b
  36.0 0.0 collective-permute-done.7.source_b
  36.0 2.7 %shard_map.119 = (f32[64,8,128]{2,1,0:T(8,128)S(1)}, f32[3,64,8,128]{3,2,1,0:T(8,128)S(1)}, f32[8,256]{1,0:T(8,128)S(1)}) custom-call(f32[2,64,8,128]{3,2,1,0:T(8,128)S(1)} %get-tuple-element.60.base, f32[2,3,64,8,128]{4,3,2,1,0:T(8,128)S(1)} %get-tuple-element.61.grads, bf16[6,384,256]{2,1,0:T(8,128)(2,1)S(1)} %get-tuple-element.62.hot_two, ...), custom_call_target="tpu_custom_call" | custom-call | flops 10000000000 | bytes 4820992 | tf_op jit(solution)/shard_map/pallas_call | solution.py:786
  38.8 0.3 collective-permute-done.11.source_a
  39.1 1.6 %shard_map.120 = f32[4,64,256]{2,1,0:T(8,128)} custom-call(f32[4,64,256]{2,1,0:T(8,128)S(1)} %bitcast.24, f32[64,8,128]{2,1,0:T(8,128)S(1)} %get-tuple-element.66.base, f32[3,64,8,128]{3,2,1,0:T(8,128)S(1)} %get-tuple-element.67.grads, f32[8,256]{1,0:T(8,128)S(1)} %get-tuple-element.68.scale, bf16[384,256]{1,0:T(8,128)(2,1)S(1)} %collective-permute-done.11.source_a, ...), custom_call_target="tpu_custom_call" | custom-call | flops 100000000 | bytes 1974272 | tf_op jit(solution)/shard_map/pallas_call | solution.py:786
  (7 shorter events, 0.1 us)
Async XLA Ops:
  0.6 5.7 %copy-start = (f32[1,5,256,128]{3,2,1,0:T(8,128)S(1)}, f32[1,5,256,128]{3,2,1,0:T(8,128)}, u32[]{:S(2)}) copy-start(f32[1,5,256,128]{3,2,1,0:T(8,128)} %param.9) | copy-start | bytes 1966084
  0.6 5.7 %copy-start.2 = (f32[1,256,128]{2,1,0:T(8,128)S(1)}, f32[1,256,128]{2,1,0:T(8,128)}, u32[]{:S(2)}) copy-start(f32[1,256,128]{2,1,0:T(8,128)} %param.11) | copy-start | bytes 393220
  0.7 5.7 %copy-start.7 = (s32[1,4,256]{2,1,0:T(4,128)S(1)}, s32[1,4,256]{2,1,0:T(4,128)}, u32[]{:S(2)}) copy-start(s32[1,4,256]{2,1,0:T(4,128)} %param.12) | copy-start | bytes 12292
  0.7 5.7 %copy-start.8 = (s32[1,256]{1,0:T(1,128)S(1)}, s32[1,256]{1,0:T(1,128)}, u32[]{:S(2)}) copy-start(s32[1,256]{1,0:T(1,128)} %target.1) | copy-start | bytes 3076
  0.7 8.1 %copy-start.1 = (f32[1,3,256,128]{3,2,1,0:T(8,128)S(1)}, f32[1,3,256,128]{3,2,1,0:T(8,128)}, u32[]{:S(2)}) copy-start(f32[1,3,256,128]{3,2,1,0:T(8,128)} %param.10) | copy-start | bytes 1179652
  0.7 8.1 %copy-start.3 = (f32[1,4,64,256]{3,2,1,0:T(8,128)S(1)}, f32[1,4,64,256]{3,2,1,0:T(8,128)}, u32[]{:S(2)}) copy-start(f32[1,4,64,256]{3,2,1,0:T(8,128)} %param.15) | copy-start | bytes 786436
  0.7 8.1 %copy-start.4 = (f32[64,128]{1,0:T(8,128)S(1)}, f32[64,128]{1,0:T(8,128)}, u32[]{:S(2)}) copy-start(f32[64,128]{1,0:T(8,128)} %projector.3) | copy-start | bytes 98308
  0.7 8.1 %copy-start.5 = (s32[1,6,256]{2,0,1:T(1,128)S(1)}, s32[1,6,256]{2,0,1:T(1,128)}, u32[]{:S(2)}) copy-start(s32[1,6,256]{2,0,1:T(1,128)} %param.16) | copy-start | bytes 18436
  0.7 8.1 %copy-start.6 = (s32[1,6,256]{2,0,1:T(1,128)S(1)}, s32[1,6,256]{2,0,1:T(1,128)}, u32[]{:S(2)}) copy-start(s32[1,6,256]{2,0,1:T(1,128)} %param.17) | copy-start | bytes 18436
  2.5 6.2 %collective-permute-start = (bf16[304,128]{1,0:T(8,128)(2,1)}, bf16[304,128]{1,0:T(8,128)(2,1)S(1)}, u32[]{:S(2)}, u32[]{:S(2)}) collective-permute-start(bf16[304,128]{1,0:T(8,128)(2,1)} %get-tuple-element.36), channel_id=1, source_target_pairs={{1,2},{2,1},{3,4},{4,3},{5,6},{6,5},{9,10},{10,9},{11,12},{12,11},... | collective-permute-start | bytes 233480 | tf_op jit(solution)/shard_map/ppermute | solution.py:844
  6.3 2.4 %collective-permute-start.1 = (bf16[304,128]{1,0:T(8,128)(2,1)}, bf16[304,128]{1,0:T(8,128)(2,1)S(1)}, u32[]{:S(2)}, u32[]{:S(2)}) collective-permute-start(bf16[304,128]{1,0:T(8,128)(2,1)} %get-tuple-element.37), channel_id=1, source_target_pairs={{0,1},{1,0},{2,3},{3,2},{4,5},{5,4},{6,7},{7,6},{8,9},{9,8},{10,11... | collective-permute-start | bytes 233480 | tf_op jit(solution)/shard_map/ppermute | solution.py:845
  11.3 1.4 %collective-permute-start.3 = (bf16[400,256]{1,0:T(8,128)(2,1)S(1)}, bf16[400,256]{1,0:T(8,128)(2,1)S(1)}, u32[]{:S(2)}, u32[]{:S(2)}) collective-permute-start(bf16[400,256]{1,0:T(8,128)(2,1)S(1)} %get-tuple-element.55), channel_id=1, source_target_pairs={{0,1},{1,2},{2,3},{3,4},{4,5},{5,6},{6,7},{8,9},{9,10},{10,11},{11... | collective-permute-start | bytes 614408 | tf_op jit(solution)/shard_map/ppermute | solution.py:909
  12.0 4.7 %collective-permute-start.2 = (bf16[384,256]{1,0:T(8,128)(2,1)S(1)}, bf16[384,256]{1,0:T(8,128)(2,1)S(1)}, u32[]{:S(2)}, u32[]{:S(2)}) collective-permute-start(bf16[384,256]{1,0:T(8,128)(2,1)S(1)} %get-tuple-element.53), channel_id=1, source_target_pairs={{0,1},{1,2},{2,3},{3,4},{4,5},{5,6},{6,7},{8,9},{9,10},{10,11},{11... | collective-permute-start | bytes 589832 | tf_op jit(solution)/shard_map/ppermute | solution.py:909
  12.8 13.5 %collective-permute-start.6 = (bf16[400,256]{1,0:T(8,128)(2,1)S(1)}, bf16[400,256]{1,0:T(8,128)(2,1)S(1)}, u32[]{:S(2)}, u32[]{:S(2)}) collective-permute-start(bf16[400,256]{1,0:T(8,128)(2,1)S(1)} %fusion.sums), channel_id=1, source_target_pairs={{0,8},{16,24},{1,9},{17,25},{2,10},{18,26},{3,11},{19,27},{4,12},{... | collective-permute-start | bytes 614408 | tf_op jit(solution)/shard_map/ppermute | solution.py:953
  14.1 11.1 %collective-permute-start.4 = (bf16[64,128]{1,0:T(8,128)(2,1)S(1)}, bf16[64,128]{1,0:T(8,128)(2,1)S(1)}, u32[]{:S(2)}, u32[]{:S(2)}) collective-permute-start(bf16[64,128]{1,0:T(8,128)(2,1)S(1)} %get-tuple-element.56), channel_id=1, source_target_pairs={{16,25},{17,26},{18,27},{19,28},{20,29},{21,30},{22,31}} | collective-permute-start | bytes 49160 | tf_op jit(solution)/shard_map/ppermute | solution.py:944
  15.4 9.8 %collective-permute-start.5 = (bf16[64,128]{1,0:T(8,128)(2,1)S(1)}, bf16[64,128]{1,0:T(8,128)(2,1)S(1)}, u32[]{:S(2)}, u32[]{:S(2)}) collective-permute-start(bf16[64,128]{1,0:T(8,128)(2,1)S(1)} %get-tuple-element.57), channel_id=1, source_target_pairs={{17,24},{18,25},{19,26},{20,27},{21,28},{22,29},{23,30}} | collective-permute-start | bytes 49160 | tf_op jit(solution)/shard_map/ppermute | solution.py:944
  16.8 13.5 %collective-permute-start.10 = (bf16[384,256]{1,0:T(8,128)(2,1)S(1)}, bf16[384,256]{1,0:T(8,128)(2,1)S(1)}, u32[]{:S(2)}, u32[]{:S(2)}) collective-permute-start(bf16[384,256]{1,0:T(8,128)(2,1)S(1)} %fusion.3.after), channel_id=1, source_target_pairs={{0,16},{8,24},{1,17},{9,25},{2,18},{10,26},{3,19},{11,27},{4,20},{... | collective-permute-start | bytes 589832 | tf_op jit(solution)/shard_map/ppermute | solution.py:956
  26.3 9.7 %collective-permute-start.7 = (bf16[400,256]{1,0:T(8,128)(2,1)S(1)}, bf16[400,256]{1,0:T(8,128)(2,1)S(1)}, u32[]{:S(2)}, u32[]{:S(2)}) collective-permute-start(bf16[400,256]{1,0:T(8,128)(2,1)S(1)} %fusion.2.sums), channel_id=1, source_target_pairs={{8,24},{9,25},{10,26},{11,27},{12,28},{13,29},{14,30},{15,31}} | collective-permute-start | bytes 614408 | tf_op jit(solution)/shard_map/ppermute | solution.py:964
  27.6 8.4 %collective-permute-start.8 = (bf16[64,128]{1,0:T(8,128)(2,1)S(1)}, bf16[64,128]{1,0:T(8,128)(2,1)S(1)}, u32[]{:S(2)}, u32[]{:S(2)}) collective-permute-start(bf16[64,128]{1,0:T(8,128)(2,1)S(1)} %get-tuple-element.64), channel_id=1, source_target_pairs={{8,25},{9,26},{10,27},{11,28},{12,29},{13,30},{14,31}} | collective-permute-start | bytes 49160 | tf_op jit(solution)/shard_map/ppermute | solution.py:944
  28.9 7.1 %collective-permute-start.9 = (bf16[64,128]{1,0:T(8,128)(2,1)S(1)}, bf16[64,128]{1,0:T(8,128)(2,1)S(1)}, u32[]{:S(2)}, u32[]{:S(2)}) collective-permute-start(bf16[64,128]{1,0:T(8,128)(2,1)S(1)} %get-tuple-element.65), channel_id=1, source_target_pairs={{9,24},{10,25},{11,26},{12,27},{13,28},{14,29},{15,30}} | collective-permute-start | bytes 49160 | tf_op jit(solution)/shard_map/ppermute | solution.py:944
  30.3 8.8 %collective-permute-start.11 = (bf16[384,256]{1,0:T(8,128)(2,1)S(1)}, bf16[384,256]{1,0:T(8,128)(2,1)S(1)}, u32[]{:S(2)}, u32[]{:S(2)}) collective-permute-start(bf16[384,256]{1,0:T(8,128)(2,1)S(1)} %add_convert_fusion), channel_id=1, source_target_pairs={{16,24},{17,25},{18,26},{19,27},{20,28},{21,29},{22,30},{23,31}} | collective-permute-start | bytes 589832 | tf_op jit(solution)/shard_map/ppermute | solution.py:966

commit v7 on v6

--- a/solution.py
+++ b/solution.py
@@ -472,12 +472,14 @@
             )
         for group in range(2):
             start = group * halves * block
-            derivatives(rows_of, start, nodes, grads.at[group], rhs)
+            derivatives(rows_of, start, nodes, grads, rhs)
             add_faces(
                 rows_of, start, nodes, remote, group * halves * 64, [m[group] for m in masks], rhs
             )
             for n in range(nodes):
-                base[group, n] = node_of(rows_of, start, nodes, n) + ACOUSTIC_STEP * rhs[n]
+                base[pl.ds(start + n, 8, stride=nodes), :] = (
+                    node_of(rows_of, start, nodes, n) + ACOUSTIC_STEP * rhs[n]
+                )
 
 
 def second_block(plan, b, carried, visc, places, new_state, new_parts):
@@ -535,7 +537,7 @@
 def output_kernel(
     flow, visc, mean, state, mean_two,
     inner_state, inner_high, inner_low, inner_mats,
-    edge_state, edge_high, edge_low, edge_mats, edge_visc, after, after_up, after_down, own_one,
+    edge_state, edge_high, edge_low, edge_mats, edge_visc, after, after_border, own_one,
     flow_out, mean_out, own_one_out, passive, zero,
 ):
     plan = FlowPlan(flow.shape[1])
@@ -614,7 +616,7 @@
                     term = F32(matrix[at, m]) * node[lines[d][m]]
                     total = term if total is None else total + term
             grads.append(total)
-            grads_out[d, n] = total
+            grads_out[d, pl.ds(start + n, 8, stride=nodes), :] = total
         div = sum(pltpu.roll(grads[d], 8 - (1 + d), 0) for d in range(3))
         coupled = jnp.where(is_v[0], div, 0.0)
         for d in range(3):
@@ -646,28 +648,18 @@
             rhs[n] = rhs[n] + PENALTY * jump
 
 
-def source_rows(total, start, nodes, lamb, mean):
-    block = 4 * nodes
-    for h in range(total.shape[1] // LANES):
-        columns = slice(h * LANES, (h + 1) * LANES)
-        low = start + h * block
-        lamb[low : low + nodes, :] = jnp.zeros((nodes, LANES), F32)
+def with_sources(total, columns, block, nodes, base, grads):
+    for v in range(4):
+        rows = slice(block * 4 * nodes + v * nodes, block * 4 * nodes + (v + 1) * nodes)
+        added = total[(v - 1) * nodes : v * nodes, columns] if v else None
         for d in range(3):
-            at = low + (1 + d) * nodes
-            lamb[at : at + nodes, :] = total[d * nodes : (d + 1) * nodes, columns]
-            value = total[(3 + d) * nodes : (4 + d) * nodes, columns]
-            for v in range(4):
-                mean[d, low + v * nodes : low + (v + 1) * nodes, :] = value
-
-
-def source_terms(start, nodes, grads, lamb, mean, n):
-    total = node_of(lamb, start, nodes, n)
-    for d in range(3):
-        total = total + mean[d, pl.ds(start + n, 8, stride=nodes), :] * grads[d, n]
-    return total
-
-
-def border_kernel(sums, up, down):
+            term = total[(3 + d) * nodes : (4 + d) * nodes, columns] * grads[d, rows, :]
+            added = term if added is None else added + term
+        yield v, rows, base[rows, :] - ACOUSTIC_STEP * added
+
+
+def border_kernel(sums, *refs):
+    *_, up, down = refs
     nodes_rows = (sums.shape[0] - EXTRA) // (LANES // HE)
     group = lax.broadcasted_iota(jnp.int32, (1, LANES), 1) // HE
 
@@ -708,34 +700,26 @@
 
 def sound_one_kernel(
     base, grads, hot_two, neighbours, codes, source_a, source_b, up_a, up_b, down_a, down_b,
-    base_two, grads_two, scale_out, rows_of, facing, remote, rhs, lamb, mean,
+    base_two, grads_two, scale_out, rows_of, facing, remote, rhs,
 ):
-    nodes = base.shape[1]
     elements = source_a.shape[1]
     halves = elements // LANES
+    nodes = base_two.shape[0] // (4 * halves)
     block = 4 * nodes
 
     @pl.when(jnp.logical_not(on_flow_row()))
     def _():
         own, inverse = scaled_sums(source_a[...].astype(F32) + source_b[...].astype(F32), nodes)
         scale_out[...] = jnp.broadcast_to(inverse, scale_out.shape)
-        source_rows(own, 0, nodes, lamb, mean)
         extra = border_sums(
             up_a[...].astype(F32) + up_b[...].astype(F32),
             down_a[...].astype(F32) + down_b[...].astype(F32),
         )
         extra, _ = scaled_sums(extra, nodes)
-        none = (halves + 1) * block
-        lamb[none:, :] = jnp.zeros((block, LANES), F32)
-        for d in range(3):
-            mean[d, none:, :] = jnp.zeros((block, LANES), F32)
-        source_rows(extra, halves * block, nodes, lamb, mean)
-        for group in range(2):
-            start = group * halves * block
-            for n in range(nodes):
-                rows_of[pl.ds(start + n, 8, stride=nodes), :] = base[
-                    group, n
-                ] - ACOUSTIC_STEP * source_terms(start, nodes, grads.at[group], lamb, mean, n)
+        for h in range(halves + 1):
+            total, columns = (own, columns_of(h)) if h < halves else (extra, columns_of(0))
+            for _, rows, new in with_sources(total, columns, h, nodes, base, grads):
+                rows_of[rows, :] = new
         masks = []
         for face in range(6):
             for part in range(halves + 1):
@@ -750,15 +734,13 @@
         derivatives(rows_of, 0, nodes, grads_two, rhs)
         add_faces(rows_of, 0, nodes, remote, 0, masks, rhs)
         for n in range(nodes):
-            base_two[n] = node_of(rows_of, 0, nodes, n) + ACOUSTIC_STEP * rhs[n]
-
-
-def sound_two_kernel(
-    sound, base, grads, scale, source_a, source_b, out, rows_of, lamb, mean
-):
-    nodes = base.shape[0]
-    halves = sound.shape[2] // LANES
-    block = 4 * nodes
+            base_two[pl.ds(n, 8, stride=nodes), :] = (
+                node_of(rows_of, 0, nodes, n) + ACOUSTIC_STEP * rhs[n]
+            )
+
+
+def sound_two_kernel(sound, base, grads, scale, source_a, source_b, out):
+    nodes = sound.shape[1]
     is_flow = on_flow_row()
 
     @pl.when(is_flow)
@@ -767,17 +749,10 @@
 
     @pl.when(jnp.logical_not(is_flow))
     def _():
-        total = source_a[...].astype(F32) + source_b[...].astype(F32)
-        source_rows(total * scale[0:1, :], 0, nodes, lamb, mean)
-        for n in range(nodes):
-            rows_of[pl.ds(n, 8, stride=nodes), :] = base[n] - ACOUSTIC_STEP * source_terms(
-                0, nodes, grads, lamb, mean, n
-            )
-        for v in range(4):
-            for h in range(halves):
-                out[v, :, h * LANES : (h + 1) * LANES] = rows_of[
-                    h * block + v * nodes : h * block + (v + 1) * nodes, :
-                ]
+        total = (source_a[...].astype(F32) + source_b[...].astype(F32)) * scale[0:1, :]
+        for h in range(sound.shape[2] // LANES):
+            for v, _, new in with_sources(total, columns_of(h), h, nodes, base, grads):
+                out[v, :, columns_of(h)] = new
 
 
 def call(kernel, outs, scratch, operands, flops=10**8, in_hbm=(), limit=VMEM_LIMIT):
@@ -863,7 +838,6 @@
         [flow, visc, links, tile_target],
     )
     lines = 6 * nodes + EXTRA
-    by_node = (nodes, 8, LANES)
     node_rows = vmem((nodes, 8, LANES), F32)
     (
         own_one, next_one, mean_one, base, grads, hot_two,
@@ -874,8 +848,8 @@
             shape((lines, elements), F32),
             shape((lines, elements), BF16),
             shape(mean.shape, F32),
-            shape((2, *by_node), F32),
-            shape((2, 3, *by_node), F32),
+            shape(((halves + 2) * block, LANES), F32),
+            shape((3, (halves + 2) * block, LANES), F32),
             shape((6, elements + LANES, elements), BF16),
             shape((2 * rows, fields), F32),
             shape((2 * rows, fields), BF16),
@@ -936,11 +910,11 @@
         ],
         [visc, mean, mean_one, projector, *step_one, hits, *edges],
     )
-    def borders(sums, row):
+    def borders(sums, row, after=()):
         lines = 6 * nodes // (LANES // HE) + EXTRA
-        up, down = call(border_kernel, [shape((lines, LANES), BF16)] * 2, [], [sums])
+        up, down = call(border_kernel, [shape((lines, LANES), BF16)] * 2, [], [sums, *after])
         last = (groups - 1) * count
-        return [
+        return up, *[
             lax.ppermute(
                 x, ("grp", "sfc"),
                 [(row * count + i, last + i + step) for i in range(count) if 0 <= i + step < count],
@@ -951,32 +925,32 @@
     got_two = climb(next_two)
     sum_one = combined(own_one, got_one)
     x_one = lax.ppermute(sum_one, "grp", [(0, 1), (2, 3)])
-    up_a, down_a = borders(sum_one, 2)
+    border, up_a, down_a = borders(sum_one, 2)
     sum_two = combined(own_two, got_two)
     y_two = lax.ppermute(sum_two, "grp", [(0, 2), (1, 3)])
     flow_out, mean_out, own_one = call(
         output_kernel,
         [shape(flow.shape, F32), shape(mean.shape, F32), shape(own_one.shape, F32)],
         [vmem((band, fields), F32), vmem((HW, fields), BF16)],
-        [flow, visc, mean, state_two, mean_two, *step_one, *edges, sum_two, up_a, down_a, own_one],
+        [flow, visc, mean, state_two, mean_two, *step_one, *edges, sum_two, border, own_one],
     )
     sum_one = combined(own_one, got_one, x_one)
     y_one = lax.ppermute(sum_one, "grp", [(1, 3)])
-    up_b, down_b = borders(sum_one, 1)
+    _, up_b, down_b = borders(sum_one, 1, (up_a, down_a))
     x_two = lax.ppermute(combined(own_two, got_two, y_two), "grp", [(2, 3)])
 
-    held = vmem(((halves + 2) * block, LANES), F32)
-    held_3 = vmem((3, (halves + 2) * block, LANES), F32)
     base, grads, scale = call(
         sound_one_kernel,
-        [shape(by_node, F32), shape((3, *by_node), F32), shape((8, elements), F32)],
-        [
-            held,
+        [
+            shape((halves * block, LANES), F32),
+            shape((3, halves * block, LANES), F32),
+            shape((8, elements), F32),
+        ],
+        [
+            vmem(((halves + 1) * block, LANES), F32),
             vmem((6, halves + 1, 64, LANES), F32),
             vmem((6, halves * 64, LANES), F32),
             node_rows,
-            held,
-            held_3,
         ],
         [
             base, grads, hot_two, neighbours, codes, x_one, y_one,
@@ -987,11 +961,7 @@
     (sound_out,) = call(
         sound_two_kernel,
         [shape(sound.shape, F32)],
-        [
-            vmem((halves * block, LANES), F32),
-            vmem((halves * block, LANES), F32),
-            vmem((3, halves * block, LANES), F32),
-        ],
+        [],
         [sound, base, grads, scale, x_two, y_two],
     )
     return flow_out[None], mean_out[None], sound_out[None]

time: 41 us -> 39.2 us (0.956)
  waiting for transfers between devices: 14.1 us -> 12.4 us
    ppermute x4, waiting for transfers between devices: 11.5 us -> 5.86 us  [borders(): lax.ppermute(x, ('grp', 'sfc'), [(row * count + i, last + i + step) for i...]
    ppermute x1, waiting for transfers between devices: 0.01 us -> 3.24 us  [body(): x_one = lax.ppermute(sum_one, 'grp', [(0, 1), (2, 3)])]
    ppermute x1, waiting for transfers between devices: 0.35 us -> 1.04 us  [body(): x_two = lax.ppermute(combined(own_two, got_two, y_two), 'grp', [(2, 3)])]
  transfers between devices with their start and end apart: 12 -> 12, of which waited for: 4 -> 7; matrix products, arithmetic and copies ran while one was open for 1% -> 1% of each run, Pallas kernels for 10% -> 8%
where the time goes in v7:
time: 39.2 us; the launch traced here: 38.9 us
  starting transfers between devices  15.5 us (40%)
  waiting for transfers between devices  12.4 us (32%)
  Pallas kernels  9.77 us (25%)
  between operations  0.94 us (2%)
    pallas_call x9, Pallas kernels, call(): pl.pallas_call(kernel, out_shape=tuple(outs), in_specs=[pl.BlockSpec(memo...  9.77 us
    ppermute x4, waiting for transfers between devices, borders(): lax.ppermute(x, ('grp', 'sfc'), [(row * count + i, last + i + step) for i...  5.86 us
    ppermute x4, starting transfers between devices, borders(): lax.ppermute(x, ('grp', 'sfc'), [(row * count + i, last + i + step) for i...  5.16 us
    ppermute x1, starting transfers between devices, body(): part_a = lax.ppermute(pack_a, 'sfc', pairs_a)  3.76 us
    ppermute x1, waiting for transfers between devices, body(): x_one = lax.ppermute(sum_one, 'grp', [(0, 1), (2, 3)])  3.24 us
    ppermute x1, waiting for transfers between devices, body(): part_a = lax.ppermute(pack_a, 'sfc', pairs_a)  2.29 us
    ppermute x2, starting transfers between devices, climb(): return lax.ppermute(x, ('grp', 'sfc'), chosen)  1.35 us
    ppermute x1, starting transfers between devices, body(): x_two = lax.ppermute(combined(own_two, got_two, y_two), 'grp', [(2, 3)])  1.29 us
  transfers between devices with their start and end apart: 12, of which 7 were waited for; matrix products, arithmetic and copies ran while one was open for 1% of the time, Pallas kernels for 8%

profile of v7, /device:TPU:15, one launch (start us, length us, event | category | flops | bytes accessed | tf_op | source)
XLA Modules:
  0.0 38.9 jit_solution(3643078457217498652)
XLA Ops:
  0.6 0.0 copy-start
  0.6 0.0 copy-start.2
  0.7 0.0 copy-start.7
  0.7 0.0 copy-start.8
  0.7 0.0 copy-start.1
  0.7 0.0 copy-start.3
  0.7 0.0 copy-start.4
  0.7 0.0 copy-start.5
  0.7 0.0 copy-start.6
  0.7 1.8 %shard_map.112 = (bf16[304,128]{1,0:T(8,128)(2,1)}, bf16[304,128]{1,0:T(8,128)(2,1)}) custom-call(f32[5,256,128]{2,1,0:T(8,128)} %bitcast.10, f32[256,128]{1,0:T(8,128)} %bitcast.17, s32[4,256]{1,0:T(4,128)} %bitcast.31, f32[4,64,256]{2,1,0:T(8,128)} %bitcast.22, s32[6,1,256]{2,1,0:T(1,128)} %bitcast.25, s32[6,1,256]{2,1,0:T(1,128)} %bitcast.28), custom_call_target="tpu_custom_call" | custom-call | flops 10000000000 | bytes 1220608 | tf_op jit(solution)/shard_map/pallas_call | solution.py:761
  2.5 3.8 %collective-permute-start = (bf16[304,128]{1,0:T(8,128)(2,1)}, bf16[304,128]{1,0:T(8,128)(2,1)S(1)}, u32[]{:S(2)}, u32[]{:S(2)}) collective-permute-start(bf16[304,128]{1,0:T(8,128)(2,1)} %get-tuple-element.36), channel_id=1, source_target_pairs={{1,2},{2,1},{3,4},{4,3},{5,6},{6,5},{9,10},{10,9},{11,12},{12,11},... | collective-permute-start | bytes 233480 | tf_op jit(solution)/shard_map/ppermute | solution.py:819
  6.3 0.1 collective-permute-start.1
  6.4 0.0 copy-done
  6.4 0.0 copy-done.2
  6.4 0.0 copy-done.7
  6.4 0.0 copy-done.8
  6.4 2.3 %collective-permute-done.part_a = bf16[304,128]{1,0:T(8,128)(2,1)S(1)} collective-permute-done((bf16[304,128]{1,0:T(8,128)(2,1)}, bf16[304,128]{1,0:T(8,128)(2,1)S(1)}, u32[]{:S(2)}, u32[]{:S(2)}) %collective-permute-start) | collective-permute-done | bytes 77856 | tf_op jit(solution)/shard_map/ppermute | solution.py:819
  8.7 0.0 collective-permute-done.1.part_b
  8.7 0.0 copy-done.3
  8.8 3.9 %shard_map.114 = (f32[400,256]{1,0:T(8,128)S(1)}, bf16[400,256]{1,0:T(8,128)(2,1)S(1)}, f32[3,256,128]{2,1,0:T(8,128)S(1)}, f32[1024,128]{1,0:T(8,128)S(1)}, f32...) custom-call(f32[5,256,128]{2,1,0:T(8,128)S(1)} %bitcast.12, ...), custom_call_target="tpu_custom_call" | custom-call | flops 100000000 | bytes 8470528 | tf_op jit(solution)/shard_map/pallas_call | solution.py:761
  12.7 0.7 %collective-permute-start.3 = (bf16[400,256]{1,0:T(8,128)(2,1)S(1)}, bf16[400,256]{1,0:T(8,128)(2,1)S(1)}, u32[]{:S(2)}, u32[]{:S(2)}) collective-permute-start(bf16[400,256]{1,0:T(8,128)(2,1)S(1)} %get-tuple-element.55), channel_id=1, source_target_pairs={{0,1},{1,2},{2,3},{3,4},{4,5},{5,6},{6,7},{8,9},{9,10},{10,11},{11... | collective-permute-start | bytes 614408 | tf_op jit(solution)/shard_map/ppermute | solution.py:883
  13.4 0.1 shard_map.115
  13.5 0.7 %collective-permute-start.2 = (bf16[384,256]{1,0:T(8,128)(2,1)S(1)}, bf16[384,256]{1,0:T(8,128)(2,1)S(1)}, u32[]{:S(2)}, u32[]{:S(2)}) collective-permute-start(bf16[384,256]{1,0:T(8,128)(2,1)S(1)} %get-tuple-element.53), channel_id=1, source_target_pairs={{0,1},{1,2},{2,3},{3,4},{4,5},{5,6},{6,7},{8,9},{9,10},{10,11},{11... | collective-permute-start | bytes 589832 | tf_op jit(solution)/shard_map/ppermute | solution.py:883
  14.1 0.0 collective-permute-done.3
  14.1 0.1 fusion.sums
  14.2 1.3 %collective-permute-start.4 = (bf16[400,256]{1,0:T(8,128)(2,1)S(1)}, bf16[400,256]{1,0:T(8,128)(2,1)S(1)}, u32[]{:S(2)}, u32[]{:S(2)}) collective-permute-start(bf16[400,256]{1,0:T(8,128)(2,1)S(1)} %fusion.sums), channel_id=1, source_target_pairs={{0,8},{16,24},{1,9},{17,25},{2,10},{18,26},{3,11},{19,27},{4,12},{... | collective-permute-start | bytes 614408 | tf_op jit(solution)/shard_map/ppermute | solution.py:927
  15.5 0.0 collective-permute-done.2
  15.5 0.1 fusion.3.after
  15.6 1.3 %collective-permute-start.10 = (bf16[384,256]{1,0:T(8,128)(2,1)S(1)}, bf16[384,256]{1,0:T(8,128)(2,1)S(1)}, u32[]{:S(2)}, u32[]{:S(2)}) collective-permute-start(bf16[384,256]{1,0:T(8,128)(2,1)S(1)} %fusion.3.after), channel_id=1, source_target_pairs={{0,16},{8,24},{1,17},{9,25},{2,18},{10,26},{3,19},{11,27},{4,20},{... | collective-permute-start | bytes 589832 | tf_op jit(solution)/shard_map/ppermute | solution.py:930
  16.9 1.3 %collective-permute-start.6 = (bf16[64,128]{1,0:T(8,128)(2,1)S(1)}, bf16[64,128]{1,0:T(8,128)(2,1)S(1)}, u32[]{:S(2)}, u32[]{:S(2)}) collective-permute-start(bf16[64,128]{1,0:T(8,128)(2,1)S(1)} %get-tuple-element.56.after_border), channel_id=1, source_target_pairs={{16,25},{17,26},{18,27},{19,28},{20,29},{21,30},{22,31}} | collective-permute-start | bytes 49160 | tf_op jit(solution)/shard_map/ppermute | solution.py:918
  18.2 1.3 %collective-permute-start.7 = (bf16[64,128]{1,0:T(8,128)(2,1)S(1)}, bf16[64,128]{1,0:T(8,128)(2,1)S(1)}, u32[]{:S(2)}, u32[]{:S(2)}) collective-permute-start(bf16[64,128]{1,0:T(8,128)(2,1)S(1)} %get-tuple-element.63), channel_id=1, source_target_pairs={{17,24},{18,25},{19,26},{20,27},{21,28},{22,29},{23,30}} | collective-permute-start | bytes 49160 | tf_op jit(solution)/shard_map/ppermute | solution.py:918
  19.5 1.1 %shard_map.117 = (f32[5,256,128]{2,1,0:T(8,128)}, f32[3,256,128]{2,1,0:T(8,128)}, f32[400,256]{1,0:T(8,128)S(1)}) custom-call(f32[5,256,128]{2,1,0:T(8,128)S(1)} %bitcast.13, f32[256,128]{1,0:T(8,128)S(1)} %bitcast.21, f32[3,256,128]{2,1,0:T(8,128)S(1)} %bitcast.16, f32[320,384]{1,0:T(8,128)S(1)} %get-tuple-element.50.state, ...), custom_call_target="tpu_custom_call" | custom-call | flops 100000000 | bytes 6295552 | tf_op jit(solution)/shard_map/pallas_call | solution.py:761
  20.6 3.2 %collective-permute-done.4.source_a = bf16[400,256]{1,0:T(8,128)(2,1)S(1)} collective-permute-done((bf16[400,256]{1,0:T(8,128)(2,1)S(1)}, bf16[400,256]{1,0:T(8,128)(2,1)S(1)}, u32[]{:S(2)}, u32[]{:S(2)}) %collective-permute-start.4) | collective-permute-done | bytes 204832 | tf_op jit(solution)/shard_map/ppermute | solution.py:927
  23.8 0.1 fusion.2.sums
  23.9 1.3 %collective-permute-start.5 = (bf16[400,256]{1,0:T(8,128)(2,1)S(1)}, bf16[400,256]{1,0:T(8,128)(2,1)S(1)}, u32[]{:S(2)}, u32[]{:S(2)}) collective-permute-start(bf16[400,256]{1,0:T(8,128)(2,1)S(1)} %fusion.2.sums), channel_id=1, source_target_pairs={{8,24},{9,25},{10,26},{11,27},{12,28},{13,29},{14,30},{15,31}} | collective-permute-start | bytes 614408 | tf_op jit(solution)/shard_map/ppermute | solution.py:938
  25.2 0.6 %collective-permute-done.6.refs_0_.up_a = bf16[64,128]{1,0:T(8,128)(2,1)S(1)} collective-permute-done((bf16[64,128]{1,0:T(8,128)(2,1)S(1)}, bf16[64,128]{1,0:T(8,128)(2,1)S(1)}, u32[]{:S(2)}, u32[]{:S(2)}) %collective-permute-start.6) | collective-permute-done | bytes 16416 | tf_op jit(solution)/shard_map/ppermute | solution.py:918
  25.7 2.0 %collective-permute-done.7.refs_1_.down_a = bf16[64,128]{1,0:T(8,128)(2,1)S(1)} collective-permute-done((bf16[64,128]{1,0:T(8,128)(2,1)S(1)}, bf16[64,128]{1,0:T(8,128)(2,1)S(1)}, u32[]{:S(2)}, u32[]{:S(2)}) %collective-permute-start.7) | collective-permute-done | bytes 16416 | tf_op jit(solution)/shard_map/ppermute | solution.py:918
  27.8 1.3 %collective-permute-start.8 = (bf16[64,128]{1,0:T(8,128)(2,1)S(1)}, bf16[64,128]{1,0:T(8,128)(2,1)S(1)}, u32[]{:S(2)}, u32[]{:S(2)}) collective-permute-start(bf16[64,128]{1,0:T(8,128)(2,1)S(1)} %get-tuple-element.64), channel_id=1, source_target_pairs={{8,25},{9,26},{10,27},{11,28},{12,29},{13,30},{14,31}} | collective-permute-start | bytes 49160 | tf_op jit(solution)/shard_map/ppermute | solution.py:918
  29.1 1.3 %collective-permute-start.9 = (bf16[64,128]{1,0:T(8,128)(2,1)S(1)}, bf16[64,128]{1,0:T(8,128)(2,1)S(1)}, u32[]{:S(2)}, u32[]{:S(2)}) collective-permute-start(bf16[64,128]{1,0:T(8,128)(2,1)S(1)} %get-tuple-element.65), channel_id=1, source_target_pairs={{9,24},{10,25},{11,26},{12,27},{13,28},{14,29},{15,30}} | collective-permute-start | bytes 49160 | tf_op jit(solution)/shard_map/ppermute | solution.py:918
  30.4 0.0 collective-permute-done.10.source_b
  30.4 0.1 add_convert_fusion
  30.4 1.3 %collective-permute-start.11 = (bf16[384,256]{1,0:T(8,128)(2,1)S(1)}, bf16[384,256]{1,0:T(8,128)(2,1)S(1)}, u32[]{:S(2)}, u32[]{:S(2)}) collective-permute-start(bf16[384,256]{1,0:T(8,128)(2,1)S(1)} %add_convert_fusion), channel_id=1, source_target_pairs={{16,24},{17,25},{18,26},{19,27},{20,28},{21,29},{22,30},{23,31}} | collective-permute-start | bytes 589832 | tf_op jit(solution)/shard_map/ppermute | solution.py:940
  31.7 1.5 %collective-permute-done.8.up_b = bf16[64,128]{1,0:T(8,128)(2,1)S(1)} collective-permute-done((bf16[64,128]{1,0:T(8,128)(2,1)S(1)}, bf16[64,128]{1,0:T(8,128)(2,1)S(1)}, u32[]{:S(2)}, u32[]{:S(2)}) %collective-permute-start.8) | collective-permute-done | bytes 16416 | tf_op jit(solution)/shard_map/ppermute | solution.py:918
  33.2 1.8 %collective-permute-done.9.down_b = bf16[64,128]{1,0:T(8,128)(2,1)S(1)} collective-permute-done((bf16[64,128]{1,0:T(8,128)(2,1)S(1)}, bf16[64,128]{1,0:T(8,128)(2,1)S(1)}, u32[]{:S(2)}, u32[]{:S(2)}) %collective-permute-start.9) | collective-permute-done | bytes 16416 | tf_op jit(solution)/shard_map/ppermute | solution.py:918
  35.0 0.0 collective-permute-done.5.source_b
  35.0 2.1 %shard_map.119 = (f32[512,128]{1,0:T(8,128)S(1)}, f32[3,512,128]{2,1,0:T(8,128)S(1)}, f32[8,256]{1,0:T(8,128)S(1)}) custom-call(f32[1024,128]{1,0:T(8,128)S(1)} %get-tuple-element.59.base, f32[3,1024,128]{2,1,0:T(8,128)S(1)} %get-tuple-element.60.grads, bf16[6,384,256]{2,1,0:T(8,128)(2,1)S(1)} %get-tuple-element.61.hot_two, s32[6,1,256]{2,1,0:T(1,128)S(1)} %bitcast.27, ...), custom_call_target="tpu_custom_call" | custom-call | flops 10000000000 | bytes 4820992 | tf_op jit(solution)/shard_map/pallas_call | solution.py:761
  37.1 1.0 %collective-permute-done.11.source_a = bf16[384,256]{1,0:T(8,128)(2,1)S(1)} collective-permute-done((bf16[384,256]{1,0:T(8,128)(2,1)S(1)}, bf16[384,256]{1,0:T(8,128)(2,1)S(1)}, u32[]{:S(2)}, u32[]{:S(2)}) %collective-permute-start.11) | collective-permute-done | bytes 196640 | tf_op jit(solution)/shard_map/ppermute | solution.py:940
  38.1 0.8 %shard_map.120 = f32[4,64,256]{2,1,0:T(8,128)} custom-call(f32[4,64,256]{2,1,0:T(8,128)S(1)} %bitcast.24, f32[512,128]{1,0:T(8,128)S(1)} %get-tuple-element.66.base, f32[3,512,128]{2,1,0:T(8,128)S(1)} %get-tuple-element.67.grads, f32[8,256]{1,0:T(8,128)S(1)} %get-tuple-element.68.scale, bf16[384,256]{1,0:T(8,128)(2,1)S(1)} %collective-permute-done.11.source_a, ...), custom_call_target="tpu_custom_call" | custom-call | flops 100000000 | bytes 1974272 | tf_op jit(solution)/shard_map/pallas_call | solution.py:761
  (7 shorter events, 0.0 us)
Async XLA Ops:
  0.6 5.7 %copy-start = (f32[1,5,256,128]{3,2,1,0:T(8,128)S(1)}, f32[1,5,256,128]{3,2,1,0:T(8,128)}, u32[]{:S(2)}) copy-start(f32[1,5,256,128]{3,2,1,0:T(8,128)} %param.9) | copy-start | bytes 1966084
  0.6 5.7 %copy-start.2 = (f32[1,256,128]{2,1,0:T(8,128)S(1)}, f32[1,256,128]{2,1,0:T(8,128)}, u32[]{:S(2)}) copy-start(f32[1,256,128]{2,1,0:T(8,128)} %param.11) | copy-start | bytes 393220
  0.7 5.7 %copy-start.7 = (s32[1,4,256]{2,1,0:T(4,128)S(1)}, s32[1,4,256]{2,1,0:T(4,128)}, u32[]{:S(2)}) copy-start(s32[1,4,256]{2,1,0:T(4,128)} %param.12) | copy-start | bytes 12292
  0.7 5.7 %copy-start.8 = (s32[1,256]{1,0:T(1,128)S(1)}, s32[1,256]{1,0:T(1,128)}, u32[]{:S(2)}) copy-start(s32[1,256]{1,0:T(1,128)} %target.1) | copy-start | bytes 3076
  0.7 8.1 %copy-start.1 = (f32[1,3,256,128]{3,2,1,0:T(8,128)S(1)}, f32[1,3,256,128]{3,2,1,0:T(8,128)}, u32[]{:S(2)}) copy-start(f32[1,3,256,128]{3,2,1,0:T(8,128)} %param.10) | copy-start | bytes 1179652
  0.7 8.1 %copy-start.3 = (f32[1,4,64,256]{3,2,1,0:T(8,128)S(1)}, f32[1,4,64,256]{3,2,1,0:T(8,128)}, u32[]{:S(2)}) copy-start(f32[1,4,64,256]{3,2,1,0:T(8,128)} %param.15) | copy-start | bytes 786436
  0.7 8.1 %copy-start.4 = (f32[64,128]{1,0:T(8,128)S(1)}, f32[64,128]{1,0:T(8,128)}, u32[]{:S(2)}) copy-start(f32[64,128]{1,0:T(8,128)} %projector.3) | copy-start | bytes 98308
  0.7 8.1 %copy-start.5 = (s32[1,6,256]{2,0,1:T(1,128)S(1)}, s32[1,6,256]{2,0,1:T(1,128)}, u32[]{:S(2)}) copy-start(s32[1,6,256]{2,0,1:T(1,128)} %param.16) | copy-start | bytes 18436
  0.7 8.1 %copy-start.6 = (s32[1,6,256]{2,0,1:T(1,128)S(1)}, s32[1,6,256]{2,0,1:T(1,128)}, u32[]{:S(2)}) copy-start(s32[1,6,256]{2,0,1:T(1,128)} %param.17) | copy-start | bytes 18436
  2.5 6.2 %collective-permute-start = (bf16[304,128]{1,0:T(8,128)(2,1)}, bf16[304,128]{1,0:T(8,128)(2,1)S(1)}, u32[]{:S(2)}, u32[]{:S(2)}) collective-permute-start(bf16[304,128]{1,0:T(8,128)(2,1)} %get-tuple-element.36), channel_id=1, source_target_pairs={{1,2},{2,1},{3,4},{4,3},{5,6},{6,5},{9,10},{10,9},{11,12},{12,11},... | collective-permute-start | bytes 233480 | tf_op jit(solution)/shard_map/ppermute | solution.py:819
  6.3 2.4 %collective-permute-start.1 = (bf16[304,128]{1,0:T(8,128)(2,1)}, bf16[304,128]{1,0:T(8,128)(2,1)S(1)}, u32[]{:S(2)}, u32[]{:S(2)}) collective-permute-start(bf16[304,128]{1,0:T(8,128)(2,1)} %get-tuple-element.37), channel_id=1, source_target_pairs={{0,1},{1,0},{2,3},{3,2},{4,5},{5,4},{6,7},{7,6},{8,9},{9,8},{10,11... | collective-permute-start | bytes 233480 | tf_op jit(solution)/shard_map/ppermute | solution.py:820
  12.7 1.4 %collective-permute-start.3 = (bf16[400,256]{1,0:T(8,128)(2,1)S(1)}, bf16[400,256]{1,0:T(8,128)(2,1)S(1)}, u32[]{:S(2)}, u32[]{:S(2)}) collective-permute-start(bf16[400,256]{1,0:T(8,128)(2,1)S(1)} %get-tuple-element.55), channel_id=1, source_target_pairs={{0,1},{1,2},{2,3},{3,4},{4,5},{5,6},{6,7},{8,9},{9,10},{10,11},{11... | collective-permute-start | bytes 614408 | tf_op jit(solution)/shard_map/ppermute | solution.py:883
  13.5 2.1 %collective-permute-start.2 = (bf16[384,256]{1,0:T(8,128)(2,1)S(1)}, bf16[384,256]{1,0:T(8,128)(2,1)S(1)}, u32[]{:S(2)}, u32[]{:S(2)}) collective-permute-start(bf16[384,256]{1,0:T(8,128)(2,1)S(1)} %get-tuple-element.53), channel_id=1, source_target_pairs={{0,1},{1,2},{2,3},{3,4},{4,5},{5,6},{6,7},{8,9},{9,10},{10,11},{11... | collective-permute-start | bytes 589832 | tf_op jit(solution)/shard_map/ppermute | solution.py:883
  14.2 9.6 %collective-permute-start.4 = (bf16[400,256]{1,0:T(8,128)(2,1)S(1)}, bf16[400,256]{1,0:T(8,128)(2,1)S(1)}, u32[]{:S(2)}, u32[]{:S(2)}) collective-permute-start(bf16[400,256]{1,0:T(8,128)(2,1)S(1)} %fusion.sums), channel_id=1, source_target_pairs={{0,8},{16,24},{1,9},{17,25},{2,10},{18,26},{3,11},{19,27},{4,12},{... | collective-permute-start | bytes 614408 | tf_op jit(solution)/shard_map/ppermute | solution.py:927
  15.6 14.8 %collective-permute-start.10 = (bf16[384,256]{1,0:T(8,128)(2,1)S(1)}, bf16[384,256]{1,0:T(8,128)(2,1)S(1)}, u32[]{:S(2)}, u32[]{:S(2)}) collective-permute-start(bf16[384,256]{1,0:T(8,128)(2,1)S(1)} %fusion.3.after), channel_id=1, source_target_pairs={{0,16},{8,24},{1,17},{9,25},{2,18},{10,26},{3,19},{11,27},{4,20},{... | collective-permute-start | bytes 589832 | tf_op jit(solution)/shard_map/ppermute | solution.py:930
  16.9 8.8 %collective-permute-start.6 = (bf16[64,128]{1,0:T(8,128)(2,1)S(1)}, bf16[64,128]{1,0:T(8,128)(2,1)S(1)}, u32[]{:S(2)}, u32[]{:S(2)}) collective-permute-start(bf16[64,128]{1,0:T(8,128)(2,1)S(1)} %get-tuple-element.56.after_border), channel_id=1, source_target_pairs={{16,25},{17,26},{18,27},{19,28},{20,29},{21,30},{22,31}} | collective-permute-start | bytes 49160 | tf_op jit(solution)/shard_map/ppermute | solution.py:918
  18.2 9.6 %collective-permute-start.7 = (bf16[64,128]{1,0:T(8,128)(2,1)S(1)}, bf16[64,128]{1,0:T(8,128)(2,1)S(1)}, u32[]{:S(2)}, u32[]{:S(2)}) collective-permute-start(bf16[64,128]{1,0:T(8,128)(2,1)S(1)} %get-tuple-element.63), channel_id=1, source_target_pairs={{17,24},{18,25},{19,26},{20,27},{21,28},{22,29},{23,30}} | collective-permute-start | bytes 49160 | tf_op jit(solution)/shard_map/ppermute | solution.py:918
  23.9 11.1 %collective-permute-start.5 = (bf16[400,256]{1,0:T(8,128)(2,1)S(1)}, bf16[400,256]{1,0:T(8,128)(2,1)S(1)}, u32[]{:S(2)}, u32[]{:S(2)}) collective-permute-start(bf16[400,256]{1,0:T(8,128)(2,1)S(1)} %fusion.2.sums), channel_id=1, source_target_pairs={{8,24},{9,25},{10,26},{11,27},{12,28},{13,29},{14,30},{15,31}} | collective-permute-start | bytes 614408 | tf_op jit(solution)/shard_map/ppermute | solution.py:938
  27.8 5.5 %collective-permute-start.8 = (bf16[64,128]{1,0:T(8,128)(2,1)S(1)}, bf16[64,128]{1,0:T(8,128)(2,1)S(1)}, u32[]{:S(2)}, u32[]{:S(2)}) collective-permute-start(bf16[64,128]{1,0:T(8,128)(2,1)S(1)} %get-tuple-element.64), channel_id=1, source_target_pairs={{8,25},{9,26},{10,27},{11,28},{12,29},{13,30},{14,31}} | collective-permute-start | bytes 49160 | tf_op jit(solution)/shard_map/ppermute | solution.py:918
  29.1 6.0 %collective-permute-start.9 = (bf16[64,128]{1,0:T(8,128)(2,1)S(1)}, bf16[64,128]{1,0:T(8,128)(2,1)S(1)}, u32[]{:S(2)}, u32[]{:S(2)}) collective-permute-start(bf16[64,128]{1,0:T(8,128)(2,1)S(1)} %get-tuple-element.65), channel_id=1, source_target_pairs={{9,24},{10,25},{11,26},{12,27},{13,28},{14,29},{15,30}} | collective-permute-start | bytes 49160 | tf_op jit(solution)/shard_map/ppermute | solution.py:918
  30.4 7.7 %collective-permute-start.11 = (bf16[384,256]{1,0:T(8,128)(2,1)S(1)}, bf16[384,256]{1,0:T(8,128)(2,1)S(1)}, u32[]{:S(2)}, u32[]{:S(2)}) collective-permute-start(bf16[384,256]{1,0:T(8,128)(2,1)S(1)} %add_convert_fusion), channel_id=1, source_target_pairs={{16,24},{17,25},{18,26},{19,27},{20,28},{21,29},{22,30},{23,31}} | collective-permute-start | bytes 589832 | tf_op jit(solution)/shard_map/ppermute | solution.py:940

commit v8 on v7

--- a/solution.py
+++ b/solution.py
@@ -21,6 +21,7 @@
 ALL_FIELDS = ((0, 2), (2, 4), (4, 5))
 BASE = 32.0
 EXTRA = 16
+PACK_COST, SECOND_COST, OUTPUT_COST, SOUND_COST = 10**10, 10**10, 10**9, 10**9
 VMEM_LIMIT = 20 * 1024 * 1024
 PACK_LIMIT = 60 * 1024 * 1024
 
@@ -537,7 +538,7 @@
 def output_kernel(
     flow, visc, mean, state, mean_two,
     inner_state, inner_high, inner_low, inner_mats,
-    edge_state, edge_high, edge_low, edge_mats, edge_visc, after, after_border, own_one,
+    edge_state, edge_high, edge_low, edge_mats, edge_visc, after, after_up, after_down, own_one,
     flow_out, mean_out, own_one_out, passive, zero,
 ):
     plan = FlowPlan(flow.shape[1])
@@ -658,25 +659,32 @@
         yield v, rows, base[rows, :] - ACOUSTIC_STEP * added
 
 
-def border_kernel(sums, *refs):
-    *_, up, down = refs
+def gated_sum_kernel(own, *refs):
+    *others, _, out = refs
+
+    @pl.when(on_flow_row())
+    def _():
+        total = own[...]
+        for other in others:
+            total = total + other[...].astype(F32)
+        out[...] = total.astype(BF16)
+
+
+def border_kernel(sums, up, down):
     nodes_rows = (sums.shape[0] - EXTRA) // (LANES // HE)
     group = lax.broadcasted_iota(jnp.int32, (1, LANES), 1) // HE
-
-    @pl.when(on_flow_row())
-    def _():
-        for out, tile, shift in ((up, sums.shape[1] - LANES, HE), (down, 0, 0)):
-            columns = slice(tile, tile + LANES)
-            total = jnp.zeros((nodes_rows, LANES), F32)
-            for i in range(LANES // HE):
-                x = sums[i * nodes_rows : (i + 1) * nodes_rows, columns].astype(F32)
-                turn = (HE * i + shift) % LANES
-                x = pltpu.roll(x, turn, 1) if turn else x
-                total = jnp.where(group == i, x, total)
-            out[:nodes_rows, :] = total.astype(BF16)
-            x = sums[sums.shape[0] - EXTRA :, columns].astype(F32)
-            x = pltpu.roll(x, shift, 1) if shift else x
-            out[nodes_rows:, :] = jnp.where(group == 0, x, 0.0).astype(BF16)
+    for out, tile, shift in ((up, sums.shape[1] - LANES, HE), (down, 0, 0)):
+        columns = slice(tile, tile + LANES)
+        total = jnp.zeros((nodes_rows, LANES), F32)
+        for i in range(LANES // HE):
+            x = sums[i * nodes_rows : (i + 1) * nodes_rows, columns].astype(F32)
+            turn = (HE * i + shift) % LANES
+            x = pltpu.roll(x, turn, 1) if turn else x
+            total = jnp.where(group == i, x, total)
+        out[:nodes_rows, :] = total.astype(BF16)
+        x = sums[sums.shape[0] - EXTRA :, columns].astype(F32)
+        x = pltpu.roll(x, shift, 1) if shift else x
+        out[nodes_rows:, :] = jnp.where(group == 0, x, 0.0).astype(BF16)
 
 
 def border_sums(up, down):
@@ -699,7 +707,7 @@
 
 
 def sound_one_kernel(
-    base, grads, hot_two, neighbours, codes, source_a, source_b, up_a, up_b, down_a, down_b,
+    base, grads, hot_two, neighbours, codes, source_a, source_b, up_a, down_a, up_b, down_b, after,
     base_two, grads_two, scale_out, rows_of, facing, remote, rhs,
 ):
     elements = source_a.shape[1]
@@ -755,7 +763,7 @@
                 out[v, :, columns_of(h)] = new
 
 
-def call(kernel, outs, scratch, operands, flops=10**8, in_hbm=(), limit=VMEM_LIMIT):
+def call(kernel, outs, scratch, operands, cost=None, in_hbm=(), limit=VMEM_LIMIT):
     spaces = [pltpu.HBM if at in in_hbm else pltpu.VMEM for at in range(len(operands))]
     moved = sum(int(np.prod(x.shape)) * x.dtype.itemsize for x in (*operands, *outs))
     return pl.pallas_call(
@@ -765,7 +773,7 @@
         out_specs=tuple([pl.BlockSpec(memory_space=pltpu.VMEM)] * len(outs)),
         scratch_shapes=scratch,
         compiler_params=pltpu.CompilerParams(vmem_limit_bytes=limit),
-        cost_estimate=pl.CostEstimate(flops=flops, bytes_accessed=moved, transcendentals=0),
+        cost_estimate=pl.CostEstimate(flops=10**8 if cost is None else cost, bytes_accessed=moved if cost is None else 0, transcendentals=0),
     )(*operands)
 
 
@@ -814,7 +822,7 @@
         [flow, visc, links, sound, neighbours, codes],
         in_hbm=(0, 1, 2, 3, 4, 5),
         limit=PACK_LIMIT,
-        flops=10**10,
+        cost=PACK_COST,
     )
     part_a = lax.ppermute(pack_a, "sfc", pairs_a)
     part_b = lax.ppermute(pack_b, "sfc", pairs_b)
@@ -909,35 +917,51 @@
             vmem((6 * nodes, tiles), BF16),
         ],
         [visc, mean, mean_one, projector, *step_one, hits, *edges],
-    )
-    def borders(sums, row, after=()):
-        lines = 6 * nodes // (LANES // HE) + EXTRA
-        up, down = call(border_kernel, [shape((lines, LANES), BF16)] * 2, [], [sums, *after])
-        last = (groups - 1) * count
-        return up, *[
+        cost=SECOND_COST,
+    )
+    last = (groups - 1) * count
+    lines_beside = 6 * nodes // (LANES // HE) + EXTRA
+
+    def borders(sums, row):
+        up_border, down_border = call(
+            border_kernel, [shape((lines_beside, LANES), BF16)] * 2, [], [sums], cost=0
+        )
+        start = row * count
+        return up_border, [
             lax.ppermute(
-                x, ("grp", "sfc"),
-                [(row * count + i, last + i + step) for i in range(count) if 0 <= i + step < count],
-            )
-            for x, step in ((up, 1), (down, -1))
+                up_border, ("grp", "sfc"), [(start + i, last + i + 1) for i in range(count - 1)]
+            ),
+            lax.ppermute(
+                down_border, ("grp", "sfc"), [(start + i, last + i - 1) for i in range(1, count)]
+            ),
         ]
 
     got_two = climb(next_two)
-    sum_one = combined(own_one, got_one)
-    x_one = lax.ppermute(sum_one, "grp", [(0, 1), (2, 3)])
-    border, up_a, down_a = borders(sum_one, 2)
-    sum_two = combined(own_two, got_two)
-    y_two = lax.ppermute(sum_two, "grp", [(0, 2), (1, 3)])
+    sum_one_2 = combined(own_one, got_one)
+    one_0_to_1 = lax.ppermute(sum_one_2, "grp", [(0, 1)])
+    _, beside_2 = borders(sum_one_2, 2)
+    sum_two_1 = combined(own_two, got_two)
+    two_0_to_2 = lax.ppermute(sum_two_1, "grp", [(0, 2)])
+    one_2_to_3 = lax.ppermute(sum_one_2, "grp", [(2, 3)])
+    two_1_to_3 = lax.ppermute(sum_two_1, "grp", [(1, 3)])
     flow_out, mean_out, own_one = call(
         output_kernel,
         [shape(flow.shape, F32), shape(mean.shape, F32), shape(own_one.shape, F32)],
         [vmem((band, fields), F32), vmem((HW, fields), BF16)],
-        [flow, visc, mean, state_two, mean_two, *step_one, *edges, sum_two, border, own_one],
-    )
-    sum_one = combined(own_one, got_one, x_one)
-    y_one = lax.ppermute(sum_one, "grp", [(1, 3)])
-    _, up_b, down_b = borders(sum_one, 1, (up_a, down_a))
-    x_two = lax.ppermute(combined(own_two, got_two, y_two), "grp", [(2, 3)])
+        [flow, visc, mean, state_two, mean_two, *step_one, *edges, sum_two_1, *beside_2, own_one],
+        cost=OUTPUT_COST,
+    )
+    sum_one_1 = combined(own_one, got_one, one_0_to_1)
+    one_1_to_3 = lax.ppermute(sum_one_1, "grp", [(1, 3)])
+    border, beside_1 = borders(sum_one_1, 1)
+    (sum_two_2,) = call(
+        gated_sum_kernel,
+        [shape(own_two.shape, BF16)],
+        [],
+        [own_two, got_two, two_0_to_2, border],
+        cost=0,
+    )
+    two_2_to_3 = lax.ppermute(sum_two_2, "grp", [(2, 3)])
 
     base, grads, scale = call(
         sound_one_kernel,
@@ -953,16 +977,16 @@
             node_rows,
         ],
         [
-            base, grads, hot_two, neighbours, codes, x_one, y_one,
-            up_a, up_b, down_a, down_b,
+            base, grads, hot_two, neighbours, codes, one_2_to_3, one_1_to_3,
+            *beside_1, *beside_2, two_1_to_3,
         ],
-        flops=10**10,
+        cost=SOUND_COST,
     )
     (sound_out,) = call(
         sound_two_kernel,
         [shape(sound.shape, F32)],
         [],
-        [sound, base, grads, scale, x_two, y_two],
+        [sound, base, grads, scale, two_2_to_3, two_1_to_3],
     )
     return flow_out[None], mean_out[None], sound_out[None]
 

time: 39.2 us -> 37.8 us (0.964)
  waiting for transfers between devices: 12.4 us -> 9.48 us
  starting transfers between devices: 15.5 us -> 16.9 us
    ppermute x8 -> x10, waiting for transfers between devices: 10.1 us -> 7.18 us  [the longest x2 4.46 us: borders(): lax.ppermute(down_border, ('grp', 'sfc'), [(start + i, last + i - 1) for...]
    ppermute x8 -> x10, starting transfers between devices: 10.3 us -> 11.7 us  [the longest x2 2.58 us: borders(): lax.ppermute(up_border, ('grp', 'sfc'), [(start + i, last + i + 1) for i...]
    pallas_call x9 -> x10, Pallas kernels: 9.77 us -> 9.96 us  [call(): pl.pallas_call(kernel, out_shape=tuple(outs), in_specs=[pl.BlockSpec(memo...]
  transfers between devices with their start and end apart: 12 -> 14, of which waited for: 7 -> 5; matrix products, arithmetic and copies ran while one was open for 1% -> 0% of each run, Pallas kernels for 8% -> 9%
where the time goes in v8:
time: 37.8 us; the launch traced here: 37.5 us
  starting transfers between devices  16.9 us (45%)
  Pallas kernels  9.96 us (26%)
  waiting for transfers between devices  9.48 us (25%)
  between operations  1.01 us (3%)
    pallas_call x10, Pallas kernels, call(): pl.pallas_call(kernel, out_shape=tuple(outs), in_specs=[pl.BlockSpec(memo...  9.96 us
    ppermute x2, waiting for transfers between devices, borders(): lax.ppermute(down_border, ('grp', 'sfc'), [(start + i, last + i - 1) for...  4.46 us
    ppermute x1, starting transfers between devices, body(): part_a = lax.ppermute(pack_a, 'sfc', pairs_a)  3.76 us
    ppermute x2, waiting for transfers between devices, borders(): lax.ppermute(up_border, ('grp', 'sfc'), [(start + i, last + i + 1) for i...  2.7 us
    ppermute x2, starting transfers between devices, borders(): lax.ppermute(up_border, ('grp', 'sfc'), [(start + i, last + i + 1) for i...  2.58 us
    ppermute x2, starting transfers between devices, borders(): lax.ppermute(down_border, ('grp', 'sfc'), [(start + i, last + i - 1) for...  2.58 us
    ppermute x1, waiting for transfers between devices, body(): part_a = lax.ppermute(pack_a, 'sfc', pairs_a)  2.29 us
    ppermute x2, starting transfers between devices, climb(): return lax.ppermute(x, ('grp', 'sfc'), chosen)  1.35 us
  transfers between devices with their start and end apart: 14, of which 5 were waited for; matrix products, arithmetic and copies ran while one was open for 0% of the time, Pallas kernels for 9%

profile of v8, /device:TPU:15, one launch (start us, length us, event | category | flops | bytes accessed | tf_op | source)
XLA Modules:
  0.0 37.5 jit_solution(11598559355308075575)
XLA Ops:
  0.6 0.0 copy-start
  0.6 0.0 copy-start.2
  0.7 0.0 copy-start.7
  0.7 0.0 copy-start.8
  0.7 0.0 copy-start.1
  0.7 0.0 copy-start.3
  0.7 1.8 %shard_map.112 = (bf16[304,128]{1,0:T(8,128)(2,1)}, bf16[304,128]{1,0:T(8,128)(2,1)}) custom-call(f32[5,256,128]{2,1,0:T(8,128)} %bitcast.10, f32[256,128]{1,0:T(8,128)} %bitcast.17, s32[4,256]{1,0:T(4,128)} %bitcast.31, f32[4,64,256]{2,1,0:T(8,128)} %bitcast.22, s32[6,1,256]{2,1,0:T(1,128)} %bitcast.25, s32[6,1,256]{2,1,0:T(1,128)} %bitcast.28), custom_call_target="tpu_custom_call" | custom-call | flops 10000000000 | tf_op jit(solution)/shard_map/pallas_call | solution.py:769
  2.5 3.8 %collective-permute-start = (bf16[304,128]{1,0:T(8,128)(2,1)}, bf16[304,128]{1,0:T(8,128)(2,1)S(1)}, u32[]{:S(2)}, u32[]{:S(2)}) collective-permute-start(bf16[304,128]{1,0:T(8,128)(2,1)} %get-tuple-element.36), channel_id=1, source_target_pairs={{1,2},{2,1},{3,4},{4,3},{5,6},{6,5},{9,10},{10,9},{11,12},{12,11},... | collective-permute-start | bytes 233480 | tf_op jit(solution)/shard_map/ppermute | solution.py:827
  6.3 0.1 collective-permute-start.1
  6.4 0.0 copy-done
  6.4 0.0 copy-done.2
  6.4 0.0 copy-done.7
  6.4 0.0 copy-done.8
  6.4 2.3 %collective-permute-done.part_a = bf16[304,128]{1,0:T(8,128)(2,1)S(1)} collective-permute-done((bf16[304,128]{1,0:T(8,128)(2,1)}, bf16[304,128]{1,0:T(8,128)(2,1)S(1)}, u32[]{:S(2)}, u32[]{:S(2)}) %collective-permute-start) | collective-permute-done | bytes 77856 | tf_op jit(solution)/shard_map/ppermute | solution.py:827
  8.7 0.0 collective-permute-done.1.part_b
  8.7 0.0 copy-done.1
  8.8 3.9 %shard_map.114 = (f32[400,256]{1,0:T(8,128)S(1)}, bf16[400,256]{1,0:T(8,128)(2,1)S(1)}, f32[3,256,128]{2,1,0:T(8,128)S(1)}, f32[1024,128]{1,0:T(8,128)S(1)}, f32...) custom-call(f32[5,256,128]{2,1,0:T(8,128)S(1)} %bitcast.12, ...), custom_call_target="tpu_custom_call" | custom-call | flops 100000000 | bytes 8470528 | tf_op jit(solution)/shard_map/pallas_call | solution.py:769
  12.7 0.7 %collective-permute-start.3 = (bf16[400,256]{1,0:T(8,128)(2,1)S(1)}, bf16[400,256]{1,0:T(8,128)(2,1)S(1)}, u32[]{:S(2)}, u32[]{:S(2)}) collective-permute-start(bf16[400,256]{1,0:T(8,128)(2,1)S(1)} %get-tuple-element.55), channel_id=1, source_target_pairs={{0,1},{1,2},{2,3},{3,4},{4,5},{5,6},{6,7},{8,9},{9,10},{10,11},{11... | collective-permute-start | bytes 614408 | tf_op jit(solution)/shard_map/ppermute | solution.py:891
  13.4 0.1 shard_map.115
  13.4 0.7 %collective-permute-start.2 = (bf16[384,256]{1,0:T(8,128)(2,1)S(1)}, bf16[384,256]{1,0:T(8,128)(2,1)S(1)}, u32[]{:S(2)}, u32[]{:S(2)}) collective-permute-start(bf16[384,256]{1,0:T(8,128)(2,1)S(1)} %get-tuple-element.53), channel_id=1, source_target_pairs={{0,1},{1,2},{2,3},{3,4},{4,5},{5,6},{6,7},{8,9},{9,10},{10,11},{11... | collective-permute-start | bytes 589832 | tf_op jit(solution)/shard_map/ppermute | solution.py:891
  14.1 0.0 collective-permute-done.3
  14.2 0.1 shard_map.116
  14.3 0.7 %collective-permute-start.7 = (bf16[400,256]{1,0:T(8,128)(2,1)S(1)}, bf16[400,256]{1,0:T(8,128)(2,1)S(1)}, u32[]{:S(2)}, u32[]{:S(2)}) collective-permute-start(bf16[400,256]{1,0:T(8,128)(2,1)S(1)} %fusion.sums), channel_id=1, source_target_pairs={{0,8},{1,9},{2,10},{3,11},{4,12},{5,13},{6,14},{7,15}} | collective-permute-start | bytes 614408 | tf_op jit(solution)/shard_map/ppermute | solution.py:941
  15.0 1.3 %collective-permute-start.4 = (bf16[64,128]{1,0:T(8,128)(2,1)S(1)}, bf16[64,128]{1,0:T(8,128)(2,1)S(1)}, u32[]{:S(2)}, u32[]{:S(2)}) collective-permute-start(bf16[64,128]{1,0:T(8,128)(2,1)S(1)} %get-tuple-element.56), channel_id=1, source_target_pairs={{16,25},{17,26},{18,27},{19,28},{20,29},{21,30},{22,31}} | collective-permute-start | bytes 49160 | tf_op jit(solution)/shard_map/ppermute | solution.py:931
  16.3 1.3 %collective-permute-start.5 = (bf16[64,128]{1,0:T(8,128)(2,1)S(1)}, bf16[64,128]{1,0:T(8,128)(2,1)S(1)}, u32[]{:S(2)}, u32[]{:S(2)}) collective-permute-start(bf16[64,128]{1,0:T(8,128)(2,1)S(1)} %get-tuple-element.57), channel_id=1, source_target_pairs={{17,24},{18,25},{19,26},{20,27},{21,28},{22,29},{23,30}} | collective-permute-start | bytes 49160 | tf_op jit(solution)/shard_map/ppermute | solution.py:934
  17.6 0.0 collective-permute-done.2.refs_0_
  17.7 0.7 %collective-permute-start.12 = (bf16[384,256]{1,0:T(8,128)(2,1)S(1)}, bf16[384,256]{1,0:T(8,128)(2,1)S(1)}, u32[]{:S(2)}, u32[]{:S(2)}) collective-permute-start(bf16[384,256]{1,0:T(8,128)(2,1)S(1)} %add_convert_fusion.after), channel_id=1, source_target_pairs={{0,16},{1,17},{2,18},{3,19},{4,20},{5,21},{6,22},{7,23}} | collective-permute-start | bytes 589832 | tf_op jit(solution)/shard_map/ppermute | solution.py:944
  18.3 1.3 %collective-permute-start.11 = (bf16[384,256]{1,0:T(8,128)(2,1)S(1)}, bf16[384,256]{1,0:T(8,128)(2,1)S(1)}, u32[]{:S(2)}, u32[]{:S(2)}) collective-permute-start(bf16[384,256]{1,0:T(8,128)(2,1)S(1)} %add_convert_fusion.after), channel_id=1, source_target_pairs={{8,24},{9,25},{10,26},{11,27},{12,28},{13,29},{14,30},{15,31}} | collective-permute-start | bytes 589832 | tf_op jit(solution)/shard_map/ppermute | solution.py:946
  19.6 1.8 %collective-permute-done.4.after_up.up_b = bf16[64,128]{1,0:T(8,128)(2,1)S(1)} collective-permute-done((bf16[64,128]{1,0:T(8,128)(2,1)S(1)}, bf16[64,128]{1,0:T(8,128)(2,1)S(1)}, u32[]{:S(2)}, u32[]{:S(2)}) %collective-permute-start.4) | collective-permute-done | bytes 16416 | tf_op jit(solution)/shard_map/ppermute | solution.py:931
  21.5 1.3 %collective-permute-start.6 = (bf16[400,256]{1,0:T(8,128)(2,1)S(1)}, bf16[400,256]{1,0:T(8,128)(2,1)S(1)}, u32[]{:S(2)}, u32[]{:S(2)}) collective-permute-start(bf16[400,256]{1,0:T(8,128)(2,1)S(1)} %fusion.sums), channel_id=1, source_target_pairs={{16,24},{17,25},{18,26},{19,27},{20,28},{21,29},{22,30},{23,31}} | collective-permute-start | bytes 614408 | tf_op jit(solution)/shard_map/ppermute | solution.py:945
  22.7 1.0 %collective-permute-done.5.after_down.down_b = bf16[64,128]{1,0:T(8,128)(2,1)S(1)} collective-permute-done((bf16[64,128]{1,0:T(8,128)(2,1)S(1)}, bf16[64,128]{1,0:T(8,128)(2,1)S(1)}, u32[]{:S(2)}, u32[]{:S(2)}) %collective-permute-start.5) | collective-permute-done | bytes 16416 | tf_op jit(solution)/shard_map/ppermute | solution.py:934
  23.8 1.1 %shard_map.117 = (f32[5,256,128]{2,1,0:T(8,128)}, f32[3,256,128]{2,1,0:T(8,128)}, f32[400,256]{1,0:T(8,128)S(1)}) custom-call(f32[5,256,128]{2,1,0:T(8,128)S(1)} %bitcast.13, f32[256,128]{1,0:T(8,128)S(1)} %bitcast.21, f32[3,256,128]{2,1,0:T(8,128)S(1)} %bitcast.16, f32[320,384]{1,0:T(8,128)S(1)} %get-tuple-element.50.state, ...), custom_call_target="tpu_custom_call" | custom-call | flops 1000000000 | tf_op jit(solution)/shard_map/pallas_call | solution.py:769
  24.8 0.0 collective-permute-done.7
  24.8 0.1 fusion.2.sums
  24.9 1.3 %collective-permute-start.8 = (bf16[400,256]{1,0:T(8,128)(2,1)S(1)}, bf16[400,256]{1,0:T(8,128)(2,1)S(1)}, u32[]{:S(2)}, u32[]{:S(2)}) collective-permute-start(bf16[400,256]{1,0:T(8,128)(2,1)S(1)} %fusion.2.sums), channel_id=1, source_target_pairs={{8,24},{9,25},{10,26},{11,27},{12,28},{13,29},{14,30},{15,31}} | collective-permute-start | bytes 614408 | tf_op jit(solution)/shard_map/ppermute | solution.py:955
  26.2 0.1 shard_map.118
  26.3 0.0 collective-permute-done.12.refs_1_
  26.4 1.3 %collective-permute-start.13 = (bf16[384,256]{1,0:T(8,128)(2,1)S(1)}, bf16[384,256]{1,0:T(8,128)(2,1)S(1)}, u32[]{:S(2)}, u32[]{:S(2)}) collective-permute-start(bf16[384,256]{1,0:T(8,128)(2,1)S(1)} %shard_map.120), channel_id=1, source_target_pairs={{16,24},{17,25},{18,26},{19,27},{20,28},{21,29},{22,30},{23,31}} | collective-permute-start | bytes 589832 | tf_op jit(solution)/shard_map/ppermute | solution.py:964
  27.7 1.3 %collective-permute-start.10 = (bf16[64,128]{1,0:T(8,128)(2,1)S(1)}, bf16[64,128]{1,0:T(8,128)(2,1)S(1)}, u32[]{:S(2)}, u32[]{:S(2)}) collective-permute-start(bf16[64,128]{1,0:T(8,128)(2,1)S(1)} %get-tuple-element.65), channel_id=1, source_target_pairs={{9,24},{10,25},{11,26},{12,27},{13,28},{14,29},{15,30}} | collective-permute-start | bytes 49160 | tf_op jit(solution)/shard_map/ppermute | solution.py:934
  29.0 0.0 collective-permute-done.11.after.source_b
  29.0 1.3 %collective-permute-start.9 = (bf16[64,128]{1,0:T(8,128)(2,1)S(1)}, bf16[64,128]{1,0:T(8,128)(2,1)S(1)}, u32[]{:S(2)}, u32[]{:S(2)}) collective-permute-start(bf16[64,128]{1,0:T(8,128)(2,1)S(1)} %get-tuple-element.64.refs_2_), channel_id=1, source_target_pairs={{8,25},{9,26},{10,27},{11,28},{12,29},{13,30},{14,31}} | collective-permute-start | bytes 49160 | tf_op jit(solution)/shard_map/ppermute | solution.py:931
  30.3 0.0 collective-permute-done.6.source_a
  30.3 3.4 %collective-permute-done.10.down_a = bf16[64,128]{1,0:T(8,128)(2,1)S(1)} collective-permute-done((bf16[64,128]{1,0:T(8,128)(2,1)S(1)}, bf16[64,128]{1,0:T(8,128)(2,1)S(1)}, u32[]{:S(2)}, u32[]{:S(2)}) %collective-permute-start.10) | collective-permute-done | bytes 16416 | tf_op jit(solution)/shard_map/ppermute | solution.py:934
  33.7 0.9 %collective-permute-done.9.up_a = bf16[64,128]{1,0:T(8,128)(2,1)S(1)} collective-permute-done((bf16[64,128]{1,0:T(8,128)(2,1)S(1)}, bf16[64,128]{1,0:T(8,128)(2,1)S(1)}, u32[]{:S(2)}, u32[]{:S(2)}) %collective-permute-start.9) | collective-permute-done | bytes 16416 | tf_op jit(solution)/shard_map/ppermute | solution.py:931
  34.6 0.0 collective-permute-done.8.source_b
  34.6 2.0 %shard_map.119 = (f32[512,128]{1,0:T(8,128)S(1)}, f32[3,512,128]{2,1,0:T(8,128)S(1)}, f32[8,256]{1,0:T(8,128)S(1)}) custom-call(f32[1024,128]{1,0:T(8,128)S(1)} %get-tuple-element.60.base, f32[3,1024,128]{2,1,0:T(8,128)S(1)} %get-tuple-element.61.grads, bf16[6,384,256]{2,1,0:T(8,128)(2,1)S(1)} %get-tuple-element.62.hot_two, s32[6,1,256]{2,1,0:T(1,128)S(1)} %bitcast.27, ...), custom_call_target="tpu_custom_call" | custom-call | flops 1000000000 | tf_op jit(solution)/shard_map/pallas_call | solution.py:769
  36.6 0.0 collective-permute-done.13.source_a
  36.6 0.9 %shard_map.121 = f32[4,64,256]{2,1,0:T(8,128)} custom-call(f32[4,64,256]{2,1,0:T(8,128)S(1)} %bitcast.24, f32[512,128]{1,0:T(8,128)S(1)} %get-tuple-element.66.base, f32[3,512,128]{2,1,0:T(8,128)S(1)} %get-tuple-element.67.grads, f32[8,256]{1,0:T(8,128)S(1)} %get-tuple-element.68.scale, bf16[384,256]{1,0:T(8,128)(2,1)S(1)} %collective-permute-done.13.source_a, ...), custom_call_target="tpu_custom_call" | custom-call | flops 100000000 | bytes 1974272 | tf_op jit(solution)/shard_map/pallas_call | solution.py:769
  (11 shorter events, 0.1 us)
Async XLA Ops:
  0.6 5.7 %copy-start = (f32[1,5,256,128]{3,2,1,0:T(8,128)S(1)}, f32[1,5,256,128]{3,2,1,0:T(8,128)}, u32[]{:S(2)}) copy-start(f32[1,5,256,128]{3,2,1,0:T(8,128)} %param.9) | copy-start | bytes 1966084
  0.6 5.7 %copy-start.2 = (f32[1,256,128]{2,1,0:T(8,128)S(1)}, f32[1,256,128]{2,1,0:T(8,128)}, u32[]{:S(2)}) copy-start(f32[1,256,128]{2,1,0:T(8,128)} %param.11) | copy-start | bytes 393220
  0.7 5.7 %copy-start.7 = (s32[1,4,256]{2,1,0:T(4,128)S(1)}, s32[1,4,256]{2,1,0:T(4,128)}, u32[]{:S(2)}) copy-start(s32[1,4,256]{2,1,0:T(4,128)} %param.12) | copy-start | bytes 12292
  0.7 5.7 %copy-start.8 = (s32[1,256]{1,0:T(1,128)S(1)}, s32[1,256]{1,0:T(1,128)}, u32[]{:S(2)}) copy-start(s32[1,256]{1,0:T(1,128)} %target.1) | copy-start | bytes 3076
  0.7 8.1 %copy-start.1 = (f32[1,3,256,128]{3,2,1,0:T(8,128)S(1)}, f32[1,3,256,128]{3,2,1,0:T(8,128)}, u32[]{:S(2)}) copy-start(f32[1,3,256,128]{3,2,1,0:T(8,128)} %param.10) | copy-start | bytes 1179652
  0.7 8.1 %copy-start.3 = (f32[1,4,64,256]{3,2,1,0:T(8,128)S(1)}, f32[1,4,64,256]{3,2,1,0:T(8,128)}, u32[]{:S(2)}) copy-start(f32[1,4,64,256]{3,2,1,0:T(8,128)} %param.15) | copy-start | bytes 786436
  0.7 8.1 %copy-start.4 = (f32[64,128]{1,0:T(8,128)S(1)}, f32[64,128]{1,0:T(8,128)}, u32[]{:S(2)}) copy-start(f32[64,128]{1,0:T(8,128)} %projector.3) | copy-start | bytes 98308
  0.7 8.1 %copy-start.5 = (s32[1,6,256]{2,0,1:T(1,128)S(1)}, s32[1,6,256]{2,0,1:T(1,128)}, u32[]{:S(2)}) copy-start(s32[1,6,256]{2,0,1:T(1,128)} %param.16) | copy-start | bytes 18436
  0.7 8.1 %copy-start.6 = (s32[1,6,256]{2,0,1:T(1,128)S(1)}, s32[1,6,256]{2,0,1:T(1,128)}, u32[]{:S(2)}) copy-start(s32[1,6,256]{2,0,1:T(1,128)} %param.17) | copy-start | bytes 18436
  2.5 6.2 %collective-permute-start = (bf16[304,128]{1,0:T(8,128)(2,1)}, bf16[304,128]{1,0:T(8,128)(2,1)S(1)}, u32[]{:S(2)}, u32[]{:S(2)}) collective-permute-start(bf16[304,128]{1,0:T(8,128)(2,1)} %get-tuple-element.36), channel_id=1, source_target_pairs={{1,2},{2,1},{3,4},{4,3},{5,6},{6,5},{9,10},{10,9},{11,12},{12,11},... | collective-permute-start | bytes 233480 | tf_op jit(solution)/shard_map/ppermute | solution.py:827
  6.3 2.4 %collective-permute-start.1 = (bf16[304,128]{1,0:T(8,128)(2,1)}, bf16[304,128]{1,0:T(8,128)(2,1)S(1)}, u32[]{:S(2)}, u32[]{:S(2)}) collective-permute-start(bf16[304,128]{1,0:T(8,128)(2,1)} %get-tuple-element.37), channel_id=1, source_target_pairs={{0,1},{1,0},{2,3},{3,2},{4,5},{5,4},{6,7},{7,6},{8,9},{9,8},{10,11... | collective-permute-start | bytes 233480 | tf_op jit(solution)/shard_map/ppermute | solution.py:828
  12.7 1.4 %collective-permute-start.3 = (bf16[400,256]{1,0:T(8,128)(2,1)S(1)}, bf16[400,256]{1,0:T(8,128)(2,1)S(1)}, u32[]{:S(2)}, u32[]{:S(2)}) collective-permute-start(bf16[400,256]{1,0:T(8,128)(2,1)S(1)} %get-tuple-element.55), channel_id=1, source_target_pairs={{0,1},{1,2},{2,3},{3,4},{4,5},{5,6},{6,7},{8,9},{9,10},{10,11},{11... | collective-permute-start | bytes 614408 | tf_op jit(solution)/shard_map/ppermute | solution.py:891
  13.4 4.2 %collective-permute-start.2 = (bf16[384,256]{1,0:T(8,128)(2,1)S(1)}, bf16[384,256]{1,0:T(8,128)(2,1)S(1)}, u32[]{:S(2)}, u32[]{:S(2)}) collective-permute-start(bf16[384,256]{1,0:T(8,128)(2,1)S(1)} %get-tuple-element.53), channel_id=1, source_target_pairs={{0,1},{1,2},{2,3},{3,4},{4,5},{5,6},{6,7},{8,9},{9,10},{10,11},{11... | collective-permute-start | bytes 589832 | tf_op jit(solution)/shard_map/ppermute | solution.py:891
  14.3 10.5 %collective-permute-start.7 = (bf16[400,256]{1,0:T(8,128)(2,1)S(1)}, bf16[400,256]{1,0:T(8,128)(2,1)S(1)}, u32[]{:S(2)}, u32[]{:S(2)}) collective-permute-start(bf16[400,256]{1,0:T(8,128)(2,1)S(1)} %fusion.sums), channel_id=1, source_target_pairs={{0,8},{1,9},{2,10},{3,11},{4,12},{5,13},{6,14},{7,15}} | collective-permute-start | bytes 614408 | tf_op jit(solution)/shard_map/ppermute | solution.py:941
  15.0 6.5 %collective-permute-start.4 = (bf16[64,128]{1,0:T(8,128)(2,1)S(1)}, bf16[64,128]{1,0:T(8,128)(2,1)S(1)}, u32[]{:S(2)}, u32[]{:S(2)}) collective-permute-start(bf16[64,128]{1,0:T(8,128)(2,1)S(1)} %get-tuple-element.56), channel_id=1, source_target_pairs={{16,25},{17,26},{18,27},{19,28},{20,29},{21,30},{22,31}} | collective-permute-start | bytes 49160 | tf_op jit(solution)/shard_map/ppermute | solution.py:931
  16.3 7.5 %collective-permute-start.5 = (bf16[64,128]{1,0:T(8,128)(2,1)S(1)}, bf16[64,128]{1,0:T(8,128)(2,1)S(1)}, u32[]{:S(2)}, u32[]{:S(2)}) collective-permute-start(bf16[64,128]{1,0:T(8,128)(2,1)S(1)} %get-tuple-element.57), channel_id=1, source_target_pairs={{17,24},{18,25},{19,26},{20,27},{21,28},{22,29},{23,30}} | collective-permute-start | bytes 49160 | tf_op jit(solution)/shard_map/ppermute | solution.py:934
  17.7 8.7 %collective-permute-start.12 = (bf16[384,256]{1,0:T(8,128)(2,1)S(1)}, bf16[384,256]{1,0:T(8,128)(2,1)S(1)}, u32[]{:S(2)}, u32[]{:S(2)}) collective-permute-start(bf16[384,256]{1,0:T(8,128)(2,1)S(1)} %add_convert_fusion.after), channel_id=1, source_target_pairs={{0,16},{1,17},{2,18},{3,19},{4,20},{5,21},{6,22},{7,23}} | collective-permute-start | bytes 589832 | tf_op jit(solution)/shard_map/ppermute | solution.py:944
  18.3 10.6 %collective-permute-start.11 = (bf16[384,256]{1,0:T(8,128)(2,1)S(1)}, bf16[384,256]{1,0:T(8,128)(2,1)S(1)}, u32[]{:S(2)}, u32[]{:S(2)}) collective-permute-start(bf16[384,256]{1,0:T(8,128)(2,1)S(1)} %add_convert_fusion.after), channel_id=1, source_target_pairs={{8,24},{9,25},{10,26},{11,27},{12,28},{13,29},{14,30},{15,31}} | collective-permute-start | bytes 589832 | tf_op jit(solution)/shard_map/ppermute | solution.py:946
  21.5 8.8 %collective-permute-start.6 = (bf16[400,256]{1,0:T(8,128)(2,1)S(1)}, bf16[400,256]{1,0:T(8,128)(2,1)S(1)}, u32[]{:S(2)}, u32[]{:S(2)}) collective-permute-start(bf16[400,256]{1,0:T(8,128)(2,1)S(1)} %fusion.sums), channel_id=1, source_target_pairs={{16,24},{17,25},{18,26},{19,27},{20,28},{21,29},{22,30},{23,31}} | collective-permute-start | bytes 614408 | tf_op jit(solution)/shard_map/ppermute | solution.py:945
  24.9 9.7 %collective-permute-start.8 = (bf16[400,256]{1,0:T(8,128)(2,1)S(1)}, bf16[400,256]{1,0:T(8,128)(2,1)S(1)}, u32[]{:S(2)}, u32[]{:S(2)}) collective-permute-start(bf16[400,256]{1,0:T(8,128)(2,1)S(1)} %fusion.2.sums), channel_id=1, source_target_pairs={{8,24},{9,25},{10,26},{11,27},{12,28},{13,29},{14,30},{15,31}} | collective-permute-start | bytes 614408 | tf_op jit(solution)/shard_map/ppermute | solution.py:955
  26.4 10.3 %collective-permute-start.13 = (bf16[384,256]{1,0:T(8,128)(2,1)S(1)}, bf16[384,256]{1,0:T(8,128)(2,1)S(1)}, u32[]{:S(2)}, u32[]{:S(2)}) collective-permute-start(bf16[384,256]{1,0:T(8,128)(2,1)S(1)} %shard_map.120), channel_id=1, source_target_pairs={{16,24},{17,25},{18,26},{19,27},{20,28},{21,29},{22,30},{23,31}} | collective-permute-start | bytes 589832 | tf_op jit(solution)/shard_map/ppermute | solution.py:964
  27.7 6.1 %collective-permute-start.10 = (bf16[64,128]{1,0:T(8,128)(2,1)S(1)}, bf16[64,128]{1,0:T(8,128)(2,1)S(1)}, u32[]{:S(2)}, u32[]{:S(2)}) collective-permute-start(bf16[64,128]{1,0:T(8,128)(2,1)S(1)} %get-tuple-element.65), channel_id=1, source_target_pairs={{9,24},{10,25},{11,26},{12,27},{13,28},{14,29},{15,30}} | collective-permute-start | bytes 49160 | tf_op jit(solution)/shard_map/ppermute | solution.py:934
  29.0 5.6 %collective-permute-start.9 = (bf16[64,128]{1,0:T(8,128)(2,1)S(1)}, bf16[64,128]{1,0:T(8,128)(2,1)S(1)}, u32[]{:S(2)}, u32[]{:S(2)}) collective-permute-start(bf16[64,128]{1,0:T(8,128)(2,1)S(1)} %get-tuple-element.64.refs_2_), channel_id=1, source_target_pairs={{8,25},{9,26},{10,27},{11,28},{12,29},{13,30},{14,31}} | collective-permute-start | bytes 49160 | tf_op jit(solution)/shard_map/ppermute | solution.py:931

commit v9 on v8

--- a/solution.py
+++ b/solution.py
@@ -21,7 +21,7 @@
 ALL_FIELDS = ((0, 2), (2, 4), (4, 5))
 BASE = 32.0
 EXTRA = 16
-PACK_COST, SECOND_COST, OUTPUT_COST, SOUND_COST = 10**10, 10**10, 10**9, 10**9
+PACK_COST, SECOND_COST, OUTPUT_COST, SOUND_COST = 10**10, 10**10, 10**9, 2 * 10**9
 VMEM_LIMIT = 20 * 1024 * 1024
 PACK_LIMIT = 60 * 1024 * 1024
 
@@ -359,7 +359,7 @@
 def first_kernel(
     flow, visc, mean, projector, part_a, part_b, sound, neighbours, codes,
     inner_state, inner_high, inner_low, lcol, inner_mats, hits,
-    own_one, next_one, mean_one, base, grads, hot_two,
+    own_one, next_one, mean_one, base, grads,
     edge_state, edge_high, edge_low, edge_mats, edge_visc,
     square, state0, high0, low0, zero, packed, pay, rows_of, facing, remote, rhs,
 ):
@@ -459,9 +459,6 @@
             )
             hot = hot_columns(jnp.where(valid, place, -1), elements + 2 * LANES)
             remote_rows([facing[face, at] for at in range(4)], hot, remote, face)
-            near = link - first
-            place = jnp.where(near < 0, elements + LANES + near, near)
-            hot_two[face] = hot_columns(jnp.where(link < 0, -1, place), elements + LANES)
             masks.append(
                 (
                     face_masks(link[:, :LANES], link[:, LANES:], code[:, :LANES], code[:, LANES:]),
@@ -587,6 +584,10 @@
 
 def node_of(rows_of, start, nodes, n):
     return rows_of[pl.ds(start + n, 8, stride=nodes), :]
+
+
+def taken(x, at):
+    return jnp.take_along_axis(x, at, axis=1, mode="promise_in_bounds")
 
 
 def remote_rows(parts, hot, remote, face):
@@ -707,7 +708,7 @@
 
 
 def sound_one_kernel(
-    base, grads, hot_two, neighbours, codes, source_a, source_b, up_a, down_a, up_b, down_b, after,
+    base, grads, neighbours, codes, source_a, source_b, up_a, down_a, up_b, down_b, after,
     base_two, grads_two, scale_out, rows_of, facing, remote, rhs,
 ):
     elements = source_a.shape[1]
@@ -732,10 +733,16 @@
         for face in range(6):
             for part in range(halves + 1):
                 facing_rows(rows_of, part * block, nodes, face ^ 1, facing.at[face, part])
-            remote_rows(
-                [facing[face, part] for part in range(halves + 1)], hot_two[face], remote, face
-            )
             link, code = neighbours[face], codes[face]
+            near = link - lax.axis_index("sfc") * elements
+            for h in range(halves):
+                here = near[:, columns_of(h)]
+                at = jnp.broadcast_to(here & (LANES - 1), (64, LANES))
+                got = taken(facing[face, halves], at)
+                for part in range(halves):
+                    inside = (here >= part * LANES) & (here < (part + 1) * LANES)
+                    got = jnp.where(inside, taken(facing[face, part], at), got)
+                remote[face, h * 64 : (h + 1) * 64, :] = got
             masks.append(
                 face_masks(link[:, :LANES], link[:, LANES:], code[:, :LANES], code[:, LANES:])
             )
@@ -848,7 +855,7 @@
     lines = 6 * nodes + EXTRA
     node_rows = vmem((nodes, 8, LANES), F32)
     (
-        own_one, next_one, mean_one, base, grads, hot_two,
+        own_one, next_one, mean_one, base, grads,
         edge_state, edge_high, edge_low, edge_mats, edge_visc,
     ) = call(
         first_kernel,
@@ -858,7 +865,6 @@
             shape(mean.shape, F32),
             shape(((halves + 2) * block, LANES), F32),
             shape((3, (halves + 2) * block, LANES), F32),
-            shape((6, elements + LANES, elements), BF16),
             shape((2 * rows, fields), F32),
             shape((2 * rows, fields), BF16),
             shape((2 * rows, fields), BF16),
@@ -977,7 +983,7 @@
             node_rows,
         ],
         [
-            base, grads, hot_two, neighbours, codes, one_2_to_3, one_1_to_3,
+            base, grads, neighbours, codes, one_2_to_3, one_1_to_3,
             *beside_1, *beside_2, two_1_to_3,
         ],
         cost=SOUND_COST,

time: 37.8 us -> 38.9 us (1.029)
  waiting for transfers between devices: 9.48 us -> 10.5 us
    ppermute x2, waiting for transfers between devices: 2.7 us -> 4.23 us  [borders(): lax.ppermute(up_border, ('grp', 'sfc'), [(start + i, last + i + 1) for i...]
    ppermute x2, waiting for transfers between devices: 4.46 us -> 3.05 us  [borders(): lax.ppermute(down_border, ('grp', 'sfc'), [(start + i, last + i - 1) for...]
    ppermute x1, waiting for transfers between devices: 0.01 us -> 0.95 us  [body(): two_2_to_3 = lax.ppermute(sum_two_2, 'grp', [(2, 3)])]
  transfers between devices with their start and end apart: 14 -> 14, of which waited for: 5 -> 6; matrix products, arithmetic and copies ran while one was open for 0% -> 0% of each run, Pallas kernels for 9% -> 9%
where the time goes in v9:
time: 38.9 us; the launch traced here: 38.5 us
  starting transfers between devices  16.9 us (43%)
  waiting for transfers between devices  10.5 us (27%)
  Pallas kernels  9.9 us (25%)
  between operations  1 us (3%)
    pallas_call x10, Pallas kernels, call(): pl.pallas_call(kernel, out_shape=tuple(outs), in_specs=[pl.BlockSpec(memo...  9.9 us
    ppermute x2, waiting for transfers between devices, borders(): lax.ppermute(up_border, ('grp', 'sfc'), [(start + i, last + i + 1) for i...  4.23 us
    ppermute x1, starting transfers between devices, body(): part_a = lax.ppermute(pack_a, 'sfc', pairs_a)  3.76 us
    ppermute x2, waiting for transfers between devices, borders(): lax.ppermute(down_border, ('grp', 'sfc'), [(start + i, last + i - 1) for...  3.05 us
    ppermute x2, starting transfers between devices, borders(): lax.ppermute(up_border, ('grp', 'sfc'), [(start + i, last + i + 1) for i...  2.58 us
    ppermute x2, starting transfers between devices, borders(): lax.ppermute(down_border, ('grp', 'sfc'), [(start + i, last + i - 1) for...  2.58 us
    ppermute x1, waiting for transfers between devices, body(): part_a = lax.ppermute(pack_a, 'sfc', pairs_a)  2.29 us
    ppermute x2, starting transfers between devices, climb(): return lax.ppermute(x, ('grp', 'sfc'), chosen)  1.35 us
  transfers between devices with their start and end apart: 14, of which 6 were waited for; matrix products, arithmetic and copies ran while one was open for 0% of the time, Pallas kernels for 9%

profile of v9, /device:TPU:15, one launch (start us, length us, event | category | flops | bytes accessed | tf_op | source)
XLA Modules:
  0.0 38.5 jit_solution(3357055009052319566)
XLA Ops:
  0.6 0.0 copy-start
  0.6 0.0 copy-start.2
  0.7 0.0 copy-start.7
  0.7 0.0 copy-start.8
  0.7 0.0 copy-start.1
  0.7 0.0 copy-start.3
  0.7 0.0 copy-start.4
  0.7 0.0 copy-start.5
  0.7 0.0 copy-start.6
  0.7 1.8 %shard_map.112 = (bf16[304,128]{1,0:T(8,128)(2,1)}, bf16[304,128]{1,0:T(8,128)(2,1)}) custom-call(f32[5,256,128]{2,1,0:T(8,128)} %bitcast.10, f32[256,128]{1,0:T(8,128)} %bitcast.17, s32[4,256]{1,0:T(4,128)} %bitcast.31, f32[4,64,256]{2,1,0:T(8,128)} %bitcast.22, s32[6,1,256]{2,1,0:T(1,128)} %bitcast.25, s32[6,1,256]{2,1,0:T(1,128)} %bitcast.28), custom_call_target="tpu_custom_call" | custom-call | flops 10000000000 | tf_op jit(solution)/shard_map/pallas_call | solution.py:776
  2.5 3.8 %collective-permute-start = (bf16[304,128]{1,0:T(8,128)(2,1)}, bf16[304,128]{1,0:T(8,128)(2,1)S(1)}, u32[]{:S(2)}, u32[]{:S(2)}) collective-permute-start(bf16[304,128]{1,0:T(8,128)(2,1)} %get-tuple-element.35), channel_id=1, source_target_pairs={{1,2},{2,1},{3,4},{4,3},{5,6},{6,5},{9,10},{10,9},{11,12},{12,11},... | collective-permute-start | bytes 233480 | tf_op jit(solution)/shard_map/ppermute | solution.py:834
  6.3 0.1 collective-permute-start.1
  6.4 2.3 %collective-permute-done.part_a = bf16[304,128]{1,0:T(8,128)(2,1)S(1)} collective-permute-done((bf16[304,128]{1,0:T(8,128)(2,1)}, bf16[304,128]{1,0:T(8,128)(2,1)S(1)}, u32[]{:S(2)}, u32[]{:S(2)}) %collective-permute-start) | collective-permute-done | bytes 77856 | tf_op jit(solution)/shard_map/ppermute | solution.py:834
  8.7 0.0 collective-permute-done.1.part_b
  8.7 0.0 copy-done.4
  8.8 0.0 copy-done.5
  8.8 3.8 %shard_map.114 = (f32[400,256]{1,0:T(8,128)S(1)}, bf16[400,256]{1,0:T(8,128)(2,1)S(1)}, f32[3,256,128]{2,1,0:T(8,128)S(1)}, f32[1024,128]{1,0:T(8,128)S(1)}, f32...) custom-call(f32[5,256,128]{2,1,0:T(8,128)S(1)} %bitcast.12, ...), custom_call_target="tpu_custom_call" | custom-call | flops 100000000 | bytes 7290880 | tf_op jit(solution)/shard_map/pallas_call | solution.py:776
  12.6 0.7 %collective-permute-start.3 = (bf16[400,256]{1,0:T(8,128)(2,1)S(1)}, bf16[400,256]{1,0:T(8,128)(2,1)S(1)}, u32[]{:S(2)}, u32[]{:S(2)}) collective-permute-start(bf16[400,256]{1,0:T(8,128)(2,1)S(1)} %get-tuple-element.54), channel_id=1, source_target_pairs={{0,1},{1,2},{2,3},{3,4},{4,5},{5,6},{6,7},{8,9},{9,10},{10,11},{11... | collective-permute-start | bytes 614408 | tf_op jit(solution)/shard_map/ppermute | solution.py:897
  13.3 0.1 shard_map.115
  13.3 0.7 %collective-permute-start.2 = (bf16[384,256]{1,0:T(8,128)(2,1)S(1)}, bf16[384,256]{1,0:T(8,128)(2,1)S(1)}, u32[]{:S(2)}, u32[]{:S(2)}) collective-permute-start(bf16[384,256]{1,0:T(8,128)(2,1)S(1)} %get-tuple-element.52), channel_id=1, source_target_pairs={{0,1},{1,2},{2,3},{3,4},{4,5},{5,6},{6,7},{8,9},{9,10},{10,11},{11... | collective-permute-start | bytes 589832 | tf_op jit(solution)/shard_map/ppermute | solution.py:897
  14.0 0.0 collective-permute-done.3
  14.1 0.1 shard_map.116
  14.2 0.7 %collective-permute-start.7 = (bf16[400,256]{1,0:T(8,128)(2,1)S(1)}, bf16[400,256]{1,0:T(8,128)(2,1)S(1)}, u32[]{:S(2)}, u32[]{:S(2)}) collective-permute-start(bf16[400,256]{1,0:T(8,128)(2,1)S(1)} %fusion.sums), channel_id=1, source_target_pairs={{0,8},{1,9},{2,10},{3,11},{4,12},{5,13},{6,14},{7,15}} | collective-permute-start | bytes 614408 | tf_op jit(solution)/shard_map/ppermute | solution.py:947
  14.9 1.3 %collective-permute-start.4 = (bf16[64,128]{1,0:T(8,128)(2,1)S(1)}, bf16[64,128]{1,0:T(8,128)(2,1)S(1)}, u32[]{:S(2)}, u32[]{:S(2)}) collective-permute-start(bf16[64,128]{1,0:T(8,128)(2,1)S(1)} %get-tuple-element.55), channel_id=1, source_target_pairs={{16,25},{17,26},{18,27},{19,28},{20,29},{21,30},{22,31}} | collective-permute-start | bytes 49160 | tf_op jit(solution)/shard_map/ppermute | solution.py:937
  16.2 1.3 %collective-permute-start.5 = (bf16[64,128]{1,0:T(8,128)(2,1)S(1)}, bf16[64,128]{1,0:T(8,128)(2,1)S(1)}, u32[]{:S(2)}, u32[]{:S(2)}) collective-permute-start(bf16[64,128]{1,0:T(8,128)(2,1)S(1)} %get-tuple-element.56), channel_id=1, source_target_pairs={{17,24},{18,25},{19,26},{20,27},{21,28},{22,29},{23,30}} | collective-permute-start | bytes 49160 | tf_op jit(solution)/shard_map/ppermute | solution.py:940
  17.5 0.0 collective-permute-done.2.refs_0_
  17.5 0.7 %collective-permute-start.12 = (bf16[384,256]{1,0:T(8,128)(2,1)S(1)}, bf16[384,256]{1,0:T(8,128)(2,1)S(1)}, u32[]{:S(2)}, u32[]{:S(2)}) collective-permute-start(bf16[384,256]{1,0:T(8,128)(2,1)S(1)} %add_convert_fusion.after), channel_id=1, source_target_pairs={{0,16},{1,17},{2,18},{3,19},{4,20},{5,21},{6,22},{7,23}} | collective-permute-start | bytes 589832 | tf_op jit(solution)/shard_map/ppermute | solution.py:950
  18.2 1.3 %collective-permute-start.11 = (bf16[384,256]{1,0:T(8,128)(2,1)S(1)}, bf16[384,256]{1,0:T(8,128)(2,1)S(1)}, u32[]{:S(2)}, u32[]{:S(2)}) collective-permute-start(bf16[384,256]{1,0:T(8,128)(2,1)S(1)} %add_convert_fusion.after), channel_id=1, source_target_pairs={{8,24},{9,25},{10,26},{11,27},{12,28},{13,29},{14,30},{15,31}} | collective-permute-start | bytes 589832 | tf_op jit(solution)/shard_map/ppermute | solution.py:952
  19.5 1.9 %collective-permute-done.4.after_up.up_b = bf16[64,128]{1,0:T(8,128)(2,1)S(1)} collective-permute-done((bf16[64,128]{1,0:T(8,128)(2,1)S(1)}, bf16[64,128]{1,0:T(8,128)(2,1)S(1)}, u32[]{:S(2)}, u32[]{:S(2)}) %collective-permute-start.4) | collective-permute-done | bytes 16416 | tf_op jit(solution)/shard_map/ppermute | solution.py:937
  21.5 1.3 %collective-permute-start.6 = (bf16[400,256]{1,0:T(8,128)(2,1)S(1)}, bf16[400,256]{1,0:T(8,128)(2,1)S(1)}, u32[]{:S(2)}, u32[]{:S(2)}) collective-permute-start(bf16[400,256]{1,0:T(8,128)(2,1)S(1)} %fusion.sums), channel_id=1, source_target_pairs={{16,24},{17,25},{18,26},{19,27},{20,28},{21,29},{22,30},{23,31}} | collective-permute-start | bytes 614408 | tf_op jit(solution)/shard_map/ppermute | solution.py:951
  22.7 1.0 %collective-permute-done.5.after_down.down_b = bf16[64,128]{1,0:T(8,128)(2,1)S(1)} collective-permute-done((bf16[64,128]{1,0:T(8,128)(2,1)S(1)}, bf16[64,128]{1,0:T(8,128)(2,1)S(1)}, u32[]{:S(2)}, u32[]{:S(2)}) %collective-permute-start.5) | collective-permute-done | bytes 16416 | tf_op jit(solution)/shard_map/ppermute | solution.py:940
  23.8 1.1 %shard_map.117 = (f32[5,256,128]{2,1,0:T(8,128)}, f32[3,256,128]{2,1,0:T(8,128)}, f32[400,256]{1,0:T(8,128)S(1)}) custom-call(f32[5,256,128]{2,1,0:T(8,128)S(1)} %bitcast.13, f32[256,128]{1,0:T(8,128)S(1)} %bitcast.21, f32[3,256,128]{2,1,0:T(8,128)S(1)} %bitcast.16, f32[320,384]{1,0:T(8,128)S(1)} %get-tuple-element.49.state, ...), custom_call_target="tpu_custom_call" | custom-call | flops 1000000000 | tf_op jit(solution)/shard_map/pallas_call | solution.py:776
  24.8 0.0 collective-permute-done.7
  24.8 0.1 fusion.2.sums
  24.9 1.3 %collective-permute-start.8 = (bf16[400,256]{1,0:T(8,128)(2,1)S(1)}, bf16[400,256]{1,0:T(8,128)(2,1)S(1)}, u32[]{:S(2)}, u32[]{:S(2)}) collective-permute-start(bf16[400,256]{1,0:T(8,128)(2,1)S(1)} %fusion.2.sums), channel_id=1, source_target_pairs={{8,24},{9,25},{10,26},{11,27},{12,28},{13,29},{14,30},{15,31}} | collective-permute-start | bytes 614408 | tf_op jit(solution)/shard_map/ppermute | solution.py:961
  26.2 0.1 shard_map.118
  26.3 1.3 %collective-permute-start.10 = (bf16[64,128]{1,0:T(8,128)(2,1)S(1)}, bf16[64,128]{1,0:T(8,128)(2,1)S(1)}, u32[]{:S(2)}, u32[]{:S(2)}) collective-permute-start(bf16[64,128]{1,0:T(8,128)(2,1)S(1)} %get-tuple-element.63), channel_id=1, source_target_pairs={{9,24},{10,25},{11,26},{12,27},{13,28},{14,29},{15,30}} | collective-permute-start | bytes 49160 | tf_op jit(solution)/shard_map/ppermute | solution.py:940
  27.6 0.0 collective-permute-done.12.refs_1_
  27.6 1.3 %collective-permute-start.9 = (bf16[64,128]{1,0:T(8,128)(2,1)S(1)}, bf16[64,128]{1,0:T(8,128)(2,1)S(1)}, u32[]{:S(2)}, u32[]{:S(2)}) collective-permute-start(bf16[64,128]{1,0:T(8,128)(2,1)S(1)} %get-tuple-element.62.refs_2_), channel_id=1, source_target_pairs={{8,25},{9,26},{10,27},{11,28},{12,29},{13,30},{14,31}} | collective-permute-start | bytes 49160 | tf_op jit(solution)/shard_map/ppermute | solution.py:937
  29.0 0.0 collective-permute-done.11.after.source_b
  29.0 1.3 %collective-permute-start.13 = (bf16[384,256]{1,0:T(8,128)(2,1)S(1)}, bf16[384,256]{1,0:T(8,128)(2,1)S(1)}, u32[]{:S(2)}, u32[]{:S(2)}) collective-permute-start(bf16[384,256]{1,0:T(8,128)(2,1)S(1)} %shard_map.120), channel_id=1, source_target_pairs={{16,24},{17,25},{18,26},{19,27},{20,28},{21,29},{22,30},{23,31}} | collective-permute-start | bytes 589832 | tf_op jit(solution)/shard_map/ppermute | solution.py:970
  30.3 0.0 collective-permute-done.6.source_a
  30.3 2.0 %collective-permute-done.10.down_a = bf16[64,128]{1,0:T(8,128)(2,1)S(1)} collective-permute-done((bf16[64,128]{1,0:T(8,128)(2,1)S(1)}, bf16[64,128]{1,0:T(8,128)(2,1)S(1)}, u32[]{:S(2)}, u32[]{:S(2)}) %collective-permute-start.10) | collective-permute-done | bytes 16416 | tf_op jit(solution)/shard_map/ppermute | solution.py:940
  32.3 2.3 %collective-permute-done.9.up_a = bf16[64,128]{1,0:T(8,128)(2,1)S(1)} collective-permute-done((bf16[64,128]{1,0:T(8,128)(2,1)S(1)}, bf16[64,128]{1,0:T(8,128)(2,1)S(1)}, u32[]{:S(2)}, u32[]{:S(2)}) %collective-permute-start.9) | collective-permute-done | bytes 16416 | tf_op jit(solution)/shard_map/ppermute | solution.py:937
  34.6 0.0 collective-permute-done.8.source_b
  34.6 2.1 %shard_map.119 = (f32[512,128]{1,0:T(8,128)S(1)}, f32[3,512,128]{2,1,0:T(8,128)S(1)}, f32[8,256]{1,0:T(8,128)S(1)}) custom-call(f32[1024,128]{1,0:T(8,128)S(1)} %get-tuple-element.59.base, f32[3,1024,128]{2,1,0:T(8,128)S(1)} %get-tuple-element.60.grads, s32[6,1,256]{2,1,0:T(1,128)S(1)} %bitcast.27, s32[6,1,256]{2,1,0:T(1,128)S(1)} %bitcast.30, ...), custom_call_target="tpu_custom_call" | custom-call | flops 2000000000 | tf_op jit(solution)/shard_map/pallas_call | solution.py:776
  36.7 1.0 %collective-permute-done.13.source_a = bf16[384,256]{1,0:T(8,128)(2,1)S(1)} collective-permute-done((bf16[384,256]{1,0:T(8,128)(2,1)S(1)}, bf16[384,256]{1,0:T(8,128)(2,1)S(1)}, u32[]{:S(2)}, u32[]{:S(2)}) %collective-permute-start.13) | collective-permute-done | bytes 196640 | tf_op jit(solution)/shard_map/ppermute | solution.py:970
  37.7 0.8 %shard_map.121 = f32[4,64,256]{2,1,0:T(8,128)} custom-call(f32[4,64,256]{2,1,0:T(8,128)S(1)} %bitcast.24, f32[512,128]{1,0:T(8,128)S(1)} %get-tuple-element.64.base, f32[3,512,128]{2,1,0:T(8,128)S(1)} %get-tuple-element.65.grads, f32[8,256]{1,0:T(8,128)S(1)} %get-tuple-element.66.scale, bf16[384,256]{1,0:T(8,128)(2,1)S(1)} %collective-permute-done.13.source_a, ...), custom_call_target="tpu_custom_call" | custom-call | flops 100000000 | bytes 1974272 | tf_op jit(solution)/shard_map/pallas_call | solution.py:776
  (11 shorter events, 0.1 us)
Async XLA Ops:
  0.6 5.7 %copy-start = (f32[1,5,256,128]{3,2,1,0:T(8,128)S(1)}, f32[1,5,256,128]{3,2,1,0:T(8,128)}, u32[]{:S(2)}) copy-start(f32[1,5,256,128]{3,2,1,0:T(8,128)} %param.9) | copy-start | bytes 1966084
  0.6 5.7 %copy-start.2 = (f32[1,256,128]{2,1,0:T(8,128)S(1)}, f32[1,256,128]{2,1,0:T(8,128)}, u32[]{:S(2)}) copy-start(f32[1,256,128]{2,1,0:T(8,128)} %param.11) | copy-start | bytes 393220
  0.7 5.7 %copy-start.7 = (s32[1,4,256]{2,1,0:T(4,128)S(1)}, s32[1,4,256]{2,1,0:T(4,128)}, u32[]{:S(2)}) copy-start(s32[1,4,256]{2,1,0:T(4,128)} %param.12) | copy-start | bytes 12292
  0.7 5.7 %copy-start.8 = (s32[1,256]{1,0:T(1,128)S(1)}, s32[1,256]{1,0:T(1,128)}, u32[]{:S(2)}) copy-start(s32[1,256]{1,0:T(1,128)} %target.1) | copy-start | bytes 3076
  0.7 8.1 %copy-start.1 = (f32[1,3,256,128]{3,2,1,0:T(8,128)S(1)}, f32[1,3,256,128]{3,2,1,0:T(8,128)}, u32[]{:S(2)}) copy-start(f32[1,3,256,128]{3,2,1,0:T(8,128)} %param.10) | copy-start | bytes 1179652
  0.7 8.1 %copy-start.3 = (f32[1,4,64,256]{3,2,1,0:T(8,128)S(1)}, f32[1,4,64,256]{3,2,1,0:T(8,128)}, u32[]{:S(2)}) copy-start(f32[1,4,64,256]{3,2,1,0:T(8,128)} %param.15) | copy-start | bytes 786436
  0.7 8.1 %copy-start.4 = (f32[64,128]{1,0:T(8,128)S(1)}, f32[64,128]{1,0:T(8,128)}, u32[]{:S(2)}) copy-start(f32[64,128]{1,0:T(8,128)} %projector.3) | copy-start | bytes 98308
  0.7 8.1 %copy-start.5 = (s32[1,6,256]{2,0,1:T(1,128)S(1)}, s32[1,6,256]{2,0,1:T(1,128)}, u32[]{:S(2)}) copy-start(s32[1,6,256]{2,0,1:T(1,128)} %param.16) | copy-start | bytes 18436
  0.7 8.1 %copy-start.6 = (s32[1,6,256]{2,0,1:T(1,128)S(1)}, s32[1,6,256]{2,0,1:T(1,128)}, u32[]{:S(2)}) copy-start(s32[1,6,256]{2,0,1:T(1,128)} %param.17) | copy-start | bytes 18436
  2.5 6.2 %collective-permute-start = (bf16[304,128]{1,0:T(8,128)(2,1)}, bf16[304,128]{1,0:T(8,128)(2,1)S(1)}, u32[]{:S(2)}, u32[]{:S(2)}) collective-permute-start(bf16[304,128]{1,0:T(8,128)(2,1)} %get-tuple-element.35), channel_id=1, source_target_pairs={{1,2},{2,1},{3,4},{4,3},{5,6},{6,5},{9,10},{10,9},{11,12},{12,11},... | collective-permute-start | bytes 233480 | tf_op jit(solution)/shard_map/ppermute | solution.py:834
  6.3 2.4 %collective-permute-start.1 = (bf16[304,128]{1,0:T(8,128)(2,1)}, bf16[304,128]{1,0:T(8,128)(2,1)S(1)}, u32[]{:S(2)}, u32[]{:S(2)}) collective-permute-start(bf16[304,128]{1,0:T(8,128)(2,1)} %get-tuple-element.36), channel_id=1, source_target_pairs={{0,1},{1,0},{2,3},{3,2},{4,5},{5,4},{6,7},{7,6},{8,9},{9,8},{10,11... | collective-permute-start | bytes 233480 | tf_op jit(solution)/shard_map/ppermute | solution.py:835
  12.6 1.4 %collective-permute-start.3 = (bf16[400,256]{1,0:T(8,128)(2,1)S(1)}, bf16[400,256]{1,0:T(8,128)(2,1)S(1)}, u32[]{:S(2)}, u32[]{:S(2)}) collective-permute-start(bf16[400,256]{1,0:T(8,128)(2,1)S(1)} %get-tuple-element.54), channel_id=1, source_target_pairs={{0,1},{1,2},{2,3},{3,4},{4,5},{5,6},{6,7},{8,9},{9,10},{10,11},{11... | collective-permute-start | bytes 614408 | tf_op jit(solution)/shard_map/ppermute | solution.py:897
  13.3 4.2 %collective-permute-start.2 = (bf16[384,256]{1,0:T(8,128)(2,1)S(1)}, bf16[384,256]{1,0:T(8,128)(2,1)S(1)}, u32[]{:S(2)}, u32[]{:S(2)}) collective-permute-start(bf16[384,256]{1,0:T(8,128)(2,1)S(1)} %get-tuple-element.52), channel_id=1, source_target_pairs={{0,1},{1,2},{2,3},{3,4},{4,5},{5,6},{6,7},{8,9},{9,10},{10,11},{11... | collective-permute-start | bytes 589832 | tf_op jit(solution)/shard_map/ppermute | solution.py:897
  14.2 10.6 %collective-permute-start.7 = (bf16[400,256]{1,0:T(8,128)(2,1)S(1)}, bf16[400,256]{1,0:T(8,128)(2,1)S(1)}, u32[]{:S(2)}, u32[]{:S(2)}) collective-permute-start(bf16[400,256]{1,0:T(8,128)(2,1)S(1)} %fusion.sums), channel_id=1, source_target_pairs={{0,8},{1,9},{2,10},{3,11},{4,12},{5,13},{6,14},{7,15}} | collective-permute-start | bytes 614408 | tf_op jit(solution)/shard_map/ppermute | solution.py:947
  14.9 6.6 %collective-permute-start.4 = (bf16[64,128]{1,0:T(8,128)(2,1)S(1)}, bf16[64,128]{1,0:T(8,128)(2,1)S(1)}, u32[]{:S(2)}, u32[]{:S(2)}) collective-permute-start(bf16[64,128]{1,0:T(8,128)(2,1)S(1)} %get-tuple-element.55), channel_id=1, source_target_pairs={{16,25},{17,26},{18,27},{19,28},{20,29},{21,30},{22,31}} | collective-permute-start | bytes 49160 | tf_op jit(solution)/shard_map/ppermute | solution.py:937
  16.2 7.6 %collective-permute-start.5 = (bf16[64,128]{1,0:T(8,128)(2,1)S(1)}, bf16[64,128]{1,0:T(8,128)(2,1)S(1)}, u32[]{:S(2)}, u32[]{:S(2)}) collective-permute-start(bf16[64,128]{1,0:T(8,128)(2,1)S(1)} %get-tuple-element.56), channel_id=1, source_target_pairs={{17,24},{18,25},{19,26},{20,27},{21,28},{22,29},{23,30}} | collective-permute-start | bytes 49160 | tf_op jit(solution)/shard_map/ppermute | solution.py:940
  17.5 10.1 %collective-permute-start.12 = (bf16[384,256]{1,0:T(8,128)(2,1)S(1)}, bf16[384,256]{1,0:T(8,128)(2,1)S(1)}, u32[]{:S(2)}, u32[]{:S(2)}) collective-permute-start(bf16[384,256]{1,0:T(8,128)(2,1)S(1)} %add_convert_fusion.after), channel_id=1, source_target_pairs={{0,16},{1,17},{2,18},{3,19},{4,20},{5,21},{6,22},{7,23}} | collective-permute-start | bytes 589832 | tf_op jit(solution)/shard_map/ppermute | solution.py:950
  18.2 10.8 %collective-permute-start.11 = (bf16[384,256]{1,0:T(8,128)(2,1)S(1)}, bf16[384,256]{1,0:T(8,128)(2,1)S(1)}, u32[]{:S(2)}, u32[]{:S(2)}) collective-permute-start(bf16[384,256]{1,0:T(8,128)(2,1)S(1)} %add_convert_fusion.after), channel_id=1, source_target_pairs={{8,24},{9,25},{10,26},{11,27},{12,28},{13,29},{14,30},{15,31}} | collective-permute-start | bytes 589832 | tf_op jit(solution)/shard_map/ppermute | solution.py:952
  21.5 8.8 %collective-permute-start.6 = (bf16[400,256]{1,0:T(8,128)(2,1)S(1)}, bf16[400,256]{1,0:T(8,128)(2,1)S(1)}, u32[]{:S(2)}, u32[]{:S(2)}) collective-permute-start(bf16[400,256]{1,0:T(8,128)(2,1)S(1)} %fusion.sums), channel_id=1, source_target_pairs={{16,24},{17,25},{18,26},{19,27},{20,28},{21,29},{22,30},{23,31}} | collective-permute-start | bytes 614408 | tf_op jit(solution)/shard_map/ppermute | solution.py:951
  24.9 9.7 %collective-permute-start.8 = (bf16[400,256]{1,0:T(8,128)(2,1)S(1)}, bf16[400,256]{1,0:T(8,128)(2,1)S(1)}, u32[]{:S(2)}, u32[]{:S(2)}) collective-permute-start(bf16[400,256]{1,0:T(8,128)(2,1)S(1)} %fusion.2.sums), channel_id=1, source_target_pairs={{8,24},{9,25},{10,26},{11,27},{12,28},{13,29},{14,30},{15,31}} | collective-permute-start | bytes 614408 | tf_op jit(solution)/shard_map/ppermute | solution.py:961
  26.3 6.0 %collective-permute-start.10 = (bf16[64,128]{1,0:T(8,128)(2,1)S(1)}, bf16[64,128]{1,0:T(8,128)(2,1)S(1)}, u32[]{:S(2)}, u32[]{:S(2)}) collective-permute-start(bf16[64,128]{1,0:T(8,128)(2,1)S(1)} %get-tuple-element.63), channel_id=1, source_target_pairs={{9,24},{10,25},{11,26},{12,27},{13,28},{14,29},{15,30}} | collective-permute-start | bytes 49160 | tf_op jit(solution)/shard_map/ppermute | solution.py:940
  27.6 7.0 %collective-permute-start.9 = (bf16[64,128]{1,0:T(8,128)(2,1)S(1)}, bf16[64,128]{1,0:T(8,128)(2,1)S(1)}, u32[]{:S(2)}, u32[]{:S(2)}) collective-permute-start(bf16[64,128]{1,0:T(8,128)(2,1)S(1)} %get-tuple-element.62.refs_2_), channel_id=1, source_target_pairs={{8,25},{9,26},{10,27},{11,28},{12,29},{13,30},{14,31}} | collective-permute-start | bytes 49160 | tf_op jit(solution)/shard_map/ppermute | solution.py:937
  29.0 8.7 %collective-permute-start.13 = (bf16[384,256]{1,0:T(8,128)(2,1)S(1)}, bf16[384,256]{1,0:T(8,128)(2,1)S(1)}, u32[]{:S(2)}, u32[]{:S(2)}) collective-permute-start(bf16[384,256]{1,0:T(8,128)(2,1)S(1)} %shard_map.120), channel_id=1, source_target_pairs={{16,24},{17,25},{18,26},{19,27},{20,28},{21,29},{22,30},{23,31}} | collective-permute-start | bytes 589832 | tf_op jit(solution)/shard_map/ppermute | solution.py:970

commit v10 on v8

--- a/solution.py
+++ b/solution.py
@@ -279,12 +279,17 @@
     nodes = projector.shape[0]
     count, elements = own_ref.shape
     proj_high, proj_low = split_parts(projector[...])
-    proj_both = jnp.concatenate([proj_high, proj_low], 0)
+    proj_both = jnp.concatenate(
+        [
+            jnp.concatenate([proj_high, proj_high], 1),
+            jnp.concatenate([proj_low, jnp.zeros_like(proj_low)], 1),
+        ],
+        0,
+    )
     for c in range(6):
         x_high, x_low = split_parts(packed[c])
-        main = dot_t(proj_both, x_high)
-        mapped = main[:nodes] + main[nodes:] + dot_t(proj_high, x_low)
-        pay[c * nodes : (c + 1) * nodes, :] = mapped.astype(BF16)
+        main = dot_t(proj_both, jnp.concatenate([x_high, x_low], 1))
+        pay[c * nodes : (c + 1) * nodes, :] = (main[:nodes] + main[nodes:]).astype(BF16)
     if count > 6 * nodes:
         pay[6 * nodes :, :] = jnp.ones((count - 6 * nodes, pay.shape[1]), BF16)
     sums = dot_t(pay[...], hits[...])

time: 37.8 us -> 37.8 us (level)
  no operation moved by 1% of the time
where the time goes in v10:
time: 37.8 us; the launch traced here: 37.5 us
  starting transfers between devices  16.9 us (45%)
  Pallas kernels  9.96 us (26%)
  waiting for transfers between devices  9.44 us (25%)
  between operations  1.01 us (3%)
    pallas_call x10, Pallas kernels, call(): pl.pallas_call(kernel, out_shape=tuple(outs), in_specs=[pl.BlockSpec(memo...  9.96 us
    ppermute x2, waiting for transfers between devices, borders(): lax.ppermute(down_border, ('grp', 'sfc'), [(start + i, last + i - 1) for...  4.45 us
    ppermute x1, starting transfers between devices, body(): part_a = lax.ppermute(pack_a, 'sfc', pairs_a)  3.76 us
    ppermute x2, waiting for transfers between devices, borders(): lax.ppermute(up_border, ('grp', 'sfc'), [(start + i, last + i + 1) for i...  2.68 us
    ppermute x2, starting transfers between devices, borders(): lax.ppermute(up_border, ('grp', 'sfc'), [(start + i, last + i + 1) for i...  2.58 us
    ppermute x2, starting transfers between devices, borders(): lax.ppermute(down_border, ('grp', 'sfc'), [(start + i, last + i - 1) for...  2.58 us
    ppermute x1, waiting for transfers between devices, body(): part_a = lax.ppermute(pack_a, 'sfc', pairs_a)  2.29 us
    ppermute x2, starting transfers between devices, climb(): return lax.ppermute(x, ('grp', 'sfc'), chosen)  1.35 us
  transfers between devices with their start and end apart: 14, of which 5 were waited for; matrix products, arithmetic and copies ran while one was open for 0% of the time, Pallas kernels for 9%

profile of v10, /device:TPU:15, one launch (start us, length us, event | category | flops | bytes accessed | tf_op | source)
XLA Modules:
  0.0 37.5 jit_solution(9837226644277569131)
XLA Ops:
  0.6 0.0 copy-start
  0.6 0.0 copy-start.2
  0.7 0.0 copy-start.7
  0.7 0.0 copy-start.8
  0.7 0.0 copy-start.1
  0.7 0.0 copy-start.3
  0.7 1.8 %shard_map.112 = (bf16[304,128]{1,0:T(8,128)(2,1)}, bf16[304,128]{1,0:T(8,128)(2,1)}) custom-call(f32[5,256,128]{2,1,0:T(8,128)} %bitcast.10, f32[256,128]{1,0:T(8,128)} %bitcast.17, s32[4,256]{1,0:T(4,128)} %bitcast.31, f32[4,64,256]{2,1,0:T(8,128)} %bitcast.22, s32[6,1,256]{2,1,0:T(1,128)} %bitcast.25, s32[6,1,256]{2,1,0:T(1,128)} %bitcast.28), custom_call_target="tpu_custom_call" | custom-call | flops 10000000000 | tf_op jit(solution)/shard_map/pallas_call | solution.py:774
  2.5 3.8 %collective-permute-start = (bf16[304,128]{1,0:T(8,128)(2,1)}, bf16[304,128]{1,0:T(8,128)(2,1)S(1)}, u32[]{:S(2)}, u32[]{:S(2)}) collective-permute-start(bf16[304,128]{1,0:T(8,128)(2,1)} %get-tuple-element.36), channel_id=1, source_target_pairs={{1,2},{2,1},{3,4},{4,3},{5,6},{6,5},{9,10},{10,9},{11,12},{12,11},... | collective-permute-start | bytes 233480 | tf_op jit(solution)/shard_map/ppermute | solution.py:832
  6.3 0.1 collective-permute-start.1
  6.4 0.0 copy-done
  6.4 0.0 copy-done.2
  6.4 0.0 copy-done.7
  6.4 0.0 copy-done.8
  6.4 2.3 %collective-permute-done.part_a = bf16[304,128]{1,0:T(8,128)(2,1)S(1)} collective-permute-done((bf16[304,128]{1,0:T(8,128)(2,1)}, bf16[304,128]{1,0:T(8,128)(2,1)S(1)}, u32[]{:S(2)}, u32[]{:S(2)}) %collective-permute-start) | collective-permute-done | bytes 77856 | tf_op jit(solution)/shard_map/ppermute | solution.py:832
  8.7 0.0 collective-permute-done.1.part_b
  8.7 0.0 copy-done.1
  8.8 3.9 %shard_map.114 = (f32[400,256]{1,0:T(8,128)S(1)}, bf16[400,256]{1,0:T(8,128)(2,1)S(1)}, f32[3,256,128]{2,1,0:T(8,128)S(1)}, f32[1024,128]{1,0:T(8,128)S(1)}, f32...) custom-call(f32[5,256,128]{2,1,0:T(8,128)S(1)} %bitcast.12, ...), custom_call_target="tpu_custom_call" | custom-call | flops 100000000 | bytes 8470528 | tf_op jit(solution)/shard_map/pallas_call | solution.py:774
  12.7 0.7 %collective-permute-start.3 = (bf16[400,256]{1,0:T(8,128)(2,1)S(1)}, bf16[400,256]{1,0:T(8,128)(2,1)S(1)}, u32[]{:S(2)}, u32[]{:S(2)}) collective-permute-start(bf16[400,256]{1,0:T(8,128)(2,1)S(1)} %get-tuple-element.55), channel_id=1, source_target_pairs={{0,1},{1,2},{2,3},{3,4},{4,5},{5,6},{6,7},{8,9},{9,10},{10,11},{11... | collective-permute-start | bytes 614408 | tf_op jit(solution)/shard_map/ppermute | solution.py:896
  13.4 0.1 shard_map.115
  13.4 0.7 %collective-permute-start.2 = (bf16[384,256]{1,0:T(8,128)(2,1)S(1)}, bf16[384,256]{1,0:T(8,128)(2,1)S(1)}, u32[]{:S(2)}, u32[]{:S(2)}) collective-permute-start(bf16[384,256]{1,0:T(8,128)(2,1)S(1)} %get-tuple-element.53), channel_id=1, source_target_pairs={{0,1},{1,2},{2,3},{3,4},{4,5},{5,6},{6,7},{8,9},{9,10},{10,11},{11... | collective-permute-start | bytes 589832 | tf_op jit(solution)/shard_map/ppermute | solution.py:896
  14.1 0.0 collective-permute-done.3
  14.2 0.1 shard_map.116
  14.3 0.7 %collective-permute-start.7 = (bf16[400,256]{1,0:T(8,128)(2,1)S(1)}, bf16[400,256]{1,0:T(8,128)(2,1)S(1)}, u32[]{:S(2)}, u32[]{:S(2)}) collective-permute-start(bf16[400,256]{1,0:T(8,128)(2,1)S(1)} %fusion.sums), channel_id=1, source_target_pairs={{0,8},{1,9},{2,10},{3,11},{4,12},{5,13},{6,14},{7,15}} | collective-permute-start | bytes 614408 | tf_op jit(solution)/shard_map/ppermute | solution.py:946
  15.0 1.3 %collective-permute-start.4 = (bf16[64,128]{1,0:T(8,128)(2,1)S(1)}, bf16[64,128]{1,0:T(8,128)(2,1)S(1)}, u32[]{:S(2)}, u32[]{:S(2)}) collective-permute-start(bf16[64,128]{1,0:T(8,128)(2,1)S(1)} %get-tuple-element.56), channel_id=1, source_target_pairs={{16,25},{17,26},{18,27},{19,28},{20,29},{21,30},{22,31}} | collective-permute-start | bytes 49160 | tf_op jit(solution)/shard_map/ppermute | solution.py:936
  16.3 1.3 %collective-permute-start.5 = (bf16[64,128]{1,0:T(8,128)(2,1)S(1)}, bf16[64,128]{1,0:T(8,128)(2,1)S(1)}, u32[]{:S(2)}, u32[]{:S(2)}) collective-permute-start(bf16[64,128]{1,0:T(8,128)(2,1)S(1)} %get-tuple-element.57), channel_id=1, source_target_pairs={{17,24},{18,25},{19,26},{20,27},{21,28},{22,29},{23,30}} | collective-permute-start | bytes 49160 | tf_op jit(solution)/shard_map/ppermute | solution.py:939
  17.6 0.0 collective-permute-done.2.refs_0_
  17.7 0.7 %collective-permute-start.12 = (bf16[384,256]{1,0:T(8,128)(2,1)S(1)}, bf16[384,256]{1,0:T(8,128)(2,1)S(1)}, u32[]{:S(2)}, u32[]{:S(2)}) collective-permute-start(bf16[384,256]{1,0:T(8,128)(2,1)S(1)} %add_convert_fusion.after), channel_id=1, source_target_pairs={{0,16},{1,17},{2,18},{3,19},{4,20},{5,21},{6,22},{7,23}} | collective-permute-start | bytes 589832 | tf_op jit(solution)/shard_map/ppermute | solution.py:949
  18.3 1.3 %collective-permute-start.11 = (bf16[384,256]{1,0:T(8,128)(2,1)S(1)}, bf16[384,256]{1,0:T(8,128)(2,1)S(1)}, u32[]{:S(2)}, u32[]{:S(2)}) collective-permute-start(bf16[384,256]{1,0:T(8,128)(2,1)S(1)} %add_convert_fusion.after), channel_id=1, source_target_pairs={{8,24},{9,25},{10,26},{11,27},{12,28},{13,29},{14,30},{15,31}} | collective-permute-start | bytes 589832 | tf_op jit(solution)/shard_map/ppermute | solution.py:951
  19.6 1.8 %collective-permute-done.4.after_up.up_b = bf16[64,128]{1,0:T(8,128)(2,1)S(1)} collective-permute-done((bf16[64,128]{1,0:T(8,128)(2,1)S(1)}, bf16[64,128]{1,0:T(8,128)(2,1)S(1)}, u32[]{:S(2)}, u32[]{:S(2)}) %collective-permute-start.4) | collective-permute-done | bytes 16416 | tf_op jit(solution)/shard_map/ppermute | solution.py:936
  21.4 1.3 %collective-permute-start.6 = (bf16[400,256]{1,0:T(8,128)(2,1)S(1)}, bf16[400,256]{1,0:T(8,128)(2,1)S(1)}, u32[]{:S(2)}, u32[]{:S(2)}) collective-permute-start(bf16[400,256]{1,0:T(8,128)(2,1)S(1)} %fusion.sums), channel_id=1, source_target_pairs={{16,24},{17,25},{18,26},{19,27},{20,28},{21,29},{22,30},{23,31}} | collective-permute-start | bytes 614408 | tf_op jit(solution)/shard_map/ppermute | solution.py:950
  22.7 1.0 %collective-permute-done.5.after_down.down_b = bf16[64,128]{1,0:T(8,128)(2,1)S(1)} collective-permute-done((bf16[64,128]{1,0:T(8,128)(2,1)S(1)}, bf16[64,128]{1,0:T(8,128)(2,1)S(1)}, u32[]{:S(2)}, u32[]{:S(2)}) %collective-permute-start.5) | collective-permute-done | bytes 16416 | tf_op jit(solution)/shard_map/ppermute | solution.py:939
  23.7 1.1 %shard_map.117 = (f32[5,256,128]{2,1,0:T(8,128)}, f32[3,256,128]{2,1,0:T(8,128)}, f32[400,256]{1,0:T(8,128)S(1)}) custom-call(f32[5,256,128]{2,1,0:T(8,128)S(1)} %bitcast.13, f32[256,128]{1,0:T(8,128)S(1)} %bitcast.21, f32[3,256,128]{2,1,0:T(8,128)S(1)} %bitcast.16, f32[320,384]{1,0:T(8,128)S(1)} %get-tuple-element.50.state, ...), custom_call_target="tpu_custom_call" | custom-call | flops 1000000000 | tf_op jit(solution)/shard_map/pallas_call | solution.py:774
  24.8 0.0 collective-permute-done.7
  24.8 0.1 fusion.2.sums
  24.9 1.3 %collective-permute-start.8 = (bf16[400,256]{1,0:T(8,128)(2,1)S(1)}, bf16[400,256]{1,0:T(8,128)(2,1)S(1)}, u32[]{:S(2)}, u32[]{:S(2)}) collective-permute-start(bf16[400,256]{1,0:T(8,128)(2,1)S(1)} %fusion.2.sums), channel_id=1, source_target_pairs={{8,24},{9,25},{10,26},{11,27},{12,28},{13,29},{14,30},{15,31}} | collective-permute-start | bytes 614408 | tf_op jit(solution)/shard_map/ppermute | solution.py:960
  26.2 0.1 shard_map.118
  26.3 0.0 collective-permute-done.12.refs_1_
  26.3 1.3 %collective-permute-start.13 = (bf16[384,256]{1,0:T(8,128)(2,1)S(1)}, bf16[384,256]{1,0:T(8,128)(2,1)S(1)}, u32[]{:S(2)}, u32[]{:S(2)}) collective-permute-start(bf16[384,256]{1,0:T(8,128)(2,1)S(1)} %shard_map.120), channel_id=1, source_target_pairs={{16,24},{17,25},{18,26},{19,27},{20,28},{21,29},{22,30},{23,31}} | collective-permute-start | bytes 589832 | tf_op jit(solution)/shard_map/ppermute | solution.py:969
  27.6 1.3 %collective-permute-start.10 = (bf16[64,128]{1,0:T(8,128)(2,1)S(1)}, bf16[64,128]{1,0:T(8,128)(2,1)S(1)}, u32[]{:S(2)}, u32[]{:S(2)}) collective-permute-start(bf16[64,128]{1,0:T(8,128)(2,1)S(1)} %get-tuple-element.65), channel_id=1, source_target_pairs={{9,24},{10,25},{11,26},{12,27},{13,28},{14,29},{15,30}} | collective-permute-start | bytes 49160 | tf_op jit(solution)/shard_map/ppermute | solution.py:939
  28.9 0.0 collective-permute-done.11.after.source_b
  28.9 1.3 %collective-permute-start.9 = (bf16[64,128]{1,0:T(8,128)(2,1)S(1)}, bf16[64,128]{1,0:T(8,128)(2,1)S(1)}, u32[]{:S(2)}, u32[]{:S(2)}) collective-permute-start(bf16[64,128]{1,0:T(8,128)(2,1)S(1)} %get-tuple-element.64.refs_2_), channel_id=1, source_target_pairs={{8,25},{9,26},{10,27},{11,28},{12,29},{13,30},{14,31}} | collective-permute-start | bytes 49160 | tf_op jit(solution)/shard_map/ppermute | solution.py:936
  30.2 0.0 collective-permute-done.6.source_a
  30.3 3.4 %collective-permute-done.10.down_a = bf16[64,128]{1,0:T(8,128)(2,1)S(1)} collective-permute-done((bf16[64,128]{1,0:T(8,128)(2,1)S(1)}, bf16[64,128]{1,0:T(8,128)(2,1)S(1)}, u32[]{:S(2)}, u32[]{:S(2)}) %collective-permute-start.10) | collective-permute-done | bytes 16416 | tf_op jit(solution)/shard_map/ppermute | solution.py:939
  33.7 0.9 %collective-permute-done.9.up_a = bf16[64,128]{1,0:T(8,128)(2,1)S(1)} collective-permute-done((bf16[64,128]{1,0:T(8,128)(2,1)S(1)}, bf16[64,128]{1,0:T(8,128)(2,1)S(1)}, u32[]{:S(2)}, u32[]{:S(2)}) %collective-permute-start.9) | collective-permute-done | bytes 16416 | tf_op jit(solution)/shard_map/ppermute | solution.py:936
  34.6 0.0 collective-permute-done.8.source_b
  34.6 2.0 %shard_map.119 = (f32[512,128]{1,0:T(8,128)S(1)}, f32[3,512,128]{2,1,0:T(8,128)S(1)}, f32[8,256]{1,0:T(8,128)S(1)}) custom-call(f32[1024,128]{1,0:T(8,128)S(1)} %get-tuple-element.60.base, f32[3,1024,128]{2,1,0:T(8,128)S(1)} %get-tuple-element.61.grads, bf16[6,384,256]{2,1,0:T(8,128)(2,1)S(1)} %get-tuple-element.62.hot_two, s32[6,1,256]{2,1,0:T(1,128)S(1)} %bitcast.27, ...), custom_call_target="tpu_custom_call" | custom-call | flops 1000000000 | tf_op jit(solution)/shard_map/pallas_call | solution.py:774
  36.6 0.0 collective-permute-done.13.source_a
  36.6 0.9 %shard_map.121 = f32[4,64,256]{2,1,0:T(8,128)} custom-call(f32[4,64,256]{2,1,0:T(8,128)S(1)} %bitcast.24, f32[512,128]{1,0:T(8,128)S(1)} %get-tuple-element.66.base, f32[3,512,128]{2,1,0:T(8,128)S(1)} %get-tuple-element.67.grads, f32[8,256]{1,0:T(8,128)S(1)} %get-tuple-element.68.scale, bf16[384,256]{1,0:T(8,128)(2,1)S(1)} %collective-permute-done.13.source_a, ...), custom_call_target="tpu_custom_call" | custom-call | flops 100000000 | bytes 1974272 | tf_op jit(solution)/shard_map/pallas_call | solution.py:774
  (11 shorter events, 0.1 us)
Async XLA Ops:
  0.6 5.7 %copy-start = (f32[1,5,256,128]{3,2,1,0:T(8,128)S(1)}, f32[1,5,256,128]{3,2,1,0:T(8,128)}, u32[]{:S(2)}) copy-start(f32[1,5,256,128]{3,2,1,0:T(8,128)} %param.9) | copy-start | bytes 1966084
  0.6 5.7 %copy-start.2 = (f32[1,256,128]{2,1,0:T(8,128)S(1)}, f32[1,256,128]{2,1,0:T(8,128)}, u32[]{:S(2)}) copy-start(f32[1,256,128]{2,1,0:T(8,128)} %param.11) | copy-start | bytes 393220
  0.7 5.7 %copy-start.7 = (s32[1,4,256]{2,1,0:T(4,128)S(1)}, s32[1,4,256]{2,1,0:T(4,128)}, u32[]{:S(2)}) copy-start(s32[1,4,256]{2,1,0:T(4,128)} %param.12) | copy-start | bytes 12292
  0.7 5.7 %copy-start.8 = (s32[1,256]{1,0:T(1,128)S(1)}, s32[1,256]{1,0:T(1,128)}, u32[]{:S(2)}) copy-start(s32[1,256]{1,0:T(1,128)} %target.1) | copy-start | bytes 3076
  0.7 8.1 %copy-start.1 = (f32[1,3,256,128]{3,2,1,0:T(8,128)S(1)}, f32[1,3,256,128]{3,2,1,0:T(8,128)}, u32[]{:S(2)}) copy-start(f32[1,3,256,128]{3,2,1,0:T(8,128)} %param.10) | copy-start | bytes 1179652
  0.7 8.1 %copy-start.3 = (f32[1,4,64,256]{3,2,1,0:T(8,128)S(1)}, f32[1,4,64,256]{3,2,1,0:T(8,128)}, u32[]{:S(2)}) copy-start(f32[1,4,64,256]{3,2,1,0:T(8,128)} %param.15) | copy-start | bytes 786436
  0.7 8.1 %copy-start.4 = (f32[64,128]{1,0:T(8,128)S(1)}, f32[64,128]{1,0:T(8,128)}, u32[]{:S(2)}) copy-start(f32[64,128]{1,0:T(8,128)} %projector.3) | copy-start | bytes 98308
  0.7 8.1 %copy-start.5 = (s32[1,6,256]{2,0,1:T(1,128)S(1)}, s32[1,6,256]{2,0,1:T(1,128)}, u32[]{:S(2)}) copy-start(s32[1,6,256]{2,0,1:T(1,128)} %param.16) | copy-start | bytes 18436
  0.7 8.1 %copy-start.6 = (s32[1,6,256]{2,0,1:T(1,128)S(1)}, s32[1,6,256]{2,0,1:T(1,128)}, u32[]{:S(2)}) copy-start(s32[1,6,256]{2,0,1:T(1,128)} %param.17) | copy-start | bytes 18436
  2.5 6.2 %collective-permute-start = (bf16[304,128]{1,0:T(8,128)(2,1)}, bf16[304,128]{1,0:T(8,128)(2,1)S(1)}, u32[]{:S(2)}, u32[]{:S(2)}) collective-permute-start(bf16[304,128]{1,0:T(8,128)(2,1)} %get-tuple-element.36), channel_id=1, source_target_pairs={{1,2},{2,1},{3,4},{4,3},{5,6},{6,5},{9,10},{10,9},{11,12},{12,11},... | collective-permute-start | bytes 233480 | tf_op jit(solution)/shard_map/ppermute | solution.py:832
  6.3 2.4 %collective-permute-start.1 = (bf16[304,128]{1,0:T(8,128)(2,1)}, bf16[304,128]{1,0:T(8,128)(2,1)S(1)}, u32[]{:S(2)}, u32[]{:S(2)}) collective-permute-start(bf16[304,128]{1,0:T(8,128)(2,1)} %get-tuple-element.37), channel_id=1, source_target_pairs={{0,1},{1,0},{2,3},{3,2},{4,5},{5,4},{6,7},{7,6},{8,9},{9,8},{10,11... | collective-permute-start | bytes 233480 | tf_op jit(solution)/shard_map/ppermute | solution.py:833
  12.7 1.4 %collective-permute-start.3 = (bf16[400,256]{1,0:T(8,128)(2,1)S(1)}, bf16[400,256]{1,0:T(8,128)(2,1)S(1)}, u32[]{:S(2)}, u32[]{:S(2)}) collective-permute-start(bf16[400,256]{1,0:T(8,128)(2,1)S(1)} %get-tuple-element.55), channel_id=1, source_target_pairs={{0,1},{1,2},{2,3},{3,4},{4,5},{5,6},{6,7},{8,9},{9,10},{10,11},{11... | collective-permute-start | bytes 614408 | tf_op jit(solution)/shard_map/ppermute | solution.py:896
  13.4 4.2 %collective-permute-start.2 = (bf16[384,256]{1,0:T(8,128)(2,1)S(1)}, bf16[384,256]{1,0:T(8,128)(2,1)S(1)}, u32[]{:S(2)}, u32[]{:S(2)}) collective-permute-start(bf16[384,256]{1,0:T(8,128)(2,1)S(1)} %get-tuple-element.53), channel_id=1, source_target_pairs={{0,1},{1,2},{2,3},{3,4},{4,5},{5,6},{6,7},{8,9},{9,10},{10,11},{11... | collective-permute-start | bytes 589832 | tf_op jit(solution)/shard_map/ppermute | solution.py:896
  14.3 10.5 %collective-permute-start.7 = (bf16[400,256]{1,0:T(8,128)(2,1)S(1)}, bf16[400,256]{1,0:T(8,128)(2,1)S(1)}, u32[]{:S(2)}, u32[]{:S(2)}) collective-permute-start(bf16[400,256]{1,0:T(8,128)(2,1)S(1)} %fusion.sums), channel_id=1, source_target_pairs={{0,8},{1,9},{2,10},{3,11},{4,12},{5,13},{6,14},{7,15}} | collective-permute-start | bytes 614408 | tf_op jit(solution)/shard_map/ppermute | solution.py:946
  15.0 6.4 %collective-permute-start.4 = (bf16[64,128]{1,0:T(8,128)(2,1)S(1)}, bf16[64,128]{1,0:T(8,128)(2,1)S(1)}, u32[]{:S(2)}, u32[]{:S(2)}) collective-permute-start(bf16[64,128]{1,0:T(8,128)(2,1)S(1)} %get-tuple-element.56), channel_id=1, source_target_pairs={{16,25},{17,26},{18,27},{19,28},{20,29},{21,30},{22,31}} | collective-permute-start | bytes 49160 | tf_op jit(solution)/shard_map/ppermute | solution.py:936
  16.3 7.4 %collective-permute-start.5 = (bf16[64,128]{1,0:T(8,128)(2,1)S(1)}, bf16[64,128]{1,0:T(8,128)(2,1)S(1)}, u32[]{:S(2)}, u32[]{:S(2)}) collective-permute-start(bf16[64,128]{1,0:T(8,128)(2,1)S(1)} %get-tuple-element.57), channel_id=1, source_target_pairs={{17,24},{18,25},{19,26},{20,27},{21,28},{22,29},{23,30}} | collective-permute-start | bytes 49160 | tf_op jit(solution)/shard_map/ppermute | solution.py:939
  17.7 8.6 %collective-permute-start.12 = (bf16[384,256]{1,0:T(8,128)(2,1)S(1)}, bf16[384,256]{1,0:T(8,128)(2,1)S(1)}, u32[]{:S(2)}, u32[]{:S(2)}) collective-permute-start(bf16[384,256]{1,0:T(8,128)(2,1)S(1)} %add_convert_fusion.after), channel_id=1, source_target_pairs={{0,16},{1,17},{2,18},{3,19},{4,20},{5,21},{6,22},{7,23}} | collective-permute-start | bytes 589832 | tf_op jit(solution)/shard_map/ppermute | solution.py:949
  18.3 10.6 %collective-permute-start.11 = (bf16[384,256]{1,0:T(8,128)(2,1)S(1)}, bf16[384,256]{1,0:T(8,128)(2,1)S(1)}, u32[]{:S(2)}, u32[]{:S(2)}) collective-permute-start(bf16[384,256]{1,0:T(8,128)(2,1)S(1)} %add_convert_fusion.after), channel_id=1, source_target_pairs={{8,24},{9,25},{10,26},{11,27},{12,28},{13,29},{14,30},{15,31}} | collective-permute-start | bytes 589832 | tf_op jit(solution)/shard_map/ppermute | solution.py:951
  21.4 8.8 %collective-permute-start.6 = (bf16[400,256]{1,0:T(8,128)(2,1)S(1)}, bf16[400,256]{1,0:T(8,128)(2,1)S(1)}, u32[]{:S(2)}, u32[]{:S(2)}) collective-permute-start(bf16[400,256]{1,0:T(8,128)(2,1)S(1)} %fusion.sums), channel_id=1, source_target_pairs={{16,24},{17,25},{18,26},{19,27},{20,28},{21,29},{22,30},{23,31}} | collective-permute-start | bytes 614408 | tf_op jit(solution)/shard_map/ppermute | solution.py:950
  24.9 9.7 %collective-permute-start.8 = (bf16[400,256]{1,0:T(8,128)(2,1)S(1)}, bf16[400,256]{1,0:T(8,128)(2,1)S(1)}, u32[]{:S(2)}, u32[]{:S(2)}) collective-permute-start(bf16[400,256]{1,0:T(8,128)(2,1)S(1)} %fusion.2.sums), channel_id=1, source_target_pairs={{8,24},{9,25},{10,26},{11,27},{12,28},{13,29},{14,30},{15,31}} | collective-permute-start | bytes 614408 | tf_op jit(solution)/shard_map/ppermute | solution.py:960
  26.3 10.3 %collective-permute-start.13 = (bf16[384,256]{1,0:T(8,128)(2,1)S(1)}, bf16[384,256]{1,0:T(8,128)(2,1)S(1)}, u32[]{:S(2)}, u32[]{:S(2)}) collective-permute-start(bf16[384,256]{1,0:T(8,128)(2,1)S(1)} %shard_map.120), channel_id=1, source_target_pairs={{16,24},{17,25},{18,26},{19,27},{20,28},{21,29},{22,30},{23,31}} | collective-permute-start | bytes 589832 | tf_op jit(solution)/shard_map/ppermute | solution.py:969
  27.6 6.0 %collective-permute-start.10 = (bf16[64,128]{1,0:T(8,128)(2,1)S(1)}, bf16[64,128]{1,0:T(8,128)(2,1)S(1)}, u32[]{:S(2)}, u32[]{:S(2)}) collective-permute-start(bf16[64,128]{1,0:T(8,128)(2,1)S(1)} %get-tuple-element.65), channel_id=1, source_target_pairs={{9,24},{10,25},{11,26},{12,27},{13,28},{14,29},{15,30}} | collective-permute-start | bytes 49160 | tf_op jit(solution)/shard_map/ppermute | solution.py:939
  28.9 5.6 %collective-permute-start.9 = (bf16[64,128]{1,0:T(8,128)(2,1)S(1)}, bf16[64,128]{1,0:T(8,128)(2,1)S(1)}, u32[]{:S(2)}, u32[]{:S(2)}) collective-permute-start(bf16[64,128]{1,0:T(8,128)(2,1)S(1)} %get-tuple-element.64.refs_2_), channel_id=1, source_target_pairs={{8,25},{9,26},{10,27},{11,28},{12,29},{13,30},{14,31}} | collective-permute-start | bytes 49160 | tf_op jit(solution)/shard_map/ppermute | solution.py:936

commit v11 on v10

--- a/solution.py
+++ b/solution.py
@@ -478,7 +478,8 @@
             )
         for group in range(2):
             start = group * halves * block
-            derivatives(rows_of, start, nodes, grads, rhs)
+            derivatives(rows_of, start, nodes, grads)
+            rhs[...] = jnp.zeros_like(rhs)
             add_faces(
                 rows_of, start, nodes, remote, group * halves * 64, [m[group] for m in masks], rhs
             )
@@ -602,10 +603,8 @@
         remote[face, h * 64 : (h + 1) * 64, :] = got[:, h * LANES : (h + 1) * LANES]
 
 
-def derivatives(rows_of, start, nodes, grads_out, rhs):
+def derivatives(rows_of, start, nodes, grads_out):
     matrix = lobatto_matrix()
-    line = lax.broadcasted_iota(jnp.int32, (8, LANES), 0)
-    is_v = [line % 4 == v for v in range(4)]
     node = [node_of(rows_of, start, nodes, n) for n in range(nodes)]
     for n in range(nodes):
         i, j, k = n % 4, n // 4 % 4, n // 16
@@ -614,20 +613,13 @@
             [i + 4 * m + 16 * k for m in range(4)],
             [i + 4 * j + 16 * m for m in range(4)],
         )
-        grads = []
         for d, at in enumerate((i, j, k)):
             total = None
             for m in range(4):
                 if abs(matrix[at, m]) > 1e-12:
                     term = F32(matrix[at, m]) * node[lines[d][m]]
                     total = term if total is None else total + term
-            grads.append(total)
             grads_out[d, pl.ds(start + n, 8, stride=nodes), :] = total
-        div = sum(pltpu.roll(grads[d], 8 - (1 + d), 0) for d in range(3))
-        coupled = jnp.where(is_v[0], div, 0.0)
-        for d in range(3):
-            coupled = jnp.where(is_v[1 + d], pltpu.roll(grads[d], 1 + d, 0), coupled)
-        rhs[n] = -coupled
 
 
 def face_masks(link_low, link_high, code_low, code_high):
@@ -655,12 +647,17 @@
 
 
 def with_sources(total, columns, block, nodes, base, grads):
+    def rows_at(v):
+        return slice((block * 4 + v) * nodes, (block * 4 + v + 1) * nodes)
+
     for v in range(4):
-        rows = slice(block * 4 * nodes + v * nodes, block * 4 * nodes + (v + 1) * nodes)
-        added = total[(v - 1) * nodes : v * nodes, columns] if v else None
+        rows = rows_at(v)
+        if v:
+            added = grads[v - 1, rows_at(0), :] + total[(v - 1) * nodes : v * nodes, columns]
+        else:
+            added = sum(grads[d, rows_at(1 + d), :] for d in range(3))
         for d in range(3):
-            term = total[(3 + d) * nodes : (4 + d) * nodes, columns] * grads[d, rows, :]
-            added = term if added is None else added + term
+            added = added + total[(3 + d) * nodes : (4 + d) * nodes, columns] * grads[d, rows, :]
         yield v, rows, base[rows, :] - ACOUSTIC_STEP * added
 
 
@@ -744,7 +741,8 @@
             masks.append(
                 face_masks(link[:, :LANES], link[:, LANES:], code[:, :LANES], code[:, LANES:])
             )
-        derivatives(rows_of, 0, nodes, grads_two, rhs)
+        derivatives(rows_of, 0, nodes, grads_two)
+        rhs[...] = jnp.zeros_like(rhs)
         add_faces(rows_of, 0, nodes, remote, 0, masks, rhs)
         for n in range(nodes):
             base_two[pl.ds(n, 8, stride=nodes), :] = (

time: 37.8 us -> 37.7 us (level)
  no operation moved by 1% of the time
where the time goes in v11:
time: 37.7 us; the launch traced here: 37.4 us
  starting transfers between devices  16.9 us (45%)
  Pallas kernels  9.75 us (26%)
  waiting for transfers between devices  9.63 us (26%)
  between operations  1 us (3%)
    pallas_call x10, Pallas kernels, call(): pl.pallas_call(kernel, out_shape=tuple(outs), in_specs=[pl.BlockSpec(memo...  9.75 us
    ppermute x2, waiting for transfers between devices, borders(): lax.ppermute(down_border, ('grp', 'sfc'), [(start + i, last + i - 1) for...  4.45 us
    ppermute x1, starting transfers between devices, body(): part_a = lax.ppermute(pack_a, 'sfc', pairs_a)  3.76 us
    ppermute x2, waiting for transfers between devices, borders(): lax.ppermute(up_border, ('grp', 'sfc'), [(start + i, last + i + 1) for i...  2.87 us
    ppermute x2, starting transfers between devices, borders(): lax.ppermute(up_border, ('grp', 'sfc'), [(start + i, last + i + 1) for i...  2.58 us
    ppermute x2, starting transfers between devices, borders(): lax.ppermute(down_border, ('grp', 'sfc'), [(start + i, last + i - 1) for...  2.58 us
    ppermute x1, waiting for transfers between devices, body(): part_a = lax.ppermute(pack_a, 'sfc', pairs_a)  2.29 us
    ppermute x2, starting transfers between devices, climb(): return lax.ppermute(x, ('grp', 'sfc'), chosen)  1.35 us
  transfers between devices with their start and end apart: 14, of which 5 were waited for; matrix products, arithmetic and copies ran while one was open for 0% of the time, Pallas kernels for 9%

profile of v11, /device:TPU:15, one launch (start us, length us, event | category | flops | bytes accessed | tf_op | source)
XLA Modules:
  0.0 37.4 jit_solution(14503512005829261071)
XLA Ops:
  0.6 0.0 copy-start
  0.6 0.0 copy-start.2
  0.7 0.0 copy-start.7
  0.7 0.0 copy-start.8
  0.7 0.0 copy-start.1
  0.7 0.0 copy-start.3
  0.7 1.8 %shard_map.112 = (bf16[304,128]{1,0:T(8,128)(2,1)}, bf16[304,128]{1,0:T(8,128)(2,1)}) custom-call(f32[5,256,128]{2,1,0:T(8,128)} %bitcast.10, f32[256,128]{1,0:T(8,128)} %bitcast.17, s32[4,256]{1,0:T(4,128)} %bitcast.31, f32[4,64,256]{2,1,0:T(8,128)} %bitcast.22, s32[6,1,256]{2,1,0:T(1,128)} %bitcast.25, s32[6,1,256]{2,1,0:T(1,128)} %bitcast.28), custom_call_target="tpu_custom_call" | custom-call | flops 10000000000 | tf_op jit(solution)/shard_map/pallas_call | solution.py:772
  2.5 3.8 %collective-permute-start = (bf16[304,128]{1,0:T(8,128)(2,1)}, bf16[304,128]{1,0:T(8,128)(2,1)S(1)}, u32[]{:S(2)}, u32[]{:S(2)}) collective-permute-start(bf16[304,128]{1,0:T(8,128)(2,1)} %get-tuple-element.36), channel_id=1, source_target_pairs={{1,2},{2,1},{3,4},{4,3},{5,6},{6,5},{9,10},{10,9},{11,12},{12,11},... | collective-permute-start | bytes 233480 | tf_op jit(solution)/shard_map/ppermute | solution.py:830
  6.3 0.1 collective-permute-start.1
  6.4 0.0 copy-done
  6.4 0.0 copy-done.2
  6.4 0.0 copy-done.7
  6.4 0.0 copy-done.8
  6.4 2.3 %collective-permute-done.part_a = bf16[304,128]{1,0:T(8,128)(2,1)S(1)} collective-permute-done((bf16[304,128]{1,0:T(8,128)(2,1)}, bf16[304,128]{1,0:T(8,128)(2,1)S(1)}, u32[]{:S(2)}, u32[]{:S(2)}) %collective-permute-start) | collective-permute-done | bytes 77856 | tf_op jit(solution)/shard_map/ppermute | solution.py:830
  8.7 0.0 collective-permute-done.1.part_b
  8.7 0.0 copy-done.1
  8.8 3.7 %shard_map.114 = (f32[400,256]{1,0:T(8,128)S(1)}, bf16[400,256]{1,0:T(8,128)(2,1)S(1)}, f32[3,256,128]{2,1,0:T(8,128)S(1)}, f32[1024,128]{1,0:T(8,128)S(1)}, f32...) custom-call(f32[5,256,128]{2,1,0:T(8,128)S(1)} %bitcast.12, ...), custom_call_target="tpu_custom_call" | custom-call | flops 100000000 | bytes 8470528 | tf_op jit(solution)/shard_map/pallas_call | solution.py:772
  12.5 0.7 %collective-permute-start.3 = (bf16[400,256]{1,0:T(8,128)(2,1)S(1)}, bf16[400,256]{1,0:T(8,128)(2,1)S(1)}, u32[]{:S(2)}, u32[]{:S(2)}) collective-permute-start(bf16[400,256]{1,0:T(8,128)(2,1)S(1)} %get-tuple-element.55), channel_id=1, source_target_pairs={{0,1},{1,2},{2,3},{3,4},{4,5},{5,6},{6,7},{8,9},{9,10},{10,11},{11... | collective-permute-start | bytes 614408 | tf_op jit(solution)/shard_map/ppermute | solution.py:894
  13.2 0.1 shard_map.115
  13.3 0.7 %collective-permute-start.2 = (bf16[384,256]{1,0:T(8,128)(2,1)S(1)}, bf16[384,256]{1,0:T(8,128)(2,1)S(1)}, u32[]{:S(2)}, u32[]{:S(2)}) collective-permute-start(bf16[384,256]{1,0:T(8,128)(2,1)S(1)} %get-tuple-element.53), channel_id=1, source_target_pairs={{0,1},{1,2},{2,3},{3,4},{4,5},{5,6},{6,7},{8,9},{9,10},{10,11},{11... | collective-permute-start | bytes 589832 | tf_op jit(solution)/shard_map/ppermute | solution.py:894
  13.9 0.0 collective-permute-done.3
  14.0 0.1 shard_map.116
  14.1 0.7 %collective-permute-start.7 = (bf16[400,256]{1,0:T(8,128)(2,1)S(1)}, bf16[400,256]{1,0:T(8,128)(2,1)S(1)}, u32[]{:S(2)}, u32[]{:S(2)}) collective-permute-start(bf16[400,256]{1,0:T(8,128)(2,1)S(1)} %fusion.sums), channel_id=1, source_target_pairs={{0,8},{1,9},{2,10},{3,11},{4,12},{5,13},{6,14},{7,15}} | collective-permute-start | bytes 614408 | tf_op jit(solution)/shard_map/ppermute | solution.py:944
  14.8 1.3 %collective-permute-start.4 = (bf16[64,128]{1,0:T(8,128)(2,1)S(1)}, bf16[64,128]{1,0:T(8,128)(2,1)S(1)}, u32[]{:S(2)}, u32[]{:S(2)}) collective-permute-start(bf16[64,128]{1,0:T(8,128)(2,1)S(1)} %get-tuple-element.56), channel_id=1, source_target_pairs={{16,25},{17,26},{18,27},{19,28},{20,29},{21,30},{22,31}} | collective-permute-start | bytes 49160 | tf_op jit(solution)/shard_map/ppermute | solution.py:934
  16.1 1.3 %collective-permute-start.5 = (bf16[64,128]{1,0:T(8,128)(2,1)S(1)}, bf16[64,128]{1,0:T(8,128)(2,1)S(1)}, u32[]{:S(2)}, u32[]{:S(2)}) collective-permute-start(bf16[64,128]{1,0:T(8,128)(2,1)S(1)} %get-tuple-element.57), channel_id=1, source_target_pairs={{17,24},{18,25},{19,26},{20,27},{21,28},{22,29},{23,30}} | collective-permute-start | bytes 49160 | tf_op jit(solution)/shard_map/ppermute | solution.py:937
  17.4 0.0 collective-permute-done.2.refs_0_
  17.5 0.7 %collective-permute-start.12 = (bf16[384,256]{1,0:T(8,128)(2,1)S(1)}, bf16[384,256]{1,0:T(8,128)(2,1)S(1)}, u32[]{:S(2)}, u32[]{:S(2)}) collective-permute-start(bf16[384,256]{1,0:T(8,128)(2,1)S(1)} %add_convert_fusion.after), channel_id=1, source_target_pairs={{0,16},{1,17},{2,18},{3,19},{4,20},{5,21},{6,22},{7,23}} | collective-permute-start | bytes 589832 | tf_op jit(solution)/shard_map/ppermute | solution.py:947
  18.1 1.3 %collective-permute-start.11 = (bf16[384,256]{1,0:T(8,128)(2,1)S(1)}, bf16[384,256]{1,0:T(8,128)(2,1)S(1)}, u32[]{:S(2)}, u32[]{:S(2)}) collective-permute-start(bf16[384,256]{1,0:T(8,128)(2,1)S(1)} %add_convert_fusion.after), channel_id=1, source_target_pairs={{8,24},{9,25},{10,26},{11,27},{12,28},{13,29},{14,30},{15,31}} | collective-permute-start | bytes 589832 | tf_op jit(solution)/shard_map/ppermute | solution.py:949
  19.4 2.0 %collective-permute-done.4.after_up.up_b = bf16[64,128]{1,0:T(8,128)(2,1)S(1)} collective-permute-done((bf16[64,128]{1,0:T(8,128)(2,1)S(1)}, bf16[64,128]{1,0:T(8,128)(2,1)S(1)}, u32[]{:S(2)}, u32[]{:S(2)}) %collective-permute-start.4) | collective-permute-done | bytes 16416 | tf_op jit(solution)/shard_map/ppermute | solution.py:934
  21.4 1.3 %collective-permute-start.6 = (bf16[400,256]{1,0:T(8,128)(2,1)S(1)}, bf16[400,256]{1,0:T(8,128)(2,1)S(1)}, u32[]{:S(2)}, u32[]{:S(2)}) collective-permute-start(bf16[400,256]{1,0:T(8,128)(2,1)S(1)} %fusion.sums), channel_id=1, source_target_pairs={{16,24},{17,25},{18,26},{19,27},{20,28},{21,29},{22,30},{23,31}} | collective-permute-start | bytes 614408 | tf_op jit(solution)/shard_map/ppermute | solution.py:948
  22.7 1.0 %collective-permute-done.5.after_down.down_b = bf16[64,128]{1,0:T(8,128)(2,1)S(1)} collective-permute-done((bf16[64,128]{1,0:T(8,128)(2,1)S(1)}, bf16[64,128]{1,0:T(8,128)(2,1)S(1)}, u32[]{:S(2)}, u32[]{:S(2)}) %collective-permute-start.5) | collective-permute-done | bytes 16416 | tf_op jit(solution)/shard_map/ppermute | solution.py:937
  23.7 1.1 %shard_map.117 = (f32[5,256,128]{2,1,0:T(8,128)}, f32[3,256,128]{2,1,0:T(8,128)}, f32[400,256]{1,0:T(8,128)S(1)}) custom-call(f32[5,256,128]{2,1,0:T(8,128)S(1)} %bitcast.13, f32[256,128]{1,0:T(8,128)S(1)} %bitcast.21, f32[3,256,128]{2,1,0:T(8,128)S(1)} %bitcast.16, f32[320,384]{1,0:T(8,128)S(1)} %get-tuple-element.50.state, ...), custom_call_target="tpu_custom_call" | custom-call | flops 1000000000 | tf_op jit(solution)/shard_map/pallas_call | solution.py:772
  24.8 0.0 collective-permute-done.7
  24.8 0.1 fusion.2.sums
  24.9 1.3 %collective-permute-start.8 = (bf16[400,256]{1,0:T(8,128)(2,1)S(1)}, bf16[400,256]{1,0:T(8,128)(2,1)S(1)}, u32[]{:S(2)}, u32[]{:S(2)}) collective-permute-start(bf16[400,256]{1,0:T(8,128)(2,1)S(1)} %fusion.2.sums), channel_id=1, source_target_pairs={{8,24},{9,25},{10,26},{11,27},{12,28},{13,29},{14,30},{15,31}} | collective-permute-start | bytes 614408 | tf_op jit(solution)/shard_map/ppermute | solution.py:958
  26.2 0.1 shard_map.118
  26.3 0.0 collective-permute-done.12.refs_1_
  26.3 1.3 %collective-permute-start.13 = (bf16[384,256]{1,0:T(8,128)(2,1)S(1)}, bf16[384,256]{1,0:T(8,128)(2,1)S(1)}, u32[]{:S(2)}, u32[]{:S(2)}) collective-permute-start(bf16[384,256]{1,0:T(8,128)(2,1)S(1)} %shard_map.120), channel_id=1, source_target_pairs={{16,24},{17,25},{18,26},{19,27},{20,28},{21,29},{22,30},{23,31}} | collective-permute-start | bytes 589832 | tf_op jit(solution)/shard_map/ppermute | solution.py:967
  27.6 1.3 %collective-permute-start.10 = (bf16[64,128]{1,0:T(8,128)(2,1)S(1)}, bf16[64,128]{1,0:T(8,128)(2,1)S(1)}, u32[]{:S(2)}, u32[]{:S(2)}) collective-permute-start(bf16[64,128]{1,0:T(8,128)(2,1)S(1)} %get-tuple-element.65), channel_id=1, source_target_pairs={{9,24},{10,25},{11,26},{12,27},{13,28},{14,29},{15,30}} | collective-permute-start | bytes 49160 | tf_op jit(solution)/shard_map/ppermute | solution.py:937
  28.9 0.0 collective-permute-done.11.after.source_b
  28.9 1.3 %collective-permute-start.9 = (bf16[64,128]{1,0:T(8,128)(2,1)S(1)}, bf16[64,128]{1,0:T(8,128)(2,1)S(1)}, u32[]{:S(2)}, u32[]{:S(2)}) collective-permute-start(bf16[64,128]{1,0:T(8,128)(2,1)S(1)} %get-tuple-element.64.refs_2_), channel_id=1, source_target_pairs={{8,25},{9,26},{10,27},{11,28},{12,29},{13,30},{14,31}} | collective-permute-start | bytes 49160 | tf_op jit(solution)/shard_map/ppermute | solution.py:934
  30.2 0.0 collective-permute-done.6.source_a
  30.3 3.4 %collective-permute-done.10.down_a = bf16[64,128]{1,0:T(8,128)(2,1)S(1)} collective-permute-done((bf16[64,128]{1,0:T(8,128)(2,1)S(1)}, bf16[64,128]{1,0:T(8,128)(2,1)S(1)}, u32[]{:S(2)}, u32[]{:S(2)}) %collective-permute-start.10) | collective-permute-done | bytes 16416 | tf_op jit(solution)/shard_map/ppermute | solution.py:937
  33.7 0.9 %collective-permute-done.9.up_a = bf16[64,128]{1,0:T(8,128)(2,1)S(1)} collective-permute-done((bf16[64,128]{1,0:T(8,128)(2,1)S(1)}, bf16[64,128]{1,0:T(8,128)(2,1)S(1)}, u32[]{:S(2)}, u32[]{:S(2)}) %collective-permute-start.9) | collective-permute-done | bytes 16416 | tf_op jit(solution)/shard_map/ppermute | solution.py:934
  34.6 0.0 collective-permute-done.8.source_b
  34.6 2.0 %shard_map.119 = (f32[512,128]{1,0:T(8,128)S(1)}, f32[3,512,128]{2,1,0:T(8,128)S(1)}, f32[8,256]{1,0:T(8,128)S(1)}) custom-call(f32[1024,128]{1,0:T(8,128)S(1)} %get-tuple-element.60.base, f32[3,1024,128]{2,1,0:T(8,128)S(1)} %get-tuple-element.61.grads, bf16[6,384,256]{2,1,0:T(8,128)(2,1)S(1)} %get-tuple-element.62.hot_two, s32[6,1,256]{2,1,0:T(1,128)S(1)} %bitcast.27, ...), custom_call_target="tpu_custom_call" | custom-call | flops 1000000000 | tf_op jit(solution)/shard_map/pallas_call | solution.py:772
  36.5 0.0 collective-permute-done.13.source_a
  36.6 0.9 %shard_map.121 = f32[4,64,256]{2,1,0:T(8,128)} custom-call(f32[4,64,256]{2,1,0:T(8,128)S(1)} %bitcast.24, f32[512,128]{1,0:T(8,128)S(1)} %get-tuple-element.66.base, f32[3,512,128]{2,1,0:T(8,128)S(1)} %get-tuple-element.67.grads, f32[8,256]{1,0:T(8,128)S(1)} %get-tuple-element.68.scale, bf16[384,256]{1,0:T(8,128)(2,1)S(1)} %collective-permute-done.13.source_a, ...), custom_call_target="tpu_custom_call" | custom-call | flops 100000000 | bytes 1974272 | tf_op jit(solution)/shard_map/pallas_call | solution.py:772
  (11 shorter events, 0.1 us)
Async XLA Ops:
  0.6 5.7 %copy-start = (f32[1,5,256,128]{3,2,1,0:T(8,128)S(1)}, f32[1,5,256,128]{3,2,1,0:T(8,128)}, u32[]{:S(2)}) copy-start(f32[1,5,256,128]{3,2,1,0:T(8,128)} %param.9) | copy-start | bytes 1966084
  0.6 5.7 %copy-start.2 = (f32[1,256,128]{2,1,0:T(8,128)S(1)}, f32[1,256,128]{2,1,0:T(8,128)}, u32[]{:S(2)}) copy-start(f32[1,256,128]{2,1,0:T(8,128)} %param.11) | copy-start | bytes 393220
  0.7 5.7 %copy-start.7 = (s32[1,4,256]{2,1,0:T(4,128)S(1)}, s32[1,4,256]{2,1,0:T(4,128)}, u32[]{:S(2)}) copy-start(s32[1,4,256]{2,1,0:T(4,128)} %param.12) | copy-start | bytes 12292
  0.7 5.7 %copy-start.8 = (s32[1,256]{1,0:T(1,128)S(1)}, s32[1,256]{1,0:T(1,128)}, u32[]{:S(2)}) copy-start(s32[1,256]{1,0:T(1,128)} %target.1) | copy-start | bytes 3076
  0.7 8.1 %copy-start.1 = (f32[1,3,256,128]{3,2,1,0:T(8,128)S(1)}, f32[1,3,256,128]{3,2,1,0:T(8,128)}, u32[]{:S(2)}) copy-start(f32[1,3,256,128]{3,2,1,0:T(8,128)} %param.10) | copy-start | bytes 1179652
  0.7 8.1 %copy-start.3 = (f32[1,4,64,256]{3,2,1,0:T(8,128)S(1)}, f32[1,4,64,256]{3,2,1,0:T(8,128)}, u32[]{:S(2)}) copy-start(f32[1,4,64,256]{3,2,1,0:T(8,128)} %param.15) | copy-start | bytes 786436
  0.7 8.1 %copy-start.4 = (f32[64,128]{1,0:T(8,128)S(1)}, f32[64,128]{1,0:T(8,128)}, u32[]{:S(2)}) copy-start(f32[64,128]{1,0:T(8,128)} %projector.3) | copy-start | bytes 98308
  0.7 8.1 %copy-start.5 = (s32[1,6,256]{2,0,1:T(1,128)S(1)}, s32[1,6,256]{2,0,1:T(1,128)}, u32[]{:S(2)}) copy-start(s32[1,6,256]{2,0,1:T(1,128)} %param.16) | copy-start | bytes 18436
  0.7 8.1 %copy-start.6 = (s32[1,6,256]{2,0,1:T(1,128)S(1)}, s32[1,6,256]{2,0,1:T(1,128)}, u32[]{:S(2)}) copy-start(s32[1,6,256]{2,0,1:T(1,128)} %param.17) | copy-start | bytes 18436
  2.5 6.2 %collective-permute-start = (bf16[304,128]{1,0:T(8,128)(2,1)}, bf16[304,128]{1,0:T(8,128)(2,1)S(1)}, u32[]{:S(2)}, u32[]{:S(2)}) collective-permute-start(bf16[304,128]{1,0:T(8,128)(2,1)} %get-tuple-element.36), channel_id=1, source_target_pairs={{1,2},{2,1},{3,4},{4,3},{5,6},{6,5},{9,10},{10,9},{11,12},{12,11},... | collective-permute-start | bytes 233480 | tf_op jit(solution)/shard_map/ppermute | solution.py:830
  6.3 2.4 %collective-permute-start.1 = (bf16[304,128]{1,0:T(8,128)(2,1)}, bf16[304,128]{1,0:T(8,128)(2,1)S(1)}, u32[]{:S(2)}, u32[]{:S(2)}) collective-permute-start(bf16[304,128]{1,0:T(8,128)(2,1)} %get-tuple-element.37), channel_id=1, source_target_pairs={{0,1},{1,0},{2,3},{3,2},{4,5},{5,4},{6,7},{7,6},{8,9},{9,8},{10,11... | collective-permute-start | bytes 233480 | tf_op jit(solution)/shard_map/ppermute | solution.py:831
  12.5 1.4 %collective-permute-start.3 = (bf16[400,256]{1,0:T(8,128)(2,1)S(1)}, bf16[400,256]{1,0:T(8,128)(2,1)S(1)}, u32[]{:S(2)}, u32[]{:S(2)}) collective-permute-start(bf16[400,256]{1,0:T(8,128)(2,1)S(1)} %get-tuple-element.55), channel_id=1, source_target_pairs={{0,1},{1,2},{2,3},{3,4},{4,5},{5,6},{6,7},{8,9},{9,10},{10,11},{11... | collective-permute-start | bytes 614408 | tf_op jit(solution)/shard_map/ppermute | solution.py:894
  13.3 4.2 %collective-permute-start.2 = (bf16[384,256]{1,0:T(8,128)(2,1)S(1)}, bf16[384,256]{1,0:T(8,128)(2,1)S(1)}, u32[]{:S(2)}, u32[]{:S(2)}) collective-permute-start(bf16[384,256]{1,0:T(8,128)(2,1)S(1)} %get-tuple-element.53), channel_id=1, source_target_pairs={{0,1},{1,2},{2,3},{3,4},{4,5},{5,6},{6,7},{8,9},{9,10},{10,11},{11... | collective-permute-start | bytes 589832 | tf_op jit(solution)/shard_map/ppermute | solution.py:894
  14.1 10.7 %collective-permute-start.7 = (bf16[400,256]{1,0:T(8,128)(2,1)S(1)}, bf16[400,256]{1,0:T(8,128)(2,1)S(1)}, u32[]{:S(2)}, u32[]{:S(2)}) collective-permute-start(bf16[400,256]{1,0:T(8,128)(2,1)S(1)} %fusion.sums), channel_id=1, source_target_pairs={{0,8},{1,9},{2,10},{3,11},{4,12},{5,13},{6,14},{7,15}} | collective-permute-start | bytes 614408 | tf_op jit(solution)/shard_map/ppermute | solution.py:944
  14.8 6.6 %collective-permute-start.4 = (bf16[64,128]{1,0:T(8,128)(2,1)S(1)}, bf16[64,128]{1,0:T(8,128)(2,1)S(1)}, u32[]{:S(2)}, u32[]{:S(2)}) collective-permute-start(bf16[64,128]{1,0:T(8,128)(2,1)S(1)} %get-tuple-element.56), channel_id=1, source_target_pairs={{16,25},{17,26},{18,27},{19,28},{20,29},{21,30},{22,31}} | collective-permute-start | bytes 49160 | tf_op jit(solution)/shard_map/ppermute | solution.py:934
  16.1 7.6 %collective-permute-start.5 = (bf16[64,128]{1,0:T(8,128)(2,1)S(1)}, bf16[64,128]{1,0:T(8,128)(2,1)S(1)}, u32[]{:S(2)}, u32[]{:S(2)}) collective-permute-start(bf16[64,128]{1,0:T(8,128)(2,1)S(1)} %get-tuple-element.57), channel_id=1, source_target_pairs={{17,24},{18,25},{19,26},{20,27},{21,28},{22,29},{23,30}} | collective-permute-start | bytes 49160 | tf_op jit(solution)/shard_map/ppermute | solution.py:937
  17.5 8.8 %collective-permute-start.12 = (bf16[384,256]{1,0:T(8,128)(2,1)S(1)}, bf16[384,256]{1,0:T(8,128)(2,1)S(1)}, u32[]{:S(2)}, u32[]{:S(2)}) collective-permute-start(bf16[384,256]{1,0:T(8,128)(2,1)S(1)} %add_convert_fusion.after), channel_id=1, source_target_pairs={{0,16},{1,17},{2,18},{3,19},{4,20},{5,21},{6,22},{7,23}} | collective-permute-start | bytes 589832 | tf_op jit(solution)/shard_map/ppermute | solution.py:947
  18.1 10.8 %collective-permute-start.11 = (bf16[384,256]{1,0:T(8,128)(2,1)S(1)}, bf16[384,256]{1,0:T(8,128)(2,1)S(1)}, u32[]{:S(2)}, u32[]{:S(2)}) collective-permute-start(bf16[384,256]{1,0:T(8,128)(2,1)S(1)} %add_convert_fusion.after), channel_id=1, source_target_pairs={{8,24},{9,25},{10,26},{11,27},{12,28},{13,29},{14,30},{15,31}} | collective-permute-start | bytes 589832 | tf_op jit(solution)/shard_map/ppermute | solution.py:949
  21.4 8.8 %collective-permute-start.6 = (bf16[400,256]{1,0:T(8,128)(2,1)S(1)}, bf16[400,256]{1,0:T(8,128)(2,1)S(1)}, u32[]{:S(2)}, u32[]{:S(2)}) collective-permute-start(bf16[400,256]{1,0:T(8,128)(2,1)S(1)} %fusion.sums), channel_id=1, source_target_pairs={{16,24},{17,25},{18,26},{19,27},{20,28},{21,29},{22,30},{23,31}} | collective-permute-start | bytes 614408 | tf_op jit(solution)/shard_map/ppermute | solution.py:948
  24.9 9.7 %collective-permute-start.8 = (bf16[400,256]{1,0:T(8,128)(2,1)S(1)}, bf16[400,256]{1,0:T(8,128)(2,1)S(1)}, u32[]{:S(2)}, u32[]{:S(2)}) collective-permute-start(bf16[400,256]{1,0:T(8,128)(2,1)S(1)} %fusion.2.sums), channel_id=1, source_target_pairs={{8,24},{9,25},{10,26},{11,27},{12,28},{13,29},{14,30},{15,31}} | collective-permute-start | bytes 614408 | tf_op jit(solution)/shard_map/ppermute | solution.py:958
  26.3 10.2 %collective-permute-start.13 = (bf16[384,256]{1,0:T(8,128)(2,1)S(1)}, bf16[384,256]{1,0:T(8,128)(2,1)S(1)}, u32[]{:S(2)}, u32[]{:S(2)}) collective-permute-start(bf16[384,256]{1,0:T(8,128)(2,1)S(1)} %shard_map.120), channel_id=1, source_target_pairs={{16,24},{17,25},{18,26},{19,27},{20,28},{21,29},{22,30},{23,31}} | collective-permute-start | bytes 589832 | tf_op jit(solution)/shard_map/ppermute | solution.py:967
  27.6 6.0 %collective-permute-start.10 = (bf16[64,128]{1,0:T(8,128)(2,1)S(1)}, bf16[64,128]{1,0:T(8,128)(2,1)S(1)}, u32[]{:S(2)}, u32[]{:S(2)}) collective-permute-start(bf16[64,128]{1,0:T(8,128)(2,1)S(1)} %get-tuple-element.65), channel_id=1, source_target_pairs={{9,24},{10,25},{11,26},{12,27},{13,28},{14,29},{15,30}} | collective-permute-start | bytes 49160 | tf_op jit(solution)/shard_map/ppermute | solution.py:937
  28.9 5.6 %collective-permute-start.9 = (bf16[64,128]{1,0:T(8,128)(2,1)S(1)}, bf16[64,128]{1,0:T(8,128)(2,1)S(1)}, u32[]{:S(2)}, u32[]{:S(2)}) collective-permute-start(bf16[64,128]{1,0:T(8,128)(2,1)S(1)} %get-tuple-element.64.refs_2_), channel_id=1, source_target_pairs={{8,25},{9,26},{10,27},{11,28},{12,29},{13,30},{14,31}} | collective-permute-start | bytes 49160 | tf_op jit(solution)/shard_map/ppermute | solution.py:934

commit v12 on v11

--- a/solution.py
+++ b/solution.py
@@ -542,10 +542,10 @@
 
 
 def output_kernel(
-    flow, visc, mean, state, mean_two,
+    flow, visc, state,
     inner_state, inner_high, inner_low, inner_mats,
     edge_state, edge_high, edge_low, edge_mats, edge_visc, after, after_up, after_down, own_one,
-    flow_out, mean_out, own_one_out, passive, zero,
+    flow_out, own_one_out, passive, zero,
 ):
     plan = FlowPlan(flow.shape[1])
     is_flow = on_flow_row()
@@ -554,12 +554,10 @@
     @pl.when(jnp.logical_not(is_flow))
     def _():
         flow_out[...] = flow[...]
-        mean_out[...] = mean[...]
 
     @pl.when(is_flow)
     def _():
         zero[...] = jnp.zeros_like(zero)
-        mean_out[...] = mean_two[...]
         carried = (
             inner_state, inner_high, inner_low, inner_mats,
             edge_state, edge_high, edge_low, edge_mats, edge_visc, zero,
@@ -571,6 +569,18 @@
             second_block(plan, b, carried, visc, ((3, 5),), passive, (None, None))
         for place in (3, 4):
             flow_out[FIELD_ORDER[place]] = passive[own, columns_of(place)]
+
+
+def mean_kernel(mean, mean_two, after, mean_out):
+    is_flow = on_flow_row()
+
+    @pl.when(is_flow)
+    def _():
+        mean_out[...] = mean_two[...]
+
+    @pl.when(jnp.logical_not(is_flow))
+    def _():
+        mean_out[...] = mean[...]
 
 
 def facing_rows(rows_of, base, nodes, face, to):
@@ -946,12 +956,19 @@
     sum_two_1 = combined(own_two, got_two)
     two_0_to_2 = lax.ppermute(sum_two_1, "grp", [(0, 2)])
     one_2_to_3 = lax.ppermute(sum_one_2, "grp", [(2, 3)])
+    (sum_two_1,) = call(
+        gated_sum_kernel,
+        [shape(own_two.shape, BF16)],
+        [],
+        [own_two, got_two, sum_two_1],
+        cost=0,
+    )
     two_1_to_3 = lax.ppermute(sum_two_1, "grp", [(1, 3)])
-    flow_out, mean_out, own_one = call(
+    flow_out, own_one = call(
         output_kernel,
-        [shape(flow.shape, F32), shape(mean.shape, F32), shape(own_one.shape, F32)],
+        [shape(flow.shape, F32), shape(own_one.shape, F32)],
         [vmem((band, fields), F32), vmem((HW, fields), BF16)],
-        [flow, visc, mean, state_two, mean_two, *step_one, *edges, sum_two_1, *beside_2, own_one],
+        [flow, visc, state_two, *step_one, *edges, sum_two_1, *beside_2, own_one],
         cost=OUTPUT_COST,
     )
     sum_one_1 = combined(own_one, got_one, one_0_to_1)
@@ -963,6 +980,9 @@
         [],
         [own_two, got_two, two_0_to_2, border],
         cost=0,
+    )
+    (mean_out,) = call(
+        mean_kernel, [shape(mean.shape, F32)], [], [mean, mean_two, sum_two_2], cost=0
     )
     two_2_to_3 = lax.ppermute(sum_two_2, "grp", [(2, 3)])
 

time: 37.7 us -> 38.1 us (1.011)
  Pallas kernels: 9.75 us -> 10.4 us
    ppermute x2, waiting for transfers between devices: 4.45 us -> 1.64 us  [borders(): lax.ppermute(down_border, ('grp', 'sfc'), [(start + i, last + i - 1) for...]
    ppermute x2, waiting for transfers between devices: 2.87 us -> 5.32 us  [borders(): lax.ppermute(up_border, ('grp', 'sfc'), [(start + i, last + i + 1) for i...]
    pallas_call x10 -> x12, Pallas kernels: 9.75 us -> 10.4 us  [call(): pl.pallas_call(kernel, out_shape=tuple(outs), in_specs=[pl.BlockSpec(memo...]
  transfers between devices with their start and end apart: 14 -> 14, of which waited for: 5 -> 5; matrix products, arithmetic and copies ran while one was open for 0% -> 0% of each run, Pallas kernels for 9% -> 11%
where the time goes in v12:
time: 38.1 us; the launch traced here: 37.8 us
  starting transfers between devices  16.9 us (44%)
  Pallas kernels  10.4 us (27%)
  waiting for transfers between devices  9.28 us (24%)
  between operations  1 us (3%)
    pallas_call x12, Pallas kernels, call(): pl.pallas_call(kernel, out_shape=tuple(outs), in_specs=[pl.BlockSpec(memo...  10.4 us
    ppermute x2, waiting for transfers between devices, borders(): lax.ppermute(up_border, ('grp', 'sfc'), [(start + i, last + i + 1) for i...  5.32 us
    ppermute x1, starting transfers between devices, body(): part_a = lax.ppermute(pack_a, 'sfc', pairs_a)  3.76 us
    ppermute x2, starting transfers between devices, borders(): lax.ppermute(up_border, ('grp', 'sfc'), [(start + i, last + i + 1) for i...  2.58 us
    ppermute x2, starting transfers between devices, borders(): lax.ppermute(down_border, ('grp', 'sfc'), [(start + i, last + i - 1) for...  2.58 us
    ppermute x1, waiting for transfers between devices, body(): part_a = lax.ppermute(pack_a, 'sfc', pairs_a)  2.29 us
    ppermute x2, waiting for transfers between devices, borders(): lax.ppermute(down_border, ('grp', 'sfc'), [(start + i, last + i - 1) for...  1.64 us
    ppermute x2, starting transfers between devices, climb(): return lax.ppermute(x, ('grp', 'sfc'), chosen)  1.35 us
  transfers between devices with their start and end apart: 14, of which 5 were waited for; matrix products, arithmetic and copies ran while one was open for 0% of the time, Pallas kernels for 11%

profile of v12, /device:TPU:15, one launch (start us, length us, event | category | flops | bytes accessed | tf_op | source)
XLA Modules:
  0.0 37.8 jit_solution(248595721869589302)
XLA Ops:
  0.6 0.0 copy-start
  0.6 0.0 copy-start.2
  0.7 0.0 copy-start.7
  0.7 0.0 copy-start.8
  0.7 1.8 %shard_map.112 = (bf16[304,128]{1,0:T(8,128)(2,1)}, bf16[304,128]{1,0:T(8,128)(2,1)}) custom-call(f32[5,256,128]{2,1,0:T(8,128)} %bitcast.10, f32[256,128]{1,0:T(8,128)} %bitcast.17, s32[4,256]{1,0:T(4,128)} %bitcast.31, f32[4,64,256]{2,1,0:T(8,128)} %bitcast.22, s32[6,1,256]{2,1,0:T(1,128)} %bitcast.25, s32[6,1,256]{2,1,0:T(1,128)} %bitcast.28), custom_call_target="tpu_custom_call" | custom-call | flops 10000000000 | tf_op jit(solution)/shard_map/pallas_call | solution.py:782
  2.5 3.8 %collective-permute-start = (bf16[304,128]{1,0:T(8,128)(2,1)}, bf16[304,128]{1,0:T(8,128)(2,1)S(1)}, u32[]{:S(2)}, u32[]{:S(2)}) collective-permute-start(bf16[304,128]{1,0:T(8,128)(2,1)} %get-tuple-element.35), channel_id=1, source_target_pairs={{1,2},{2,1},{3,4},{4,3},{5,6},{6,5},{9,10},{10,9},{11,12},{12,11},... | collective-permute-start | bytes 233480 | tf_op jit(solution)/shard_map/ppermute | solution.py:840
  6.3 0.1 collective-permute-start.1
  6.4 0.0 copy-done
  6.4 0.0 copy-done.2
  6.4 0.0 copy-done.7
  6.4 0.0 copy-done.8
  6.4 2.3 %collective-permute-done.part_a = bf16[304,128]{1,0:T(8,128)(2,1)S(1)} collective-permute-done((bf16[304,128]{1,0:T(8,128)(2,1)}, bf16[304,128]{1,0:T(8,128)(2,1)S(1)}, u32[]{:S(2)}, u32[]{:S(2)}) %collective-permute-start) | collective-permute-done | bytes 77856 | tf_op jit(solution)/shard_map/ppermute | solution.py:840
  8.7 0.0 collective-permute-done.1.part_b
  8.7 0.0 copy-done.1
  8.8 3.7 %shard_map.114 = (f32[400,256]{1,0:T(8,128)S(1)}, bf16[400,256]{1,0:T(8,128)(2,1)S(1)}, f32[3,256,128]{2,1,0:T(8,128)S(1)}, f32[1024,128]{1,0:T(8,128)S(1)}, f32...) custom-call(f32[5,256,128]{2,1,0:T(8,128)S(1)} %bitcast.12, ...), custom_call_target="tpu_custom_call" | custom-call | flops 100000000 | bytes 8470528 | tf_op jit(solution)/shard_map/pallas_call | solution.py:782
  12.5 0.7 %collective-permute-start.3 = (bf16[400,256]{1,0:T(8,128)(2,1)S(1)}, bf16[400,256]{1,0:T(8,128)(2,1)S(1)}, u32[]{:S(2)}, u32[]{:S(2)}) collective-permute-start(bf16[400,256]{1,0:T(8,128)(2,1)S(1)} %get-tuple-element.53), channel_id=1, source_target_pairs={{0,1},{1,2},{2,3},{3,4},{4,5},{5,6},{6,7},{8,9},{9,10},{10,11},{11... | collective-permute-start | bytes 614408 | tf_op jit(solution)/shard_map/ppermute | solution.py:904
  13.2 0.1 shard_map.115
  13.3 0.7 %collective-permute-start.2 = (bf16[384,256]{1,0:T(8,128)(2,1)S(1)}, bf16[384,256]{1,0:T(8,128)(2,1)S(1)}, u32[]{:S(2)}, u32[]{:S(2)}) collective-permute-start(bf16[384,256]{1,0:T(8,128)(2,1)S(1)} %get-tuple-element.51), channel_id=1, source_target_pairs={{0,1},{1,2},{2,3},{3,4},{4,5},{5,6},{6,7},{8,9},{9,10},{10,11},{11... | collective-permute-start | bytes 589832 | tf_op jit(solution)/shard_map/ppermute | solution.py:904
  13.9 0.0 collective-permute-done.3
  13.9 0.1 fusion.sums
  14.0 0.1 shard_map.117
  14.1 0.7 %collective-permute-start.7 = (bf16[400,256]{1,0:T(8,128)(2,1)S(1)}, bf16[400,256]{1,0:T(8,128)(2,1)S(1)}, u32[]{:S(2)}, u32[]{:S(2)}) collective-permute-start(bf16[400,256]{1,0:T(8,128)(2,1)S(1)} %fusion.sums), channel_id=1, source_target_pairs={{0,8},{1,9},{2,10},{3,11},{4,12},{5,13},{6,14},{7,15}} | collective-permute-start | bytes 614408 | tf_op jit(solution)/shard_map/ppermute | solution.py:954
  14.8 1.3 %collective-permute-start.4 = (bf16[64,128]{1,0:T(8,128)(2,1)S(1)}, bf16[64,128]{1,0:T(8,128)(2,1)S(1)}, u32[]{:S(2)}, u32[]{:S(2)}) collective-permute-start(bf16[64,128]{1,0:T(8,128)(2,1)S(1)} %get-tuple-element.54), channel_id=1, source_target_pairs={{16,25},{17,26},{18,27},{19,28},{20,29},{21,30},{22,31}} | collective-permute-start | bytes 49160 | tf_op jit(solution)/shard_map/ppermute | solution.py:944
  16.1 1.3 %collective-permute-start.5 = (bf16[64,128]{1,0:T(8,128)(2,1)S(1)}, bf16[64,128]{1,0:T(8,128)(2,1)S(1)}, u32[]{:S(2)}, u32[]{:S(2)}) collective-permute-start(bf16[64,128]{1,0:T(8,128)(2,1)S(1)} %get-tuple-element.55), channel_id=1, source_target_pairs={{17,24},{18,25},{19,26},{20,27},{21,28},{22,29},{23,30}} | collective-permute-start | bytes 49160 | tf_op jit(solution)/shard_map/ppermute | solution.py:947
  17.4 0.0 collective-permute-done.2.refs_0_
  17.5 0.7 %collective-permute-start.6 = (bf16[384,256]{1,0:T(8,128)(2,1)S(1)}, bf16[384,256]{1,0:T(8,128)(2,1)S(1)}, u32[]{:S(2)}, u32[]{:S(2)}) collective-permute-start(bf16[384,256]{1,0:T(8,128)(2,1)S(1)} %add_convert_fusion.refs_1_), channel_id=1, source_target_pairs={{0,16},{1,17},{2,18},{3,19},{4,20},{5,21},{6,22},{7,23}} | collective-permute-start | bytes 589832 | tf_op jit(solution)/shard_map/ppermute | solution.py:957
  18.2 1.3 %collective-permute-start.12 = (bf16[384,256]{1,0:T(8,128)(2,1)S(1)}, bf16[384,256]{1,0:T(8,128)(2,1)S(1)}, u32[]{:S(2)}, u32[]{:S(2)}) collective-permute-start(bf16[384,256]{1,0:T(8,128)(2,1)S(1)} %shard_map.116.after), channel_id=1, source_target_pairs={{8,24},{9,25},{10,26},{11,27},{12,28},{13,29},{14,30},{15,31}} | collective-permute-start | bytes 589832 | tf_op jit(solution)/shard_map/ppermute | solution.py:966
  19.5 2.0 %collective-permute-done.4.after_up.up_b = bf16[64,128]{1,0:T(8,128)(2,1)S(1)} collective-permute-done((bf16[64,128]{1,0:T(8,128)(2,1)S(1)}, bf16[64,128]{1,0:T(8,128)(2,1)S(1)}, u32[]{:S(2)}, u32[]{:S(2)}) %collective-permute-start.4) | collective-permute-done | bytes 16416 | tf_op jit(solution)/shard_map/ppermute | solution.py:944
  21.4 1.3 %collective-permute-start.8 = (bf16[400,256]{1,0:T(8,128)(2,1)S(1)}, bf16[400,256]{1,0:T(8,128)(2,1)S(1)}, u32[]{:S(2)}, u32[]{:S(2)}) collective-permute-start(bf16[400,256]{1,0:T(8,128)(2,1)S(1)} %fusion.sums), channel_id=1, source_target_pairs={{16,24},{17,25},{18,26},{19,27},{20,28},{21,29},{22,30},{23,31}} | collective-permute-start | bytes 614408 | tf_op jit(solution)/shard_map/ppermute | solution.py:958
  22.7 1.0 %collective-permute-done.5.after_down.down_b = bf16[64,128]{1,0:T(8,128)(2,1)S(1)} collective-permute-done((bf16[64,128]{1,0:T(8,128)(2,1)S(1)}, bf16[64,128]{1,0:T(8,128)(2,1)S(1)}, u32[]{:S(2)}, u32[]{:S(2)}) %collective-permute-start.5) | collective-permute-done | bytes 16416 | tf_op jit(solution)/shard_map/ppermute | solution.py:947
  23.8 0.9 %shard_map.118 = (f32[5,256,128]{2,1,0:T(8,128)}, f32[400,256]{1,0:T(8,128)S(1)}) custom-call(f32[5,256,128]{2,1,0:T(8,128)S(1)} %bitcast.13, f32[256,128]{1,0:T(8,128)S(1)} %bitcast.21, f32[320,384]{1,0:T(8,128)S(1)} %get-tuple-element.49.state, f32[160,640]{1,0:T(8,128)S(1)} %get-tuple-element.37.inner_state, ...), custom_call_target="tpu_custom_call" | custom-call | flops 1000000000 | tf_op jit(solution)/shard_map/pallas_call | solution.py:782
  24.7 0.0 collective-permute-done.7
  24.7 0.1 fusion.2.sums
  24.8 1.3 %collective-permute-start.9 = (bf16[400,256]{1,0:T(8,128)(2,1)S(1)}, bf16[400,256]{1,0:T(8,128)(2,1)S(1)}, u32[]{:S(2)}, u32[]{:S(2)}) collective-permute-start(bf16[400,256]{1,0:T(8,128)(2,1)S(1)} %fusion.2.sums), channel_id=1, source_target_pairs={{8,24},{9,25},{10,26},{11,27},{12,28},{13,29},{14,30},{15,31}} | collective-permute-start | bytes 614408 | tf_op jit(solution)/shard_map/ppermute | solution.py:975
  26.1 0.1 shard_map.119
  26.2 0.0 collective-permute-done.6.refs_1_
  26.2 1.3 %collective-permute-start.13 = (bf16[384,256]{1,0:T(8,128)(2,1)S(1)}, bf16[384,256]{1,0:T(8,128)(2,1)S(1)}, u32[]{:S(2)}, u32[]{:S(2)}) collective-permute-start(bf16[384,256]{1,0:T(8,128)(2,1)S(1)} %shard_map.120.after), channel_id=1, source_target_pairs={{16,24},{17,25},{18,26},{19,27},{20,28},{21,29},{22,30},{23,31}} | collective-permute-start | bytes 589832 | tf_op jit(solution)/shard_map/ppermute | solution.py:987
  27.5 1.3 %collective-permute-start.10 = (bf16[64,128]{1,0:T(8,128)(2,1)S(1)}, bf16[64,128]{1,0:T(8,128)(2,1)S(1)}, u32[]{:S(2)}, u32[]{:S(2)}) collective-permute-start(bf16[64,128]{1,0:T(8,128)(2,1)S(1)} %get-tuple-element.59.refs_2_), channel_id=1, source_target_pairs={{8,25},{9,26},{10,27},{11,28},{12,29},{13,30},{14,31}} | collective-permute-start | bytes 49160 | tf_op jit(solution)/shard_map/ppermute | solution.py:944
  28.8 0.0 collective-permute-done.12.after.source_b
  28.8 1.3 %collective-permute-start.11 = (bf16[64,128]{1,0:T(8,128)(2,1)S(1)}, bf16[64,128]{1,0:T(8,128)(2,1)S(1)}, u32[]{:S(2)}, u32[]{:S(2)}) collective-permute-start(bf16[64,128]{1,0:T(8,128)(2,1)S(1)} %get-tuple-element.63), channel_id=1, source_target_pairs={{9,24},{10,25},{11,26},{12,27},{13,28},{14,29},{15,30}} | collective-permute-start | bytes 49160 | tf_op jit(solution)/shard_map/ppermute | solution.py:947
  30.1 0.8 %shard_map.121 = f32[3,256,128]{2,1,0:T(8,128)} custom-call(f32[3,256,128]{2,1,0:T(8,128)S(1)} %bitcast.16, f32[3,256,128]{2,1,0:T(8,128)S(1)} %get-tuple-element.57.mean_two, bf16[384,256]{1,0:T(8,128)(2,1)S(1)} %shard_map.120.after), custom_call_target="tpu_custom_call" | custom-call | tf_op jit(solution)/shard_map/pallas_call | solution.py:782
  30.9 0.0 collective-permute-done.8.source_a
  30.9 3.4 %collective-permute-done.10.up_a = bf16[64,128]{1,0:T(8,128)(2,1)S(1)} collective-permute-done((bf16[64,128]{1,0:T(8,128)(2,1)S(1)}, bf16[64,128]{1,0:T(8,128)(2,1)S(1)}, u32[]{:S(2)}, u32[]{:S(2)}) %collective-permute-start.10) | collective-permute-done | bytes 16416 | tf_op jit(solution)/shard_map/ppermute | solution.py:944
  34.3 0.6 %collective-permute-done.11.down_a = bf16[64,128]{1,0:T(8,128)(2,1)S(1)} collective-permute-done((bf16[64,128]{1,0:T(8,128)(2,1)S(1)}, bf16[64,128]{1,0:T(8,128)(2,1)S(1)}, u32[]{:S(2)}, u32[]{:S(2)}) %collective-permute-start.11) | collective-permute-done | bytes 16416 | tf_op jit(solution)/shard_map/ppermute | solution.py:947
  34.9 0.0 collective-permute-done.9.source_b
  34.9 2.0 %shard_map.122 = (f32[512,128]{1,0:T(8,128)S(1)}, f32[3,512,128]{2,1,0:T(8,128)S(1)}, f32[8,256]{1,0:T(8,128)S(1)}) custom-call(f32[1024,128]{1,0:T(8,128)S(1)} %get-tuple-element.60.base, f32[3,1024,128]{2,1,0:T(8,128)S(1)} %get-tuple-element.61.grads, bf16[6,384,256]{2,1,0:T(8,128)(2,1)S(1)} %get-tuple-element.62.hot_two, s32[6,1,256]{2,1,0:T(1,128)S(1)} %bitcast.27, ...), custom_call_target="tpu_custom_call" | custom-call | flops 1000000000 | tf_op jit(solution)/shard_map/pallas_call | solution.py:782
  36.9 0.0 collective-permute-done.13.source_a
  36.9 0.9 %shard_map.123 = f32[4,64,256]{2,1,0:T(8,128)} custom-call(f32[4,64,256]{2,1,0:T(8,128)S(1)} %bitcast.24, f32[512,128]{1,0:T(8,128)S(1)} %get-tuple-element.64.base, f32[3,512,128]{2,1,0:T(8,128)S(1)} %get-tuple-element.65.grads, f32[8,256]{1,0:T(8,128)S(1)} %get-tuple-element.66.scale, bf16[384,256]{1,0:T(8,128)(2,1)S(1)} %collective-permute-done.13.source_a, ...), custom_call_target="tpu_custom_call" | custom-call | flops 100000000 | bytes 1974272 | tf_op jit(solution)/shard_map/pallas_call | solution.py:782
  (13 shorter events, 0.1 us)
Async XLA Ops:
  0.6 5.7 %copy-start = (f32[1,5,256,128]{3,2,1,0:T(8,128)S(1)}, f32[1,5,256,128]{3,2,1,0:T(8,128)}, u32[]{:S(2)}) copy-start(f32[1,5,256,128]{3,2,1,0:T(8,128)} %param.9) | copy-start | bytes 1966084
  0.6 5.7 %copy-start.2 = (f32[1,256,128]{2,1,0:T(8,128)S(1)}, f32[1,256,128]{2,1,0:T(8,128)}, u32[]{:S(2)}) copy-start(f32[1,256,128]{2,1,0:T(8,128)} %param.11) | copy-start | bytes 393220
  0.7 5.7 %copy-start.7 = (s32[1,4,256]{2,1,0:T(4,128)S(1)}, s32[1,4,256]{2,1,0:T(4,128)}, u32[]{:S(2)}) copy-start(s32[1,4,256]{2,1,0:T(4,128)} %param.12) | copy-start | bytes 12292
  0.7 5.7 %copy-start.8 = (s32[1,256]{1,0:T(1,128)S(1)}, s32[1,256]{1,0:T(1,128)}, u32[]{:S(2)}) copy-start(s32[1,256]{1,0:T(1,128)} %target.1) | copy-start | bytes 3076
  0.7 8.1 %copy-start.1 = (f32[1,3,256,128]{3,2,1,0:T(8,128)S(1)}, f32[1,3,256,128]{3,2,1,0:T(8,128)}, u32[]{:S(2)}) copy-start(f32[1,3,256,128]{3,2,1,0:T(8,128)} %param.10) | copy-start | bytes 1179652
  0.7 8.1 %copy-start.3 = (f32[1,4,64,256]{3,2,1,0:T(8,128)S(1)}, f32[1,4,64,256]{3,2,1,0:T(8,128)}, u32[]{:S(2)}) copy-start(f32[1,4,64,256]{3,2,1,0:T(8,128)} %param.15) | copy-start | bytes 786436
  0.7 8.1 %copy-start.4 = (f32[64,128]{1,0:T(8,128)S(1)}, f32[64,128]{1,0:T(8,128)}, u32[]{:S(2)}) copy-start(f32[64,128]{1,0:T(8,128)} %projector.3) | copy-start | bytes 98308
  0.7 8.1 %copy-start.5 = (s32[1,6,256]{2,0,1:T(1,128)S(1)}, s32[1,6,256]{2,0,1:T(1,128)}, u32[]{:S(2)}) copy-start(s32[1,6,256]{2,0,1:T(1,128)} %param.16) | copy-start | bytes 18436
  0.7 8.1 %copy-start.6 = (s32[1,6,256]{2,0,1:T(1,128)S(1)}, s32[1,6,256]{2,0,1:T(1,128)}, u32[]{:S(2)}) copy-start(s32[1,6,256]{2,0,1:T(1,128)} %param.17) | copy-start | bytes 18436
  2.5 6.2 %collective-permute-start = (bf16[304,128]{1,0:T(8,128)(2,1)}, bf16[304,128]{1,0:T(8,128)(2,1)S(1)}, u32[]{:S(2)}, u32[]{:S(2)}) collective-permute-start(bf16[304,128]{1,0:T(8,128)(2,1)} %get-tuple-element.35), channel_id=1, source_target_pairs={{1,2},{2,1},{3,4},{4,3},{5,6},{6,5},{9,10},{10,9},{11,12},{12,11},... | collective-permute-start | bytes 233480 | tf_op jit(solution)/shard_map/ppermute | solution.py:840
  6.3 2.4 %collective-permute-start.1 = (bf16[304,128]{1,0:T(8,128)(2,1)}, bf16[304,128]{1,0:T(8,128)(2,1)S(1)}, u32[]{:S(2)}, u32[]{:S(2)}) collective-permute-start(bf16[304,128]{1,0:T(8,128)(2,1)} %get-tuple-element.36), channel_id=1, source_target_pairs={{0,1},{1,0},{2,3},{3,2},{4,5},{5,4},{6,7},{7,6},{8,9},{9,8},{10,11... | collective-permute-start | bytes 233480 | tf_op jit(solution)/shard_map/ppermute | solution.py:841
  12.5 1.4 %collective-permute-start.3 = (bf16[400,256]{1,0:T(8,128)(2,1)S(1)}, bf16[400,256]{1,0:T(8,128)(2,1)S(1)}, u32[]{:S(2)}, u32[]{:S(2)}) collective-permute-start(bf16[400,256]{1,0:T(8,128)(2,1)S(1)} %get-tuple-element.53), channel_id=1, source_target_pairs={{0,1},{1,2},{2,3},{3,4},{4,5},{5,6},{6,7},{8,9},{9,10},{10,11},{11... | collective-permute-start | bytes 614408 | tf_op jit(solution)/shard_map/ppermute | solution.py:904
  13.3 4.2 %collective-permute-start.2 = (bf16[384,256]{1,0:T(8,128)(2,1)S(1)}, bf16[384,256]{1,0:T(8,128)(2,1)S(1)}, u32[]{:S(2)}, u32[]{:S(2)}) collective-permute-start(bf16[384,256]{1,0:T(8,128)(2,1)S(1)} %get-tuple-element.51), channel_id=1, source_target_pairs={{0,1},{1,2},{2,3},{3,4},{4,5},{5,6},{6,7},{8,9},{9,10},{10,11},{11... | collective-permute-start | bytes 589832 | tf_op jit(solution)/shard_map/ppermute | solution.py:904
  14.1 10.5 %collective-permute-start.7 = (bf16[400,256]{1,0:T(8,128)(2,1)S(1)}, bf16[400,256]{1,0:T(8,128)(2,1)S(1)}, u32[]{:S(2)}, u32[]{:S(2)}) collective-permute-start(bf16[400,256]{1,0:T(8,128)(2,1)S(1)} %fusion.sums), channel_id=1, source_target_pairs={{0,8},{1,9},{2,10},{3,11},{4,12},{5,13},{6,14},{7,15}} | collective-permute-start | bytes 614408 | tf_op jit(solution)/shard_map/ppermute | solution.py:954
  14.8 6.6 %collective-permute-start.4 = (bf16[64,128]{1,0:T(8,128)(2,1)S(1)}, bf16[64,128]{1,0:T(8,128)(2,1)S(1)}, u32[]{:S(2)}, u32[]{:S(2)}) collective-permute-start(bf16[64,128]{1,0:T(8,128)(2,1)S(1)} %get-tuple-element.54), channel_id=1, source_target_pairs={{16,25},{17,26},{18,27},{19,28},{20,29},{21,30},{22,31}} | collective-permute-start | bytes 49160 | tf_op jit(solution)/shard_map/ppermute | solution.py:944
  16.1 7.6 %collective-permute-start.5 = (bf16[64,128]{1,0:T(8,128)(2,1)S(1)}, bf16[64,128]{1,0:T(8,128)(2,1)S(1)}, u32[]{:S(2)}, u32[]{:S(2)}) collective-permute-start(bf16[64,128]{1,0:T(8,128)(2,1)S(1)} %get-tuple-element.55), channel_id=1, source_target_pairs={{17,24},{18,25},{19,26},{20,27},{21,28},{22,29},{23,30}} | collective-permute-start | bytes 49160 | tf_op jit(solution)/shard_map/ppermute | solution.py:947
  17.5 8.7 %collective-permute-start.6 = (bf16[384,256]{1,0:T(8,128)(2,1)S(1)}, bf16[384,256]{1,0:T(8,128)(2,1)S(1)}, u32[]{:S(2)}, u32[]{:S(2)}) collective-permute-start(bf16[384,256]{1,0:T(8,128)(2,1)S(1)} %add_convert_fusion.refs_1_), channel_id=1, source_target_pairs={{0,16},{1,17},{2,18},{3,19},{4,20},{5,21},{6,22},{7,23}} | collective-permute-start | bytes 589832 | tf_op jit(solution)/shard_map/ppermute | solution.py:957
  18.2 10.6 %collective-permute-start.12 = (bf16[384,256]{1,0:T(8,128)(2,1)S(1)}, bf16[384,256]{1,0:T(8,128)(2,1)S(1)}, u32[]{:S(2)}, u32[]{:S(2)}) collective-permute-start(bf16[384,256]{1,0:T(8,128)(2,1)S(1)} %shard_map.116.after), channel_id=1, source_target_pairs={{8,24},{9,25},{10,26},{11,27},{12,28},{13,29},{14,30},{15,31}} | collective-permute-start | bytes 589832 | tf_op jit(solution)/shard_map/ppermute | solution.py:966
  21.4 9.5 %collective-permute-start.8 = (bf16[400,256]{1,0:T(8,128)(2,1)S(1)}, bf16[400,256]{1,0:T(8,128)(2,1)S(1)}, u32[]{:S(2)}, u32[]{:S(2)}) collective-permute-start(bf16[400,256]{1,0:T(8,128)(2,1)S(1)} %fusion.sums), channel_id=1, source_target_pairs={{16,24},{17,25},{18,26},{19,27},{20,28},{21,29},{22,30},{23,31}} | collective-permute-start | bytes 614408 | tf_op jit(solution)/shard_map/ppermute | solution.py:958
  24.8 10.1 %collective-permute-start.9 = (bf16[400,256]{1,0:T(8,128)(2,1)S(1)}, bf16[400,256]{1,0:T(8,128)(2,1)S(1)}, u32[]{:S(2)}, u32[]{:S(2)}) collective-permute-start(bf16[400,256]{1,0:T(8,128)(2,1)S(1)} %fusion.2.sums), channel_id=1, source_target_pairs={{8,24},{9,25},{10,26},{11,27},{12,28},{13,29},{14,30},{15,31}} | collective-permute-start | bytes 614408 | tf_op jit(solution)/shard_map/ppermute | solution.py:975
  26.2 10.7 %collective-permute-start.13 = (bf16[384,256]{1,0:T(8,128)(2,1)S(1)}, bf16[384,256]{1,0:T(8,128)(2,1)S(1)}, u32[]{:S(2)}, u32[]{:S(2)}) collective-permute-start(bf16[384,256]{1,0:T(8,128)(2,1)S(1)} %shard_map.120.after), channel_id=1, source_target_pairs={{16,24},{17,25},{18,26},{19,27},{20,28},{21,29},{22,30},{23,31}} | collective-permute-start | bytes 589832 | tf_op jit(solution)/shard_map/ppermute | solution.py:987
  27.5 6.8 %collective-permute-start.10 = (bf16[64,128]{1,0:T(8,128)(2,1)S(1)}, bf16[64,128]{1,0:T(8,128)(2,1)S(1)}, u32[]{:S(2)}, u32[]{:S(2)}) collective-permute-start(bf16[64,128]{1,0:T(8,128)(2,1)S(1)} %get-tuple-element.59.refs_2_), channel_id=1, source_target_pairs={{8,25},{9,26},{10,27},{11,28},{12,29},{13,30},{14,31}} | collective-permute-start | bytes 49160 | tf_op jit(solution)/shard_map/ppermute | solution.py:944
  28.8 6.1 %collective-permute-start.11 = (bf16[64,128]{1,0:T(8,128)(2,1)S(1)}, bf16[64,128]{1,0:T(8,128)(2,1)S(1)}, u32[]{:S(2)}, u32[]{:S(2)}) collective-permute-start(bf16[64,128]{1,0:T(8,128)(2,1)S(1)} %get-tuple-element.63), channel_id=1, source_target_pairs={{9,24},{10,25},{11,26},{12,27},{13,28},{14,29},{15,30}} | collective-permute-start | bytes 49160 | tf_op jit(solution)/shard_map/ppermute | solution.py:947
